TPU v7x, 512 devices: a whole 4x8x8 slice. The times are simulated.
512 devices in a mesh: member: 32 (over z_hi, x, core), fsdp: 16 (over y, z_lo).
Axes of the slice: x: 4, y: 8, z: 8 (z_hi: 4, z_lo: 2; z = z_hi * 2 + z_lo), core: 2. Of those that a mesh axis runs over, the one named last changes fastest.
Arguments:
- attention_out: bfloat16 [32, 2048, 2048], P('member', 'fsdp'), may hold values from -6 to 6
- residual: bfloat16 [32, 2048, 2048], P('member', 'fsdp'), may hold values from -6 to 6
- upstream: bfloat16 [32, 2048, 2048], P('member', 'fsdp'), may hold values from -6 to 6
- norm_gain: bfloat16 [32, 2048], P('member', 'fsdp'), may hold values from 0.099609375 to 1.8984375
- weight: bfloat16 [32, 2048, 2048], P('member', None, 'fsdp'), may hold values from -6 to 6
- first_moment: bfloat16 [32, 2048, 2048], P('member', None, 'fsdp'), may hold values from -4 to 4
- second_moment: bfloat16 [32, 2048, 2048], P('member', None, 'fsdp'), may hold values from 0.049804688 to 2
- sources: int32 [32], replicated, may hold values from 0 to 31, as said below
- rate_index: int32 [32], P('member'), may hold values from 0 to 4
Outputs:
- new_weight: bfloat16 [32, 2048, 2048], P('member', None, 'fsdp')
- new_first: bfloat16 [32, 2048, 2048], P('member', None, 'fsdp')
- new_second: bfloat16 [32, 2048, 2048], P('member', None, 'fsdp')
Inputs may be any that keep to these rules, and one draw needn't show every extreme that they name: `sources`: 8 members take the state of as many distinct other members, which keep their own; every other member names itself.
All inputs are finite; a program needn't handle non-finite values.
Results may differ from a plain program's by a relative error of at most 0.005.
Values may be sent and summed in bfloat16 or wider, within the bound.
No kernel may reach another device: no remote copies, remote signals or barrier semaphores. Data moves between devices by JAX's collectives and lax.ppermute only.
A program may use at most 64 MiB of HBM per device.

v0:
```python
import math

import jax
import jax.numpy as jnp
from jax import lax
from jax.sharding import PartitionSpec as P

EPS = 1e-06
ADAM_EPS = 1e-08
BETA_ONE = 0.9
BETA_TWO = 0.95
DECAY = 0.1
bias_one = 1.0 - 0.9**10
bias_two = 1.0 - 0.95**10
RATE_TABLE = (0.02, 0.032, 0.05, 0.08, 0.125)


def split_members(array, members):
    return array.reshape(members, array.shape[0] // members, array.shape[1])


def join_members(array):
    return array.reshape(array.shape[0] * array.shape[1], array.shape[2])


def adamw_update(weight_now, first_now, second_now, gradient, rate_value):
    first_sum = BETA_ONE * first_now.astype(jnp.float32) + (1.0 - BETA_ONE) * gradient
    second_sum = BETA_TWO * second_now.astype(jnp.float32) + (1.0 - BETA_TWO) * gradient * gradient
    update = first_sum / bias_one / (jnp.sqrt(second_sum / bias_two) + ADAM_EPS)
    weight_new = weight_now.astype(jnp.float32) * (1.0 - rate_value * DECAY) - rate_value * update
    return (
        weight_new.astype(jnp.bfloat16),
        first_sum.astype(jnp.bfloat16),
        second_sum.astype(jnp.bfloat16),
    )


def local(
    attention_out,
    residual,
    upstream,
    norm_gain,
    weight,
    first_moment,
    second_moment,
    sources,
    rate_index,
):
    members = lax.axis_size("member")
    shards = lax.axis_size("fsdp")
    weight_here = weight[0]
    first_here = first_moment[0]
    second_here = second_moment[0]
    outward = (
        lax.all_to_all(
            split_members(weight_here, members), "member", split_axis=0, concat_axis=0, tiled=True
        ),
        lax.all_to_all(
            split_members(first_here, members), "member", split_axis=0, concat_axis=0, tiled=True
        ),
        lax.all_to_all(
            split_members(second_here, members), "member", split_axis=0, concat_axis=0, tiled=True
        ),
    )
    picked = (outward[0][sources], outward[1][sources], outward[2][sources])
    returned = (
        lax.all_to_all(picked[0], "member", split_axis=0, concat_axis=0, tiled=True),
        lax.all_to_all(picked[1], "member", split_axis=0, concat_axis=0, tiled=True),
        lax.all_to_all(picked[2], "member", split_axis=0, concat_axis=0, tiled=True),
    )
    weight_here = join_members(returned[0])
    first_here = join_members(returned[1])
    second_here = join_members(returned[2])
    inv_scale = 1.0 / math.sqrt(weight_here.shape[0])
    local_rows = attention_out[0]
    resid_cols, upstream_cols = (
        lax.all_to_all(residual[0], "fsdp", split_axis=1, concat_axis=0, tiled=True),
        lax.all_to_all(upstream[0], "fsdp", split_axis=1, concat_axis=0, tiled=True),
    )
    gathered = lax.all_gather(local_rows, "fsdp", axis=0, tiled=True)
    linear = jnp.dot(gathered, weight_here, preferred_element_type=jnp.float32)
    hidden_sum = resid_cols.astype(jnp.float32) + linear * inv_scale
    scaled = upstream_cols.astype(jnp.float32) * norm_gain[0].astype(jnp.float32)[None, :]
    feature_count = hidden_sum.shape[1] * shards
    squares = lax.psum(jnp.sum(hidden_sum * hidden_sum, axis=1), "fsdp")
    inverse = lax.rsqrt(squares / feature_count + EPS)[:, None]
    normed = hidden_sum * inverse
    inner_sums = lax.psum(jnp.sum(scaled * normed, axis=1), "fsdp")[:, None]
    delta_rows = (scaled * inverse - normed * (inner_sums / feature_count) * inverse).astype(
        jnp.bfloat16
    )
    gradient = (
        lax.dot_general(
            gathered, delta_rows, (((0,), (0,)), ((), ())), preferred_element_type=jnp.float32
        )
        * inv_scale
    )
    rate_table = jnp.asarray(RATE_TABLE, dtype=jnp.float32)
    rate_value = jnp.sum(jnp.where(jnp.arange(5) == rate_index[0], rate_table, 0.0))
    weight_new, first_new, second_new = adamw_update(
        weight_here, first_here, second_here, gradient, rate_value
    )
    return (weight_new[None], first_new[None], second_new[None])


def solution(mesh):
    in_specs = (
        P("member", "fsdp", None),
        P("member", "fsdp", None),
        P("member", "fsdp", None),
        P("member", "fsdp"),
        P("member", None, "fsdp"),
        P("member", None, "fsdp"),
        P("member", None, "fsdp"),
        P(),
        P("member"),
    )
    out_specs = (P("member", None, "fsdp"), P("member", None, "fsdp"), P("member", None, "fsdp"))
    return jax.shard_map(local, mesh=mesh, in_specs=in_specs, out_specs=out_specs, check_vma=False)
```

profile of v0, /device:TPU:64, one launch (start us, length us, event | category | flops | bytes accessed | tf_op | source)
XLA Modules:
  0.0 368.2 jit_solution(11376855881887123218)
XLA Ops:
  7.9 1.3 copy.29
  9.2 24.2 %all_to_all.56 = bf16[128,16,128]{0,2,1:T(8,128)(2,1)S(1)} all-to-all(bf16[128,16,128]{0,2,1:T(8,128)(2,1)S(1)} %bitcast.77), channel_id=1, replica_groups=mesh['member'=32,'fsdp'=16] {'fsdp'}, dimensions={1} | all-to-all | bytes 1048576 | tf_op jit(solution)/shard_map/all_to_all | solution.py:77
  33.4 41.5 %all_to_all.57 = bf16[32,64,128]{2,1,0:T(8,128)(2,1)S(1)} all-to-all(bf16[32,64,128]{2,1,0:T(8,128)(2,1)} %bitcast.78), channel_id=1, replica_groups=mesh['member'=32,'fsdp'=16] {'member'}, dimensions={0} | all-to-all | bytes 1048576 | tf_op jit(solution)/shard_map/all_to_all | solution.py:55
  74.9 36.8 %all_to_all.58 = bf16[32,64,128]{2,1,0:T(8,128)(2,1)S(1)} all-to-all(bf16[32,64,128]{2,1,0:T(8,128)(2,1)} %bitcast.79), channel_id=1, replica_groups=mesh['member'=32,'fsdp'=16] {'member'}, dimensions={0} | all-to-all | bytes 1048576 | tf_op jit(solution)/shard_map/all_to_all | solution.py:58
  111.8 7.2 %all-to-all-start.6 = ((bf16[32,64,128]{2,1,0:T(8,128)(2,1)}), bf16[32,64,128]{2,1,0:T(8,128)(2,1)S(1)}, u32[]{:S(2)}, u32[]{:S(2)}) async-start(bf16[32,64,128]{2,1,0:T(8,128)(2,1)} %bitcast.80), calls=%async_computation.6 | async-start | bytes 1048576 | tf_op jit(solution)/shard_map/all_to_all | solution.py:61
  119.7 1.4 gather_fusion
  121.1 25.3 %all-to-all-done.6 = bf16[32,64,128]{2,1,0:T(8,128)(2,1)S(1)} async-done(((bf16[32,64,128]{2,1,0:T(8,128)(2,1)}), bf16[32,64,128]{2,1,0:T(8,128)(2,1)S(1)}, u32[]{:S(2)}, u32[]{:S(2)}) %all-to-all-start.6) | async-done | bytes 524320 | tf_op jit(solution)/shard_map/all_to_all | solution.py:61
  146.4 8.4 %all-to-all-start.1 = ((bf16[32,64,128]{2,1,0:T(8,128)(2,1)}), bf16[32,64,128]{2,1,0:T(8,128)(2,1)S(1)}, u32[]{:S(2)}, u32[]{:S(2)}) async-start(bf16[32,64,128]{2,1,0:T(8,128)(2,1)} %gather_fusion), calls=%async_computation.1 | async-start | bytes 1048576 | tf_op jit(solution)/shard_map/all_to_all | solution.py:67
  154.8 1.4 gather_fusion.2
  156.2 27.2 %all-to-all-done.1 = bf16[32,64,128]{2,1,0:T(8,128)(2,1)S(1)} async-done(((bf16[32,64,128]{2,1,0:T(8,128)(2,1)}), bf16[32,64,128]{2,1,0:T(8,128)(2,1)S(1)}, u32[]{:S(2)}, u32[]{:S(2)}) %all-to-all-start.1) | async-done | bytes 524320 | tf_op jit(solution)/shard_map/all_to_all | solution.py:67
  183.4 7.5 %all-to-all-start.7 = ((bf16[32,64,128]{2,1,0:T(8,128)(2,1)}), bf16[32,64,128]{2,1,0:T(8,128)(2,1)S(1)}, u32[]{:S(2)}, u32[]{:S(2)}) async-start(bf16[32,64,128]{2,1,0:T(8,128)(2,1)} %gather_fusion.2), calls=%async_computation.7 | async-start | bytes 1048576 | tf_op jit(solution)/shard_map/all_to_all | solution.py:69
  190.9 1.4 gather_fusion.1
  192.3 27.1 %all-to-all-done.7 = bf16[32,64,128]{2,1,0:T(8,128)(2,1)S(1)} async-done(((bf16[32,64,128]{2,1,0:T(8,128)(2,1)}), bf16[32,64,128]{2,1,0:T(8,128)(2,1)S(1)}, u32[]{:S(2)}, u32[]{:S(2)}) %all-to-all-start.7) | async-done | bytes 524320 | tf_op jit(solution)/shard_map/all_to_all | solution.py:69
  219.4 6.3 %all-to-all-start.3 = ((bf16[32,64,128]{2,1,0:T(8,128)(2,1)}), bf16[32,64,128]{2,1,0:T(8,128)(2,1)S(1)}, u32[]{:S(2)}, u32[]{:S(2)}) async-start(bf16[32,64,128]{2,1,0:T(8,128)(2,1)} %gather_fusion.1), calls=%async_computation.3 | async-start | bytes 1048576 | tf_op jit(solution)/shard_map/all_to_all | solution.py:68
  228.8 1.4 copy.32
  230.2 26.2 %all-to-all-done.3 = bf16[32,64,128]{2,1,0:T(8,128)(2,1)S(1)} async-done(((bf16[32,64,128]{2,1,0:T(8,128)(2,1)}), bf16[32,64,128]{2,1,0:T(8,128)(2,1)S(1)}, u32[]{:S(2)}, u32[]{:S(2)}) %all-to-all-start.3) | async-done | bytes 524320 | tf_op jit(solution)/shard_map/all_to_all | solution.py:68
  256.4 5.9 %all-to-all-start.4 = ((bf16[128,16,128]{0,2,1:T(8,128)(2,1)}), bf16[128,16,128]{0,2,1:T(8,128)(2,1)S(1)}, u32[]{:S(2)}, u32[]{:S(2)}) async-start(bf16[128,16,128]{0,2,1:T(8,128)(2,1)} %bitcast.76), calls=%async_computation.4 | async-start | bytes 1048576 | tf_op jit(solution)/shard_map/all_to_all | solution.py:78
  262.4 1.3 copy.31
  263.9 7.0 %all-gather.3.cloned.1.call-done = bf16[1,2048,2048]{2,1,0:T(8,128)(2,1)} async-done(((bf16[1,128,2048]{2,1,0:T(8,128)(2,1)}), bf16[1,2048,2048]{2,1,0:T(8,128)(2,1)}) %all-gather.3.cloned.1.call-update) | async-done | bytes 8388624 | tf_op jit(solution)/shard_map/all_gather | solution.py:80
  270.8 6.4 %multiply_reduce_fusion.1 = (f32[2048]{0:T(1024)S(1)}, f32[2048,128]{0,1:T(8,128)S(1)}) fusion(bf16[2048,128]{1,0:T(8,128)(2,1)S(1)} %bitcast.73, bf16[1,2048,2048]{2,1,0:T(8,128)(2,1)} %all-gather.3.cloned.1.call-done, bf16[128,16,128]{0,2,1:T(8,128)(2,1)S(1)} %all_to_all.56), kind=kOutput, calls=%fused_computation.19 | convolution fusion | flops 1075050496 | bytes 10493952 | tf_op jit(solution)/shard_map/dot_general | solution.py:81
  277.2 37.0 %psum.14 = f32[2048]{0:T(1024)S(1)} all-reduce(f32[2048]{0:T(1024)S(1)} %get-tuple-element.15), channel_id=1, replica_groups=mesh['member'=32,'fsdp'=16] {'fsdp'}, use_global_device_ids=true, to_apply=%region_2.0 | all-reduce | flops 2048 | bytes 16384 | tf_op jit(solution)/shard_map/psum | solution.py:85
  314.5 35.2 %psum.15 = f32[2048]{0:T(1024)S(1)} all-reduce(f32[2048]{0:T(1024)S(1)} %multiply_reduce_fusion), channel_id=1, replica_groups=mesh['member'=32,'fsdp'=16] {'fsdp'}, use_global_device_ids=true, to_apply=%region_4.5 | all-reduce | flops 2048 | bytes 16384 | tf_op jit(solution)/shard_map/psum | solution.py:88
  349.7 7.6 %convert_bitcast_fusion.2 = (bf16[1,2048,128]{1,2,0:T(8,128)(2,1)}, bf16[1,2048,128]{1,2,0:T(8,128)(2,1)S(1)}, bf16[1,2048,128]{1,2,0:T(8,128)(2,1)S(1)}) fusion(f32[2048,128]{0,1:T(8,128)} %copy.32, f32[2048,128]{0,1:T(8,128)} %copy.31, f32[]{:T(128)} %fusion.17, f32[]{:T(128)S(6)} %sub.9, bf16[2048,128]{0,1:T(8,128)(2,1)S(1)} %copy.26, ...), kind=kOutput, calls=%fused_computation.21 | convolution fusion | flops 1080295424 | bytes 14172680 | tf_op jit(solution)/shard_map/dot_general | solution.py:93
  357.3 2.0 copy.35
  (22 shorter events, 5.7 us)
Async XLA Ops:
  7.2 220.2 %copy-start.2 = (f32[5]{0:T(128)S(1)}, f32[5]{0:T(128)}, u32[]{:S(2)}) copy-start(f32[5]{0:T(128)} %constant.39.clone) | copy-start | bytes 64
  7.2 219.2 %copy-start = (bf16[1,128,2048]{2,1,0:T(8,128)(2,1)S(1)}, bf16[1,128,2048]{2,1,0:T(8,128)(2,1)}, u32[]{:S(2)}) copy-start(bf16[1,128,2048]{2,1,0:T(8,128)(2,1)} %param.12) | copy-start | bytes 1572868
  7.2 221.5 %copy-start.1 = (bf16[1,128]{1,0:T(2,128)(2,1)S(1)}, bf16[1,128]{1,0:T(2,128)(2,1)}, u32[]{:S(2)}) copy-start(bf16[1,128]{1,0:T(2,128)(2,1)} %param.13) | copy-start | bytes 772
  7.2 263.6 %all-gather.3.cloned.1.call-start = ((), (), s32[]{:S(2)}) async-start(), calls=%async_computation.8 | async-start | bytes 8912896 | tf_op jit(solution)/shard_map/all_gather | solution.py:80
  111.8 34.6 %all-to-all-start.6 = ((bf16[32,64,128]{2,1,0:T(8,128)(2,1)}), bf16[32,64,128]{2,1,0:T(8,128)(2,1)S(1)}, u32[]{:S(2)}, u32[]{:S(2)}) async-start(bf16[32,64,128]{2,1,0:T(8,128)(2,1)} %bitcast.80), calls=%async_computation.6 | async-start | bytes 1048576 | tf_op jit(solution)/shard_map/all_to_all | solution.py:61
  146.4 37.0 %all-to-all-start.1 = ((bf16[32,64,128]{2,1,0:T(8,128)(2,1)}), bf16[32,64,128]{2,1,0:T(8,128)(2,1)S(1)}, u32[]{:S(2)}, u32[]{:S(2)}) async-start(bf16[32,64,128]{2,1,0:T(8,128)(2,1)} %gather_fusion), calls=%async_computation.1 | async-start | bytes 1048576 | tf_op jit(solution)/shard_map/all_to_all | solution.py:67
  183.4 36.0 %all-to-all-start.7 = ((bf16[32,64,128]{2,1,0:T(8,128)(2,1)}), bf16[32,64,128]{2,1,0:T(8,128)(2,1)S(1)}, u32[]{:S(2)}, u32[]{:S(2)}) async-start(bf16[32,64,128]{2,1,0:T(8,128)(2,1)} %gather_fusion.2), calls=%async_computation.7 | async-start | bytes 1048576 | tf_op jit(solution)/shard_map/all_to_all | solution.py:69
  219.4 37.0 %all-to-all-start.3 = ((bf16[32,64,128]{2,1,0:T(8,128)(2,1)}), bf16[32,64,128]{2,1,0:T(8,128)(2,1)S(1)}, u32[]{:S(2)}, u32[]{:S(2)}) async-start(bf16[32,64,128]{2,1,0:T(8,128)(2,1)} %gather_fusion.1), calls=%async_computation.3 | async-start | bytes 1048576 | tf_op jit(solution)/shard_map/all_to_all | solution.py:68
  256.4 57.9 %all-to-all-start.4 = ((bf16[128,16,128]{0,2,1:T(8,128)(2,1)}), bf16[128,16,128]{0,2,1:T(8,128)(2,1)S(1)}, u32[]{:S(2)}, u32[]{:S(2)}) async-start(bf16[128,16,128]{0,2,1:T(8,128)(2,1)} %bitcast.76), calls=%async_computation.4 | async-start | bytes 1048576 | tf_op jit(solution)/shard_map/all_to_all | solution.py:78
Sparse Core Ops, SparseCore 0:
  10.1 260.6 all-gather.2
where the time goes:
time: 369 us; the launch traced here: 368 us
  blocking collectives  175 us (47%)
  waiting for transfers between devices  113 us (31%)
  starting transfers between devices  35.4 us (10%)
  between operations  15.5 us (4%)
  matrix products  14 us (4%)
  local copies, waits for them, and re-layouts  13.5 us (4%)
    all_to_all x1, blocking collectives, local(): lax.all_to_all(split_members(weight_here, members), 'member', split_axis=...  41.5 us
    psum x1, blocking collectives, local(): squares = lax.psum(jnp.sum(hidden_sum * hidden_sum, axis=1), 'fsdp')  37 us
    all_to_all x1, blocking collectives, local(): lax.all_to_all(split_members(first_here, members), 'member', split_axis=0...  36.8 us
    psum x1, blocking collectives, local(): inner_sums = lax.psum(jnp.sum(scaled * normed, axis=1), 'fsdp')[:, None]  35.2 us
    all_to_all x1, waiting for transfers between devices, local(): lax.all_to_all(picked[0], 'member', split_axis=0, concat_axis=0, tiled=True)  27.2 us
    all_to_all x1, waiting for transfers between devices, local(): lax.all_to_all(picked[2], 'member', split_axis=0, concat_axis=0, tiled=True)  27.1 us
    all_to_all x1, waiting for transfers between devices, local(): lax.all_to_all(picked[1], 'member', split_axis=0, concat_axis=0, tiled=True)  26.2 us
    all_to_all x1, waiting for transfers between devices, local(): lax.all_to_all(split_members(second_here, members), 'member', split_axis=...  25.3 us
  transfers between devices with their start and end apart: 6, of which 5 were waited for; matrix products, arithmetic and copies ran while one was open for 5% of the time, Pallas kernels for 0%

commit v1 on v0

v1 whole, which is shorter than its diff:
```python
import math

import jax
import jax.numpy as jnp
from jax import lax
from jax.sharding import Mesh
from jax.sharding import PartitionSpec as P

EPS = 1e-06
ADAM_EPS = 1e-08
BETA_ONE = 0.9
BETA_TWO = 0.95
DECAY = 0.1
bias_one = 1.0 - 0.9**10
bias_two = 1.0 - 0.95**10
RATE_TABLE = (0.02, 0.032, 0.05, 0.08, 0.125)
MINOR = 2


def adamw_update(weight_now, first_now, second_now, gradient, rate_value):
    first_sum = BETA_ONE * first_now.astype(jnp.float32) + (1.0 - BETA_ONE) * gradient
    second_sum = BETA_TWO * second_now.astype(jnp.float32) + (1.0 - BETA_TWO) * gradient * gradient
    update = first_sum / bias_one / (jnp.sqrt(second_sum / bias_two) + ADAM_EPS)
    weight_new = weight_now.astype(jnp.float32) * (1.0 - rate_value * DECAY) - rate_value * update
    return (
        weight_new.astype(jnp.bfloat16),
        first_sum.astype(jnp.bfloat16),
        second_sum.astype(jnp.bfloat16),
    )


def swap_minor(array):
    return lax.ppermute(array, "minor", [(0, 1), (1, 0)])


def sum_over_major(array):
    size = lax.axis_size("major")
    total = array
    parts = [
        lax.ppermute(array, "major", [(i, (i + shift) % size) for i in range(size)])
        for shift in range(1, size)
    ]
    for part in parts:
        total = total + part
    return total


def exchange(array, sources):
    out = lax.all_to_all(array, "member", split_axis=0, concat_axis=0, tiled=True)
    return lax.all_to_all(out[sources], "member", split_axis=0, concat_axis=0, tiled=True)


def local(
    attention_out,
    residual,
    upstream,
    norm_gain,
    weight,
    first_moment,
    second_moment,
    sources,
    rate_index,
):
    members = lax.axis_size("member")
    major = lax.axis_size("major")
    minor = lax.axis_index("minor")
    depth, width = weight.shape[1:]
    rows = depth // members
    tokens, features = residual.shape[1:]
    block = features // major

    weight_here = exchange(weight[0].reshape(members, rows, width), sources)
    moments = jnp.stack(
        (first_moment[0].reshape(members, rows, width), second_moment[0].reshape(members, rows, width)),
        axis=1,
    )
    moments = exchange(moments, sources)
    weight_here = weight_here.reshape(depth, width)
    first_here = moments[:, 0].reshape(depth, width)
    second_here = moments[:, 1].reshape(depth, width)

    gathered = lax.all_gather(attention_out[0], "major", axis=0, tiled=True)
    stream = jnp.stack(
        (
            residual[0].reshape(tokens, major, block).transpose(1, 0, 2),
            upstream[0].reshape(tokens, major, block).transpose(1, 0, 2),
        ),
        axis=1,
    )
    stream = lax.all_to_all(stream, "major", split_axis=0, concat_axis=0, tiled=True)
    resid_cols = stream[:, 0].reshape(major * tokens, block)
    upstream_cols = stream[:, 1].reshape(major * tokens, block)

    gain_other = swap_minor(norm_gain[0])
    weight_other = swap_minor(weight_here)
    first_half = minor == 0
    gain = jnp.where(
        first_half,
        jnp.concatenate((norm_gain[0], gain_other)),
        jnp.concatenate((gain_other, norm_gain[0])),
    )
    weight_both = jnp.where(
        first_half,
        jnp.concatenate((weight_here, weight_other), axis=1),
        jnp.concatenate((weight_other, weight_here), axis=1),
    )

    inv_scale = 1.0 / math.sqrt(depth)
    linear = jnp.dot(gathered, weight_both, preferred_element_type=jnp.float32)
    hidden_sum = resid_cols.astype(jnp.float32) + linear * inv_scale
    scaled = upstream_cols.astype(jnp.float32) * gain.astype(jnp.float32)[None, :]
    sums = jnp.stack(
        (jnp.sum(hidden_sum * hidden_sum, axis=1), jnp.sum(scaled * hidden_sum, axis=1))
    )
    sums = sum_over_major(sums)
    inverse = lax.rsqrt(sums[0] / features + EPS)
    factor = (sums[1] / features * inverse * inverse * inverse)[:, None]
    delta = (scaled * inverse[:, None] - hidden_sum * factor).astype(jnp.bfloat16)
    partial = (
        lax.dot_general(
            gathered, delta, (((0,), (0,)), ((), ())), preferred_element_type=jnp.float32
        )
        * inv_scale
    )
    low, high = partial[:, :width], partial[:, width:]
    mine = jnp.where(first_half, low, high)
    theirs = jnp.where(first_half, high, low).astype(jnp.bfloat16)
    gradient = mine + swap_minor(theirs).astype(jnp.float32)

    rate_table = jnp.asarray(RATE_TABLE, dtype=jnp.float32)
    rate_value = jnp.sum(jnp.where(jnp.arange(5) == rate_index[0], rate_table, 0.0))
    weight_new, first_new, second_new = adamw_update(
        weight_here, first_here, second_here, gradient, rate_value
    )
    return (weight_new[None], first_new[None], second_new[None])


def solution(mesh):
    members, shards = mesh.devices.shape
    split = Mesh(mesh.devices.reshape(members, shards // MINOR, MINOR), ("member", "major", "minor"))
    fsdp = ("major", "minor")
    in_specs = (
        P("member", fsdp, None),
        P("member", fsdp, None),
        P("member", fsdp, None),
        P("member", fsdp),
        P("member", None, fsdp),
        P("member", None, fsdp),
        P("member", None, fsdp),
        P(),
        P("member"),
    )
    out_specs = (P("member", None, fsdp),) * 3
    return jax.shard_map(local, mesh=split, in_specs=in_specs, out_specs=out_specs, check_vma=False)
```

time: 369 us -> 229 us (0.62)
  the two profiles are of different devices: /device:TPU:64 before, /device:TPU:1 now
where the time goes in v1:
time: 229 us; the launch traced here: 225 us
  waiting for transfers between devices  102 us (45%)
  starting transfers between devices  74.8 us (33%)
  local copies, waits for them, and re-layouts  16.1 us (7%)
  between operations  15.7 us (7%)
  other arithmetic  9.29 us (4%)
  matrix products  7.39 us (3%)
    all_to_all x1, waiting for transfers between devices, local(): lax.all_to_all(stream, 'major', split_axis=0, concat_axis=0, tiled=True)  38.2 us
    ppermute x3, waiting for transfers between devices, swap_minor(): return lax.ppermute(array, 'minor', [(0, 1), (1, 0)])  30.8 us
    ppermute x7, starting transfers between devices, sum_over_major(): lax.ppermute(array, 'major', [(i, (i + shift) % size) for i in range(size)])  23.2 us
    all_to_all x2, starting transfers between devices, exchange(): lax.all_to_all(array, 'member', split_axis=0, concat_axis=0, tiled=True)  20.2 us
    all_to_all x2, starting transfers between devices, exchange(): lax.all_to_all(out[sources], 'member', split_axis=0, concat_axis=0, tiled...  16.3 us
    all_to_all x2, waiting for transfers between devices, exchange(): lax.all_to_all(out[sources], 'member', split_axis=0, concat_axis=0, tiled...  15.8 us
    all_to_all x2, waiting for transfers between devices, exchange(): lax.all_to_all(array, 'member', split_axis=0, concat_axis=0, tiled=True)  14.1 us
    ppermute x3, starting transfers between devices, swap_minor(): return lax.ppermute(array, 'minor', [(0, 1), (1, 0)])  8.29 us
  transfers between devices with their start and end apart: 16, of which 5 were waited for; matrix products, arithmetic and copies ran while one was open for 12% of the time, Pallas kernels for 0%

profile of v1, /device:TPU:1, one launch (start us, length us, event | category | flops | bytes accessed | tf_op | source)
XLA Modules:
  0.0 225.2 jit_solution(3989493449105374057)
XLA Ops:
  7.9 14.4 %all-to-all-start = ((bf16[32,64,128]{2,1,0:T(8,128)(2,1)}), bf16[32,64,128]{2,1,0:T(8,128)(2,1)S(1)}, u32[]{:S(2)}, u32[]{:S(2)}) async-start(bf16[32,64,128]{2,1,0:T(8,128)(2,1)} %bitcast.76), calls=%async_computation | async-start | bytes 1048576 | tf_op jit(solution)/shard_map/all_to_all | solution.py:49
  25.1 14.1 %all-to-all-done = bf16[32,64,128]{2,1,0:T(8,128)(2,1)S(1)} async-done(((bf16[32,64,128]{2,1,0:T(8,128)(2,1)}), bf16[32,64,128]{2,1,0:T(8,128)(2,1)S(1)}, u32[]{:S(2)}, u32[]{:S(2)}) %all-to-all-start) | async-done | bytes 524320 | tf_op jit(solution)/shard_map/all_to_all | solution.py:49
  39.2 6.8 %all-to-all-start.4 = ((bf16[8,2,128,256]{2,3,1,0:T(8,128)(2,1)}), bf16[8,2,128,256]{2,3,1,0:T(8,128)(2,1)S(1)}, u32[]{:S(2)}, u32[]{:S(2)}) async-start(bf16[8,2,128,256]{2,3,1,0:T(8,128)(2,1)} %pad_maximum_fusion.1), calls=%async_computation.4 | async-start | bytes 2097152 | tf_op jit(solution)/shard_map/all_to_all | solution.py:90
  47.4 38.2 %all-to-all-done.4 = bf16[8,2,128,256]{2,3,1,0:T(8,128)(2,1)S(1)} async-done(((bf16[8,2,128,256]{2,3,1,0:T(8,128)(2,1)}), bf16[8,2,128,256]{2,3,1,0:T(8,128)(2,1)S(1)}, u32[]{:S(2)}, u32[]{:S(2)}) %all-to-all-start.4) | async-done | bytes 1048608 | tf_op jit(solution)/shard_map/all_to_all | solution.py:90
  85.6 7.0 %all-to-all-start.1 = ((bf16[32,64,128]{2,1,0:T(8,128)(2,1)}), bf16[32,64,128]{2,1,0:T(8,128)(2,1)}, u32[]{:S(2)}, u32[]{:S(2)}) async-start(bf16[32,64,128]{2,1,0:T(8,128)(2,1)} %gather_fusion), calls=%async_computation.1 | async-start | bytes 1048576 | tf_op jit(solution)/shard_map/all_to_all | solution.py:50
  93.7 15.8 %all-to-all-done.1 = bf16[32,64,128]{2,1,0:T(8,128)(2,1)} async-done(((bf16[32,64,128]{2,1,0:T(8,128)(2,1)}), bf16[32,64,128]{2,1,0:T(8,128)(2,1)}, u32[]{:S(2)}, u32[]{:S(2)}) %all-to-all-start.1) | async-done | bytes 524320 | tf_op jit(solution)/shard_map/all_to_all | solution.py:50
  109.6 5.7 %all-to-all-start.2 = ((bf16[32,2,64,128]{3,2,1,0:T(8,128)(2,1)}), bf16[32,2,64,128]{3,2,1,0:T(8,128)(2,1)S(1)}, u32[]{:S(2)}, u32[]{:S(2)}) async-start(bf16[32,2,64,128]{3,2,1,0:T(8,128)(2,1)} %pad_maximum_fusion), calls=%async_computation.2 | async-start | bytes 2097152 | tf_op jit(solution)/shard_map/all_to_all | solution.py:49
  115.3 3.1 %collective-permute-start.1 = (bf16[2048,128]{1,0:T(8,128)(2,1)}, bf16[2048,128]{1,0:T(8,128)(2,1)}, u32[]{:S(2)}, u32[]{:S(2)}) collective-permute-start(bf16[2048,128]{1,0:T(8,128)(2,1)} %bitcast.1), channel_id=1, source_target_pairs={{0,1},{1,0},{2,3},{3,2},{4,5},{5,4},{6,7},{7,6},{8,9},{9,8},{10,11... | collective-permute-start | bytes 1572872 | tf_op jit(solution)/shard_map/ppermute | solution.py:33
  118.5 2.2 collective-permute-start
  120.6 30.8 %collective-permute-done = bf16[128]{0:T(256)(128)(2,1)S(1)} collective-permute-done((bf16[128]{0:T(256)(128)(2,1)S(1)}, bf16[128]{0:T(256)(128)(2,1)S(1)}, u32[]{:S(2)}, u32[]{:S(2)}) %collective-permute-start) | collective-permute-done | bytes 288 | tf_op jit(solution)/shard_map/ppermute | solution.py:33
  155.6 9.3 %all-to-all-start.3 = ((bf16[32,2,64,128]{3,2,1,0:T(8,128)(2,1)}), bf16[32,2,64,128]{3,2,1,0:T(8,128)(2,1)S(1)}, u32[]{:S(2)}, u32[]{:S(2)}) async-start(bf16[32,2,64,128]{3,2,1,0:T(8,128)(2,1)} %gather_fusion.1), calls=%async_computation.3 | async-start | bytes 2097152 | tf_op jit(solution)/shard_map/all_to_all | solution.py:50
  165.0 4.7 %multiply_reduce_fusion.1 = (f32[1024]{0:T(1024)S(1)}, f32[1024]{0:T(1024)S(1)}, f32[1024,256]{0,1:T(8,128)S(1)}) fusion(f32[256]{0:T(256)S(1)} %fusion.32, f32[32,8,8,128]{3,2,1,0:T(8,128)S(1)} %bitcast.69, bf16[1,1024,2048]{2,1,0:T(8,128)(2,1)} %all-gather.3.cloned.1.call-done, bf16[2048,128]{1,0:T(8,128)(2,1)} %collective-permute-done.1, ...), kind=kOutput, calls=%fused_computation.29 | convolution fusion | flops 1080293376 | bytes 8397825 | tf_op jit(solution)/shard_map/dot_general | solution.py:109
  169.7 2.5 %collective-permute-start.2 = (f32[2,1024]{1,0:T(2,128)S(1)}, f32[2,1024]{1,0:T(2,128)S(1)}, u32[]{:S(2)}, u32[]{:S(2)}) collective-permute-start(f32[2,1024]{1,0:T(2,128)S(1)} %pad_maximum_fusion.2), channel_id=1, source_target_pairs={{0,2},{2,4},{4,6},{6,8},{8,10},{10,12},{12,14},{14,0},{1,3},{3,5},... | collective-permute-start | bytes 24584 | tf_op jit(solution)/shard_map/ppermute | solution.py:40
  174.1 3.6 %collective-permute-start.4 = (f32[2,1024]{1,0:T(2,128)S(1)}, f32[2,1024]{1,0:T(2,128)S(1)}, u32[]{:S(2)}, u32[]{:S(2)}) collective-permute-start(f32[2,1024]{1,0:T(2,128)S(1)} %pad_maximum_fusion.2), channel_id=1, source_target_pairs={{0,6},{2,8},{4,10},{6,12},{8,14},{10,0},{12,2},{14,4},{1,7},{3,9},... | collective-permute-start | bytes 24584 | tf_op jit(solution)/shard_map/ppermute | solution.py:40
  177.7 5.6 %collective-permute-start.5 = (f32[2,1024]{1,0:T(2,128)S(1)}, f32[2,1024]{1,0:T(2,128)S(1)}, u32[]{:S(2)}, u32[]{:S(2)}) collective-permute-start(f32[2,1024]{1,0:T(2,128)S(1)} %pad_maximum_fusion.2), channel_id=1, source_target_pairs={{0,8},{2,10},{4,12},{6,14},{8,0},{10,2},{12,4},{14,6},{1,9},{3,11}... | collective-permute-start | bytes 24584 | tf_op jit(solution)/shard_map/ppermute | solution.py:40
  183.3 3.3 %collective-permute-start.6 = (f32[2,1024]{1,0:T(2,128)S(1)}, f32[2,1024]{1,0:T(2,128)S(1)}, u32[]{:S(2)}, u32[]{:S(2)}) collective-permute-start(f32[2,1024]{1,0:T(2,128)S(1)} %pad_maximum_fusion.2), channel_id=1, source_target_pairs={{0,10},{2,12},{4,14},{6,0},{8,2},{10,4},{12,6},{14,8},{1,11},{3,13... | collective-permute-start | bytes 24584 | tf_op jit(solution)/shard_map/ppermute | solution.py:40
  186.6 4.2 %collective-permute-start.7 = (f32[2,1024]{1,0:T(2,128)S(1)}, f32[2,1024]{1,0:T(2,128)S(1)}, u32[]{:S(2)}, u32[]{:S(2)}) collective-permute-start(f32[2,1024]{1,0:T(2,128)S(1)} %pad_maximum_fusion.2), channel_id=1, source_target_pairs={{0,12},{2,14},{4,0},{6,2},{8,4},{10,6},{12,8},{14,10},{1,13},{3,15... | collective-permute-start | bytes 24584 | tf_op jit(solution)/shard_map/ppermute | solution.py:40
  190.8 2.1 collective-permute-start.8
  193.0 2.2 collective-permute-done.8
  195.3 2.7 %fusion.7 = f32[2048,256]{0,1:T(8,128)S(1)} fusion(bf16[1,1024,2048]{2,1,0:T(8,128)(2,1)S(1)} %copy-done, f32[1024,256]{0,1:T(8,128)S(1)} %get-tuple-element.24, f32[32,8,8,128]{3,2,1,0:T(8,128)} %bitcast.70, f32[1024]{0:T(1024)S(1)} %multiply_multiply_fusion.1, f32[1024]{0:T(1024)S(1)} %bitcast.80, f32[256]{0:T(256)S(1)} %fusion.32), kind=kOutput, calls=%fused_computation.7 | convolution fusion | flops 1075576832 | bytes 8397824 | tf_op jit(solution)/shard_map/dot_general | solution.py:120
  198.9 3.0 %collective-permute-start.9 = (bf16[2048,128]{0,1:T(8,128)(2,1)}, bf16[2048,128]{0,1:T(8,128)(2,1)}, u32[]{:S(2)}, u32[]{:S(2)}) collective-permute-start(bf16[2048,128]{0,1:T(8,128)(2,1)} %select_convert_fusion), channel_id=1, source_target_pairs={{0,1},{1,0},{2,3},{3,2},{4,5},{5,4},{6,7},{7,6},{8,9},{9,8},{10,11... | collective-permute-start | bytes 1572872 | tf_op jit(solution)/shard_map/ppermute | solution.py:33
  203.8 2.0 copy.26
  209.0 2.5 %copy.31 = f32[2048,128]{0,1:T(8,128)} copy(f32[2048,128]{1,0:T(8,128)} %bitcast.71) | data formatting | bytes 2097152 | tf_op jit(solution)/shard_map/mul | solution.py:21
  211.6 2.3 %convert_bitcast_fusion = (bf16[1,2048,128]{1,2,0:T(8,128)(2,1)}, f32[2048,128]{0,1:T(8,128)S(1)}) fusion(f32[2048,128]{0,1:T(8,128)S(1)} %copy.32, bf16[2048,128]{0,1:T(8,128)(2,1)} %collective-permute-done.9, f32[2048,256]{0,1:T(8,128)S(1)} %fusion.7, pred[]{:T(512)S(6)} %eq.11), kind=kLoop, calls=%fused_computation.34 | loop fusion | flops 1835008 | bytes 5242881 | tf_op jit(solution)/shard_map/broadcast_in_dim | solution.py:135
  (62 shorter events, 21.2 us)
Async XLA Ops:
  7.2 16.5 %copy-start.6 = (bf16[1,128,2048]{2,1,0:T(8,128)(2,1)S(1)}, bf16[1,128,2048]{2,1,0:T(8,128)(2,1)}, u32[]{:S(2)}) copy-start(bf16[1,128,2048]{2,1,0:T(8,128)(2,1)} %param.11) | copy-start | bytes 1572868
  7.2 157.8 %all-gather.3.cloned.1.call-start = ((), (), s32[]{:S(2)}) async-start(), calls=%async_computation.5 | async-start | bytes 4718592 | tf_op jit(solution)/shard_map/all_gather | solution.py:82
  7.9 31.3 %all-to-all-start = ((bf16[32,64,128]{2,1,0:T(8,128)(2,1)}), bf16[32,64,128]{2,1,0:T(8,128)(2,1)S(1)}, u32[]{:S(2)}, u32[]{:S(2)}) async-start(bf16[32,64,128]{2,1,0:T(8,128)(2,1)} %bitcast.76), calls=%async_computation | async-start | bytes 1048576 | tf_op jit(solution)/shard_map/all_to_all | solution.py:49
  24.0 22.1 %copy-start.10 = (s32[32]{0:T(128)S(1)}, s32[32]{0:T(128)}, u32[]{:S(2)}) copy-start(s32[32]{0:T(128)} %param.17) | copy-start | bytes 388
  25.1 67.5 %copy-start.7 = (bf16[1,2048,128]{2,1,0:T(8,128)(2,1)S(1)}, bf16[1,2048,128]{2,1,0:T(8,128)(2,1)}, u32[]{:S(2)}) copy-start(bf16[1,2048,128]{2,1,0:T(8,128)(2,1)} %param.16) | copy-start | bytes 1572868
  25.1 67.5 %copy-start.8 = (bf16[1,2048,128]{2,1,0:T(8,128)(2,1)S(1)}, bf16[1,2048,128]{2,1,0:T(8,128)(2,1)}, u32[]{:S(2)}) copy-start(bf16[1,2048,128]{2,1,0:T(8,128)(2,1)} %param.15) | copy-start | bytes 1572868
  39.2 46.4 %all-to-all-start.4 = ((bf16[8,2,128,256]{2,3,1,0:T(8,128)(2,1)}), bf16[8,2,128,256]{2,3,1,0:T(8,128)(2,1)S(1)}, u32[]{:S(2)}, u32[]{:S(2)}) async-start(bf16[8,2,128,256]{2,3,1,0:T(8,128)(2,1)} %pad_maximum_fusion.1), calls=%async_computation.4 | async-start | bytes 2097152 | tf_op jit(solution)/shard_map/all_to_all | solution.py:90
  85.6 23.9 %all-to-all-start.1 = ((bf16[32,64,128]{2,1,0:T(8,128)(2,1)}), bf16[32,64,128]{2,1,0:T(8,128)(2,1)}, u32[]{:S(2)}, u32[]{:S(2)}) async-start(bf16[32,64,128]{2,1,0:T(8,128)(2,1)} %gather_fusion), calls=%async_computation.1 | async-start | bytes 1048576 | tf_op jit(solution)/shard_map/all_to_all | solution.py:50
  92.6 25.9 %copy-start.9 = (bf16[1,128]{1,0:T(2,128)(2,1)S(1)}, bf16[1,128]{1,0:T(2,128)(2,1)}, u32[]{:S(2)}) copy-start(bf16[1,128]{1,0:T(2,128)(2,1)} %param.13) | copy-start | bytes 772
  109.6 44.3 %all-to-all-start.2 = ((bf16[32,2,64,128]{3,2,1,0:T(8,128)(2,1)}), bf16[32,2,64,128]{3,2,1,0:T(8,128)(2,1)S(1)}, u32[]{:S(2)}, u32[]{:S(2)}) async-start(bf16[32,2,64,128]{3,2,1,0:T(8,128)(2,1)} %pad_maximum_fusion), calls=%async_computation.2 | async-start | bytes 2097152 | tf_op jit(solution)/shard_map/all_to_all | solution.py:49
  115.3 49.6 %collective-permute-start.1 = (bf16[2048,128]{1,0:T(8,128)(2,1)}, bf16[2048,128]{1,0:T(8,128)(2,1)}, u32[]{:S(2)}, u32[]{:S(2)}) collective-permute-start(bf16[2048,128]{1,0:T(8,128)(2,1)} %bitcast.1), channel_id=1, source_target_pairs={{0,1},{1,0},{2,3},{3,2},{4,5},{5,4},{6,7},{7,6},{8,9},{9,8},{10,11... | collective-permute-start | bytes 1572872 | tf_op jit(solution)/shard_map/ppermute | solution.py:33
  118.5 33.0 %collective-permute-start = (bf16[128]{0:T(256)(128)(2,1)S(1)}, bf16[128]{0:T(256)(128)(2,1)S(1)}, u32[]{:S(2)}, u32[]{:S(2)}) collective-permute-start(bf16[128]{0:T(256)(128)(2,1)S(1)} %bitcast.86), channel_id=1, source_target_pairs={{0,1},{1,0},{2,3},{3,2},{4,5},{5,4},{6,7},{7,6},{8,9},{9,8},{10,11... | collective-permute-start | bytes 776 | tf_op jit(solution)/shard_map/ppermute | solution.py:33
  152.3 12.7 %copy-start.1 = (f32[8,1,128,256]{2,0,3,1:T(8,128)}, f32[8,1,128,256]{2,0,3,1:T(8,128)S(1)}, u32[]{:S(2)}) copy-start(f32[8,1,128,256]{2,0,3,1:T(8,128)S(1)} %copy.29) | copy-start | bytes 3145732
  155.6 9.4 %copy-start.5 = (f32[8,1,128,256]{2,0,3,1:T(8,128)S(1)}, f32[8,1,128,256]{2,0,3,1:T(8,128)}, u32[]{:S(2)}) copy-start(f32[8,1,128,256]{2,0,3,1:T(8,128)} %copy.30) | copy-start | bytes 3145732
  155.6 50.3 %all-to-all-start.3 = ((bf16[32,2,64,128]{3,2,1,0:T(8,128)(2,1)}), bf16[32,2,64,128]{3,2,1,0:T(8,128)(2,1)S(1)}, u32[]{:S(2)}, u32[]{:S(2)}) async-start(bf16[32,2,64,128]{3,2,1,0:T(8,128)(2,1)} %gather_fusion.1), calls=%async_computation.3 | async-start | bytes 2097152 | tf_op jit(solution)/shard_map/all_to_all | solution.py:50
  165.0 30.3 %copy-start = (bf16[1,1024,2048]{2,1,0:T(8,128)(2,1)S(1)}, bf16[1,1024,2048]{2,1,0:T(8,128)(2,1)}, u32[]{:S(2)}) copy-start(bf16[1,1024,2048]{2,1,0:T(8,128)(2,1)} %all-gather.3.cloned.1.call-done) | copy-start | bytes 12582916
  169.7 16.9 %collective-permute-start.2 = (f32[2,1024]{1,0:T(2,128)S(1)}, f32[2,1024]{1,0:T(2,128)S(1)}, u32[]{:S(2)}, u32[]{:S(2)}) collective-permute-start(f32[2,1024]{1,0:T(2,128)S(1)} %pad_maximum_fusion.2), channel_id=1, source_target_pairs={{0,2},{2,4},{4,6},{6,8},{8,10},{10,12},{12,14},{14,0},{1,3},{3,5},... | collective-permute-start | bytes 24584 | tf_op jit(solution)/shard_map/ppermute | solution.py:40
  172.2 18.6 %collective-permute-start.3 = (f32[2,1024]{1,0:T(2,128)S(1)}, f32[2,1024]{1,0:T(2,128)S(1)}, u32[]{:S(2)}, u32[]{:S(2)}) collective-permute-start(f32[2,1024]{1,0:T(2,128)S(1)} %pad_maximum_fusion.2), channel_id=1, source_target_pairs={{0,4},{2,6},{4,8},{6,10},{8,12},{10,14},{12,0},{14,2},{1,5},{3,7},... | collective-permute-start | bytes 24584 | tf_op jit(solution)/shard_map/ppermute | solution.py:40
  174.1 18.8 %collective-permute-start.4 = (f32[2,1024]{1,0:T(2,128)S(1)}, f32[2,1024]{1,0:T(2,128)S(1)}, u32[]{:S(2)}, u32[]{:S(2)}) collective-permute-start(f32[2,1024]{1,0:T(2,128)S(1)} %pad_maximum_fusion.2), channel_id=1, source_target_pairs={{0,6},{2,8},{4,10},{6,12},{8,14},{10,0},{12,2},{14,4},{1,7},{3,9},... | collective-permute-start | bytes 24584 | tf_op jit(solution)/shard_map/ppermute | solution.py:40
  177.7 15.2 %collective-permute-start.5 = (f32[2,1024]{1,0:T(2,128)S(1)}, f32[2,1024]{1,0:T(2,128)S(1)}, u32[]{:S(2)}, u32[]{:S(2)}) collective-permute-start(f32[2,1024]{1,0:T(2,128)S(1)} %pad_maximum_fusion.2), channel_id=1, source_target_pairs={{0,8},{2,10},{4,12},{6,14},{8,0},{10,2},{12,4},{14,6},{1,9},{3,11}... | collective-permute-start | bytes 24584 | tf_op jit(solution)/shard_map/ppermute | solution.py:40
  183.3 9.7 %collective-permute-start.6 = (f32[2,1024]{1,0:T(2,128)S(1)}, f32[2,1024]{1,0:T(2,128)S(1)}, u32[]{:S(2)}, u32[]{:S(2)}) collective-permute-start(f32[2,1024]{1,0:T(2,128)S(1)} %pad_maximum_fusion.2), channel_id=1, source_target_pairs={{0,10},{2,12},{4,14},{6,0},{8,2},{10,4},{12,6},{14,8},{1,11},{3,13... | collective-permute-start | bytes 24584 | tf_op jit(solution)/shard_map/ppermute | solution.py:40
  186.6 6.4 %collective-permute-start.7 = (f32[2,1024]{1,0:T(2,128)S(1)}, f32[2,1024]{1,0:T(2,128)S(1)}, u32[]{:S(2)}, u32[]{:S(2)}) collective-permute-start(f32[2,1024]{1,0:T(2,128)S(1)} %pad_maximum_fusion.2), channel_id=1, source_target_pairs={{0,12},{2,14},{4,0},{6,2},{8,4},{10,6},{12,8},{14,10},{1,13},{3,15... | collective-permute-start | bytes 24584 | tf_op jit(solution)/shard_map/ppermute | solution.py:40
  190.8 4.4 %collective-permute-start.8 = (f32[2,1024]{1,0:T(2,128)S(1)}, f32[2,1024]{1,0:T(2,128)S(1)}, u32[]{:S(2)}, u32[]{:S(2)}) collective-permute-start(f32[2,1024]{1,0:T(2,128)S(1)} %pad_maximum_fusion.2), channel_id=1, source_target_pairs={{0,14},{2,0},{4,2},{6,4},{8,6},{10,8},{12,10},{14,12},{1,15},{3,1}... | collective-permute-start | bytes 24584 | tf_op jit(solution)/shard_map/ppermute | solution.py:40
  198.9 12.7 %collective-permute-start.9 = (bf16[2048,128]{0,1:T(8,128)(2,1)}, bf16[2048,128]{0,1:T(8,128)(2,1)}, u32[]{:S(2)}, u32[]{:S(2)}) collective-permute-start(bf16[2048,128]{0,1:T(8,128)(2,1)} %select_convert_fusion), channel_id=1, source_target_pairs={{0,1},{1,0},{2,3},{3,2},{4,5},{5,4},{6,7},{7,6},{8,9},{9,8},{10,11... | collective-permute-start | bytes 1572872 | tf_op jit(solution)/shard_map/ppermute | solution.py:33
  (4 other events, 13.8 us)
Sparse Core Ops, SparseCore 0:
  10.1 85.0 all-gather.2

commit v2 on v1

v2 whole, which is shorter than its diff:
```python
import functools
import math

import jax
import jax.numpy as jnp
from jax import lax
from jax.experimental import pallas as pl
from jax.experimental.pallas import tpu as pltpu
from jax.sharding import Mesh
from jax.sharding import PartitionSpec as P

EPS = 1e-06
ADAM_EPS = 1e-08
BETA_ONE = 0.9
BETA_TWO = 0.95
DECAY = 0.1
bias_one = 1.0 - 0.9**10
bias_two = 1.0 - 0.95**10
RATE_TABLE = (0.02, 0.032, 0.05, 0.08, 0.125)
MINOR = 2
LANES = 128
VMEM_LIMIT = 24 * 1024 * 1024


def adamw_update(weight_now, first_now, second_now, gradient, rate_value):
    first_sum = BETA_ONE * first_now.astype(jnp.float32) + (1.0 - BETA_ONE) * gradient
    second_sum = BETA_TWO * second_now.astype(jnp.float32) + (1.0 - BETA_TWO) * gradient * gradient
    update = first_sum / bias_one / (jnp.sqrt(second_sum / bias_two) + ADAM_EPS)
    weight_new = weight_now.astype(jnp.float32) * (1.0 - rate_value * DECAY) - rate_value * update
    return (
        weight_new.astype(jnp.bfloat16),
        first_sum.astype(jnp.bfloat16),
        second_sum.astype(jnp.bfloat16),
    )


def forward_kernel(inv_scale, minor_ref, rows_ref, own_ref, other_ref, stream_ref, gain_ref, hidden_ref, sums_ref, both_ref):
    width = own_ref.shape[1]

    @pl.when(pl.program_id(0) == 0)
    def _():
        @pl.when(minor_ref[0] == 0)
        def _():
            both_ref[:, :width] = own_ref[...]
            both_ref[:, width:] = other_ref[...]

        @pl.when(minor_ref[0] != 0)
        def _():
            both_ref[:, :width] = other_ref[...]
            both_ref[:, width:] = own_ref[...]

    linear = jnp.dot(rows_ref[...], both_ref[...], preferred_element_type=jnp.float32)
    count = rows_ref.shape[0]
    stream = stream_ref[...]
    resid = stream[:, 0].reshape(count, 2 * width).astype(jnp.float32)
    upstream = stream[:, 1].reshape(count, 2 * width).astype(jnp.float32)
    hidden = resid + linear * inv_scale
    hidden_ref[...] = hidden
    scaled = upstream * gain_ref[...]
    squares = jnp.sum(hidden * hidden, axis=1, keepdims=True)
    inner = jnp.sum(scaled * hidden, axis=1, keepdims=True)
    lane = lax.broadcasted_iota(jnp.int32, (count, LANES), 1)
    packed = jnp.where(lane == 0, squares, jnp.where(lane == 1, inner, 0.0))
    sums_ref[...] = packed.T[: sums_ref.shape[0]]


def forward(minor, rows, own, other, stream, gain, inv_scale):
    tokens, depth = rows.shape
    width = own.shape[1]
    per = stream.shape[2]
    step = 2 * per
    return pl.pallas_call(
        functools.partial(forward_kernel, inv_scale),
        grid_spec=pltpu.PrefetchScalarGridSpec(
            num_scalar_prefetch=1,
            grid=(tokens // step,),
            in_specs=[
                pl.BlockSpec((step, depth), lambda i, m: (i, 0)),
                pl.BlockSpec((depth, width), lambda i, m: (0, 0)),
                pl.BlockSpec((depth, width), lambda i, m: (0, 0)),
                pl.BlockSpec((2, 2, per, 2 * width), lambda i, m: (i, 0, 0, 0)),
                pl.BlockSpec((1, 2 * width), lambda i, m: (0, 0)),
            ],
            out_specs=[
                pl.BlockSpec((step, 2 * width), lambda i, m: (i, 0)),
                pl.BlockSpec((8, step), lambda i, m: (0, i)),
            ],
            scratch_shapes=[pltpu.VMEM((depth, 2 * width), jnp.bfloat16)],
        ),
        out_shape=[
            jax.ShapeDtypeStruct((tokens, 2 * width), jnp.float32),
            jax.ShapeDtypeStruct((8, tokens), jnp.float32),
        ],
        compiler_params=pltpu.CompilerParams(vmem_limit_bytes=VMEM_LIMIT),
        cost_estimate=pl.CostEstimate(
            flops=4 * tokens * depth * width, bytes_accessed=7 * 1024 * 1024, transcendentals=0
        ),
        name="forward",
    )(minor, rows, own, other, stream, gain)


def backward_kernel(inv_scale, features, minor_ref, rows_ref, hidden_ref, stream_ref, gain_ref, sums_ref, mine_ref, theirs_ref, delta_ref):
    width = mine_ref.shape[1]
    tokens = hidden_ref.shape[0]
    blocks, _, per, _ = stream_ref.shape

    @pl.when(pl.program_id(0) == 0)
    def _():
        squares = sums_ref[0:1, :]
        inner = sums_ref[1:2, :]
        inverse = lax.rsqrt(squares / features + EPS)
        factor = inner / features * (inverse * inverse * inverse)
        for block in range(blocks):
            part = slice(block * per, (block + 1) * per)
            inverse_here = jnp.broadcast_to(inverse[:, part], (LANES, per)).T
            factor_here = jnp.broadcast_to(factor[:, part], (LANES, per)).T
            for half in range(2):
                cols = slice(half * width, (half + 1) * width)
                scaled = stream_ref[block, 1, :, cols].astype(jnp.float32) * gain_ref[:, cols]
                delta = scaled * inverse_here - hidden_ref[part, cols] * factor_here
                delta_ref[cols, part] = delta.T.astype(jnp.bfloat16)

    grad = jnp.dot(delta_ref[...], rows_ref[...], preferred_element_type=jnp.float32) * inv_scale
    low = grad[:width].T
    high = grad[width:].T
    first = minor_ref[0] == 0
    mine_ref[...] = jnp.where(first, low, high)
    theirs_ref[...] = jnp.where(first, high, low).astype(jnp.bfloat16)


def backward(minor, rows, hidden, stream, gain, sums, inv_scale, features):
    tokens, depth = rows.shape
    block = hidden.shape[1]
    width = block // 2
    step = 256
    return pl.pallas_call(
        functools.partial(backward_kernel, inv_scale, features),
        grid_spec=pltpu.PrefetchScalarGridSpec(
            num_scalar_prefetch=1,
            grid=(depth // step,),
            in_specs=[
                pl.BlockSpec((tokens, step), lambda i, m: (0, i)),
                pl.BlockSpec(hidden.shape, lambda i, m: (0, 0)),
                pl.BlockSpec(stream.shape, lambda i, m: (0, 0, 0, 0)),
                pl.BlockSpec((1, block), lambda i, m: (0, 0)),
                pl.BlockSpec(sums.shape, lambda i, m: (0, 0)),
            ],
            out_specs=[
                pl.BlockSpec((step, width), lambda i, m: (i, 0)),
                pl.BlockSpec((step, width), lambda i, m: (i, 0)),
            ],
            scratch_shapes=[pltpu.VMEM((block, tokens), jnp.bfloat16)],
        ),
        out_shape=[
            jax.ShapeDtypeStruct((depth, width), jnp.float32),
            jax.ShapeDtypeStruct((depth, width), jnp.bfloat16),
        ],
        compiler_params=pltpu.CompilerParams(vmem_limit_bytes=VMEM_LIMIT),
        cost_estimate=pl.CostEstimate(
            flops=2 * tokens * depth * block, bytes_accessed=8 * 1024 * 1024, transcendentals=0
        ),
        name="backward",
    )(minor, rows, hidden, stream, gain, sums)


def swap_minor(array):
    return lax.ppermute(array, "minor", [(0, 1), (1, 0)])


def sum_over_major(array):
    size = lax.axis_size("major")
    reach = 1
    while reach < size:
        array = array + lax.ppermute(array, "major", [(i, i ^ reach) for i in range(size)])
        reach *= 2
    return array


def exchange(array, sources):
    out = lax.all_to_all(array, "member", split_axis=0, concat_axis=0, tiled=True)
    return lax.all_to_all(out[sources], "member", split_axis=0, concat_axis=0, tiled=True)


def spread_features(residual, upstream):
    size = lax.axis_size("major")
    me = lax.axis_index("major")
    block = residual.shape[1] // size
    received = []
    for shift in range(size):
        start = lax.rem(me + shift, size) * block
        part = jnp.stack(
            (
                lax.dynamic_slice_in_dim(residual, start, block, axis=1),
                lax.dynamic_slice_in_dim(upstream, start, block, axis=1),
            )
        )
        if shift:
            part = lax.ppermute(part, "major", [(i, (i + shift) % size) for i in range(size)])
        received.append(part)
    return jnp.stack(received)[lax.rem(me + size - jnp.arange(size), size)]


def local(
    attention_out,
    residual,
    upstream,
    norm_gain,
    weight,
    first_moment,
    second_moment,
    sources,
    rate_index,
):
    members = lax.axis_size("member")
    minor = lax.axis_index("minor")
    depth, width = weight.shape[1:]
    rows = depth // members
    features = residual.shape[2]

    gathered = lax.all_gather(attention_out[0], "major", axis=0, tiled=True)
    weight_here = exchange(weight[0].reshape(members, rows, width), sources)
    stream = spread_features(residual[0], upstream[0])
    moments = jnp.stack(
        (first_moment[0].reshape(members, rows, width), second_moment[0].reshape(members, rows, width)),
        axis=1,
    )
    weight_here, moments = lax.optimization_barrier((weight_here, moments))
    moments = exchange(moments, sources)
    weight_here = weight_here.reshape(depth, width)
    first_here = moments[:, 0].reshape(depth, width)
    second_here = moments[:, 1].reshape(depth, width)

    gain_other = swap_minor(norm_gain[0])
    weight_other = swap_minor(weight_here)
    gain = jnp.where(
        minor == 0,
        jnp.concatenate((norm_gain[0], gain_other)),
        jnp.concatenate((gain_other, norm_gain[0])),
    ).astype(jnp.float32)[None, :]

    inv_scale = 1.0 / math.sqrt(depth)
    side = minor.astype(jnp.int32)[None]
    hidden, sums = forward(side, gathered, weight_here, weight_other, stream, gain, inv_scale)
    sums = sum_over_major(sums)
    mine, theirs = backward(side, gathered, hidden, stream, gain, sums, inv_scale, features)
    gradient = mine + swap_minor(theirs).astype(jnp.float32)

    rate_table = jnp.asarray(RATE_TABLE, dtype=jnp.float32)
    rate_value = jnp.sum(jnp.where(jnp.arange(5) == rate_index[0], rate_table, 0.0))
    weight_new, first_new, second_new = adamw_update(
        weight_here, first_here, second_here, gradient, rate_value
    )
    return (weight_new[None], first_new[None], second_new[None])


def solution(mesh):
    members, shards = mesh.devices.shape
    split = Mesh(mesh.devices.reshape(members, shards // MINOR, MINOR), ("member", "major", "minor"))
    fsdp = ("major", "minor")
    in_specs = (
        P("member", fsdp, None),
        P("member", fsdp, None),
        P("member", fsdp, None),
        P("member", fsdp),
        P("member", None, fsdp),
        P("member", None, fsdp),
        P("member", None, fsdp),
        P(),
        P("member"),
    )
    out_specs = (P("member", None, fsdp),) * 3
    return jax.shard_map(local, mesh=split, in_specs=in_specs, out_specs=out_specs, check_vma=False)
```

time: 229 us -> 204 us (0.89)
  the two profiles are of different devices: /device:TPU:1 before, /device:TPU:2 now
where the time goes in v2:
time: 204 us; the launch traced here: 203 us
  starting transfers between devices  81.6 us (40%)
  waiting for transfers between devices  77.4 us (38%)
  between operations  15.8 us (8%)
  other arithmetic  12.6 us (6%)
  local copies, waits for them, and re-layouts  8.84 us (4%)
  Pallas kernels  7.01 us (3%)
    ppermute x7, starting transfers between devices, spread_features(): lax.ppermute(part, 'major', [(i, (i + shift) % size) for i in range(size)])  29.1 us
    ppermute x3, waiting for transfers between devices, swap_minor(): return lax.ppermute(array, 'minor', [(0, 1), (1, 0)])  26.1 us
    all_to_all x2, starting transfers between devices, exchange(): lax.all_to_all(array, 'member', split_axis=0, concat_axis=0, tiled=True)  19.7 us
    all_to_all x2, starting transfers between devices, exchange(): lax.all_to_all(out[sources], 'member', split_axis=0, concat_axis=0, tiled...  16.2 us
    all_to_all x2, waiting for transfers between devices, exchange(): lax.all_to_all(array, 'member', split_axis=0, concat_axis=0, tiled=True)  15.8 us
    ppermute x3, waiting for transfers between devices, sum_over_major(): lax.ppermute(array, 'major', [(i, i ^ reach) for i in range(size)])  15.4 us
    all_to_all x2, waiting for transfers between devices, exchange(): lax.all_to_all(out[sources], 'member', split_axis=0, concat_axis=0, tiled...  14.1 us
    ppermute x3, starting transfers between devices, swap_minor(): return lax.ppermute(array, 'minor', [(0, 1), (1, 0)])  9.24 us
  transfers between devices with their start and end apart: 18, of which 10 were waited for; matrix products, arithmetic and copies ran while one was open for 8% of the time, Pallas kernels for 3%

profile of v2, /device:TPU:2, one launch (start us, length us, event | category | flops | bytes accessed | tf_op | source)
XLA Modules:
  0.0 203.3 jit_solution(13809176049898713828)
XLA Ops:
  7.9 13.5 %all-to-all-start = ((bf16[32,64,128]{2,1,0:T(8,128)(2,1)}), bf16[32,64,128]{2,1,0:T(8,128)(2,1)S(1)}, u32[]{:S(2)}, u32[]{:S(2)}) async-start(bf16[32,64,128]{2,1,0:T(8,128)(2,1)} %bitcast.53), calls=%async_computation | async-start | bytes 1048576 | tf_op jit(solution)/shard_map/all_to_all | solution.py:180
  22.1 15.8 %all-to-all-done = bf16[32,64,128]{2,1,0:T(8,128)(2,1)S(1)} async-done(((bf16[32,64,128]{2,1,0:T(8,128)(2,1)}), bf16[32,64,128]{2,1,0:T(8,128)(2,1)S(1)}, u32[]{:S(2)}, u32[]{:S(2)}) %all-to-all-start) | async-done | bytes 524320 | tf_op jit(solution)/shard_map/all_to_all | solution.py:180
  39.3 6.2 %all-to-all-start.1 = ((bf16[32,64,128]{2,1,0:T(8,128)(2,1)}), bf16[32,64,128]{2,1,0:T(8,128)(2,1)S(1)}, u32[]{:S(2)}, u32[]{:S(2)}) async-start(bf16[32,64,128]{2,1,0:T(8,128)(2,1)} %gather_fusion), calls=%async_computation.1 | async-start | bytes 1048576 | tf_op jit(solution)/shard_map/all_to_all | solution.py:181
  47.8 14.1 %all-to-all-done.1 = bf16[32,64,128]{2,1,0:T(8,128)(2,1)S(1)} async-done(((bf16[32,64,128]{2,1,0:T(8,128)(2,1)}), bf16[32,64,128]{2,1,0:T(8,128)(2,1)S(1)}, u32[]{:S(2)}, u32[]{:S(2)}) %all-to-all-start.1) | async-done | bytes 524320 | tf_op jit(solution)/shard_map/all_to_all | solution.py:181
  62.0 6.2 %all-to-all-start.2 = ((bf16[32,2,64,128]{3,2,1,0:T(8,128)(2,1)}), bf16[32,2,64,128]{3,2,1,0:T(8,128)(2,1)S(1)}, u32[]{:S(2)}, u32[]{:S(2)}) async-start(bf16[32,2,64,128]{3,2,1,0:T(8,128)(2,1)} %pad_maximum_fusion), calls=%async_computation.2 | async-start | bytes 2097152 | tf_op jit(solution)/shard_map/all_to_all | solution.py:180
  68.2 3.4 %collective-permute-start.8 = (bf16[128]{0:T(256)(128)(2,1)S(1)}, bf16[128]{0:T(256)(128)(2,1)}, u32[]{:S(2)}, u32[]{:S(2)}) collective-permute-start(bf16[128]{0:T(256)(128)(2,1)S(1)} %bitcast.56), channel_id=1, source_target_pairs={{0,1},{1,0},{2,3},{3,2},{4,5},{5,4},{6,7},{7,6},{8,9},{9,8},{10,11... | collective-permute-start | bytes 776 | tf_op jit(solution)/shard_map/ppermute | solution.py:167
  71.8 6.2 %collective-permute-start.6 = (bf16[2,128,256]{2,1,0:T(8,128)(2,1)S(1)}, bf16[2,128,256]{2,1,0:T(8,128)(2,1)S(1)}, u32[]{:S(2)}, u32[]{:S(2)}) collective-permute-start(bf16[2,128,256]{2,1,0:T(8,128)(2,1)S(1)} %pad_maximum_fusion.6), channel_id=1, source_target_pairs={{0,12},{2,14},{4,0},{6,2},{8,4},{10,6},{12,8},{14,10},{1,13},{3,15... | collective-permute-start | bytes 393224 | tf_op jit(solution)/shard_map/ppermute | solution.py:198
  78.7 2.6 %collective-permute-start.1 = (bf16[2,128,256]{2,1,0:T(8,128)(2,1)}, bf16[2,128,256]{2,1,0:T(8,128)(2,1)}, u32[]{:S(2)}, u32[]{:S(2)}) collective-permute-start(bf16[2,128,256]{2,1,0:T(8,128)(2,1)} %pad_maximum_fusion.1), channel_id=1, source_target_pairs={{0,2},{2,4},{4,6},{6,8},{8,10},{10,12},{12,14},{14,0},{1,3},{3,5},... | collective-permute-start | bytes 393224 | tf_op jit(solution)/shard_map/ppermute | solution.py:198
  84.5 6.3 %collective-permute-start.3 = (bf16[2,128,256]{2,1,0:T(8,128)(2,1)}, bf16[2,128,256]{2,1,0:T(8,128)(2,1)}, u32[]{:S(2)}, u32[]{:S(2)}) collective-permute-start(bf16[2,128,256]{2,1,0:T(8,128)(2,1)} %pad_maximum_fusion.3), channel_id=1, source_target_pairs={{0,6},{2,8},{4,10},{6,12},{8,14},{10,0},{12,2},{14,4},{1,7},{3,9},... | collective-permute-start | bytes 393224 | tf_op jit(solution)/shard_map/ppermute | solution.py:198
  92.1 7.7 %collective-permute-start.4 = (bf16[2,128,256]{2,1,0:T(8,128)(2,1)S(1)}, bf16[2,128,256]{2,1,0:T(8,128)(2,1)S(1)}, u32[]{:S(2)}, u32[]{:S(2)}) collective-permute-start(bf16[2,128,256]{2,1,0:T(8,128)(2,1)S(1)} %pad_maximum_fusion.4), channel_id=1, source_target_pairs={{0,8},{2,10},{4,12},{6,14},{8,0},{10,2},{12,4},{14,6},{1,9},{3,11}... | collective-permute-start | bytes 393224 | tf_op jit(solution)/shard_map/ppermute | solution.py:198
  102.3 10.0 %all-to-all-start.3 = ((bf16[32,2,64,128]{3,2,1,0:T(8,128)(2,1)}), bf16[32,2,64,128]{3,2,1,0:T(8,128)(2,1)}, u32[]{:S(2)}, u32[]{:S(2)}) async-start(bf16[32,2,64,128]{3,2,1,0:T(8,128)(2,1)} %gather_fusion.1), calls=%async_computation.3 | async-start | bytes 2097152 | tf_op jit(solution)/shard_map/all_to_all | solution.py:181
  119.6 3.3 %collective-permute-start = (bf16[2048,128]{1,0:T(8,128)(2,1)S(1)}, bf16[2048,128]{1,0:T(8,128)(2,1)S(1)}, u32[]{:S(2)}, u32[]{:S(2)}) collective-permute-start(bf16[2048,128]{1,0:T(8,128)(2,1)S(1)} %bitcast.51), channel_id=1, source_target_pairs={{0,1},{1,0},{2,3},{3,2},{4,5},{5,4},{6,7},{7,6},{8,9},{9,8},{10,11... | collective-permute-start | bytes 1572872 | tf_op jit(solution)/shard_map/ppermute | solution.py:167
  123.0 3.1 %collective-permute-done.5 = bf16[2,128,256]{2,1,0:T(8,128)(2,1)S(1)} collective-permute-done((bf16[2,128,256]{2,1,0:T(8,128)(2,1)}, bf16[2,128,256]{2,1,0:T(8,128)(2,1)S(1)}, u32[]{:S(2)}, u32[]{:S(2)}) %collective-permute-start.5) | collective-permute-done | bytes 131104 | tf_op jit(solution)/shard_map/ppermute | solution.py:198
  128.9 19.6 %collective-permute-done.other_ref = bf16[2048,128]{1,0:T(8,128)(2,1)S(1)} collective-permute-done((bf16[2048,128]{1,0:T(8,128)(2,1)S(1)}, bf16[2048,128]{1,0:T(8,128)(2,1)S(1)}, u32[]{:S(2)}, u32[]{:S(2)}) %collective-permute-start) | collective-permute-done | bytes 524320 | tf_op jit(solution)/shard_map/ppermute | solution.py:167
  150.7 2.5 %forward.1 = (f32[1024,256]{1,0:T(8,128)S(1)}, f32[8,1024]{1,0:T(8,128)S(1)}) custom-call(s32[1]{0:T(128)} %bitcast.6.minor_ref, bf16[1024,2048]{1,0:T(8,128)(2,1)S(1)} %bitcast.49, bf16[2048,128]{1,0:T(8,128)(2,1)S(1)} %bitcast.52, bf16[2048,128]{1,0:T(8,128)(2,1)S(1)} %collective-permute-done.other_ref, bf16[8,2,128,256]{3,2,1,0:T(8,128)(2,1)S(1)} %gather_fusion.2, ...), custom_call_target="tpu_custom_call" | custom-call | flops 1073741824 | bytes 7340032 | tf_op jit(solution)/shard_map/forward/pallas_call | solution.py:72
  153.1 2.7 %collective-permute-start.9 = (f32[8,1024]{1,0:T(8,128)S(1)}, f32[8,1024]{1,0:T(8,128)S(1)}, u32[]{:S(2)}, u32[]{:S(2)}) collective-permute-start(f32[8,1024]{1,0:T(8,128)S(1)} %get-tuple-element.12), channel_id=1, source_target_pairs={{0,2},{2,0},{4,6},{6,4},{8,10},{10,8},{12,14},{14,12},{1,3},{3,1},... | collective-permute-start | bytes 98312 | tf_op jit(solution)/shard_map/ppermute | solution.py:174
  155.9 3.2 %collective-permute-done.9 = f32[8,1024]{1,0:T(8,128)S(1)} collective-permute-done((f32[8,1024]{1,0:T(8,128)S(1)}, f32[8,1024]{1,0:T(8,128)S(1)}, u32[]{:S(2)}, u32[]{:S(2)}) %collective-permute-start.9) | collective-permute-done | bytes 32800 | tf_op jit(solution)/shard_map/ppermute | solution.py:174
  159.1 2.7 %collective-permute-start.10 = (f32[8,1024]{1,0:T(8,128)S(1)}, f32[8,1024]{1,0:T(8,128)S(1)}, u32[]{:S(2)}, u32[]{:S(2)}) collective-permute-start(f32[8,1024]{1,0:T(8,128)S(1)} %add.112), channel_id=1, source_target_pairs={{0,4},{2,6},{4,0},{6,2},{8,12},{10,14},{12,8},{14,10},{1,5},{3,7},... | collective-permute-start | bytes 98312 | tf_op jit(solution)/shard_map/ppermute | solution.py:174
  161.8 4.4 %collective-permute-done.10 = f32[8,1024]{1,0:T(8,128)S(1)} collective-permute-done((f32[8,1024]{1,0:T(8,128)S(1)}, f32[8,1024]{1,0:T(8,128)S(1)}, u32[]{:S(2)}, u32[]{:S(2)}) %collective-permute-start.10) | collective-permute-done | bytes 32800 | tf_op jit(solution)/shard_map/ppermute | solution.py:174
  168.1 7.9 %collective-permute-done.11 = f32[8,1024]{1,0:T(8,128)S(1)} collective-permute-done((f32[8,1024]{1,0:T(8,128)S(1)}, f32[8,1024]{1,0:T(8,128)S(1)}, u32[]{:S(2)}, u32[]{:S(2)}) %collective-permute-start.11) | collective-permute-done | bytes 32800 | tf_op jit(solution)/shard_map/ppermute | solution.py:174
  176.0 4.5 %backward.1 = (f32[2048,128]{1,0:T(8,128)S(1)}, bf16[2048,128]{1,0:T(8,128)(2,1)S(1)}) custom-call(s32[1]{0:T(128)} %bitcast.6.minor_ref, bf16[1024,2048]{1,0:T(8,128)(2,1)S(1)} %bitcast.50, f32[1024,256]{1,0:T(8,128)S(1)} %get-tuple-element.11.hidden_ref, bf16[8,2,128,256]{3,2,1,0:T(8,128)(2,1)S(1)} %gather_fusion.2, f32[1,256]{1,0:T(1,128)S(1)} %fusion.3.gain_ref, ...), custom_call_target="tpu_custom_call" | custom-call | flops 1073741824 | bytes 8388608 | tf_op jit(solution)/shard_map/backward/pallas_call | solution.py:136
  180.5 2.5 %collective-permute-start.12 = (bf16[2048,128]{1,0:T(8,128)(2,1)S(1)}, bf16[2048,128]{1,0:T(8,128)(2,1)}, u32[]{:S(2)}, u32[]{:S(2)}) collective-permute-start(bf16[2048,128]{1,0:T(8,128)(2,1)S(1)} %get-tuple-element.14), channel_id=1, source_target_pairs={{0,1},{1,0},{2,3},{3,2},{4,5},{5,4},{6,7},{7,6},{8,9},{9,8},{10,11... | collective-permute-start | bytes 1572872 | tf_op jit(solution)/shard_map/ppermute | solution.py:167
  186.5 5.9 %collective-permute-done.12 = bf16[2048,128]{1,0:T(8,128)(2,1)} collective-permute-done((bf16[2048,128]{1,0:T(8,128)(2,1)S(1)}, bf16[2048,128]{1,0:T(8,128)(2,1)}, u32[]{:S(2)}, u32[]{:S(2)}) %collective-permute-start.12) | collective-permute-done | bytes 524320 | tf_op jit(solution)/shard_map/ppermute | solution.py:167
  192.4 4.0 %convert_bitcast_fusion = (bf16[1,2048,128]{2,1,0:T(8,128)(2,1)}, bf16[1,2048,128]{2,1,0:T(8,128)(2,1)}, bf16[1,2048,128]{2,1,0:T(8,128)(2,1)}) fusion(f32[2048,128]{1,0:T(8,128)S(1)} %get-tuple-element.13, bf16[2048,128]{1,0:T(8,128)(2,1)} %collective-permute-done.12, f32[32,1,64,128]{3,2,1,0:T(8,128)S(1)} %get-tuple-element.18, ...), kind=kLoop, calls=%fused_computation.11 | loop fusion | flops 4718592 | bytes 5767176 | tf_op jit(solution)/shard_map/broadcast_in_dim | solution.py:253
  (56 shorter events, 29.3 us)
Async XLA Ops:
  7.2 61.0 %copy-start.3 = (bf16[1,128]{1,0:T(2,128)(2,1)S(1)}, bf16[1,128]{1,0:T(2,128)(2,1)}, u32[]{:S(2)}) copy-start(bf16[1,128]{1,0:T(2,128)(2,1)} %param.13) | copy-start | bytes 772
  7.2 64.4 %copy-start.1 = (bf16[1,128,2048]{2,1,0:T(8,128)(2,1)S(1)}, bf16[1,128,2048]{2,1,0:T(8,128)(2,1)}, u32[]{:S(2)}) copy-start(bf16[1,128,2048]{2,1,0:T(8,128)(2,1)} %param.12) | copy-start | bytes 1572868
  7.2 64.4 %copy-start.2 = (bf16[1,128,2048]{2,1,0:T(8,128)(2,1)S(1)}, bf16[1,128,2048]{2,1,0:T(8,128)(2,1)}, u32[]{:S(2)}) copy-start(bf16[1,128,2048]{2,1,0:T(8,128)(2,1)} %param.11) | copy-start | bytes 1572868
  7.2 141.3 %all-gather.3.cloned.1.call-start = ((), (), s32[]{:S(2)}) async-start(), calls=%async_computation.4 | async-start | bytes 4718592 | tf_op jit(solution)/shard_map/all_gather | solution.py:220
  7.9 30.0 %all-to-all-start = ((bf16[32,64,128]{2,1,0:T(8,128)(2,1)}), bf16[32,64,128]{2,1,0:T(8,128)(2,1)S(1)}, u32[]{:S(2)}, u32[]{:S(2)}) async-start(bf16[32,64,128]{2,1,0:T(8,128)(2,1)} %bitcast.53), calls=%async_computation | async-start | bytes 1048576 | tf_op jit(solution)/shard_map/all_to_all | solution.py:180
  39.3 22.6 %all-to-all-start.1 = ((bf16[32,64,128]{2,1,0:T(8,128)(2,1)}), bf16[32,64,128]{2,1,0:T(8,128)(2,1)S(1)}, u32[]{:S(2)}, u32[]{:S(2)}) async-start(bf16[32,64,128]{2,1,0:T(8,128)(2,1)} %gather_fusion), calls=%async_computation.1 | async-start | bytes 1048576 | tf_op jit(solution)/shard_map/all_to_all | solution.py:181
  62.0 38.7 %all-to-all-start.2 = ((bf16[32,2,64,128]{3,2,1,0:T(8,128)(2,1)}), bf16[32,2,64,128]{3,2,1,0:T(8,128)(2,1)S(1)}, u32[]{:S(2)}, u32[]{:S(2)}) async-start(bf16[32,2,64,128]{3,2,1,0:T(8,128)(2,1)} %pad_maximum_fusion), calls=%async_computation.2 | async-start | bytes 2097152 | tf_op jit(solution)/shard_map/all_to_all | solution.py:180
  68.2 23.9 %collective-permute-start.8 = (bf16[128]{0:T(256)(128)(2,1)S(1)}, bf16[128]{0:T(256)(128)(2,1)}, u32[]{:S(2)}, u32[]{:S(2)}) collective-permute-start(bf16[128]{0:T(256)(128)(2,1)S(1)} %bitcast.56), channel_id=1, source_target_pairs={{0,1},{1,0},{2,3},{3,2},{4,5},{5,4},{6,7},{7,6},{8,9},{9,8},{10,11... | collective-permute-start | bytes 776 | tf_op jit(solution)/shard_map/ppermute | solution.py:167
  71.8 54.2 %collective-permute-start.6 = (bf16[2,128,256]{2,1,0:T(8,128)(2,1)S(1)}, bf16[2,128,256]{2,1,0:T(8,128)(2,1)S(1)}, u32[]{:S(2)}, u32[]{:S(2)}) collective-permute-start(bf16[2,128,256]{2,1,0:T(8,128)(2,1)S(1)} %pad_maximum_fusion.6), channel_id=1, source_target_pairs={{0,12},{2,14},{4,0},{6,2},{8,4},{10,6},{12,8},{14,10},{1,13},{3,15... | collective-permute-start | bytes 393224 | tf_op jit(solution)/shard_map/ppermute | solution.py:198
  78.7 33.7 %collective-permute-start.1 = (bf16[2,128,256]{2,1,0:T(8,128)(2,1)}, bf16[2,128,256]{2,1,0:T(8,128)(2,1)}, u32[]{:S(2)}, u32[]{:S(2)}) collective-permute-start(bf16[2,128,256]{2,1,0:T(8,128)(2,1)} %pad_maximum_fusion.1), channel_id=1, source_target_pairs={{0,2},{2,4},{4,6},{6,8},{8,10},{10,12},{12,14},{14,0},{1,3},{3,5},... | collective-permute-start | bytes 393224 | tf_op jit(solution)/shard_map/ppermute | solution.py:198
  81.9 33.5 %collective-permute-start.2 = (bf16[2,128,256]{2,1,0:T(8,128)(2,1)}, bf16[2,128,256]{2,1,0:T(8,128)(2,1)}, u32[]{:S(2)}, u32[]{:S(2)}) collective-permute-start(bf16[2,128,256]{2,1,0:T(8,128)(2,1)} %pad_maximum_fusion.2), channel_id=1, source_target_pairs={{0,4},{2,6},{4,8},{6,10},{8,12},{10,14},{12,0},{14,2},{1,5},{3,7},... | collective-permute-start | bytes 393224 | tf_op jit(solution)/shard_map/ppermute | solution.py:198
  84.5 34.2 %collective-permute-start.3 = (bf16[2,128,256]{2,1,0:T(8,128)(2,1)}, bf16[2,128,256]{2,1,0:T(8,128)(2,1)}, u32[]{:S(2)}, u32[]{:S(2)}) collective-permute-start(bf16[2,128,256]{2,1,0:T(8,128)(2,1)} %pad_maximum_fusion.3), channel_id=1, source_target_pairs={{0,6},{2,8},{4,10},{6,12},{8,14},{10,0},{12,2},{14,4},{1,7},{3,9},... | collective-permute-start | bytes 393224 | tf_op jit(solution)/shard_map/ppermute | solution.py:198
  92.1 27.5 %collective-permute-start.4 = (bf16[2,128,256]{2,1,0:T(8,128)(2,1)S(1)}, bf16[2,128,256]{2,1,0:T(8,128)(2,1)S(1)}, u32[]{:S(2)}, u32[]{:S(2)}) collective-permute-start(bf16[2,128,256]{2,1,0:T(8,128)(2,1)S(1)} %pad_maximum_fusion.4), channel_id=1, source_target_pairs={{0,8},{2,10},{4,12},{6,14},{8,0},{10,2},{12,4},{14,6},{1,9},{3,11}... | collective-permute-start | bytes 393224 | tf_op jit(solution)/shard_map/ppermute | solution.py:198
  102.3 82.8 %all-to-all-start.3 = ((bf16[32,2,64,128]{3,2,1,0:T(8,128)(2,1)}), bf16[32,2,64,128]{3,2,1,0:T(8,128)(2,1)}, u32[]{:S(2)}, u32[]{:S(2)}) async-start(bf16[32,2,64,128]{3,2,1,0:T(8,128)(2,1)} %gather_fusion.1), calls=%async_computation.3 | async-start | bytes 2097152 | tf_op jit(solution)/shard_map/all_to_all | solution.py:181
  112.3 13.7 %collective-permute-start.5 = (bf16[2,128,256]{2,1,0:T(8,128)(2,1)}, bf16[2,128,256]{2,1,0:T(8,128)(2,1)S(1)}, u32[]{:S(2)}, u32[]{:S(2)}) collective-permute-start(bf16[2,128,256]{2,1,0:T(8,128)(2,1)} %pad_maximum_fusion.5), channel_id=1, source_target_pairs={{0,10},{2,12},{4,14},{6,0},{8,2},{10,4},{12,6},{14,8},{1,11},{3,13... | collective-permute-start | bytes 393224 | tf_op jit(solution)/shard_map/ppermute | solution.py:198
  115.4 12.9 %collective-permute-start.7 = (bf16[2,128,256]{2,1,0:T(8,128)(2,1)S(1)}, bf16[2,128,256]{2,1,0:T(8,128)(2,1)S(1)}, u32[]{:S(2)}, u32[]{:S(2)}) collective-permute-start(bf16[2,128,256]{2,1,0:T(8,128)(2,1)S(1)} %pad_maximum_fusion.7), channel_id=1, source_target_pairs={{0,14},{2,0},{4,2},{6,4},{8,6},{10,8},{12,10},{14,12},{1,15},{3,1}... | collective-permute-start | bytes 393224 | tf_op jit(solution)/shard_map/ppermute | solution.py:198
  119.6 28.9 %collective-permute-start = (bf16[2048,128]{1,0:T(8,128)(2,1)S(1)}, bf16[2048,128]{1,0:T(8,128)(2,1)S(1)}, u32[]{:S(2)}, u32[]{:S(2)}) collective-permute-start(bf16[2048,128]{1,0:T(8,128)(2,1)S(1)} %bitcast.51), channel_id=1, source_target_pairs={{0,1},{1,0},{2,3},{3,2},{4,5},{5,4},{6,7},{7,6},{8,9},{9,8},{10,11... | collective-permute-start | bytes 1572872 | tf_op jit(solution)/shard_map/ppermute | solution.py:167
  148.5 2.2 %copy-start = (bf16[1,1024,2048]{2,1,0:T(8,128)(2,1)S(1)}, bf16[1,1024,2048]{2,1,0:T(8,128)(2,1)}, u32[]{:S(2)}) copy-start(bf16[1,1024,2048]{2,1,0:T(8,128)(2,1)} %all-gather.3.cloned.1.call-done) | copy-start | bytes 12582916
  153.1 30.5 %copy-start.4 = (f32[5]{0:T(128)S(1)}, f32[5]{0:T(128)}, u32[]{:S(2)}) copy-start(f32[5]{0:T(128)} %constant.92.clone) | copy-start | bytes 64
  153.1 5.9 %collective-permute-start.9 = (f32[8,1024]{1,0:T(8,128)S(1)}, f32[8,1024]{1,0:T(8,128)S(1)}, u32[]{:S(2)}, u32[]{:S(2)}) collective-permute-start(f32[8,1024]{1,0:T(8,128)S(1)} %get-tuple-element.12), channel_id=1, source_target_pairs={{0,2},{2,0},{4,6},{6,4},{8,10},{10,8},{12,14},{14,12},{1,3},{3,1},... | collective-permute-start | bytes 98312 | tf_op jit(solution)/shard_map/ppermute | solution.py:174
  159.1 7.0 %collective-permute-start.10 = (f32[8,1024]{1,0:T(8,128)S(1)}, f32[8,1024]{1,0:T(8,128)S(1)}, u32[]{:S(2)}, u32[]{:S(2)}) collective-permute-start(f32[8,1024]{1,0:T(8,128)S(1)} %add.112), channel_id=1, source_target_pairs={{0,4},{2,6},{4,0},{6,2},{8,12},{10,14},{12,8},{14,10},{1,5},{3,7},... | collective-permute-start | bytes 98312 | tf_op jit(solution)/shard_map/ppermute | solution.py:174
  166.1 9.8 %collective-permute-start.11 = (f32[8,1024]{1,0:T(8,128)S(1)}, f32[8,1024]{1,0:T(8,128)S(1)}, u32[]{:S(2)}, u32[]{:S(2)}) collective-permute-start(f32[8,1024]{1,0:T(8,128)S(1)} %add.113), channel_id=1, source_target_pairs={{0,8},{2,10},{4,12},{6,14},{8,0},{10,2},{12,4},{14,6},{1,9},{3,11}... | collective-permute-start | bytes 98312 | tf_op jit(solution)/shard_map/ppermute | solution.py:174
  180.5 11.9 %collective-permute-start.12 = (bf16[2048,128]{1,0:T(8,128)(2,1)S(1)}, bf16[2048,128]{1,0:T(8,128)(2,1)}, u32[]{:S(2)}, u32[]{:S(2)}) collective-permute-start(bf16[2048,128]{1,0:T(8,128)(2,1)S(1)} %get-tuple-element.14), channel_id=1, source_target_pairs={{0,1},{1,0},{2,3},{3,2},{4,5},{5,4},{6,7},{7,6},{8,9},{9,8},{10,11... | collective-permute-start | bytes 1572872 | tf_op jit(solution)/shard_map/ppermute | solution.py:167
Sparse Core Ops, SparseCore 0:
  10.1 61.7 all-gather.2

commit v3 on v2

--- a/solution.py
+++ b/solution.py
@@ -106,8 +106,9 @@
 
     @pl.when(pl.program_id(0) == 0)
     def _():
-        squares = sums_ref[0:1, :]
-        inner = sums_ref[1:2, :]
+        sums = jnp.sum(sums_ref[...].reshape(-1, 8, tokens), axis=0)
+        squares = sums[0:1, :]
+        inner = sums[1:2, :]
         inverse = lax.rsqrt(squares / features + EPS)
         factor = inner / features * (inverse * inverse * inverse)
         for block in range(blocks):
@@ -167,18 +168,8 @@
     return lax.ppermute(array, "minor", [(0, 1), (1, 0)])
 
 
-def sum_over_major(array):
-    size = lax.axis_size("major")
-    reach = 1
-    while reach < size:
-        array = array + lax.ppermute(array, "major", [(i, i ^ reach) for i in range(size)])
-        reach *= 2
-    return array
-
-
-def exchange(array, sources):
-    out = lax.all_to_all(array, "member", split_axis=0, concat_axis=0, tiled=True)
-    return lax.all_to_all(out[sources], "member", split_axis=0, concat_axis=0, tiled=True)
+def spread_members(array):
+    return lax.all_to_all(array, "member", split_axis=0, concat_axis=0, tiled=True)
 
 
 def spread_features(residual, upstream):
@@ -197,7 +188,7 @@
         if shift:
             part = lax.ppermute(part, "major", [(i, (i + shift) % size) for i in range(size)])
         received.append(part)
-    return jnp.stack(received)[lax.rem(me + size - jnp.arange(size), size)]
+    return received
 
 
 def local(
@@ -218,20 +209,26 @@
     features = residual.shape[2]
 
     gathered = lax.all_gather(attention_out[0], "major", axis=0, tiled=True)
-    weight_here = exchange(weight[0].reshape(members, rows, width), sources)
-    stream = spread_features(residual[0], upstream[0])
+    parts = spread_features(residual[0], upstream[0])
+    gain_other = swap_minor(norm_gain[0])
+    picked = spread_members(weight[0].reshape(members, rows, width))[sources]
+    picked, gain_other, parts[1], parts[2], parts[7] = lax.optimization_barrier(
+        (picked, gain_other, parts[1], parts[2], parts[7])
+    )
+    weight_here = spread_members(picked)
     moments = jnp.stack(
         (first_moment[0].reshape(members, rows, width), second_moment[0].reshape(members, rows, width)),
         axis=1,
     )
-    weight_here, moments = lax.optimization_barrier((weight_here, moments))
-    moments = exchange(moments, sources)
+    weight_here, moments, *parts = lax.optimization_barrier((weight_here, moments, *parts))
     weight_here = weight_here.reshape(depth, width)
+    weight_other = swap_minor(weight_here)
+    moments = spread_members(spread_members(moments)[sources])
     first_here = moments[:, 0].reshape(depth, width)
     second_here = moments[:, 1].reshape(depth, width)
-
-    gain_other = swap_minor(norm_gain[0])
-    weight_other = swap_minor(weight_here)
+    size = len(parts)
+    stream = jnp.stack(parts)[lax.rem(lax.axis_index("major") + size - jnp.arange(size), size)]
+
     gain = jnp.where(
         minor == 0,
         jnp.concatenate((norm_gain[0], gain_other)),
@@ -241,7 +238,7 @@
     inv_scale = 1.0 / math.sqrt(depth)
     side = minor.astype(jnp.int32)[None]
     hidden, sums = forward(side, gathered, weight_here, weight_other, stream, gain, inv_scale)
-    sums = sum_over_major(sums)
+    sums = lax.all_gather(sums, "major", axis=0, tiled=True)
     mine, theirs = backward(side, gathered, hidden, stream, gain, sums, inv_scale, features)
     gradient = mine + swap_minor(theirs).astype(jnp.float32)
 

time: 204 us -> 200 us (0.980)
  the two profiles are of different devices: /device:TPU:2 before, /device:TPU:4 now
where the time goes in v3:
time: 200 us; the launch traced here: 199 us
  starting transfers between devices  76.2 us (38%)
  waiting for transfers between devices  52.7 us (26%)
  blocking collectives  27.7 us (14%)
  between operations  15.7 us (8%)
  local copies, waits for them, and re-layouts  13.7 us (7%)
  Pallas kernels  7.02 us (4%)
  other arithmetic  6.24 us (3%)
    all_to_all x4, starting transfers between devices, spread_members(): lax.all_to_all(array, 'member', split_axis=0, concat_axis=0, tiled=True)  38.9 us
    ppermute x7, starting transfers between devices, spread_features(): lax.ppermute(part, 'major', [(i, (i + shift) % size) for i in range(size)])  29 us
    all_gather x1, blocking collectives, local(): sums = lax.all_gather(sums, 'major', axis=0, tiled=True)  27.7 us
    all_to_all x4, waiting for transfers between devices, spread_members(): lax.all_to_all(array, 'member', split_axis=0, concat_axis=0, tiled=True)  26.4 us
    ppermute x7, waiting for transfers between devices, spread_features(): lax.ppermute(part, 'major', [(i, (i + shift) % size) for i in range(size)])  19.5 us
    ppermute x3, starting transfers between devices, swap_minor(): return lax.ppermute(array, 'minor', [(0, 1), (1, 0)])  8.27 us
    unnamed x19, local copies, waits for them, and re-layouts  6.82 us
    ppermute x3, waiting for transfers between devices, swap_minor(): return lax.ppermute(array, 'minor', [(0, 1), (1, 0)])  6.01 us
  transfers between devices with their start and end apart: 15, of which 6 were waited for; matrix products, arithmetic and copies ran while one was open for 7% of the time, Pallas kernels for 4%

profile of v3, /device:TPU:4, one launch (start us, length us, event | category | flops | bytes accessed | tf_op | source)
XLA Modules:
  0.0 199.2 jit_solution(15057823022790742683)
XLA Ops:
  7.9 13.4 %all-to-all-start = ((bf16[32,64,128]{2,1,0:T(8,128)(2,1)}), bf16[32,64,128]{2,1,0:T(8,128)(2,1)S(1)}, u32[]{:S(2)}, u32[]{:S(2)}) async-start(bf16[32,64,128]{2,1,0:T(8,128)(2,1)} %bitcast.51), calls=%async_computation | async-start | bytes 1048576 | tf_op jit(solution)/shard_map/all_to_all | solution.py:172
  21.4 3.4 %collective-permute-start = (bf16[128]{0:T(256)(128)(2,1)}, bf16[128]{0:T(256)(128)(2,1)S(1)}, u32[]{:S(2)}, u32[]{:S(2)}) collective-permute-start(bf16[128]{0:T(256)(128)(2,1)} %bitcast.54), channel_id=1, source_target_pairs={{0,1},{1,0},{2,3},{3,2},{4,5},{5,4},{6,7},{7,6},{8,9},{9,8},{10,11... | collective-permute-start | bytes 776 | tf_op jit(solution)/shard_map/ppermute | solution.py:168
  26.2 3.5 %collective-permute-start.1 = (bf16[2,128,256]{2,1,0:T(8,128)(2,1)S(1)}, bf16[2,128,256]{2,1,0:T(8,128)(2,1)S(1)}, u32[]{:S(2)}, u32[]{:S(2)}) collective-permute-start(bf16[2,128,256]{2,1,0:T(8,128)(2,1)S(1)} %pad_maximum_fusion.1), channel_id=1, source_target_pairs={{0,2},{2,4},{4,6},{6,8},{8,10},{10,12},{12,14},{14,0},{1,3},{3,5},... | collective-permute-start | bytes 393224 | tf_op jit(solution)/shard_map/ppermute | solution.py:189
  29.7 4.5 %collective-permute-start.2 = (bf16[2,128,256]{2,1,0:T(8,128)(2,1)S(1)}, bf16[2,128,256]{2,1,0:T(8,128)(2,1)S(1)}, u32[]{:S(2)}, u32[]{:S(2)}) collective-permute-start(bf16[2,128,256]{2,1,0:T(8,128)(2,1)S(1)} %pad_maximum_fusion.2), channel_id=1, source_target_pairs={{0,4},{2,6},{4,8},{6,10},{8,12},{10,14},{12,0},{14,2},{1,5},{3,7},... | collective-permute-start | bytes 393224 | tf_op jit(solution)/shard_map/ppermute | solution.py:189
  34.2 3.6 %collective-permute-start.3 = (bf16[2,128,256]{2,1,0:T(8,128)(2,1)S(1)}, bf16[2,128,256]{2,1,0:T(8,128)(2,1)S(1)}, u32[]{:S(2)}, u32[]{:S(2)}) collective-permute-start(bf16[2,128,256]{2,1,0:T(8,128)(2,1)S(1)} %pad_maximum_fusion.3), channel_id=1, source_target_pairs={{0,14},{2,0},{4,2},{6,4},{8,6},{10,8},{12,10},{14,12},{1,15},{3,1}... | collective-permute-start | bytes 393224 | tf_op jit(solution)/shard_map/ppermute | solution.py:189
  40.5 7.2 %collective-permute-done.2 = bf16[2,128,256]{2,1,0:T(8,128)(2,1)S(1)} collective-permute-done((bf16[2,128,256]{2,1,0:T(8,128)(2,1)S(1)}, bf16[2,128,256]{2,1,0:T(8,128)(2,1)S(1)}, u32[]{:S(2)}, u32[]{:S(2)}) %collective-permute-start.2) | collective-permute-done | bytes 131104 | tf_op jit(solution)/shard_map/ppermute | solution.py:189
  47.7 9.7 %all-to-all-start.1 = ((bf16[32,64,128]{2,1,0:T(8,128)(2,1)}), bf16[32,64,128]{2,1,0:T(8,128)(2,1)S(1)}, u32[]{:S(2)}, u32[]{:S(2)}) async-start(bf16[32,64,128]{2,1,0:T(8,128)(2,1)} %gather_fusion), calls=%async_computation.1 | async-start | bytes 1048576 | tf_op jit(solution)/shard_map/all_to_all | solution.py:172
  57.4 6.7 %collective-permute-start.6 = (bf16[2,128,256]{2,1,0:T(8,128)(2,1)S(1)}, bf16[2,128,256]{2,1,0:T(8,128)(2,1)S(1)}, u32[]{:S(2)}, u32[]{:S(2)}) collective-permute-start(bf16[2,128,256]{2,1,0:T(8,128)(2,1)S(1)} %pad_maximum_fusion.7), channel_id=1, source_target_pairs={{0,10},{2,12},{4,14},{6,0},{8,2},{10,4},{12,6},{14,8},{1,11},{3,13... | collective-permute-start | bytes 393224 | tf_op jit(solution)/shard_map/ppermute | solution.py:189
  64.1 1.9 collective-permute-start.4
  66.0 4.2 %collective-permute-start.5 = (bf16[2,128,256]{2,1,0:T(8,128)(2,1)S(1)}, bf16[2,128,256]{2,1,0:T(8,128)(2,1)S(1)}, u32[]{:S(2)}, u32[]{:S(2)}) collective-permute-start(bf16[2,128,256]{2,1,0:T(8,128)(2,1)S(1)} %pad_maximum_fusion.6), channel_id=1, source_target_pairs={{0,8},{2,10},{4,12},{6,14},{8,0},{10,2},{12,4},{14,6},{1,9},{3,11}... | collective-permute-start | bytes 393224 | tf_op jit(solution)/shard_map/ppermute | solution.py:189
  70.3 4.6 %collective-permute-start.7 = (bf16[2,128,256]{2,1,0:T(8,128)(2,1)S(1)}, bf16[2,128,256]{2,1,0:T(8,128)(2,1)S(1)}, u32[]{:S(2)}, u32[]{:S(2)}) collective-permute-start(bf16[2,128,256]{2,1,0:T(8,128)(2,1)S(1)} %pad_maximum_fusion.8), channel_id=1, source_target_pairs={{0,12},{2,14},{4,0},{6,2},{8,4},{10,6},{12,8},{14,10},{1,13},{3,15... | collective-permute-start | bytes 393224 | tf_op jit(solution)/shard_map/ppermute | solution.py:189
  76.1 7.5 %collective-permute-done.4 = bf16[2,128,256]{2,1,0:T(8,128)(2,1)S(1)} collective-permute-done((bf16[2,128,256]{2,1,0:T(8,128)(2,1)S(1)}, bf16[2,128,256]{2,1,0:T(8,128)(2,1)S(1)}, u32[]{:S(2)}, u32[]{:S(2)}) %collective-permute-start.4) | collective-permute-done | bytes 131104 | tf_op jit(solution)/shard_map/ppermute | solution.py:189
  83.6 4.8 %collective-permute-done.5 = bf16[2,128,256]{2,1,0:T(8,128)(2,1)S(1)} collective-permute-done((bf16[2,128,256]{2,1,0:T(8,128)(2,1)S(1)}, bf16[2,128,256]{2,1,0:T(8,128)(2,1)S(1)}, u32[]{:S(2)}, u32[]{:S(2)}) %collective-permute-start.5) | collective-permute-done | bytes 131104 | tf_op jit(solution)/shard_map/ppermute | solution.py:189
  88.4 9.8 %all-to-all-start.2 = ((bf16[32,2,64,128]{3,2,1,0:T(8,128)(2,1)}), bf16[32,2,64,128]{3,2,1,0:T(8,128)(2,1)S(1)}, u32[]{:S(2)}, u32[]{:S(2)}) async-start(bf16[32,2,64,128]{3,2,1,0:T(8,128)(2,1)} %pad_maximum_fusion), calls=%async_computation.2 | async-start | bytes 2097152 | tf_op jit(solution)/shard_map/all_to_all | solution.py:172
  98.3 2.5 %collective-permute-start.8 = (bf16[2048,128]{1,0:T(8,128)(2,1)S(1)}, bf16[2048,128]{1,0:T(8,128)(2,1)S(1)}, u32[]{:S(2)}, u32[]{:S(2)}) collective-permute-start(bf16[2048,128]{1,0:T(8,128)(2,1)S(1)} %bitcast.49), channel_id=1, source_target_pairs={{0,1},{1,0},{2,3},{3,2},{4,5},{5,4},{6,7},{7,6},{8,9},{9,8},{10,11... | collective-permute-start | bytes 1572872 | tf_op jit(solution)/shard_map/ppermute | solution.py:168
  101.5 25.2 %all-to-all-done.2 = bf16[32,2,64,128]{3,2,1,0:T(8,128)(2,1)S(1)} async-done(((bf16[32,2,64,128]{3,2,1,0:T(8,128)(2,1)}), bf16[32,2,64,128]{3,2,1,0:T(8,128)(2,1)S(1)}, u32[]{:S(2)}, u32[]{:S(2)}) %all-to-all-start.2) | async-done | bytes 1048608 | tf_op jit(solution)/shard_map/all_to_all | solution.py:172
  128.3 6.0 %all-to-all-start.3 = ((bf16[32,2,64,128]{3,2,1,0:T(8,128)(2,1)}), bf16[32,2,64,128]{3,2,1,0:T(8,128)(2,1)}, u32[]{:S(2)}, u32[]{:S(2)}) async-start(bf16[32,2,64,128]{3,2,1,0:T(8,128)(2,1)} %gather_fusion.1), calls=%async_computation.3 | async-start | bytes 2097152 | tf_op jit(solution)/shard_map/all_to_all | solution.py:172
  140.8 2.2 %copy-done = bf16[1,1024,2048]{2,1,0:T(8,128)(2,1)S(1)} copy-done((bf16[1,1024,2048]{2,1,0:T(8,128)(2,1)S(1)}, bf16[1,1024,2048]{2,1,0:T(8,128)(2,1)}, u32[]{:S(2)}) %copy-start) | copy-done | bytes 4194328
  143.0 2.5 %forward.1 = (f32[1024,256]{1,0:T(8,128)S(1)}, f32[8,1024]{1,0:T(8,128)S(1)}) custom-call(s32[1]{0:T(128)} %bitcast.7.minor_ref, bf16[1024,2048]{1,0:T(8,128)(2,1)S(1)} %bitcast.47, bf16[2048,128]{1,0:T(8,128)(2,1)S(1)} %bitcast.50, bf16[2048,128]{1,0:T(8,128)(2,1)S(1)} %collective-permute-done.8.other_ref, bf16[8,2,128,256]{3,2,1,0:T(8,128)(2,1)S(1)} %gather_fusion.2, ...), custom_call_target="tpu_custom_call" | custom-call | flops 1073741824 | bytes 7340032 | tf_op jit(solution)/shard_map/forward/pallas_call | solution.py:72
  145.4 27.7 %all_gather.7.sums_ref = f32[64,1024]{1,0:T(8,128)S(1)} all-gather(f32[8,1024]{1,0:T(8,128)S(1)} %get-tuple-element.38), channel_id=1, replica_groups=mesh['member'=32,'major'=8,'minor'=2] {'major'}, dimensions={0}, use_global_device_ids=true | all-gather | bytes 294912 | tf_op jit(solution)/shard_map/all_gather | solution.py:241
  173.1 4.6 %backward.1 = (f32[2048,128]{1,0:T(8,128)S(1)}, bf16[2048,128]{1,0:T(8,128)(2,1)S(1)}) custom-call(s32[1]{0:T(128)} %bitcast.7.minor_ref, bf16[1024,2048]{1,0:T(8,128)(2,1)S(1)} %bitcast.48, f32[1024,256]{1,0:T(8,128)S(1)} %get-tuple-element.37.hidden_ref, bf16[8,2,128,256]{3,2,1,0:T(8,128)(2,1)S(1)} %gather_fusion.2, f32[1,256]{1,0:T(1,128)S(1)} %fusion.2.gain_ref, ...), custom_call_target="tpu_custom_call" | custom-call | flops 1073741824 | bytes 8388608 | tf_op jit(solution)/shard_map/backward/pallas_call | solution.py:137
  177.7 2.4 %collective-permute-start.9 = (bf16[2048,128]{1,0:T(8,128)(2,1)S(1)}, bf16[2048,128]{1,0:T(8,128)(2,1)S(1)}, u32[]{:S(2)}, u32[]{:S(2)}) collective-permute-start(bf16[2048,128]{1,0:T(8,128)(2,1)S(1)} %get-tuple-element.40), channel_id=1, source_target_pairs={{0,1},{1,0},{2,3},{3,2},{4,5},{5,4},{6,7},{7,6},{8,9},{9,8},{10,11... | collective-permute-start | bytes 1572872 | tf_op jit(solution)/shard_map/ppermute | solution.py:168
  183.5 6.0 %collective-permute-done.9 = bf16[2048,128]{1,0:T(8,128)(2,1)S(1)} collective-permute-done((bf16[2048,128]{1,0:T(8,128)(2,1)S(1)}, bf16[2048,128]{1,0:T(8,128)(2,1)S(1)}, u32[]{:S(2)}, u32[]{:S(2)}) %collective-permute-start.9) | collective-permute-done | bytes 524320 | tf_op jit(solution)/shard_map/ppermute | solution.py:168
  189.5 2.9 %convert_bitcast_fusion = (bf16[1,2048,128]{2,1,0:T(8,128)(2,1)}, bf16[1,2048,128]{2,1,0:T(8,128)(2,1)}, bf16[1,2048,128]{2,1,0:T(8,128)(2,1)}) fusion(f32[2048,128]{1,0:T(8,128)S(1)} %get-tuple-element.39, bf16[2048,128]{1,0:T(8,128)(2,1)S(1)} %collective-permute-done.9, f32[32,1,64,128]{3,2,1,0:T(8,128)S(1)} %get-tuple-element.44, ...), kind=kLoop, calls=%fused_computation.11 | loop fusion | flops 4718592 | bytes 5767176 | tf_op jit(solution)/shard_map/broadcast_in_dim | solution.py:250
  (51 shorter events, 16.9 us)
Async XLA Ops:
  7.2 30.7 %copy-start.4 = (s32[32]{0:T(128)S(1)}, s32[32]{0:T(128)}, u32[]{:S(2)}) copy-start(s32[32]{0:T(128)} %param.17) | copy-start | bytes 388
  7.2 67.8 %copy-start.1 = (bf16[1,2048,128]{2,1,0:T(8,128)(2,1)S(1)}, bf16[1,2048,128]{2,1,0:T(8,128)(2,1)}, u32[]{:S(2)}) copy-start(bf16[1,2048,128]{2,1,0:T(8,128)(2,1)} %param.16) | copy-start | bytes 1572868
  7.2 67.8 %copy-start.2 = (bf16[1,2048,128]{2,1,0:T(8,128)(2,1)S(1)}, bf16[1,2048,128]{2,1,0:T(8,128)(2,1)}, u32[]{:S(2)}) copy-start(bf16[1,2048,128]{2,1,0:T(8,128)(2,1)} %param.15) | copy-start | bytes 1572868
  7.2 133.6 %all-gather.3.cloned.1.call-start = ((), (), s32[]{:S(2)}) async-start(), calls=%async_computation.4 | async-start | bytes 4718592 | tf_op jit(solution)/shard_map/all_gather | solution.py:211
  7.9 31.2 %all-to-all-start = ((bf16[32,64,128]{2,1,0:T(8,128)(2,1)}), bf16[32,64,128]{2,1,0:T(8,128)(2,1)S(1)}, u32[]{:S(2)}, u32[]{:S(2)}) async-start(bf16[32,64,128]{2,1,0:T(8,128)(2,1)} %bitcast.51), calls=%async_computation | async-start | bytes 1048576 | tf_op jit(solution)/shard_map/all_to_all | solution.py:172
  21.4 19.1 %collective-permute-start = (bf16[128]{0:T(256)(128)(2,1)}, bf16[128]{0:T(256)(128)(2,1)S(1)}, u32[]{:S(2)}, u32[]{:S(2)}) collective-permute-start(bf16[128]{0:T(256)(128)(2,1)} %bitcast.54), channel_id=1, source_target_pairs={{0,1},{1,0},{2,3},{3,2},{4,5},{5,4},{6,7},{7,6},{8,9},{9,8},{10,11... | collective-permute-start | bytes 776 | tf_op jit(solution)/shard_map/ppermute | solution.py:168
  26.2 72.1 %copy-start.3 = (bf16[1,128]{1,0:T(2,128)(2,1)S(1)}, bf16[1,128]{1,0:T(2,128)(2,1)}, u32[]{:S(2)}) copy-start(bf16[1,128]{1,0:T(2,128)(2,1)} %param.13) | copy-start | bytes 772
  26.2 14.3 %collective-permute-start.1 = (bf16[2,128,256]{2,1,0:T(8,128)(2,1)S(1)}, bf16[2,128,256]{2,1,0:T(8,128)(2,1)S(1)}, u32[]{:S(2)}, u32[]{:S(2)}) collective-permute-start(bf16[2,128,256]{2,1,0:T(8,128)(2,1)S(1)} %pad_maximum_fusion.1), channel_id=1, source_target_pairs={{0,2},{2,4},{4,6},{6,8},{8,10},{10,12},{12,14},{14,0},{1,3},{3,5},... | collective-permute-start | bytes 393224 | tf_op jit(solution)/shard_map/ppermute | solution.py:189
  29.7 17.9 %collective-permute-start.2 = (bf16[2,128,256]{2,1,0:T(8,128)(2,1)S(1)}, bf16[2,128,256]{2,1,0:T(8,128)(2,1)S(1)}, u32[]{:S(2)}, u32[]{:S(2)}) collective-permute-start(bf16[2,128,256]{2,1,0:T(8,128)(2,1)S(1)} %pad_maximum_fusion.2), channel_id=1, source_target_pairs={{0,4},{2,6},{4,8},{6,10},{8,12},{10,14},{12,0},{14,2},{1,5},{3,7},... | collective-permute-start | bytes 393224 | tf_op jit(solution)/shard_map/ppermute | solution.py:189
  34.2 13.4 %collective-permute-start.3 = (bf16[2,128,256]{2,1,0:T(8,128)(2,1)S(1)}, bf16[2,128,256]{2,1,0:T(8,128)(2,1)S(1)}, u32[]{:S(2)}, u32[]{:S(2)}) collective-permute-start(bf16[2,128,256]{2,1,0:T(8,128)(2,1)S(1)} %pad_maximum_fusion.3), channel_id=1, source_target_pairs={{0,14},{2,0},{4,2},{6,4},{8,6},{10,8},{12,10},{14,12},{1,15},{3,1}... | collective-permute-start | bytes 393224 | tf_op jit(solution)/shard_map/ppermute | solution.py:189
  47.7 40.8 %all-to-all-start.1 = ((bf16[32,64,128]{2,1,0:T(8,128)(2,1)}), bf16[32,64,128]{2,1,0:T(8,128)(2,1)S(1)}, u32[]{:S(2)}, u32[]{:S(2)}) async-start(bf16[32,64,128]{2,1,0:T(8,128)(2,1)} %gather_fusion), calls=%async_computation.1 | async-start | bytes 1048576 | tf_op jit(solution)/shard_map/all_to_all | solution.py:172
  57.4 18.7 %collective-permute-start.6 = (bf16[2,128,256]{2,1,0:T(8,128)(2,1)S(1)}, bf16[2,128,256]{2,1,0:T(8,128)(2,1)S(1)}, u32[]{:S(2)}, u32[]{:S(2)}) collective-permute-start(bf16[2,128,256]{2,1,0:T(8,128)(2,1)S(1)} %pad_maximum_fusion.7), channel_id=1, source_target_pairs={{0,10},{2,12},{4,14},{6,0},{8,2},{10,4},{12,6},{14,8},{1,11},{3,13... | collective-permute-start | bytes 393224 | tf_op jit(solution)/shard_map/ppermute | solution.py:189
  64.1 19.5 %collective-permute-start.4 = (bf16[2,128,256]{2,1,0:T(8,128)(2,1)S(1)}, bf16[2,128,256]{2,1,0:T(8,128)(2,1)S(1)}, u32[]{:S(2)}, u32[]{:S(2)}) collective-permute-start(bf16[2,128,256]{2,1,0:T(8,128)(2,1)S(1)} %pad_maximum_fusion.5), channel_id=1, source_target_pairs={{0,6},{2,8},{4,10},{6,12},{8,14},{10,0},{12,2},{14,4},{1,7},{3,9},... | collective-permute-start | bytes 393224 | tf_op jit(solution)/shard_map/ppermute | solution.py:189
  66.0 22.4 %collective-permute-start.5 = (bf16[2,128,256]{2,1,0:T(8,128)(2,1)S(1)}, bf16[2,128,256]{2,1,0:T(8,128)(2,1)S(1)}, u32[]{:S(2)}, u32[]{:S(2)}) collective-permute-start(bf16[2,128,256]{2,1,0:T(8,128)(2,1)S(1)} %pad_maximum_fusion.6), channel_id=1, source_target_pairs={{0,8},{2,10},{4,12},{6,14},{8,0},{10,2},{12,4},{14,6},{1,9},{3,11}... | collective-permute-start | bytes 393224 | tf_op jit(solution)/shard_map/ppermute | solution.py:189
  70.3 18.2 %collective-permute-start.7 = (bf16[2,128,256]{2,1,0:T(8,128)(2,1)S(1)}, bf16[2,128,256]{2,1,0:T(8,128)(2,1)S(1)}, u32[]{:S(2)}, u32[]{:S(2)}) collective-permute-start(bf16[2,128,256]{2,1,0:T(8,128)(2,1)S(1)} %pad_maximum_fusion.8), channel_id=1, source_target_pairs={{0,12},{2,14},{4,0},{6,2},{8,4},{10,6},{12,8},{14,10},{1,13},{3,15... | collective-permute-start | bytes 393224 | tf_op jit(solution)/shard_map/ppermute | solution.py:189
  88.4 38.2 %all-to-all-start.2 = ((bf16[32,2,64,128]{3,2,1,0:T(8,128)(2,1)}), bf16[32,2,64,128]{3,2,1,0:T(8,128)(2,1)S(1)}, u32[]{:S(2)}, u32[]{:S(2)}) async-start(bf16[32,2,64,128]{3,2,1,0:T(8,128)(2,1)} %pad_maximum_fusion), calls=%async_computation.2 | async-start | bytes 2097152 | tf_op jit(solution)/shard_map/all_to_all | solution.py:172
  98.3 42.4 %collective-permute-start.8 = (bf16[2048,128]{1,0:T(8,128)(2,1)S(1)}, bf16[2048,128]{1,0:T(8,128)(2,1)S(1)}, u32[]{:S(2)}, u32[]{:S(2)}) collective-permute-start(bf16[2048,128]{1,0:T(8,128)(2,1)S(1)} %bitcast.49), channel_id=1, source_target_pairs={{0,1},{1,0},{2,3},{3,2},{4,5},{5,4},{6,7},{7,6},{8,9},{9,8},{10,11... | collective-permute-start | bytes 1572872 | tf_op jit(solution)/shard_map/ppermute | solution.py:168
  128.3 53.7 %all-to-all-start.3 = ((bf16[32,2,64,128]{3,2,1,0:T(8,128)(2,1)}), bf16[32,2,64,128]{3,2,1,0:T(8,128)(2,1)}, u32[]{:S(2)}, u32[]{:S(2)}) async-start(bf16[32,2,64,128]{3,2,1,0:T(8,128)(2,1)} %gather_fusion.1), calls=%async_computation.3 | async-start | bytes 2097152 | tf_op jit(solution)/shard_map/all_to_all | solution.py:172
  140.8 2.2 %copy-start = (bf16[1,1024,2048]{2,1,0:T(8,128)(2,1)S(1)}, bf16[1,1024,2048]{2,1,0:T(8,128)(2,1)}, u32[]{:S(2)}) copy-start(bf16[1,1024,2048]{2,1,0:T(8,128)(2,1)} %all-gather.3.cloned.1.call-done) | copy-start | bytes 12582916
  145.4 35.3 %copy-start.5 = (f32[5]{0:T(128)S(1)}, f32[5]{0:T(128)}, u32[]{:S(2)}) copy-start(f32[5]{0:T(128)} %constant.92.clone) | copy-start | bytes 64
  177.7 11.8 %collective-permute-start.9 = (bf16[2048,128]{1,0:T(8,128)(2,1)S(1)}, bf16[2048,128]{1,0:T(8,128)(2,1)S(1)}, u32[]{:S(2)}, u32[]{:S(2)}) collective-permute-start(bf16[2048,128]{1,0:T(8,128)(2,1)S(1)} %get-tuple-element.40), channel_id=1, source_target_pairs={{0,1},{1,0},{2,3},{3,2},{4,5},{5,4},{6,7},{7,6},{8,9},{9,8},{10,11... | collective-permute-start | bytes 1572872 | tf_op jit(solution)/shard_map/ppermute | solution.py:168
Sparse Core Ops, SparseCore 0:
  10.1 86.3 all-gather.2

commit v4 on v3

--- a/solution.py
+++ b/solution.py
@@ -22,16 +22,51 @@
 VMEM_LIMIT = 24 * 1024 * 1024
 
 
-def adamw_update(weight_now, first_now, second_now, gradient, rate_value):
-    first_sum = BETA_ONE * first_now.astype(jnp.float32) + (1.0 - BETA_ONE) * gradient
-    second_sum = BETA_TWO * second_now.astype(jnp.float32) + (1.0 - BETA_TWO) * gradient * gradient
+def adamw_kernel(rate_ref, weight_ref, moments_ref, mine_ref, theirs_ref, weight_out, first_out, second_out):
+    rate = jnp.float32(0.0)
+    for slot, value in enumerate(RATE_TABLE):
+        rate = jnp.where(rate_ref[0] == slot, jnp.float32(value), rate)
+    shape = weight_ref.shape
+    gradient = mine_ref[...] + theirs_ref[...].astype(jnp.float32)
+    weight_now = weight_ref[...].astype(jnp.float32)
+    first_now = moments_ref[:, 0].reshape(shape).astype(jnp.float32)
+    second_now = moments_ref[:, 1].reshape(shape).astype(jnp.float32)
+    first_sum = BETA_ONE * first_now + (1.0 - BETA_ONE) * gradient
+    second_sum = BETA_TWO * second_now + (1.0 - BETA_TWO) * gradient * gradient
     update = first_sum / bias_one / (jnp.sqrt(second_sum / bias_two) + ADAM_EPS)
-    weight_new = weight_now.astype(jnp.float32) * (1.0 - rate_value * DECAY) - rate_value * update
-    return (
-        weight_new.astype(jnp.bfloat16),
-        first_sum.astype(jnp.bfloat16),
-        second_sum.astype(jnp.bfloat16),
-    )
+    weight_new = weight_now * (1.0 - rate * DECAY) - rate * update
+    weight_out[0] = weight_new.astype(jnp.bfloat16)
+    first_out[0] = first_sum.astype(jnp.bfloat16)
+    second_out[0] = second_sum.astype(jnp.bfloat16)
+
+
+def adamw(rate_index, weight, moments, mine, theirs):
+    depth, width = weight.shape
+    members, kinds, rows = moments.shape[:3]
+    pieces = 4
+    step = pieces * rows
+    flat = pl.BlockSpec((step, width), lambda i, r: (i, 0))
+    out = pl.BlockSpec((1, step, width), lambda i, r: (0, i, 0))
+    return pl.pallas_call(
+        adamw_kernel,
+        grid_spec=pltpu.PrefetchScalarGridSpec(
+            num_scalar_prefetch=1,
+            grid=(members // pieces,),
+            in_specs=[
+                flat,
+                pl.BlockSpec((pieces, kinds, rows, width), lambda i, r: (i, 0, 0, 0)),
+                flat,
+                flat,
+            ],
+            out_specs=[out, out, out],
+        ),
+        out_shape=[jax.ShapeDtypeStruct((1, depth, width), jnp.bfloat16)] * 3,
+        compiler_params=pltpu.CompilerParams(vmem_limit_bytes=VMEM_LIMIT),
+        cost_estimate=pl.CostEstimate(
+            flops=20 * depth * width, bytes_accessed=18 * depth * width, transcendentals=depth * width
+        ),
+        name="adamw",
+    )(rate_index, weight, moments, mine, theirs)
 
 
 def forward_kernel(inv_scale, minor_ref, rows_ref, own_ref, other_ref, stream_ref, gain_ref, hidden_ref, sums_ref, both_ref):
@@ -106,9 +141,8 @@
 
     @pl.when(pl.program_id(0) == 0)
     def _():
-        sums = jnp.sum(sums_ref[...].reshape(-1, 8, tokens), axis=0)
-        squares = sums[0:1, :]
-        inner = sums[1:2, :]
+        squares = sums_ref[0:1, :]
+        inner = sums_ref[1:2, :]
         inverse = lax.rsqrt(squares / features + EPS)
         factor = inner / features * (inverse * inverse * inverse)
         for block in range(blocks):
@@ -166,6 +200,15 @@
 
 def swap_minor(array):
     return lax.ppermute(array, "minor", [(0, 1), (1, 0)])
+
+
+def sum_over_major(array):
+    size = lax.axis_size("major")
+    reach = 1
+    while reach < size:
+        array = array + lax.ppermute(array, "major", [(i, i ^ reach) for i in range(size)])
+        reach *= 2
+    return array
 
 
 def spread_members(array):
@@ -212,20 +255,18 @@
     parts = spread_features(residual[0], upstream[0])
     gain_other = swap_minor(norm_gain[0])
     picked = spread_members(weight[0].reshape(members, rows, width))[sources]
-    picked, gain_other, parts[1], parts[2], parts[7] = lax.optimization_barrier(
-        (picked, gain_other, parts[1], parts[2], parts[7])
-    )
+    picked, gain_other, parts[1] = lax.optimization_barrier((picked, gain_other, parts[1]))
     weight_here = spread_members(picked)
     moments = jnp.stack(
         (first_moment[0].reshape(members, rows, width), second_moment[0].reshape(members, rows, width)),
         axis=1,
     )
-    weight_here, moments, *parts = lax.optimization_barrier((weight_here, moments, *parts))
+    weight_here, moments, parts[2], parts[6], parts[7] = lax.optimization_barrier(
+        (weight_here, moments, parts[2], parts[6], parts[7])
+    )
     weight_here = weight_here.reshape(depth, width)
     weight_other = swap_minor(weight_here)
-    moments = spread_members(spread_members(moments)[sources])
-    first_here = moments[:, 0].reshape(depth, width)
-    second_here = moments[:, 1].reshape(depth, width)
+    moments = spread_members(moments)
     size = len(parts)
     stream = jnp.stack(parts)[lax.rem(lax.axis_index("major") + size - jnp.arange(size), size)]
 
@@ -238,16 +279,11 @@
     inv_scale = 1.0 / math.sqrt(depth)
     side = minor.astype(jnp.int32)[None]
     hidden, sums = forward(side, gathered, weight_here, weight_other, stream, gain, inv_scale)
-    sums = lax.all_gather(sums, "major", axis=0, tiled=True)
+    moments, sums = lax.optimization_barrier((moments, sums))
+    moments = spread_members(moments[sources])
+    sums = sum_over_major(sums)
     mine, theirs = backward(side, gathered, hidden, stream, gain, sums, inv_scale, features)
-    gradient = mine + swap_minor(theirs).astype(jnp.float32)
-
-    rate_table = jnp.asarray(RATE_TABLE, dtype=jnp.float32)
-    rate_value = jnp.sum(jnp.where(jnp.arange(5) == rate_index[0], rate_table, 0.0))
-    weight_new, first_new, second_new = adamw_update(
-        weight_here, first_here, second_here, gradient, rate_value
-    )
-    return (weight_new[None], first_new[None], second_new[None])
+    return adamw(rate_index, weight_here, moments, mine, swap_minor(theirs))
 
 
 def solution(mesh):

time: 200 us -> 199 us (level)
  the two profiles are of different devices: /device:TPU:4 before, /device:TPU:60 now
where the time goes in v4:
time: 199 us; the launch traced here: 198 us
  starting transfers between devices  84.1 us (42%)
  waiting for transfers between devices  66.7 us (34%)
  local copies, waits for them, and re-layouts  17.8 us (9%)
  between operations  15.1 us (8%)
  Pallas kernels  10.4 us (5%)
  other arithmetic  3.86 us (2%)
    all_to_all x4, starting transfers between devices, spread_members(): lax.all_to_all(array, 'member', split_axis=0, concat_axis=0, tiled=True)  38.9 us
    ppermute x3, waiting for transfers between devices, swap_minor(): return lax.ppermute(array, 'minor', [(0, 1), (1, 0)])  38.9 us
    ppermute x7, starting transfers between devices, spread_features(): lax.ppermute(part, 'major', [(i, (i + shift) % size) for i in range(size)])  29.2 us
    ppermute x3, waiting for transfers between devices, sum_over_major(): lax.ppermute(array, 'major', [(i, i ^ reach) for i in range(size)])  14.8 us
    unnamed x30, local copies, waits for them, and re-layouts  10.7 us
    all_to_all x4, waiting for transfers between devices, spread_members(): lax.all_to_all(array, 'member', split_axis=0, concat_axis=0, tiled=True)  10.3 us
    ppermute x3, starting transfers between devices, swap_minor(): return lax.ppermute(array, 'minor', [(0, 1), (1, 0)])  8.49 us
    ppermute x3, starting transfers between devices, sum_over_major(): lax.ppermute(array, 'major', [(i, i ^ reach) for i in range(size)])  7.43 us
  transfers between devices with their start and end apart: 18, of which 7 were waited for; matrix products, arithmetic and copies ran while one was open for 5% of the time, Pallas kernels for 4%

profile of v4, /device:TPU:60, one launch (start us, length us, event | category | flops | bytes accessed | tf_op | source)
XLA Modules:
  0.0 197.9 jit_solution(5121342227624631269)
XLA Ops:
  7.9 13.4 %all-to-all-start = ((bf16[32,64,128]{2,1,0:T(8,128)(2,1)}), bf16[32,64,128]{2,1,0:T(8,128)(2,1)S(1)}, u32[]{:S(2)}, u32[]{:S(2)}) async-start(bf16[32,64,128]{2,1,0:T(8,128)(2,1)} %bitcast.33), calls=%async_computation | async-start | bytes 1048576 | tf_op jit(solution)/shard_map/all_to_all | solution.py:215
  21.4 3.4 %collective-permute-start = (bf16[128]{0:T(256)(128)(2,1)}, bf16[128]{0:T(256)(128)(2,1)S(1)}, u32[]{:S(2)}, u32[]{:S(2)}) collective-permute-start(bf16[128]{0:T(256)(128)(2,1)} %bitcast.36), channel_id=1, source_target_pairs={{0,1},{1,0},{2,3},{3,2},{4,5},{5,4},{6,7},{7,6},{8,9},{9,8},{10,11... | collective-permute-start | bytes 776 | tf_op jit(solution)/shard_map/ppermute | solution.py:202
  28.8 10.3 %all-to-all-done = bf16[32,64,128]{2,1,0:T(8,128)(2,1)S(1)} async-done(((bf16[32,64,128]{2,1,0:T(8,128)(2,1)}), bf16[32,64,128]{2,1,0:T(8,128)(2,1)S(1)}, u32[]{:S(2)}, u32[]{:S(2)}) %all-to-all-start) | async-done | bytes 524320 | tf_op jit(solution)/shard_map/all_to_all | solution.py:215
  40.5 5.8 %all-to-all-start.1 = ((bf16[32,64,128]{2,1,0:T(8,128)(2,1)}), bf16[32,64,128]{2,1,0:T(8,128)(2,1)S(1)}, u32[]{:S(2)}, u32[]{:S(2)}) async-start(bf16[32,64,128]{2,1,0:T(8,128)(2,1)} %gather_fusion), calls=%async_computation.1 | async-start | bytes 1048576 | tf_op jit(solution)/shard_map/all_to_all | solution.py:215
  46.4 5.3 %collective-permute-start.7 = (bf16[2,128,256]{2,1,0:T(8,128)(2,1)S(1)}, bf16[2,128,256]{2,1,0:T(8,128)(2,1)S(1)}, u32[]{:S(2)}, u32[]{:S(2)}) collective-permute-start(bf16[2,128,256]{2,1,0:T(8,128)(2,1)S(1)} %pad_maximum_fusion.6), channel_id=1, source_target_pairs={{0,8},{2,10},{4,12},{6,14},{8,0},{10,2},{12,4},{14,6},{1,9},{3,11}... | collective-permute-start | bytes 393224 | tf_op jit(solution)/shard_map/ppermute | solution.py:232
  51.7 4.0 %collective-permute-start.2 = (bf16[2,128,256]{2,1,0:T(8,128)(2,1)S(1)}, bf16[2,128,256]{2,1,0:T(8,128)(2,1)S(1)}, u32[]{:S(2)}, u32[]{:S(2)}) collective-permute-start(bf16[2,128,256]{2,1,0:T(8,128)(2,1)S(1)} %pad_maximum_fusion.2), channel_id=1, source_target_pairs={{0,4},{2,6},{4,8},{6,10},{8,12},{10,14},{12,0},{14,2},{1,5},{3,7},... | collective-permute-start | bytes 393224 | tf_op jit(solution)/shard_map/ppermute | solution.py:232
  55.8 2.7 %collective-permute-start.3 = (bf16[2,128,256]{2,1,0:T(8,128)(2,1)S(1)}, bf16[2,128,256]{2,1,0:T(8,128)(2,1)S(1)}, u32[]{:S(2)}, u32[]{:S(2)}) collective-permute-start(bf16[2,128,256]{2,1,0:T(8,128)(2,1)S(1)} %pad_maximum_fusion.3), channel_id=1, source_target_pairs={{0,12},{2,14},{4,0},{6,2},{8,4},{10,6},{12,8},{14,10},{1,13},{3,15... | collective-permute-start | bytes 393224 | tf_op jit(solution)/shard_map/ppermute | solution.py:232
  58.5 4.2 %collective-permute-start.4 = (bf16[2,128,256]{2,1,0:T(8,128)(2,1)S(1)}, bf16[2,128,256]{2,1,0:T(8,128)(2,1)S(1)}, u32[]{:S(2)}, u32[]{:S(2)}) collective-permute-start(bf16[2,128,256]{2,1,0:T(8,128)(2,1)S(1)} %pad_maximum_fusion.4), channel_id=1, source_target_pairs={{0,14},{2,0},{4,2},{6,4},{8,6},{10,8},{12,10},{14,12},{1,15},{3,1}... | collective-permute-start | bytes 393224 | tf_op jit(solution)/shard_map/ppermute | solution.py:232
  63.3 4.5 %collective-permute-start.6 = (bf16[2,128,256]{2,1,0:T(8,128)(2,1)}, bf16[2,128,256]{2,1,0:T(8,128)(2,1)}, u32[]{:S(2)}, u32[]{:S(2)}) collective-permute-start(bf16[2,128,256]{2,1,0:T(8,128)(2,1)} %pad_maximum_fusion.5), channel_id=1, source_target_pairs={{0,6},{2,8},{4,10},{6,12},{8,14},{10,0},{12,2},{14,4},{1,7},{3,9},... | collective-permute-start | bytes 393224 | tf_op jit(solution)/shard_map/ppermute | solution.py:232
  69.6 6.6 %collective-permute-start.8 = (bf16[2,128,256]{2,1,0:T(8,128)(2,1)}, bf16[2,128,256]{2,1,0:T(8,128)(2,1)S(1)}, u32[]{:S(2)}, u32[]{:S(2)}) collective-permute-start(bf16[2,128,256]{2,1,0:T(8,128)(2,1)} %pad_maximum_fusion.7), channel_id=1, source_target_pairs={{0,10},{2,12},{4,14},{6,0},{8,2},{10,4},{12,6},{14,8},{1,11},{3,13... | collective-permute-start | bytes 393224 | tf_op jit(solution)/shard_map/ppermute | solution.py:232
  78.3 10.0 %all-to-all-start.2 = ((bf16[32,2,64,128]{3,2,1,0:T(8,128)(2,1)}), bf16[32,2,64,128]{3,2,1,0:T(8,128)(2,1)}, u32[]{:S(2)}, u32[]{:S(2)}) async-start(bf16[32,2,64,128]{3,2,1,0:T(8,128)(2,1)} %pad_maximum_fusion), calls=%async_computation.2 | async-start | bytes 2097152 | tf_op jit(solution)/shard_map/all_to_all | solution.py:215
  89.0 2.6 %collective-permute-start.5 = (bf16[2048,128]{1,0:T(8,128)(2,1)S(1)}, bf16[2048,128]{1,0:T(8,128)(2,1)S(1)}, u32[]{:S(2)}, u32[]{:S(2)}) collective-permute-start(bf16[2048,128]{1,0:T(8,128)(2,1)S(1)} %bitcast.30), channel_id=1, source_target_pairs={{0,1},{1,0},{2,3},{3,2},{4,5},{5,4},{6,7},{7,6},{8,9},{9,8},{10,11... | collective-permute-start | bytes 1572872 | tf_op jit(solution)/shard_map/ppermute | solution.py:202
  95.1 28.7 %collective-permute-done.5.other_ref = bf16[2048,128]{1,0:T(8,128)(2,1)S(1)} collective-permute-done((bf16[2048,128]{1,0:T(8,128)(2,1)S(1)}, bf16[2048,128]{1,0:T(8,128)(2,1)S(1)}, u32[]{:S(2)}, u32[]{:S(2)}) %collective-permute-start.5) | collective-permute-done | bytes 524320 | tf_op jit(solution)/shard_map/ppermute | solution.py:202
  125.9 2.5 %forward.1 = (f32[1024,256]{1,0:T(8,128)S(1)}, f32[8,1024]{1,0:T(8,128)S(1)}) custom-call(s32[1]{0:T(128)} %bitcast.5.minor_ref, bf16[1024,2048]{1,0:T(8,128)(2,1)S(1)} %bitcast.28, bf16[2048,128]{1,0:T(8,128)(2,1)S(1)} %bitcast.31, bf16[2048,128]{1,0:T(8,128)(2,1)S(1)} %collective-permute-done.5.other_ref, bf16[8,2,128,256]{3,2,1,0:T(8,128)(2,1)S(1)} %gather_fusion.1, ...), custom_call_target="tpu_custom_call" | custom-call | flops 1073741824 | bytes 7340032 | tf_op jit(solution)/shard_map/forward/pallas_call | solution.py:107
  129.4 2.9 %gather_fusion.2 = bf16[32,2,64,128]{3,2,1,0:T(8,128)(2,1)} fusion(bf16[32,2,64,128]{3,2,1,0:T(8,128)(2,1)} %all-to-all-done.2, s32[1024]{0:T(1024)S(1)} %pad_clamp_fusion.1), kind=kCustom, calls=%fused_computation.2 | custom fusion | bytes 2097280 | tf_op jit(solution)/shard_map/gather | solution.py:283
  132.3 9.7 %all-to-all-start.3 = ((bf16[32,2,64,128]{3,2,1,0:T(8,128)(2,1)}), bf16[32,2,64,128]{3,2,1,0:T(8,128)(2,1)S(1)}, u32[]{:S(2)}, u32[]{:S(2)}) async-start(bf16[32,2,64,128]{3,2,1,0:T(8,128)(2,1)} %gather_fusion.2), calls=%async_computation.3 | async-start | bytes 2097152 | tf_op jit(solution)/shard_map/all_to_all | solution.py:215
  143.9 3.9 %collective-permute-done.9 = f32[8,1024]{1,0:T(8,128)S(1)} collective-permute-done((f32[8,1024]{1,0:T(8,128)S(1)}, f32[8,1024]{1,0:T(8,128)S(1)}, u32[]{:S(2)}, u32[]{:S(2)}) %collective-permute-start.9) | collective-permute-done | bytes 32800 | tf_op jit(solution)/shard_map/ppermute | solution.py:209
  147.8 3.4 %collective-permute-start.10 = (f32[8,1024]{1,0:T(8,128)S(1)}, f32[8,1024]{1,0:T(8,128)S(1)}, u32[]{:S(2)}, u32[]{:S(2)}) collective-permute-start(f32[8,1024]{1,0:T(8,128)S(1)} %add.97), channel_id=1, source_target_pairs={{0,4},{2,6},{4,0},{6,2},{8,12},{10,14},{12,8},{14,10},{1,5},{3,7},... | collective-permute-start | bytes 98312 | tf_op jit(solution)/shard_map/ppermute | solution.py:209
  151.2 3.3 %collective-permute-done.10 = f32[8,1024]{1,0:T(8,128)S(1)} collective-permute-done((f32[8,1024]{1,0:T(8,128)S(1)}, f32[8,1024]{1,0:T(8,128)S(1)}, u32[]{:S(2)}, u32[]{:S(2)}) %collective-permute-start.10) | collective-permute-done | bytes 32800 | tf_op jit(solution)/shard_map/ppermute | solution.py:209
  156.6 7.6 %collective-permute-done.11 = f32[8,1024]{1,0:T(8,128)S(1)} collective-permute-done((f32[8,1024]{1,0:T(8,128)S(1)}, f32[8,1024]{1,0:T(8,128)S(1)}, u32[]{:S(2)}, u32[]{:S(2)}) %collective-permute-start.11) | collective-permute-done | bytes 32800 | tf_op jit(solution)/shard_map/ppermute | solution.py:209
  167.6 4.5 %backward.1 = (f32[2048,128]{1,0:T(8,128)S(1)}, bf16[2048,128]{1,0:T(8,128)(2,1)S(1)}) custom-call(s32[1]{0:T(128)} %bitcast.5.minor_ref, bf16[1024,2048]{1,0:T(8,128)(2,1)S(1)} %bitcast.29, f32[1024,256]{1,0:T(8,128)S(1)} %copy-done.5, bf16[8,2,128,256]{3,2,1,0:T(8,128)(2,1)S(1)} %gather_fusion.1, f32[1,256]{1,0:T(1,128)S(1)} %fusion.1.gain_ref, ...), custom_call_target="tpu_custom_call" | custom-call | flops 1073741824 | bytes 8388608 | tf_op jit(solution)/shard_map/backward/pallas_call | solution.py:171
  173.1 2.5 %collective-permute-start.12 = (bf16[2048,128]{1,0:T(8,128)(2,1)S(1)}, bf16[2048,128]{1,0:T(8,128)(2,1)S(1)}, u32[]{:S(2)}, u32[]{:S(2)}) collective-permute-start(bf16[2048,128]{1,0:T(8,128)(2,1)S(1)} %get-tuple-element.30), channel_id=1, source_target_pairs={{0,1},{1,0},{2,3},{3,2},{4,5},{5,4},{6,7},{7,6},{8,9},{9,8},{10,11... | collective-permute-start | bytes 1572872 | tf_op jit(solution)/shard_map/ppermute | solution.py:202
  176.3 10.2 %collective-permute-done.12.theirs_ref = bf16[2048,128]{1,0:T(8,128)(2,1)S(1)} collective-permute-done((bf16[2048,128]{1,0:T(8,128)(2,1)S(1)}, bf16[2048,128]{1,0:T(8,128)(2,1)S(1)}, u32[]{:S(2)}, u32[]{:S(2)}) %collective-permute-start.12) | collective-permute-done | bytes 524320 | tf_op jit(solution)/shard_map/ppermute | solution.py:202
  187.7 3.4 %adamw.1 = (bf16[1,2048,128]{2,1,0:T(8,128)(2,1)}, bf16[1,2048,128]{2,1,0:T(8,128)(2,1)}, bf16[1,2048,128]{2,1,0:T(8,128)(2,1)}) custom-call(s32[1]{0:T(128)S(6)} %copy.19.rate_ref, bf16[2048,128]{1,0:T(8,128)(2,1)S(1)} %bitcast.32, bf16[32,2,64,128]{3,2,1,0:T(8,128)(2,1)S(1)} %all-to-all-done.3.moments_ref, f32[2048,128]{1,0:T(8,128)S(1)} %copy-done.3, ...), custom_call_target="tpu_custom_call" | custom-call | flops 5242880 | bytes 4718592 | tf_op jit(solution)/shard_map/adamw/pallas_call | solution.py:50
  (68 shorter events, 27.6 us)
Async XLA Ops:
  7.2 61.3 %copy-start.6 = (bf16[1,2048,128]{2,1,0:T(8,128)(2,1)S(1)}, bf16[1,2048,128]{2,1,0:T(8,128)(2,1)}, u32[]{:S(2)}) copy-start(bf16[1,2048,128]{2,1,0:T(8,128)(2,1)} %param.15) | copy-start | bytes 1572868
  7.2 61.3 %copy-start.7 = (bf16[1,2048,128]{2,1,0:T(8,128)(2,1)S(1)}, bf16[1,2048,128]{2,1,0:T(8,128)(2,1)}, u32[]{:S(2)}) copy-start(bf16[1,2048,128]{2,1,0:T(8,128)(2,1)} %param.14) | copy-start | bytes 1572868
  7.2 116.6 %all-gather.3.cloned.1.call-start = ((), (), s32[]{:S(2)}) async-start(), calls=%async_computation.4 | async-start | bytes 4718592 | tf_op jit(solution)/shard_map/all_gather | solution.py:254
  7.9 31.2 %all-to-all-start = ((bf16[32,64,128]{2,1,0:T(8,128)(2,1)}), bf16[32,64,128]{2,1,0:T(8,128)(2,1)S(1)}, u32[]{:S(2)}, u32[]{:S(2)}) async-start(bf16[32,64,128]{2,1,0:T(8,128)(2,1)} %bitcast.33), calls=%async_computation | async-start | bytes 1048576 | tf_op jit(solution)/shard_map/all_to_all | solution.py:215
  21.4 19.1 %collective-permute-start = (bf16[128]{0:T(256)(128)(2,1)}, bf16[128]{0:T(256)(128)(2,1)S(1)}, u32[]{:S(2)}, u32[]{:S(2)}) collective-permute-start(bf16[128]{0:T(256)(128)(2,1)} %bitcast.36), channel_id=1, source_target_pairs={{0,1},{1,0},{2,3},{3,2},{4,5},{5,4},{6,7},{7,6},{8,9},{9,8},{10,11... | collective-permute-start | bytes 776 | tf_op jit(solution)/shard_map/ppermute | solution.py:202
  26.2 62.1 %copy-start.10 = (bf16[1,128]{1,0:T(2,128)(2,1)S(1)}, bf16[1,128]{1,0:T(2,128)(2,1)}, u32[]{:S(2)}) copy-start(bf16[1,128]{1,0:T(2,128)(2,1)} %param.12) | copy-start | bytes 772
  26.2 14.3 %collective-permute-start.1 = (bf16[2,128,256]{2,1,0:T(8,128)(2,1)S(1)}, bf16[2,128,256]{2,1,0:T(8,128)(2,1)S(1)}, u32[]{:S(2)}, u32[]{:S(2)}) collective-permute-start(bf16[2,128,256]{2,1,0:T(8,128)(2,1)S(1)} %pad_maximum_fusion.1), channel_id=1, source_target_pairs={{0,2},{2,4},{4,6},{6,8},{8,10},{10,12},{12,14},{14,0},{1,3},{3,5},... | collective-permute-start | bytes 393224 | tf_op jit(solution)/shard_map/ppermute | solution.py:232
  40.5 47.8 %copy-start.11 = (bf16[128]{0:T(256)(128)(2,1)}, bf16[128]{0:T(256)(128)(2,1)S(1)}, u32[]{:S(2)}) copy-start(bf16[128]{0:T(256)(128)(2,1)S(1)} %collective-permute-done) | copy-start | bytes 772
  40.5 37.8 %all-to-all-start.1 = ((bf16[32,64,128]{2,1,0:T(8,128)(2,1)}), bf16[32,64,128]{2,1,0:T(8,128)(2,1)S(1)}, u32[]{:S(2)}, u32[]{:S(2)}) async-start(bf16[32,64,128]{2,1,0:T(8,128)(2,1)} %gather_fusion), calls=%async_computation.1 | async-start | bytes 1048576 | tf_op jit(solution)/shard_map/all_to_all | solution.py:215
  46.4 47.1 %collective-permute-start.7 = (bf16[2,128,256]{2,1,0:T(8,128)(2,1)S(1)}, bf16[2,128,256]{2,1,0:T(8,128)(2,1)S(1)}, u32[]{:S(2)}, u32[]{:S(2)}) collective-permute-start(bf16[2,128,256]{2,1,0:T(8,128)(2,1)S(1)} %pad_maximum_fusion.6), channel_id=1, source_target_pairs={{0,8},{2,10},{4,12},{6,14},{8,0},{10,2},{12,4},{14,6},{1,9},{3,11}... | collective-permute-start | bytes 393224 | tf_op jit(solution)/shard_map/ppermute | solution.py:232
  51.7 17.9 %collective-permute-start.2 = (bf16[2,128,256]{2,1,0:T(8,128)(2,1)S(1)}, bf16[2,128,256]{2,1,0:T(8,128)(2,1)S(1)}, u32[]{:S(2)}, u32[]{:S(2)}) collective-permute-start(bf16[2,128,256]{2,1,0:T(8,128)(2,1)S(1)} %pad_maximum_fusion.2), channel_id=1, source_target_pairs={{0,4},{2,6},{4,8},{6,10},{8,12},{10,14},{12,0},{14,2},{1,5},{3,7},... | collective-permute-start | bytes 393224 | tf_op jit(solution)/shard_map/ppermute | solution.py:232
  55.8 20.5 %collective-permute-start.3 = (bf16[2,128,256]{2,1,0:T(8,128)(2,1)S(1)}, bf16[2,128,256]{2,1,0:T(8,128)(2,1)S(1)}, u32[]{:S(2)}, u32[]{:S(2)}) collective-permute-start(bf16[2,128,256]{2,1,0:T(8,128)(2,1)S(1)} %pad_maximum_fusion.3), channel_id=1, source_target_pairs={{0,12},{2,14},{4,0},{6,2},{8,4},{10,6},{12,8},{14,10},{1,13},{3,15... | collective-permute-start | bytes 393224 | tf_op jit(solution)/shard_map/ppermute | solution.py:232
  58.5 19.8 %collective-permute-start.4 = (bf16[2,128,256]{2,1,0:T(8,128)(2,1)S(1)}, bf16[2,128,256]{2,1,0:T(8,128)(2,1)S(1)}, u32[]{:S(2)}, u32[]{:S(2)}) collective-permute-start(bf16[2,128,256]{2,1,0:T(8,128)(2,1)S(1)} %pad_maximum_fusion.4), channel_id=1, source_target_pairs={{0,14},{2,0},{4,2},{6,4},{8,6},{10,8},{12,10},{14,12},{1,15},{3,1}... | collective-permute-start | bytes 393224 | tf_op jit(solution)/shard_map/ppermute | solution.py:232
  63.3 29.2 %collective-permute-start.6 = (bf16[2,128,256]{2,1,0:T(8,128)(2,1)}, bf16[2,128,256]{2,1,0:T(8,128)(2,1)}, u32[]{:S(2)}, u32[]{:S(2)}) collective-permute-start(bf16[2,128,256]{2,1,0:T(8,128)(2,1)} %pad_maximum_fusion.5), channel_id=1, source_target_pairs={{0,6},{2,8},{4,10},{6,12},{8,14},{10,0},{12,2},{14,4},{1,7},{3,9},... | collective-permute-start | bytes 393224 | tf_op jit(solution)/shard_map/ppermute | solution.py:232
  69.6 19.4 %copy-start.9 = (bf16[2,128,256]{2,1,0:T(8,128)(2,1)}, bf16[2,128,256]{2,1,0:T(8,128)(2,1)S(1)}, u32[]{:S(2)}) copy-start(bf16[2,128,256]{2,1,0:T(8,128)(2,1)S(1)} %collective-permute-done.2) | copy-start | bytes 393220
  69.6 23.9 %collective-permute-start.8 = (bf16[2,128,256]{2,1,0:T(8,128)(2,1)}, bf16[2,128,256]{2,1,0:T(8,128)(2,1)S(1)}, u32[]{:S(2)}, u32[]{:S(2)}) collective-permute-start(bf16[2,128,256]{2,1,0:T(8,128)(2,1)} %pad_maximum_fusion.7), channel_id=1, source_target_pairs={{0,10},{2,12},{4,14},{6,0},{8,2},{10,4},{12,6},{14,8},{1,11},{3,13... | collective-permute-start | bytes 393224 | tf_op jit(solution)/shard_map/ppermute | solution.py:232
  78.3 10.7 %copy-start.8 = (bf16[2,128,256]{2,1,0:T(8,128)(2,1)}, bf16[2,128,256]{2,1,0:T(8,128)(2,1)S(1)}, u32[]{:S(2)}) copy-start(bf16[2,128,256]{2,1,0:T(8,128)(2,1)S(1)} %collective-permute-done.4) | copy-start | bytes 393220
  78.3 51.1 %all-to-all-start.2 = ((bf16[32,2,64,128]{3,2,1,0:T(8,128)(2,1)}), bf16[32,2,64,128]{3,2,1,0:T(8,128)(2,1)}, u32[]{:S(2)}, u32[]{:S(2)}) async-start(bf16[32,2,64,128]{3,2,1,0:T(8,128)(2,1)} %pad_maximum_fusion), calls=%async_computation.2 | async-start | bytes 2097152 | tf_op jit(solution)/shard_map/all_to_all | solution.py:215
  89.0 34.7 %collective-permute-start.5 = (bf16[2048,128]{1,0:T(8,128)(2,1)S(1)}, bf16[2048,128]{1,0:T(8,128)(2,1)S(1)}, u32[]{:S(2)}, u32[]{:S(2)}) collective-permute-start(bf16[2048,128]{1,0:T(8,128)(2,1)S(1)} %bitcast.30), channel_id=1, source_target_pairs={{0,1},{1,0},{2,3},{3,2},{4,5},{5,4},{6,7},{7,6},{8,9},{9,8},{10,11... | collective-permute-start | bytes 1572872 | tf_op jit(solution)/shard_map/ppermute | solution.py:202
  132.3 54.2 %all-to-all-start.3 = ((bf16[32,2,64,128]{3,2,1,0:T(8,128)(2,1)}), bf16[32,2,64,128]{3,2,1,0:T(8,128)(2,1)S(1)}, u32[]{:S(2)}, u32[]{:S(2)}) async-start(bf16[32,2,64,128]{3,2,1,0:T(8,128)(2,1)} %gather_fusion.2), calls=%async_computation.3 | async-start | bytes 2097152 | tf_op jit(solution)/shard_map/all_to_all | solution.py:215
  142.0 5.8 %collective-permute-start.9 = (f32[8,1024]{1,0:T(8,128)S(1)}, f32[8,1024]{1,0:T(8,128)S(1)}, u32[]{:S(2)}, u32[]{:S(2)}) collective-permute-start(f32[8,1024]{1,0:T(8,128)S(1)} %get-tuple-element.28), channel_id=1, source_target_pairs={{0,2},{2,0},{4,6},{6,4},{8,10},{10,8},{12,14},{14,12},{1,3},{3,1},... | collective-permute-start | bytes 98312 | tf_op jit(solution)/shard_map/ppermute | solution.py:209
  147.8 6.7 %collective-permute-start.10 = (f32[8,1024]{1,0:T(8,128)S(1)}, f32[8,1024]{1,0:T(8,128)S(1)}, u32[]{:S(2)}, u32[]{:S(2)}) collective-permute-start(f32[8,1024]{1,0:T(8,128)S(1)} %add.97), channel_id=1, source_target_pairs={{0,4},{2,6},{4,0},{6,2},{8,12},{10,14},{12,8},{14,10},{1,5},{3,7},... | collective-permute-start | bytes 98312 | tf_op jit(solution)/shard_map/ppermute | solution.py:209
  154.5 9.7 %collective-permute-start.11 = (f32[8,1024]{1,0:T(8,128)S(1)}, f32[8,1024]{1,0:T(8,128)S(1)}, u32[]{:S(2)}, u32[]{:S(2)}) collective-permute-start(f32[8,1024]{1,0:T(8,128)S(1)} %add.98), channel_id=1, source_target_pairs={{0,8},{2,10},{4,12},{6,14},{8,0},{10,2},{12,4},{14,6},{1,9},{3,11}... | collective-permute-start | bytes 98312 | tf_op jit(solution)/shard_map/ppermute | solution.py:209
  173.1 13.4 %collective-permute-start.12 = (bf16[2048,128]{1,0:T(8,128)(2,1)S(1)}, bf16[2048,128]{1,0:T(8,128)(2,1)S(1)}, u32[]{:S(2)}, u32[]{:S(2)}) collective-permute-start(bf16[2048,128]{1,0:T(8,128)(2,1)S(1)} %get-tuple-element.30), channel_id=1, source_target_pairs={{0,1},{1,0},{2,3},{3,2},{4,5},{5,4},{6,7},{7,6},{8,9},{9,8},{10,11... | collective-permute-start | bytes 1572872 | tf_op jit(solution)/shard_map/ppermute | solution.py:202
  (6 other events, 8.8 us)
Sparse Core Ops, SparseCore 0:
  10.1 83.9 all-gather.2

commit v5 on v4

--- a/solution.py
+++ b/solution.py
@@ -18,6 +18,8 @@
 bias_two = 1.0 - 0.95**10
 RATE_TABLE = (0.02, 0.032, 0.05, 0.08, 0.125)
 MINOR = 2
+PLANES = 4
+FEW = 2
 LANES = 128
 VMEM_LIMIT = 24 * 1024 * 1024
 
@@ -43,7 +45,7 @@
 def adamw(rate_index, weight, moments, mine, theirs):
     depth, width = weight.shape
     members, kinds, rows = moments.shape[:3]
-    pieces = 4
+    pieces = 1
     step = pieces * rows
     flat = pl.BlockSpec((step, width), lambda i, r: (i, 0))
     out = pl.BlockSpec((1, step, width), lambda i, r: (0, i, 0))
@@ -141,8 +143,9 @@
 
     @pl.when(pl.program_id(0) == 0)
     def _():
-        squares = sums_ref[0:1, :]
-        inner = sums_ref[1:2, :]
+        sums = jnp.sum(sums_ref[...], axis=0)
+        squares = sums[0:1, :]
+        inner = sums[1:2, :]
         inverse = lax.rsqrt(squares / features + EPS)
         factor = inner / features * (inverse * inverse * inverse)
         for block in range(blocks):
@@ -178,7 +181,7 @@
                 pl.BlockSpec(hidden.shape, lambda i, m: (0, 0)),
                 pl.BlockSpec(stream.shape, lambda i, m: (0, 0, 0, 0)),
                 pl.BlockSpec((1, block), lambda i, m: (0, 0)),
-                pl.BlockSpec(sums.shape, lambda i, m: (0, 0)),
+                pl.BlockSpec(sums.shape, lambda i, m: (0, 0, 0)),
             ],
             out_specs=[
                 pl.BlockSpec((step, width), lambda i, m: (i, 0)),
@@ -202,17 +205,68 @@
     return lax.ppermute(array, "minor", [(0, 1), (1, 0)])
 
 
-def sum_over_major(array):
+def sums_of_all(sums):
     size = lax.axis_size("major")
-    reach = 1
-    while reach < size:
-        array = array + lax.ppermute(array, "major", [(i, i ^ reach) for i in range(size)])
-        reach *= 2
-    return array
-
-
-def spread_members(array):
-    return lax.all_to_all(array, "member", split_axis=0, concat_axis=0, tiled=True)
+    copies = jnp.broadcast_to(sums[None, :2], (size, 2, sums.shape[1]))
+    return lax.all_to_all(copies, "major", split_axis=0, concat_axis=0, tiled=True)
+
+
+def spread_columns(array):
+    return lax.all_to_all(array, "column", split_axis=0, concat_axis=0, tiled=True)
+
+
+def plan_moves(sources):
+    planes = lax.axis_size("plane")
+    columns = lax.axis_size("column")
+    me = lax.axis_index("plane")
+    member = jnp.arange(planes * columns, dtype=jnp.int32)
+    here, there = member // columns, sources // columns
+    offset = lax.rem(here - there + planes, planes)
+    earlier = member[None, :] < member[:, None]
+    same = (here[None, :] == here[:, None]) & (there[None, :] == there[:, None])
+    rank = jnp.sum((earlier & same).astype(jnp.int32), axis=1)
+    most = jnp.max(jnp.where(offset > 0, rank, 0))
+    shifts = jnp.arange(1, planes, dtype=jnp.int32)[:, None, None]
+    slots = jnp.arange(columns, dtype=jnp.int32)[None, :, None]
+    leaving = (there == me)[None, None, :] & (offset[None, None, :] == shifts) & (rank[None, None, :] == slots)
+    outgoing = jnp.sum(jnp.where(leaving, lax.rem(sources, columns)[None, None, :], 0), axis=2)
+    mine = lambda values: lax.dynamic_slice_in_dim(values, me * columns, columns)
+    return mine(lax.rem(sources, columns)), mine(offset), mine(rank), outgoing, most
+
+
+def send_planes(pieces, outgoing):
+    planes = lax.axis_size("plane")
+    count = outgoing.shape[1]
+    packed = pieces[outgoing.reshape(-1)]
+    return [
+        lax.ppermute(
+            packed[(shift - 1) * count : shift * count],
+            "plane",
+            [(i, (i + shift) % planes) for i in range(planes)],
+        )
+        for shift in range(1, planes)
+    ]
+
+
+def choose(pieces, received, plan):
+    column, offset, rank = plan[:3]
+    count = received[0].shape[0]
+    index = jnp.where(offset == 0, column, pieces.shape[0] + (offset - 1) * count + rank)
+    return jnp.concatenate((pieces, *received))[index]
+
+
+def cross_planes(pieces, received, plan):
+    few = received[0].shape[0]
+
+    def all_slots(pieces, received):
+        rest = send_planes(pieces, plan[3][:, few:])
+        whole = [jnp.concatenate(pair) for pair in zip(received, rest)]
+        return choose(pieces, whole, plan)
+
+    def few_slots(pieces, received):
+        return choose(pieces, received, plan)
+
+    return lax.cond(plan[4] >= few, all_slots, few_slots, pieces, received)
 
 
 def spread_features(residual, upstream):
@@ -245,28 +299,34 @@
     sources,
     rate_index,
 ):
-    members = lax.axis_size("member")
+    columns = lax.axis_size("column")
     minor = lax.axis_index("minor")
     depth, width = weight.shape[1:]
-    rows = depth // members
+    rows = depth // columns
     features = residual.shape[2]
 
     gathered = lax.all_gather(attention_out[0], "major", axis=0, tiled=True)
+    plan = plan_moves(sources)
+    few = plan[3][:, :FEW]
     parts = spread_features(residual[0], upstream[0])
     gain_other = swap_minor(norm_gain[0])
-    picked = spread_members(weight[0].reshape(members, rows, width))[sources]
-    picked, gain_other, parts[1] = lax.optimization_barrier((picked, gain_other, parts[1]))
-    weight_here = spread_members(picked)
+    weights = spread_columns(weight[0].reshape(columns, rows, width))
     moments = jnp.stack(
-        (first_moment[0].reshape(members, rows, width), second_moment[0].reshape(members, rows, width)),
+        (first_moment[0].reshape(columns, rows, width), second_moment[0].reshape(columns, rows, width)),
         axis=1,
     )
-    weight_here, moments, parts[2], parts[6], parts[7] = lax.optimization_barrier(
-        (weight_here, moments, parts[2], parts[6], parts[7])
-    )
-    weight_here = weight_here.reshape(depth, width)
+    weights, moments, gain_other, parts[1] = lax.optimization_barrier(
+        (weights, moments, gain_other, parts[1])
+    )
+    weights_in = send_planes(weights, few)
+    moments = spread_columns(moments)
+    weights = cross_planes(weights, weights_in, plan)
+    weights, moments, parts[2], parts[7] = lax.optimization_barrier(
+        (weights, moments, parts[2], parts[7])
+    )
+    weight_here = spread_columns(weights).reshape(depth, width)
     weight_other = swap_minor(weight_here)
-    moments = spread_members(moments)
+    moments_in = send_planes(moments, few)
     size = len(parts)
     stream = jnp.stack(parts)[lax.rem(lax.axis_index("major") + size - jnp.arange(size), size)]
 
@@ -279,27 +339,32 @@
     inv_scale = 1.0 / math.sqrt(depth)
     side = minor.astype(jnp.int32)[None]
     hidden, sums = forward(side, gathered, weight_here, weight_other, stream, gain, inv_scale)
+    moments_in, sums = lax.optimization_barrier((moments_in, sums))
+    sums = sums_of_all(sums)
+    moments = cross_planes(moments, moments_in, plan)
     moments, sums = lax.optimization_barrier((moments, sums))
-    moments = spread_members(moments[sources])
-    sums = sum_over_major(sums)
+    moments = spread_columns(moments)
     mine, theirs = backward(side, gathered, hidden, stream, gain, sums, inv_scale, features)
     return adamw(rate_index, weight_here, moments, mine, swap_minor(theirs))
 
 
 def solution(mesh):
     members, shards = mesh.devices.shape
-    split = Mesh(mesh.devices.reshape(members, shards // MINOR, MINOR), ("member", "major", "minor"))
-    fsdp = ("major", "minor")
+    split = Mesh(
+        mesh.devices.reshape(PLANES, members // PLANES, shards // MINOR, MINOR),
+        ("plane", "column", "major", "minor"),
+    )
+    member, fsdp = ("plane", "column"), ("major", "minor")
     in_specs = (
-        P("member", fsdp, None),
-        P("member", fsdp, None),
-        P("member", fsdp, None),
-        P("member", fsdp),
-        P("member", None, fsdp),
-        P("member", None, fsdp),
-        P("member", None, fsdp),
+        P(member, fsdp, None),
+        P(member, fsdp, None),
+        P(member, fsdp, None),
+        P(member, fsdp),
+        P(member, None, fsdp),
+        P(member, None, fsdp),
+        P(member, None, fsdp),
         P(),
-        P("member"),
-    )
-    out_specs = (P("member", None, fsdp),) * 3
+        P(member),
+    )
+    out_specs = (P(member, None, fsdp),) * 3
     return jax.shard_map(local, mesh=split, in_specs=in_specs, out_specs=out_specs, check_vma=False)

time: 199 us -> 200 us (level)
  the two profiles are of different devices: /device:TPU:60 before, /device:TPU:1 now
where the time goes in v5:
time: 200 us; the launch traced here: 199 us
  starting transfers between devices  96.4 us (48%)
  waiting for transfers between devices  39 us (20%)
  local copies, waits for them, and re-layouts  27.2 us (14%)
  between operations  15.9 us (8%)
  Pallas kernels  10.4 us (5%)
  other arithmetic  10.3 us (5%)
    ppermute x6, starting transfers between devices, send_planes(): lax.ppermute(packed[(shift - 1) * count:shift * count], 'plane', [(i, (i...  31.1 us
    ppermute x3, waiting for transfers between devices, swap_minor(): return lax.ppermute(array, 'minor', [(0, 1), (1, 0)])  29.8 us
    all_to_all x4, starting transfers between devices, spread_columns(): lax.all_to_all(array, 'column', split_axis=0, concat_axis=0, tiled=True)  28.7 us
    ppermute x7, starting transfers between devices, spread_features(): lax.ppermute(part, 'major', [(i, (i + shift) % size) for i in range(size)])  21.7 us
    unnamed x50, local copies, waits for them, and re-layouts  15.9 us
    ppermute x3, starting transfers between devices, swap_minor(): return lax.ppermute(array, 'minor', [(0, 1), (1, 0)])  9.06 us
    all_to_all x1, starting transfers between devices, sums_of_all(): lax.all_to_all(copies, 'major', split_axis=0, concat_axis=0, tiled=True)  5.87 us
    pallas_call x1, Pallas kernels, backward(): pl.pallas_call(functools.partial(backward_kernel, inv_scale, features), g...  4.55 us
  transfers between devices with their start and end apart: 22, of which 7 were waited for; matrix products, arithmetic and copies ran while one was open for 13% of the time, Pallas kernels for 4%

profile of v5, /device:TPU:1, one launch (start us, length us, event | category | flops | bytes accessed | tf_op | source)
XLA Modules:
  0.0 199.2 jit_solution(3782596510866989851)
XLA Ops:
  8.0 10.3 %all-to-all-start = ((bf16[8,256,128]{2,1,0:T(8,128)(2,1)}), bf16[8,256,128]{2,1,0:T(8,128)(2,1)S(1)}, u32[]{:S(2)}, u32[]{:S(2)}) async-start(bf16[8,256,128]{2,1,0:T(8,128)(2,1)} %bitcast.40), calls=%async_computation | async-start | bytes 1048576 | tf_op jit(solution)/shard_map/all_to_all | solution.py:215
  21.0 4.3 %collective-permute-start.19 = (bf16[2,128,256]{2,1,0:T(8,128)(2,1)}, bf16[2,128,256]{2,1,0:T(8,128)(2,1)}, u32[]{:S(2)}, u32[]{:S(2)}) collective-permute-start(bf16[2,128,256]{2,1,0:T(8,128)(2,1)} %pad_maximum_fusion.8), channel_id=1, source_target_pairs={{0,10},{2,12},{4,14},{6,0},{8,2},{10,4},{12,6},{14,8},{1,11},{3,13... | collective-permute-start | bytes 393224 | tf_op jit(solution)/shard_map/ppermute | solution.py:286
  30.0 3.1 %collective-permute-done.7 = bf16[2,128,256]{2,1,0:T(8,128)(2,1)S(1)} collective-permute-done((bf16[2,128,256]{2,1,0:T(8,128)(2,1)S(1)}, bf16[2,128,256]{2,1,0:T(8,128)(2,1)S(1)}, u32[]{:S(2)}, u32[]{:S(2)}) %collective-permute-start.7) | collective-permute-done | bytes 131104 | tf_op jit(solution)/shard_map/ppermute | solution.py:286
  33.7 13.0 %collective-permute-start.10 = (bf16[2,256,128]{2,1,0:T(8,128)(2,1)S(1)}, bf16[2,256,128]{2,1,0:T(8,128)(2,1)S(1)}, u32[]{:S(2)}, u32[]{:S(2)}) collective-permute-start(bf16[2,256,128]{2,1,0:T(8,128)(2,1)S(1)} %get-tuple-element.165), channel_id=1, source_target_pairs={{0,384},{128,0},{256,128},{384,256},{1,385},{129,1},{257,129},{385... | collective-permute-start | bytes 393224 | tf_op jit(solution)/shard_map/ppermute | solution.py:242
  48.9 4.3 %collective-permute-start.8 = (bf16[2,256,128]{2,1,0:T(8,128)(2,1)S(1)}, bf16[2,256,128]{2,1,0:T(8,128)(2,1)S(1)}, u32[]{:S(2)}, u32[]{:S(2)}) collective-permute-start(bf16[2,256,128]{2,1,0:T(8,128)(2,1)S(1)} %get-tuple-element.167), channel_id=1, source_target_pairs={{0,128},{128,256},{256,384},{384,0},{1,129},{129,257},{257,385},{3... | collective-permute-start | bytes 393224 | tf_op jit(solution)/shard_map/ppermute | solution.py:242
  57.6 3.2 %collective-permute-done.9 = bf16[2,256,128]{2,1,0:T(8,128)(2,1)S(1)} collective-permute-done((bf16[2,256,128]{2,1,0:T(8,128)(2,1)S(1)}, bf16[2,256,128]{2,1,0:T(8,128)(2,1)S(1)}, u32[]{:S(2)}, u32[]{:S(2)}) %collective-permute-start.9) | collective-permute-done | bytes 131104 | tf_op jit(solution)/shard_map/ppermute | solution.py:242
  65.2 6.7 %all-to-all-start.1 = ((bf16[8,2,256,128]{3,2,1,0:T(8,128)(2,1)}), bf16[8,2,256,128]{3,2,1,0:T(8,128)(2,1)S(1)}, u32[]{:S(2)}, u32[]{:S(2)}) async-start(bf16[8,2,256,128]{3,2,1,0:T(8,128)(2,1)} %pad_maximum_fusion.2), calls=%async_computation.1 | async-start | bytes 2097152 | tf_op jit(solution)/shard_map/all_to_all | solution.py:215
  72.5 2.5 %collective-permute-start.17 = (bf16[2,128,256]{2,1,0:T(8,128)(2,1)}, bf16[2,128,256]{2,1,0:T(8,128)(2,1)}, u32[]{:S(2)}, u32[]{:S(2)}) collective-permute-start(bf16[2,128,256]{2,1,0:T(8,128)(2,1)} %pad_maximum_fusion.6), channel_id=1, source_target_pairs={{0,6},{2,8},{4,10},{6,12},{8,14},{10,0},{12,2},{14,4},{1,7},{3,9},... | collective-permute-start | bytes 393224 | tf_op jit(solution)/shard_map/ppermute | solution.py:286
  75.7 5.0 %collective-permute-start.18 = (bf16[2,128,256]{2,1,0:T(8,128)(2,1)}, bf16[2,128,256]{2,1,0:T(8,128)(2,1)}, u32[]{:S(2)}, u32[]{:S(2)}) collective-permute-start(bf16[2,128,256]{2,1,0:T(8,128)(2,1)} %pad_maximum_fusion.7), channel_id=1, source_target_pairs={{0,8},{2,10},{4,12},{6,14},{8,0},{10,2},{12,4},{14,6},{1,9},{3,11}... | collective-permute-start | bytes 393224 | tf_op jit(solution)/shard_map/ppermute | solution.py:286
  82.1 3.6 %collective-permute-start.20 = (bf16[2,128,256]{2,1,0:T(8,128)(2,1)}, bf16[2,128,256]{2,1,0:T(8,128)(2,1)}, u32[]{:S(2)}, u32[]{:S(2)}) collective-permute-start(bf16[2,128,256]{2,1,0:T(8,128)(2,1)} %pad_maximum_fusion.9), channel_id=1, source_target_pairs={{0,12},{2,14},{4,0},{6,2},{8,4},{10,6},{12,8},{14,10},{1,13},{3,15... | collective-permute-start | bytes 393224 | tf_op jit(solution)/shard_map/ppermute | solution.py:286
  86.9 5.1 %all-to-all-start.2 = ((bf16[8,256,128]{2,1,0:T(8,128)(2,1)}), bf16[8,256,128]{2,1,0:T(8,128)(2,1)S(1)}, u32[]{:S(2)}, u32[]{:S(2)}) async-start(bf16[8,256,128]{2,1,0:T(8,128)(2,1)} %get-tuple-element.176), calls=%async_computation.2 | async-start | bytes 1048576 | tf_op jit(solution)/shard_map/all_to_all | solution.py:215
  93.9 5.2 %collective-permute-start.15 = (bf16[2,2,256,128]{3,2,1,0:T(8,128)(2,1)}, bf16[2,2,256,128]{3,2,1,0:T(8,128)(2,1)}, u32[]{:S(2)}, u32[]{:S(2)}) collective-permute-start(bf16[2,2,256,128]{3,2,1,0:T(8,128)(2,1)} %get-tuple-element.146), channel_id=1, source_target_pairs={{0,384},{128,0},{256,128},{384,256},{1,385},{129,1},{257,129},{385... | collective-permute-start | bytes 786440 | tf_op jit(solution)/shard_map/ppermute | solution.py:242
  99.1 3.4 %collective-permute-start.14 = (bf16[2,2,256,128]{3,2,1,0:T(8,128)(2,1)}, bf16[2,2,256,128]{3,2,1,0:T(8,128)(2,1)}, u32[]{:S(2)}, u32[]{:S(2)}) collective-permute-start(bf16[2,2,256,128]{3,2,1,0:T(8,128)(2,1)} %get-tuple-element.147), channel_id=1, source_target_pairs={{0,256},{128,384},{256,0},{384,128},{1,257},{129,385},{257,1},{385... | collective-permute-start | bytes 786440 | tf_op jit(solution)/shard_map/ppermute | solution.py:242
  103.5 3.0 %collective-permute-start.13 = (bf16[2,2,256,128]{3,2,1,0:T(8,128)(2,1)}, bf16[2,2,256,128]{3,2,1,0:T(8,128)(2,1)}, u32[]{:S(2)}, u32[]{:S(2)}) collective-permute-start(bf16[2,2,256,128]{3,2,1,0:T(8,128)(2,1)} %get-tuple-element.148), channel_id=1, source_target_pairs={{0,128},{128,256},{256,384},{384,0},{1,129},{129,257},{257,385},{3... | collective-permute-start | bytes 786440 | tf_op jit(solution)/shard_map/ppermute | solution.py:242
  108.4 3.1 %collective-permute-start.16 = (bf16[2048,128]{1,0:T(8,128)(2,1)S(1)}, bf16[2048,128]{1,0:T(8,128)(2,1)S(1)}, u32[]{:S(2)}, u32[]{:S(2)}) collective-permute-start(bf16[2048,128]{1,0:T(8,128)(2,1)S(1)} %bitcast.37), channel_id=1, source_target_pairs={{0,1},{1,0},{2,3},{3,2},{4,5},{5,4},{6,7},{7,6},{8,9},{9,8},{10,11... | collective-permute-start | bytes 1572872 | tf_op jit(solution)/shard_map/ppermute | solution.py:205
  118.1 18.2 %collective-permute-done.16.other_ref = bf16[2048,128]{1,0:T(8,128)(2,1)S(1)} collective-permute-done((bf16[2048,128]{1,0:T(8,128)(2,1)S(1)}, bf16[2048,128]{1,0:T(8,128)(2,1)S(1)}, u32[]{:S(2)}, u32[]{:S(2)}) %collective-permute-start.16) | collective-permute-done | bytes 524320 | tf_op jit(solution)/shard_map/ppermute | solution.py:205
  142.6 5.9 %all-to-all-start.3 = ((f32[8,2,1024]{2,1,0:T(2,128)}), f32[8,2,1024]{2,1,0:T(2,128)S(1)}, u32[]{:S(2)}, u32[]{:S(2)}) async-start(f32[8,2,1024]{2,1,0:T(2,128)} %broadcast_in_dim.32), calls=%async_computation.3 | async-start | bytes 131072 | tf_op jit(solution)/shard_map/all_to_all | solution.py:211
  148.5 5.6 %conditional.3 = (bf16[8,2,256,128]{3,2,1,0:T(8,128)(2,1)S(1)}) conditional(s32[]{:T(128)} %convert_element_type.18, (bf16[8,2,256,128]{3,2,1,0:T(8,128)(2,1)S(1)}, bf16[2,2,256,128]{3,2,1,0:T(8,128)(2,1)}, bf16[2,2,256,128]{3,2,1,0:T(8,128)(2,1)}, bf16[2,2,256,128]{3,2,1,0:T(8,128)(2,1)}, s32[8]{0:T(128)}, /*index=5*/s32[8]{0:T(128)S(1)}, ...), branch_computations={%region_5.6_spmd, %region_6.7_spmd} | conditional | flops 2753608 | bytes 29369216 | solution.py:269
  148.5 2.7 %pad_maximum_fusion.1 = bf16[14,2,256,128]{3,2,1,0:T(8,128)(2,1)} fusion(bf16[2,2,256,128]{3,2,1,0:T(8,128)(2,1)} %get-tuple-element.84, bf16[2,2,256,128]{3,2,1,0:T(8,128)(2,1)} %get-tuple-element.83, bf16[2,2,256,128]{3,2,1,0:T(8,128)(2,1)} %get-tuple-element.82, bf16[8,2,256,128]{3,2,1,0:T(8,128)(2,1)S(1)} %get-tuple-element.81), kind=kLoop, calls=%fused_computation.26 | loop fusion | flops 2752512 | bytes 3670016 | tf_op jit(solution)/shard_map/cond/branch_0_fun/concatenate | solution.py:255
  155.7 6.7 %all-to-all-start.4 = ((bf16[8,2,256,128]{3,2,1,0:T(8,128)(2,1)}), bf16[8,2,256,128]{3,2,1,0:T(8,128)(2,1)S(1)}, u32[]{:S(2)}, u32[]{:S(2)}) async-start(bf16[8,2,256,128]{3,2,1,0:T(8,128)(2,1)} %copy-done.6), calls=%async_computation.4 | async-start | bytes 2097152 | tf_op jit(solution)/shard_map/all_to_all | solution.py:215
  165.8 4.6 %backward.1 = (f32[2048,128]{1,0:T(8,128)S(1)}, bf16[2048,128]{1,0:T(8,128)(2,1)S(1)}) custom-call(s32[1]{0:T(128)} %bitcast.8.minor_ref, bf16[1024,2048]{1,0:T(8,128)(2,1)S(1)} %bitcast.36, f32[1024,256]{1,0:T(8,128)S(1)} %copy-done.5, bf16[8,2,128,256]{3,2,1,0:T(8,128)(2,1)S(1)} %gather_fusion.8, f32[1,256]{1,0:T(1,128)S(1)} %fusion.4.gain_ref, ...), custom_call_target="tpu_custom_call" | custom-call | flops 1073741824 | bytes 8388608 | tf_op jit(solution)/shard_map/backward/pallas_call | solution.py:174
  171.4 4.1 %collective-permute-start.21 = (bf16[2048,128]{1,0:T(8,128)(2,1)S(1)}, bf16[2048,128]{1,0:T(8,128)(2,1)S(1)}, u32[]{:S(2)}, u32[]{:S(2)}) collective-permute-start(bf16[2048,128]{1,0:T(8,128)(2,1)S(1)} %get-tuple-element.134), channel_id=1, source_target_pairs={{0,1},{1,0},{2,3},{3,2},{4,5},{5,4},{6,7},{7,6},{8,9},{9,8},{10,11... | collective-permute-start | bytes 1572872 | tf_op jit(solution)/shard_map/ppermute | solution.py:205
  176.1 11.6 %collective-permute-done.21.theirs_ref = bf16[2048,128]{1,0:T(8,128)(2,1)S(1)} collective-permute-done((bf16[2048,128]{1,0:T(8,128)(2,1)S(1)}, bf16[2048,128]{1,0:T(8,128)(2,1)S(1)}, u32[]{:S(2)}, u32[]{:S(2)}) %collective-permute-start.21) | collective-permute-done | bytes 524320 | tf_op jit(solution)/shard_map/ppermute | solution.py:205
  189.0 3.3 %adamw.1 = (bf16[1,2048,128]{2,1,0:T(8,128)(2,1)}, bf16[1,2048,128]{2,1,0:T(8,128)(2,1)}, bf16[1,2048,128]{2,1,0:T(8,128)(2,1)}) custom-call(s32[1]{0:T(128)S(6)} %copy.35.rate_ref, bf16[2048,128]{1,0:T(8,128)(2,1)S(1)} %bitcast.39, bf16[8,2,256,128]{3,2,1,0:T(8,128)(2,1)S(1)} %all-to-all-done.4.moments_ref, f32[2048,128]{1,0:T(8,128)S(1)} %copy-done.3, ...), custom_call_target="tpu_custom_call" | custom-call | flops 5242880 | bytes 4718592 | tf_op jit(solution)/shard_map/adamw/pallas_call | solution.py:52
  (119 shorter events, 52.9 us)
Async XLA Ops:
  7.2 129.1 %all-gather.3.cloned.1.call-start = ((), (), s32[]{:S(2)}) async-start(), calls=%async_computation.5 | async-start | bytes 4718592 | tf_op jit(solution)/shard_map/all_gather | solution.py:308
  8.0 25.1 %all-to-all-start = ((bf16[8,256,128]{2,1,0:T(8,128)(2,1)}), bf16[8,256,128]{2,1,0:T(8,128)(2,1)S(1)}, u32[]{:S(2)}, u32[]{:S(2)}) async-start(bf16[8,256,128]{2,1,0:T(8,128)(2,1)} %bitcast.40), calls=%async_computation | async-start | bytes 1048576 | tf_op jit(solution)/shard_map/all_to_all | solution.py:215
  18.2 11.7 %collective-permute-start.6 = (bf16[128]{0:T(256)(128)(2,1)}, bf16[128]{0:T(256)(128)(2,1)S(1)}, u32[]{:S(2)}, u32[]{:S(2)}) collective-permute-start(bf16[128]{0:T(256)(128)(2,1)} %bitcast.44), channel_id=1, source_target_pairs={{0,1},{1,0},{2,3},{3,2},{4,5},{5,4},{6,7},{7,6},{8,9},{9,8},{10,11... | collective-permute-start | bytes 776 | tf_op jit(solution)/shard_map/ppermute | solution.py:205
  21.0 86.3 %collective-permute-start.19 = (bf16[2,128,256]{2,1,0:T(8,128)(2,1)}, bf16[2,128,256]{2,1,0:T(8,128)(2,1)}, u32[]{:S(2)}, u32[]{:S(2)}) collective-permute-start(bf16[2,128,256]{2,1,0:T(8,128)(2,1)} %pad_maximum_fusion.8), channel_id=1, source_target_pairs={{0,10},{2,12},{4,14},{6,0},{8,2},{10,4},{12,6},{14,8},{1,11},{3,13... | collective-permute-start | bytes 393224 | tf_op jit(solution)/shard_map/ppermute | solution.py:286
  25.3 7.7 %collective-permute-start.7 = (bf16[2,128,256]{2,1,0:T(8,128)(2,1)S(1)}, bf16[2,128,256]{2,1,0:T(8,128)(2,1)S(1)}, u32[]{:S(2)}, u32[]{:S(2)}) collective-permute-start(bf16[2,128,256]{2,1,0:T(8,128)(2,1)S(1)} %pad_maximum_fusion.3), channel_id=1, source_target_pairs={{0,2},{2,4},{4,6},{6,8},{8,10},{10,12},{12,14},{14,0},{1,3},{3,5},... | collective-permute-start | bytes 393224 | tf_op jit(solution)/shard_map/ppermute | solution.py:286
  30.0 30.9 %copy-start.17 = (s32[1024]{0:T(1024)}, s32[1024]{0:T(1024)S(1)}, u32[]{:S(2)}) copy-start(s32[1024]{0:T(1024)S(1)} %pad_clamp_fusion.7) | copy-start | bytes 12292
  33.0 27.8 %copy-start.12 = (bf16[2,128,256]{2,1,0:T(8,128)(2,1)}, bf16[2,128,256]{2,1,0:T(8,128)(2,1)S(1)}, u32[]{:S(2)}) copy-start(bf16[2,128,256]{2,1,0:T(8,128)(2,1)S(1)} %collective-permute-done.7) | copy-start | bytes 393220
  33.7 23.9 %collective-permute-start.10 = (bf16[2,256,128]{2,1,0:T(8,128)(2,1)S(1)}, bf16[2,256,128]{2,1,0:T(8,128)(2,1)S(1)}, u32[]{:S(2)}, u32[]{:S(2)}) collective-permute-start(bf16[2,256,128]{2,1,0:T(8,128)(2,1)S(1)} %get-tuple-element.165), channel_id=1, source_target_pairs={{0,384},{128,0},{256,128},{384,256},{1,385},{129,1},{257,129},{385... | collective-permute-start | bytes 393224 | tf_op jit(solution)/shard_map/ppermute | solution.py:242
  46.7 14.1 %collective-permute-start.9 = (bf16[2,256,128]{2,1,0:T(8,128)(2,1)S(1)}, bf16[2,256,128]{2,1,0:T(8,128)(2,1)S(1)}, u32[]{:S(2)}, u32[]{:S(2)}) collective-permute-start(bf16[2,256,128]{2,1,0:T(8,128)(2,1)S(1)} %get-tuple-element.166), channel_id=1, source_target_pairs={{0,256},{128,384},{256,0},{384,128},{1,257},{129,385},{257,1},{385... | collective-permute-start | bytes 393224 | tf_op jit(solution)/shard_map/ppermute | solution.py:242
  48.9 11.9 %collective-permute-start.8 = (bf16[2,256,128]{2,1,0:T(8,128)(2,1)S(1)}, bf16[2,256,128]{2,1,0:T(8,128)(2,1)S(1)}, u32[]{:S(2)}, u32[]{:S(2)}) collective-permute-start(bf16[2,256,128]{2,1,0:T(8,128)(2,1)S(1)} %get-tuple-element.167), channel_id=1, source_target_pairs={{0,128},{128,256},{256,384},{384,0},{1,129},{129,257},{257,385},{3... | collective-permute-start | bytes 393224 | tf_op jit(solution)/shard_map/ppermute | solution.py:242
  53.2 28.9 %collective-permute-start.11 = (bf16[2,128,256]{2,1,0:T(8,128)(2,1)S(1)}, bf16[2,128,256]{2,1,0:T(8,128)(2,1)S(1)}, u32[]{:S(2)}, u32[]{:S(2)}) collective-permute-start(bf16[2,128,256]{2,1,0:T(8,128)(2,1)S(1)} %pad_maximum_fusion.4), channel_id=1, source_target_pairs={{0,4},{2,6},{4,8},{6,10},{8,12},{10,14},{12,0},{14,2},{1,5},{3,7},... | collective-permute-start | bytes 393224 | tf_op jit(solution)/shard_map/ppermute | solution.py:286
  63.1 22.6 %collective-permute-start.12 = (bf16[2,128,256]{2,1,0:T(8,128)(2,1)}, bf16[2,128,256]{2,1,0:T(8,128)(2,1)S(1)}, u32[]{:S(2)}, u32[]{:S(2)}) collective-permute-start(bf16[2,128,256]{2,1,0:T(8,128)(2,1)} %pad_maximum_fusion.5), channel_id=1, source_target_pairs={{0,14},{2,0},{4,2},{6,4},{8,6},{10,8},{12,10},{14,12},{1,15},{3,1}... | collective-permute-start | bytes 393224 | tf_op jit(solution)/shard_map/ppermute | solution.py:286
  65.2 21.8 %all-to-all-start.1 = ((bf16[8,2,256,128]{3,2,1,0:T(8,128)(2,1)}), bf16[8,2,256,128]{3,2,1,0:T(8,128)(2,1)S(1)}, u32[]{:S(2)}, u32[]{:S(2)}) async-start(bf16[8,2,256,128]{3,2,1,0:T(8,128)(2,1)} %pad_maximum_fusion.2), calls=%async_computation.1 | async-start | bytes 2097152 | tf_op jit(solution)/shard_map/all_to_all | solution.py:215
  72.5 26.6 %collective-permute-start.17 = (bf16[2,128,256]{2,1,0:T(8,128)(2,1)}, bf16[2,128,256]{2,1,0:T(8,128)(2,1)}, u32[]{:S(2)}, u32[]{:S(2)}) collective-permute-start(bf16[2,128,256]{2,1,0:T(8,128)(2,1)} %pad_maximum_fusion.6), channel_id=1, source_target_pairs={{0,6},{2,8},{4,10},{6,12},{8,14},{10,0},{12,2},{14,4},{1,7},{3,9},... | collective-permute-start | bytes 393224 | tf_op jit(solution)/shard_map/ppermute | solution.py:286
  75.7 27.8 %collective-permute-start.18 = (bf16[2,128,256]{2,1,0:T(8,128)(2,1)}, bf16[2,128,256]{2,1,0:T(8,128)(2,1)}, u32[]{:S(2)}, u32[]{:S(2)}) collective-permute-start(bf16[2,128,256]{2,1,0:T(8,128)(2,1)} %pad_maximum_fusion.7), channel_id=1, source_target_pairs={{0,8},{2,10},{4,12},{6,14},{8,0},{10,2},{12,4},{14,6},{1,9},{3,11}... | collective-permute-start | bytes 393224 | tf_op jit(solution)/shard_map/ppermute | solution.py:286
  82.1 30.9 %collective-permute-start.20 = (bf16[2,128,256]{2,1,0:T(8,128)(2,1)}, bf16[2,128,256]{2,1,0:T(8,128)(2,1)}, u32[]{:S(2)}, u32[]{:S(2)}) collective-permute-start(bf16[2,128,256]{2,1,0:T(8,128)(2,1)} %pad_maximum_fusion.9), channel_id=1, source_target_pairs={{0,12},{2,14},{4,0},{6,2},{8,4},{10,6},{12,8},{14,10},{1,13},{3,15... | collective-permute-start | bytes 393224 | tf_op jit(solution)/shard_map/ppermute | solution.py:286
  86.9 20.4 %all-to-all-start.2 = ((bf16[8,256,128]{2,1,0:T(8,128)(2,1)}), bf16[8,256,128]{2,1,0:T(8,128)(2,1)S(1)}, u32[]{:S(2)}, u32[]{:S(2)}) async-start(bf16[8,256,128]{2,1,0:T(8,128)(2,1)} %get-tuple-element.176), calls=%async_computation.2 | async-start | bytes 1048576 | tf_op jit(solution)/shard_map/all_to_all | solution.py:215
  93.9 48.1 %collective-permute-start.15 = (bf16[2,2,256,128]{3,2,1,0:T(8,128)(2,1)}, bf16[2,2,256,128]{3,2,1,0:T(8,128)(2,1)}, u32[]{:S(2)}, u32[]{:S(2)}) collective-permute-start(bf16[2,2,256,128]{3,2,1,0:T(8,128)(2,1)} %get-tuple-element.146), channel_id=1, source_target_pairs={{0,384},{128,0},{256,128},{384,256},{1,385},{129,1},{257,129},{385... | collective-permute-start | bytes 786440 | tf_op jit(solution)/shard_map/ppermute | solution.py:242
  99.1 42.8 %collective-permute-start.14 = (bf16[2,2,256,128]{3,2,1,0:T(8,128)(2,1)}, bf16[2,2,256,128]{3,2,1,0:T(8,128)(2,1)}, u32[]{:S(2)}, u32[]{:S(2)}) collective-permute-start(bf16[2,2,256,128]{3,2,1,0:T(8,128)(2,1)} %get-tuple-element.147), channel_id=1, source_target_pairs={{0,256},{128,384},{256,0},{384,128},{1,257},{129,385},{257,1},{385... | collective-permute-start | bytes 786440 | tf_op jit(solution)/shard_map/ppermute | solution.py:242
  103.5 38.5 %collective-permute-start.13 = (bf16[2,2,256,128]{3,2,1,0:T(8,128)(2,1)}, bf16[2,2,256,128]{3,2,1,0:T(8,128)(2,1)}, u32[]{:S(2)}, u32[]{:S(2)}) collective-permute-start(bf16[2,2,256,128]{3,2,1,0:T(8,128)(2,1)} %get-tuple-element.148), channel_id=1, source_target_pairs={{0,128},{128,256},{256,384},{384,0},{1,129},{129,257},{257,385},{3... | collective-permute-start | bytes 786440 | tf_op jit(solution)/shard_map/ppermute | solution.py:242
  108.4 27.9 %collective-permute-start.16 = (bf16[2048,128]{1,0:T(8,128)(2,1)S(1)}, bf16[2048,128]{1,0:T(8,128)(2,1)S(1)}, u32[]{:S(2)}, u32[]{:S(2)}) collective-permute-start(bf16[2048,128]{1,0:T(8,128)(2,1)S(1)} %bitcast.37), channel_id=1, source_target_pairs={{0,1},{1,0},{2,3},{3,2},{4,5},{5,4},{6,7},{7,6},{8,9},{9,8},{10,11... | collective-permute-start | bytes 1572872 | tf_op jit(solution)/shard_map/ppermute | solution.py:205
  142.6 13.1 %all-to-all-start.3 = ((f32[8,2,1024]{2,1,0:T(2,128)}), f32[8,2,1024]{2,1,0:T(2,128)S(1)}, u32[]{:S(2)}, u32[]{:S(2)}) async-start(f32[8,2,1024]{2,1,0:T(2,128)} %broadcast_in_dim.32), calls=%async_computation.3 | async-start | bytes 131072 | tf_op jit(solution)/shard_map/all_to_all | solution.py:211
  155.7 32.1 %all-to-all-start.4 = ((bf16[8,2,256,128]{3,2,1,0:T(8,128)(2,1)}), bf16[8,2,256,128]{3,2,1,0:T(8,128)(2,1)S(1)}, u32[]{:S(2)}, u32[]{:S(2)}) async-start(bf16[8,2,256,128]{3,2,1,0:T(8,128)(2,1)} %copy-done.6), calls=%async_computation.4 | async-start | bytes 2097152 | tf_op jit(solution)/shard_map/all_to_all | solution.py:215
  171.4 16.4 %collective-permute-start.21 = (bf16[2048,128]{1,0:T(8,128)(2,1)S(1)}, bf16[2048,128]{1,0:T(8,128)(2,1)S(1)}, u32[]{:S(2)}, u32[]{:S(2)}) collective-permute-start(bf16[2048,128]{1,0:T(8,128)(2,1)S(1)} %get-tuple-element.134), channel_id=1, source_target_pairs={{0,1},{1,0},{2,3},{3,2},{4,5},{5,4},{6,7},{7,6},{8,9},{9,8},{10,11... | collective-permute-start | bytes 1572872 | tf_op jit(solution)/shard_map/ppermute | solution.py:205
  (20 other events, 196.0 us)
Sparse Core Ops, SparseCore 0:
  10.1 68.9 all-gather.2

commit v6 on v5

v6 whole, which is shorter than its diff:
```python
import functools
import math

import jax
import jax.numpy as jnp
from jax import lax
from jax.experimental import pallas as pl
from jax.experimental.pallas import tpu as pltpu
from jax.sharding import Mesh
from jax.sharding import PartitionSpec as P

EPS = 1e-06
ADAM_EPS = 1e-08
BETA_ONE = 0.9
BETA_TWO = 0.95
DECAY = 0.1
bias_one = 1.0 - 0.9**10
bias_two = 1.0 - 0.95**10
RATE_TABLE = (0.02, 0.032, 0.05, 0.08, 0.125)
MINOR = 2
PLANES = 4
FEW = 2
LANES = 128
VMEM_LIMIT = 56 * 1024 * 1024
KINDS = 3
HALVES = 2


def adamw_kernel(side_ref, rate_ref, weight_ref, moments_ref, mine_ref, theirs_ref, *refs):
    weight_out, first_out, second_out = refs[-3:]
    rate = jnp.float32(0.0)
    for slot, value in enumerate(RATE_TABLE):
        rate = jnp.where(rate_ref[0] == slot, jnp.float32(value), rate)
    gradient = mine_ref[...] + theirs_ref[...].astype(jnp.float32)
    weight_now = weight_ref[0, 0].astype(jnp.float32)
    first_now = moments_ref[0, 0].astype(jnp.float32)
    second_now = moments_ref[0, 1].astype(jnp.float32)
    first_sum = BETA_ONE * first_now + (1.0 - BETA_ONE) * gradient
    second_sum = BETA_TWO * second_now + (1.0 - BETA_TWO) * gradient * gradient
    update = first_sum / bias_one / (jnp.sqrt(second_sum / bias_two) + ADAM_EPS)
    weight_new = weight_now * (1.0 - rate * DECAY) - rate * update
    weight_out[0] = weight_new.astype(jnp.bfloat16)
    first_out[0] = first_sum.astype(jnp.bfloat16)
    second_out[0] = second_sum.astype(jnp.bfloat16)


def adamw(half, side, rate_index, weight, moments, mine, theirs, earlier):
    pieces, _, rows, width = weight.shape
    steps = pieces // HALVES
    first = half * steps
    flat = pl.BlockSpec((rows, width), lambda i, m, r: (i, 0))
    out = pl.BlockSpec((1, rows, width), lambda i, m, r: (0, first + i, 0))
    count = len(earlier)
    return pl.pallas_call(
        adamw_kernel,
        grid_spec=pltpu.PrefetchScalarGridSpec(
            num_scalar_prefetch=2,
            grid=(steps,),
            in_specs=[
                pl.BlockSpec((1, 1, rows, width), lambda i, m, r: (first + i, m[0], 0, 0)),
                pl.BlockSpec((1, KINDS - 1, rows, width), lambda i, m, r: (first + i, 0, 0, 0)),
                flat,
                flat,
            ]
            + [pl.BlockSpec(memory_space=pl.ANY)] * count,
            out_specs=[out, out, out],
        ),
        out_shape=[jax.ShapeDtypeStruct((1, pieces * rows, width), jnp.bfloat16)] * KINDS,
        input_output_aliases={6 + i: i for i in range(count)},
        compiler_params=pltpu.CompilerParams(vmem_limit_bytes=VMEM_LIMIT),
        cost_estimate=pl.CostEstimate(
            flops=20 * steps * rows * width,
            bytes_accessed=18 * steps * rows * width,
            transcendentals=steps * rows * width,
        ),
        name="adamw",
    )(side, rate_index, weight, moments, mine, theirs, *earlier)


def forward_kernel(inv_scale, shifts, major_ref, near_ref, far_ref, weight_ref, gain_ref, *refs):
    parts = refs[:shifts]
    hidden_ref, sums_ref, both_ref, rows_ref = refs[shifts : shifts + 4]
    part_ref = refs[-1]
    pieces, halves, rows, width = weight_ref.shape
    step = pl.program_id(0)
    per = near_ref.shape[0]

    @pl.when(step == 0)
    def _():
        for piece in range(pieces):
            for half in range(halves):
                both_ref[piece * rows : (piece + 1) * rows, half * width : (half + 1) * width] = weight_ref[piece, half]

    for now in range(shifts // 2):
        @pl.when(step == now)
        def _():
            part_ref[0] = parts[2 * now][...]
            part_ref[1] = parts[2 * now + 1][...]

    rows_ref[:per] = near_ref[...]
    rows_ref[per:] = far_ref[...]
    linear = jnp.dot(rows_ref[...], both_ref[...], preferred_element_type=jnp.float32)
    lane = lax.broadcasted_iota(jnp.int32, (per, LANES), 1)
    for which in range(2):
        origin = lax.rem(major_ref[0] + shifts - 2 * step - which, shifts)
        place = pl.ds(pl.multiple_of(origin * per, per), per)
        hidden = part_ref[which, 0].astype(jnp.float32) + linear[which * per : (which + 1) * per] * inv_scale
        hidden_ref[place, :] = hidden
        scaled = part_ref[which, 1].astype(jnp.float32) * gain_ref[...]
        squares = jnp.sum(hidden * hidden, axis=1, keepdims=True)
        inner = jnp.sum(scaled * hidden, axis=1, keepdims=True)
        packed = jnp.where(lane == 0, squares, jnp.where(lane == 1, inner, 0.0)).T[:2]
        for target in range(shifts):
            sums_ref[target, :, place] = packed


def forward(major, rows, weight, gain, parts, inv_scale):
    tokens, depth = rows.shape
    shifts = len(parts)
    per = tokens // shifts
    block = 2 * weight.shape[3]
    near = lambda which: pl.BlockSpec((per, depth), lambda i, m: (lax.rem(m[0] + shifts - 2 * i - which, shifts), 0))
    return pl.pallas_call(
        functools.partial(forward_kernel, inv_scale, shifts),
        grid_spec=pltpu.PrefetchScalarGridSpec(
            num_scalar_prefetch=1,
            grid=(shifts // 2,),
            in_specs=[
                near(0),
                near(1),
                pl.BlockSpec(weight.shape, lambda i, m: (0, 0, 0, 0)),
                pl.BlockSpec(gain.shape, lambda i, m: (0, 0)),
            ]
            + [pl.BlockSpec(part.shape, lambda i, m: (0, 0, 0)) for part in parts],
            out_specs=[
                pl.BlockSpec((tokens, block), lambda i, m: (0, 0)),
                pl.BlockSpec((shifts, 2, tokens), lambda i, m: (0, 0, 0)),
            ],
            scratch_shapes=[
                pltpu.VMEM((depth, block), jnp.bfloat16),
                pltpu.VMEM((2 * per, depth), jnp.bfloat16),
                pltpu.VMEM((2, 2, per, block), jnp.bfloat16),
            ],
        ),
        out_shape=[
            jax.ShapeDtypeStruct((tokens, block), jnp.float32),
            jax.ShapeDtypeStruct((shifts, 2, tokens), jnp.float32),
        ],
        compiler_params=pltpu.CompilerParams(vmem_limit_bytes=VMEM_LIMIT),
        cost_estimate=pl.CostEstimate(
            flops=2 * tokens * depth * block, bytes_accessed=7 * 1024 * 1024, transcendentals=0
        ),
        name="forward",
    )(major, rows, rows, weight, gain, *parts)


def multiply(inv_scale, side_ref, delta, rows_ref, mine_ref, theirs_ref):
    width = mine_ref.shape[1]
    grad = jnp.dot(delta, rows_ref[...], preferred_element_type=jnp.float32) * inv_scale
    low = grad[:width].T
    high = grad[width:].T
    first = side_ref[0] == 0
    mine_ref[...] = jnp.where(first, low, high)
    theirs_ref[...] = jnp.where(first, high, low).astype(jnp.bfloat16)


def backward_first_kernel(inv_scale, features, shifts, side_ref, major_ref, rows_ref, hidden_ref, gain_ref, sums_ref, *refs):
    parts = refs[:shifts]
    mine_ref, theirs_ref, delta_ref = refs[shifts:]
    width = mine_ref.shape[1]
    per = hidden_ref.shape[0] // shifts

    @pl.when(pl.program_id(0) == 0)
    def _():
        for shift in range(shifts):
            origin = lax.rem(major_ref[0] + shifts - shift, shifts)
            place = pl.ds(pl.multiple_of(origin * per, per), per)
            sums = jnp.sum(sums_ref[:, :, place], axis=0)
            inverse = lax.rsqrt(sums[0:1] / features + EPS)
            factor = sums[1:2] / features * (inverse * inverse * inverse)
            inverse_here = jnp.broadcast_to(inverse, (LANES, per)).T
            factor_here = jnp.broadcast_to(factor, (LANES, per)).T
            for half in range(2):
                cols = slice(half * width, (half + 1) * width)
                scaled = parts[shift][1, :, cols].astype(jnp.float32) * gain_ref[:, cols]
                delta = scaled * inverse_here - hidden_ref[place, cols] * factor_here
                delta_ref[cols, place] = delta.T.astype(jnp.bfloat16)

    multiply(inv_scale, side_ref, delta_ref[...], rows_ref, mine_ref, theirs_ref)


def backward_next_kernel(inv_scale, side_ref, rows_ref, delta_ref, mine_ref, theirs_ref):
    multiply(inv_scale, side_ref, delta_ref[...], rows_ref, mine_ref, theirs_ref)


def backward(side, major, rows, hidden, gain, sums, parts, inv_scale, features):
    tokens, depth = rows.shape
    block = hidden.shape[1]
    width = block // 2
    step = 256
    steps = depth // step // HALVES
    params = pltpu.CompilerParams(vmem_limit_bytes=VMEM_LIMIT)
    cost = pl.CostEstimate(
        flops=2 * tokens * depth * block // HALVES, bytes_accessed=5 * 1024 * 1024, transcendentals=0
    )
    outs = [
        jax.ShapeDtypeStruct((depth // HALVES, width), jnp.float32),
        jax.ShapeDtypeStruct((depth // HALVES, width), jnp.bfloat16),
    ]
    whole = lambda array: pl.BlockSpec(array.shape, lambda i, *_: (0,) * array.ndim)
    delta = jax.ShapeDtypeStruct((block, tokens), jnp.bfloat16)
    out = pl.BlockSpec((step, width), lambda i, *_: (i, 0))
    *first, delta = pl.pallas_call(
        functools.partial(backward_first_kernel, inv_scale, features, len(parts)),
        grid_spec=pltpu.PrefetchScalarGridSpec(
            num_scalar_prefetch=2,
            grid=(steps,),
            in_specs=[pl.BlockSpec((tokens, step), lambda i, *_: (0, i)), whole(hidden), whole(gain), whole(sums)]
            + [whole(part) for part in parts],
            out_specs=[out, out, whole(delta)],
        ),
        out_shape=outs + [delta],
        compiler_params=params,
        cost_estimate=cost,
        name="backward_first",
    )(side, major, rows, hidden, gain, sums, *parts)
    result = [first]
    for half in range(1, HALVES):
        result.append(
            pl.pallas_call(
                functools.partial(backward_next_kernel, inv_scale),
                grid_spec=pltpu.PrefetchScalarGridSpec(
                    num_scalar_prefetch=1,
                    grid=(steps,),
                    in_specs=[
                        pl.BlockSpec((tokens, step), lambda i, *_, half=half: (0, half * steps + i)),
                        whole(delta),
                    ],
                    out_specs=[out, out],
                ),
                out_shape=outs,
                compiler_params=params,
                cost_estimate=cost,
                name="backward_next",
            )(side, rows, delta)
        )
    return result


def swap_minor(array):
    return lax.ppermute(array, "minor", [(0, 1), (1, 0)])


def sums_of_all(sums):
    return lax.all_to_all(sums, "major", split_axis=0, concat_axis=0, tiled=True)


def spread_columns(array):
    return lax.all_to_all(array, "column", split_axis=0, concat_axis=0, tiled=True)


def plan_moves(sources):
    planes = lax.axis_size("plane")
    columns = lax.axis_size("column")
    me = lax.axis_index("plane")
    member = jnp.arange(planes * columns, dtype=jnp.int32)
    here, there = member // columns, sources // columns
    offset = lax.rem(here - there + planes, planes)
    earlier = member[None, :] < member[:, None]
    same = (here[None, :] == here[:, None]) & (there[None, :] == there[:, None])
    rank = jnp.sum((earlier & same).astype(jnp.int32), axis=1)
    most = jnp.max(jnp.where(offset > 0, rank, 0))
    shifts = jnp.arange(1, planes, dtype=jnp.int32)[:, None, None]
    slots = jnp.arange(columns, dtype=jnp.int32)[None, :, None]
    leaving = (there == me)[None, None, :] & (offset[None, None, :] == shifts) & (rank[None, None, :] == slots)
    outgoing = jnp.sum(jnp.where(leaving, lax.rem(sources, columns)[None, None, :], 0), axis=2)
    mine = lambda values: lax.dynamic_slice_in_dim(values, me * columns, columns)
    return mine(lax.rem(sources, columns)), mine(offset), mine(rank), outgoing, most


def send_planes(pieces, outgoing, low, high):
    planes = lax.axis_size("plane")
    kinds = jnp.arange(low, high, dtype=jnp.int32)
    index = (outgoing[:, :, None] * KINDS + kinds).reshape(planes - 1, -1)
    return [
        lax.ppermute(pieces[index[shift - 1]], "plane", [(i, (i + shift) % planes) for i in range(planes)])
        for shift in range(1, planes)
    ]


def choose_kernel(low, kinds, copies, column_ref, offset_ref, rank_ref, pieces_ref, *refs):
    received, out_ref, sems = refs[:-2], refs[-2], refs[-1]
    columns = out_ref.shape[0]
    slot = lambda place, copy: out_ref.at[place, copy] if copies else out_ref.at[place]
    for place in range(columns):
        column, offset, rank = column_ref[place], offset_ref[place], rank_ref[place]
        sources = [pieces_ref.at[pl.ds(column * KINDS + low, kinds)]]
        sources += [ref.at[pl.ds(rank * kinds, kinds)] for ref in received]
        for number, source in enumerate(sources):
            @pl.when(offset == number)
            def _():
                for copy in range(max(copies, 1)):
                    pltpu.make_async_copy(source, slot(place, copy), sems.at[place, copy]).start()

    for place in range(columns):
        for copy in range(max(copies, 1)):
            pltpu.make_async_copy(pieces_ref.at[pl.ds(0, kinds)], slot(place, copy), sems.at[place, copy]).wait()


def choose(pieces, received, plan, low, high, copies):
    column, offset, rank = plan[:3]
    columns = column.shape[0]
    kinds = high - low
    lead = (columns, copies) if copies else (columns,)
    limit = received[0].shape[0] // kinds - 1
    rank = jnp.where(offset == 0, 0, jnp.minimum(rank, limit))
    anywhere = pl.BlockSpec(memory_space=pl.ANY)
    return pl.pallas_call(
        functools.partial(choose_kernel, low, kinds, copies),
        grid_spec=pltpu.PrefetchScalarGridSpec(
            num_scalar_prefetch=3,
            grid=(1,),
            in_specs=[anywhere] * (1 + len(received)),
            out_specs=anywhere,
            scratch_shapes=[pltpu.SemaphoreType.DMA((columns, max(copies, 1)))],
        ),
        out_shape=jax.ShapeDtypeStruct(lead + (kinds,) + pieces.shape[1:], pieces.dtype),
        compiler_params=pltpu.CompilerParams(vmem_limit_bytes=VMEM_LIMIT),
        name="choose",
    )(column, offset, rank, pieces, *received)


def cross_planes(pieces, received, plan, low, high, copies):
    def all_slots(pieces, received):
        rest = send_planes(pieces, plan[3][:, FEW:], low, high)
        whole = [jnp.concatenate(pair) for pair in zip(received, rest)]
        return choose(pieces, whole, plan, low, high, copies)

    def few_slots(pieces, received):
        return choose(pieces, received, plan, low, high, copies)

    return lax.cond(plan[4] >= FEW, all_slots, few_slots, pieces, received)


def spread_features(residual, upstream):
    size = lax.axis_size("major")
    me = lax.axis_index("major")
    block = residual.shape[1] // size
    received = []
    for shift in range(size):
        start = lax.rem(me + shift, size) * block
        part = jnp.stack(
            (
                lax.dynamic_slice_in_dim(residual, start, block, axis=1),
                lax.dynamic_slice_in_dim(upstream, start, block, axis=1),
            )
        )
        if shift:
            part = lax.ppermute(part, "major", [(i, (i + shift) % size) for i in range(size)])
        received.append(part)
    return received


def local(
    attention_out,
    residual,
    upstream,
    norm_gain,
    weight,
    first_moment,
    second_moment,
    sources,
    rate_index,
):
    columns = lax.axis_size("column")
    minor = lax.axis_index("minor")
    depth, width = weight.shape[1:]
    rows = depth // columns
    features = residual.shape[2]

    gathered = lax.all_gather(attention_out[0], "major", axis=0, tiled=True)
    plan = plan_moves(sources)
    few = plan[3][:, :FEW]
    state = jnp.stack(
        [array[0].reshape(columns, rows, width) for array in (weight, first_moment, second_moment)], axis=1
    )
    state = spread_columns(state).reshape(columns * KINDS, rows, width)
    parts = spread_features(residual[0], upstream[0])
    gain_other = swap_minor(norm_gain[0])
    state, gain_other, parts[1], parts[7] = lax.optimization_barrier((state, gain_other, parts[1], parts[7]))
    weights_in = send_planes(state, few, 0, 1)
    weights = cross_planes(state, weights_in, plan, 0, 1, MINOR)
    weights, state, parts[2], parts[6] = lax.optimization_barrier((weights, state, parts[2], parts[6]))
    weights = lax.all_to_all(
        weights.reshape(columns * MINOR, rows, width), ("column", "minor"), split_axis=0, concat_axis=0, tiled=True
    ).reshape(columns, MINOR, rows, width)
    moments_in = send_planes(state, few, 1, KINDS)

    gain = jnp.where(
        minor == 0,
        jnp.concatenate((norm_gain[0], gain_other)),
        jnp.concatenate((gain_other, norm_gain[0])),
    ).astype(jnp.float32)[None, :]

    inv_scale = 1.0 / math.sqrt(depth)
    side = minor.astype(jnp.int32)[None]
    major = lax.axis_index("major").astype(jnp.int32)[None]
    hidden, sums = forward(major, gathered, weights, gain, parts, inv_scale)
    moments_in, sums = lax.optimization_barrier((moments_in, sums))
    sums = sums_of_all(sums)
    moments = cross_planes(state, moments_in, plan, 1, KINDS, 0)
    moments, sums = lax.optimization_barrier((moments, sums))
    moments = spread_columns(moments)
    halves = backward(side, major, gathered, hidden, gain, sums, parts, inv_scale, features)
    result = []
    for half, (mine, theirs) in enumerate(halves):
        result = adamw(half, side, rate_index, weights, moments, mine, swap_minor(theirs), result)
    return tuple(result)


def solution(mesh):
    members, shards = mesh.devices.shape
    split = Mesh(
        mesh.devices.reshape(PLANES, members // PLANES, shards // MINOR, MINOR),
        ("plane", "column", "major", "minor"),
    )
    member, fsdp = ("plane", "column"), ("major", "minor")
    in_specs = (
        P(member, fsdp, None),
        P(member, fsdp, None),
        P(member, fsdp, None),
        P(member, fsdp),
        P(member, None, fsdp),
        P(member, None, fsdp),
        P(member, None, fsdp),
        P(),
        P(member),
    )
    out_specs = (P(member, None, fsdp),) * 3
    return jax.shard_map(local, mesh=split, in_specs=in_specs, out_specs=out_specs, check_vma=False)
```

time: 200 us -> 185 us (0.925)
  Pallas kernels: 10.4 us -> 27.6 us
  local copies, waits for them, and re-layouts: 27.2 us -> 12.1 us
  starting transfers between devices: 96.4 us -> 86.8 us
  waiting for transfers between devices: 39 us -> 31.2 us
    ppermute x3, waiting for transfers between devices: 29.8 us -> 2.36 us  [swap_minor(): return lax.ppermute(array, 'minor', [(0, 1), (1, 0)])]
    all_to_all x4 -> x2, starting transfers between devices: 28.7 us -> 14.6 us  [spread_columns(): lax.all_to_all(array, 'column', split_axis=0, concat_axis=0, tiled=True)]
    all_to_all x4 -> x2, waiting for transfers between devices: 1.23 us -> 15 us  [spread_columns(): lax.all_to_all(array, 'column', split_axis=0, concat_axis=0, tiled=True)]
    pallas_call x2 -> x5, Pallas kernels: 7.02 us -> 20.3 us  [the longest x1 6.03 us: forward(): pl.pallas_call(functools.partial(forward_kernel, inv_scale, shifts), grid...]
    unnamed x50 -> x46, local copies, waits for them, and re-layouts: 15.9 us -> 3.5 us
    ppermute x7, starting transfers between devices: 21.7 us -> 28.4 us  [spread_features(): lax.ppermute(part, 'major', [(i, (i + shift) % size) for i in range(size)])]
    ppermute x6, starting transfers between devices: 31.1 us -> 25.9 us  [send_planes(): lax.ppermute(pieces[index[shift - 1]], 'plane', [(i, (i + shift) % planes...]
    pallas_call x1 -> x2, Pallas kernels: 3.35 us -> 7.27 us  [adamw(): pl.pallas_call(adamw_kernel, grid_spec=pltpu.PrefetchScalarGridSpec(num_s...]
  transfers between devices with their start and end apart: 22 -> 21, of which waited for: 7 -> 5; matrix products, arithmetic and copies ran while one was open for 13% -> 10% of each run, Pallas kernels for 4% -> 13%
where the time goes in v6:
time: 185 us; the launch traced here: 184 us
  starting transfers between devices  86.8 us (47%)
  waiting for transfers between devices  31.2 us (17%)
  Pallas kernels  27.6 us (15%)
  between operations  16 us (9%)
  local copies, waits for them, and re-layouts  12.1 us (7%)
  other arithmetic  10.4 us (6%)
    ppermute x7, starting transfers between devices, spread_features(): lax.ppermute(part, 'major', [(i, (i + shift) % size) for i in range(size)])  28.4 us
    ppermute x6, starting transfers between devices, send_planes(): lax.ppermute(pieces[index[shift - 1]], 'plane', [(i, (i + shift) % planes...  25.9 us
    all_to_all x2, waiting for transfers between devices, spread_columns(): lax.all_to_all(array, 'column', split_axis=0, concat_axis=0, tiled=True)  15 us
    all_to_all x2, starting transfers between devices, spread_columns(): lax.all_to_all(array, 'column', split_axis=0, concat_axis=0, tiled=True)  14.6 us
    ppermute x3, starting transfers between devices, swap_minor(): return lax.ppermute(array, 'minor', [(0, 1), (1, 0)])  8.5 us
    pallas_call x2, Pallas kernels, adamw(): pl.pallas_call(adamw_kernel, grid_spec=pltpu.PrefetchScalarGridSpec(num_s...  7.27 us
    pallas_call x1, Pallas kernels, forward(): pl.pallas_call(functools.partial(forward_kernel, inv_scale, shifts), grid...  6.03 us
    all_to_all x1, starting transfers between devices, local(): lax.all_to_all(weights.reshape(columns * MINOR, rows, width), ('column',...  6.03 us
  transfers between devices with their start and end apart: 21, of which 5 were waited for; matrix products, arithmetic and copies ran while one was open for 10% of the time, Pallas kernels for 13%

profile of v6, /device:TPU:1, one launch (start us, length us, event | category | flops | bytes accessed | tf_op | source)
XLA Modules:
  0.0 184.1 jit_solution(11553241652455212451)
XLA Ops:
  10.1 5.9 %collective-permute-start.8 = (bf16[2,128,256]{2,1,0:T(8,128)(2,1)S(1)}, bf16[2,128,256]{2,1,0:T(8,128)(2,1)S(1)}, u32[]{:S(2)}, u32[]{:S(2)}) collective-permute-start(bf16[2,128,256]{2,1,0:T(8,128)(2,1)S(1)} %pad_maximum_fusion.8), channel_id=1, source_target_pairs={{0,14},{2,0},{4,2},{6,4},{8,6},{10,8},{12,10},{14,12},{1,15},{3,1}... | collective-permute-start | bytes 393224 | tf_op jit(solution)/shard_map/ppermute | solution.py:359
  19.4 8.5 %all-to-all-start = ((bf16[8,3,256,128]{3,2,1,0:T(8,128)(2,1)}), bf16[8,3,256,128]{3,2,1,0:T(8,128)(2,1)S(1)}, u32[]{:S(2)}, u32[]{:S(2)}) async-start(bf16[8,3,256,128]{3,2,1,0:T(8,128)(2,1)} %pad_maximum_fusion.6), calls=%async_computation | async-start | bytes 3145728 | tf_op jit(solution)/shard_map/all_to_all | solution.py:259
  33.6 15.0 %all-to-all-done = bf16[8,3,256,128]{3,2,1,0:T(8,128)(2,1)S(1)} async-done(((bf16[8,3,256,128]{3,2,1,0:T(8,128)(2,1)}), bf16[8,3,256,128]{3,2,1,0:T(8,128)(2,1)S(1)}, u32[]{:S(2)}, u32[]{:S(2)}) %all-to-all-start) | async-done | bytes 1572896 | tf_op jit(solution)/shard_map/all_to_all | solution.py:259
  49.2 7.5 %collective-permute-start.10 = (bf16[2,256,128]{2,1,0:T(8,128)(2,1)S(1)}, bf16[2,256,128]{2,1,0:T(8,128)(2,1)S(1)}, u32[]{:S(2)}, u32[]{:S(2)}) collective-permute-start(bf16[2,256,128]{2,1,0:T(8,128)(2,1)S(1)} %gather_fusion.7), channel_id=1, source_target_pairs={{0,256},{128,384},{256,0},{384,128},{1,257},{129,385},{257,1},{385... | collective-permute-start | bytes 393224 | tf_op jit(solution)/shard_map/ppermute | solution.py:286
  59.8 4.2 %collective-permute-start.9 = (bf16[2,256,128]{2,1,0:T(8,128)(2,1)S(1)}, bf16[2,256,128]{2,1,0:T(8,128)(2,1)S(1)}, u32[]{:S(2)}, u32[]{:S(2)}) collective-permute-start(bf16[2,256,128]{2,1,0:T(8,128)(2,1)S(1)} %gather_fusion.6), channel_id=1, source_target_pairs={{0,128},{128,256},{256,384},{384,0},{1,129},{129,257},{257,385},{3... | collective-permute-start | bytes 393224 | tf_op jit(solution)/shard_map/ppermute | solution.py:286
  64.7 4.4 %collective-permute-start.13 = (bf16[2,128,256]{2,1,0:T(8,128)(2,1)}, bf16[2,128,256]{2,1,0:T(8,128)(2,1)S(1)}, u32[]{:S(2)}, u32[]{:S(2)}) collective-permute-start(bf16[2,128,256]{2,1,0:T(8,128)(2,1)} %pad_maximum_fusion.10), channel_id=1, source_target_pairs={{0,12},{2,14},{4,0},{6,2},{8,4},{10,6},{12,8},{14,10},{1,13},{3,15... | collective-permute-start | bytes 393224 | tf_op jit(solution)/shard_map/ppermute | solution.py:359
  70.6 3.5 %conditional.2 = (bf16[8,2,1,256,128]{4,3,2,1,0:T(8,128)(2,1)S(1)}) conditional(s32[]{:T(128)} %convert_element_type.18, (s32[8]{0:T(128)S(1)}, s32[8]{0:T(128)}, s32[8]{0:T(128)S(1)}, bf16[24,256,128]{2,1,0:T(8,128)(2,1)S(1)}, bf16[2,256,128]{2,1,0:T(8,128)(2,1)S(1)}, /*index=5*/bf16[2,256,128]{2,1,0:T(8,128)(2,1)S(1)}, ...), branch_computations={%region_3.4_spmd, %region_4.5_spmd} | conditional | flops 789600 | bytes 10236560 | solution.py:342
  74.2 3.4 %collective-permute-done.13.refs_6_ = bf16[2,128,256]{2,1,0:T(8,128)(2,1)S(1)} collective-permute-done((bf16[2,128,256]{2,1,0:T(8,128)(2,1)}, bf16[2,128,256]{2,1,0:T(8,128)(2,1)S(1)}, u32[]{:S(2)}, u32[]{:S(2)}) %collective-permute-start.13) | collective-permute-done | bytes 131104 | tf_op jit(solution)/shard_map/ppermute | solution.py:359
  78.3 6.0 %all-to-all-start.1 = ((bf16[16,256,128]{2,1,0:T(8,128)(2,1)}), bf16[16,256,128]{2,1,0:T(8,128)(2,1)S(1)}, u32[]{:S(2)}, u32[]{:S(2)}) async-start(bf16[16,256,128]{2,1,0:T(8,128)(2,1)} %bitcast.70), calls=%async_computation.1 | async-start | bytes 2097152 | tf_op jit(solution)/shard_map/all_to_all | solution.py:394
  84.4 6.1 %collective-permute-start.17 = (bf16[2,128,256]{2,1,0:T(8,128)(2,1)S(1)}, bf16[2,128,256]{2,1,0:T(8,128)(2,1)S(1)}, u32[]{:S(2)}, u32[]{:S(2)}) collective-permute-start(bf16[2,128,256]{2,1,0:T(8,128)(2,1)S(1)} %pad_maximum_fusion.12), channel_id=1, source_target_pairs={{0,6},{2,8},{4,10},{6,12},{8,14},{10,0},{12,2},{14,4},{1,7},{3,9},... | collective-permute-start | bytes 393224 | tf_op jit(solution)/shard_map/ppermute | solution.py:359
  91.2 4.2 %collective-permute-start.18 = (bf16[2,128,256]{2,1,0:T(8,128)(2,1)}, bf16[2,128,256]{2,1,0:T(8,128)(2,1)}, u32[]{:S(2)}, u32[]{:S(2)}) collective-permute-start(bf16[2,128,256]{2,1,0:T(8,128)(2,1)} %pad_maximum_fusion.13), channel_id=1, source_target_pairs={{0,8},{2,10},{4,12},{6,14},{8,0},{10,2},{12,4},{14,6},{1,9},{3,11}... | collective-permute-start | bytes 393224 | tf_op jit(solution)/shard_map/ppermute | solution.py:359
  96.1 3.9 %collective-permute-start.19 = (bf16[2,128,256]{2,1,0:T(8,128)(2,1)}, bf16[2,128,256]{2,1,0:T(8,128)(2,1)}, u32[]{:S(2)}, u32[]{:S(2)}) collective-permute-start(bf16[2,128,256]{2,1,0:T(8,128)(2,1)} %pad_maximum_fusion.14), channel_id=1, source_target_pairs={{0,10},{2,12},{4,14},{6,0},{8,2},{10,4},{12,6},{14,8},{1,11},{3,13... | collective-permute-start | bytes 393224 | tf_op jit(solution)/shard_map/ppermute | solution.py:359
  101.7 4.8 %collective-permute-start.15 = (bf16[4,256,128]{2,1,0:T(8,128)(2,1)}, bf16[4,256,128]{2,1,0:T(8,128)(2,1)S(1)}, u32[]{:S(2)}, u32[]{:S(2)}) collective-permute-start(bf16[4,256,128]{2,1,0:T(8,128)(2,1)} %gather_fusion.10), channel_id=1, source_target_pairs={{0,256},{128,384},{256,0},{384,128},{1,257},{129,385},{257,1},{385... | collective-permute-start | bytes 786440 | tf_op jit(solution)/shard_map/ppermute | solution.py:286
  107.8 5.5 %collective-permute-start.16 = (bf16[4,256,128]{2,1,0:T(8,128)(2,1)}, bf16[4,256,128]{2,1,0:T(8,128)(2,1)S(1)}, u32[]{:S(2)}, u32[]{:S(2)}) collective-permute-start(bf16[4,256,128]{2,1,0:T(8,128)(2,1)} %gather_fusion.11), channel_id=1, source_target_pairs={{0,384},{128,0},{256,128},{384,256},{1,385},{129,1},{257,129},{385... | collective-permute-start | bytes 786440 | tf_op jit(solution)/shard_map/ppermute | solution.py:286
  120.3 6.0 %forward.1 = (f32[1024,256]{1,0:T(8,128)}, f32[8,2,1024]{2,1,0:T(2,128)}) custom-call(s32[1]{0:T(128)} %bitcast.29.major_ref, bf16[1024,2048]{1,0:T(8,128)(2,1)} %bitcast.63, bf16[1024,2048]{1,0:T(8,128)(2,1)} %bitcast.64, bf16[8,2,256,128]{3,2,1,0:T(8,128)(2,1)} %bitcast.67, f32[1,256]{1,0:T(1,128)} %fusion.7.gain_ref, ...), custom_call_target="tpu_custom_call" | custom-call | flops 1073741824 | bytes 7340032 | tf_op jit(solution)/shard_map/forward/pallas_call | solution.py:123
  126.4 5.4 %collective-permute-done.16 = bf16[4,256,128]{2,1,0:T(8,128)(2,1)S(1)} collective-permute-done((bf16[4,256,128]{2,1,0:T(8,128)(2,1)}, bf16[4,256,128]{2,1,0:T(8,128)(2,1)S(1)}, u32[]{:S(2)}, u32[]{:S(2)}) %collective-permute-start.16) | collective-permute-done | bytes 262176 | tf_op jit(solution)/shard_map/ppermute | solution.py:286
  131.8 3.4 %all-to-all-start.2 = ((f32[8,2,1024]{2,1,0:T(2,128)}), f32[8,2,1024]{2,1,0:T(2,128)S(1)}, u32[]{:S(2)}, u32[]{:S(2)}) async-start(f32[8,2,1024]{2,1,0:T(2,128)} %get-tuple-element.135), calls=%async_computation.2 | async-start | bytes 131072 | tf_op jit(solution)/shard_map/all_to_all | solution.py:255
  138.0 4.3 %all-to-all-done.2.sums_ref = f32[8,2,1024]{2,1,0:T(2,128)S(1)} async-done(((f32[8,2,1024]{2,1,0:T(2,128)}), f32[8,2,1024]{2,1,0:T(2,128)S(1)}, u32[]{:S(2)}, u32[]{:S(2)}) %all-to-all-start.2) | async-done | bytes 65568 | tf_op jit(solution)/shard_map/all_to_all | solution.py:255
  142.3 6.1 %all-to-all-start.3 = ((bf16[8,2,256,128]{3,2,1,0:T(8,128)(2,1)}), bf16[8,2,256,128]{3,2,1,0:T(8,128)(2,1)S(1)}, u32[]{:S(2)}, u32[]{:S(2)}) async-start(bf16[8,2,256,128]{3,2,1,0:T(8,128)(2,1)} %get-tuple-element.191), calls=%async_computation.3 | async-start | bytes 2097152 | tf_op jit(solution)/shard_map/all_to_all | solution.py:259
  148.4 5.7 %backward_first.1 = (f32[1024,128]{1,0:T(8,128)}, bf16[1024,128]{1,0:T(8,128)(2,1)}, bf16[256,1024]{1,0:T(8,128)(2,1)}) custom-call(s32[1]{0:T(128)} %bitcast.9.side_ref, s32[1]{0:T(128)} %bitcast.29.major_ref, bf16[1024,2048]{1,0:T(8,128)(2,1)} %bitcast.65, f32[1024,256]{1,0:T(8,128)} %get-tuple-element.137.hidden_ref, f32[1,256]{1,0:T(1,128)} %fusion.7.gain_ref, ...), custom_call_target="tpu_custom_call" | custom-call | flops 536870912 | bytes 5242880 | tf_op jit(solution)/shard_map/backward_first/pallas_call | solution.py:213
  154.1 4.7 %collective-permute-start.21 = (bf16[1024,128]{1,0:T(8,128)(2,1)}, bf16[1024,128]{1,0:T(8,128)(2,1)S(1)}, u32[]{:S(2)}, u32[]{:S(2)}) collective-permute-start(bf16[1024,128]{1,0:T(8,128)(2,1)} %get-tuple-element.143), channel_id=1, source_target_pairs={{0,1},{1,0},{2,3},{3,2},{4,5},{5,4},{6,7},{7,6},{8,9},{9,8},{10,11... | collective-permute-start | bytes 786440 | tf_op jit(solution)/shard_map/ppermute | solution.py:251
  158.8 4.4 %backward_next.1 = (f32[1024,128]{1,0:T(8,128)}, bf16[1024,128]{1,0:T(8,128)(2,1)}) custom-call(s32[1]{0:T(128)} %bitcast.9.side_ref, bf16[1024,2048]{1,0:T(8,128)(2,1)} %bitcast.66, bf16[256,1024]{1,0:T(8,128)(2,1)} %get-tuple-element.139.delta_ref), custom_call_target="tpu_custom_call" | custom-call | flops 536870912 | bytes 5242880 | tf_op jit(solution)/shard_map/backward_next/pallas_call | solution.py:230
  166.9 3.6 %adamw.2 = (bf16[1,2048,128]{2,1,0:T(8,128)(2,1)}, bf16[1,2048,128]{2,1,0:T(8,128)(2,1)}, bf16[1,2048,128]{2,1,0:T(8,128)(2,1)}) custom-call(s32[1]{0:T(128)} %bitcast.9.side_ref, s32[1]{0:T(128)S(6)} %copy.31.rate_ref, bf16[8,2,256,128]{3,2,1,0:T(8,128)(2,1)} %bitcast.68, bf16[8,2,256,128]{3,2,1,0:T(8,128)(2,1)} %copy-done.1, ...), custom_call_target="tpu_custom_call" | custom-call | flops 2621440 | bytes 2359296 | tf_op jit(solution)/shard_map/adamw/pallas_call | solution.py:54
  173.7 3.6 %adamw.3 = (bf16[1,2048,128]{2,1,0:T(8,128)(2,1)}, bf16[1,2048,128]{2,1,0:T(8,128)(2,1)}, bf16[1,2048,128]{2,1,0:T(8,128)(2,1)}) custom-call(s32[1]{0:T(128)} %bitcast.9.side_ref, s32[1]{0:T(128)S(6)} %copy.31.rate_ref, bf16[8,2,256,128]{3,2,1,0:T(8,128)(2,1)} %bitcast.69, ...), custom_call_target="tpu_custom_call", output_to_operand_aliasing={{0}: (6, {}), {1}: (7, {}), {2}: (8, {})} | custom-call | flops 2621440 | bytes 2359296 | tf_op jit(solution)/shard_map/adamw/pallas_call | solution.py:54
  (120 shorter events, 44.1 us)
Async XLA Ops:
  7.2 112.2 %all-gather.3.cloned.1.call-start = ((), (), s32[]{:S(2)}) async-start(), calls=%async_computation.4 | async-start | bytes 4718592 | tf_op jit(solution)/shard_map/all_gather | solution.py:381
  10.1 23.5 %collective-permute-start.8 = (bf16[2,128,256]{2,1,0:T(8,128)(2,1)S(1)}, bf16[2,128,256]{2,1,0:T(8,128)(2,1)S(1)}, u32[]{:S(2)}, u32[]{:S(2)}) collective-permute-start(bf16[2,128,256]{2,1,0:T(8,128)(2,1)S(1)} %pad_maximum_fusion.8), channel_id=1, source_target_pairs={{0,14},{2,0},{4,2},{6,4},{8,6},{10,8},{12,10},{14,12},{1,15},{3,1}... | collective-permute-start | bytes 393224 | tf_op jit(solution)/shard_map/ppermute | solution.py:359
  16.0 17.5 %collective-permute-start.7 = (bf16[2,128,256]{2,1,0:T(8,128)(2,1)S(1)}, bf16[2,128,256]{2,1,0:T(8,128)(2,1)S(1)}, u32[]{:S(2)}, u32[]{:S(2)}) collective-permute-start(bf16[2,128,256]{2,1,0:T(8,128)(2,1)S(1)} %pad_maximum_fusion.7), channel_id=1, source_target_pairs={{0,2},{2,4},{4,6},{6,8},{8,10},{10,12},{12,14},{14,0},{1,3},{3,5},... | collective-permute-start | bytes 393224 | tf_op jit(solution)/shard_map/ppermute | solution.py:359
  19.4 29.2 %all-to-all-start = ((bf16[8,3,256,128]{3,2,1,0:T(8,128)(2,1)}), bf16[8,3,256,128]{3,2,1,0:T(8,128)(2,1)S(1)}, u32[]{:S(2)}, u32[]{:S(2)}) async-start(bf16[8,3,256,128]{3,2,1,0:T(8,128)(2,1)} %pad_maximum_fusion.6), calls=%async_computation | async-start | bytes 3145728 | tf_op jit(solution)/shard_map/all_to_all | solution.py:259
  27.9 5.7 %collective-permute-start.6 = (bf16[128]{0:T(256)(128)(2,1)S(1)}, bf16[128]{0:T(256)(128)(2,1)S(1)}, u32[]{:S(2)}, u32[]{:S(2)}) collective-permute-start(bf16[128]{0:T(256)(128)(2,1)S(1)} %bitcast.74), channel_id=1, source_target_pairs={{0,1},{1,0},{2,3},{3,2},{4,5},{5,4},{6,7},{7,6},{8,9},{9,8},{10,11... | collective-permute-start | bytes 776 | tf_op jit(solution)/shard_map/ppermute | solution.py:251
  30.5 43.7 %collective-permute-start.12 = (bf16[2,128,256]{2,1,0:T(8,128)(2,1)}, bf16[2,128,256]{2,1,0:T(8,128)(2,1)S(1)}, u32[]{:S(2)}, u32[]{:S(2)}) collective-permute-start(bf16[2,128,256]{2,1,0:T(8,128)(2,1)} %pad_maximum_fusion.9), channel_id=1, source_target_pairs={{0,4},{2,6},{4,8},{6,10},{8,12},{10,14},{12,0},{14,2},{1,5},{3,7},... | collective-permute-start | bytes 393224 | tf_op jit(solution)/shard_map/ppermute | solution.py:359
  33.6 25.7 %copy-start.22 = (bf16[128]{0:T(256)(128)(2,1)}, bf16[128]{0:T(256)(128)(2,1)S(1)}, u32[]{:S(2)}) copy-start(bf16[128]{0:T(256)(128)(2,1)S(1)} %collective-permute-done.6) | copy-start | bytes 772
  33.6 37.0 %copy-start.3 = (bf16[2,128,256]{2,1,0:T(8,128)(2,1)}, bf16[2,128,256]{2,1,0:T(8,128)(2,1)S(1)}, u32[]{:S(2)}) copy-start(bf16[2,128,256]{2,1,0:T(8,128)(2,1)S(1)} %collective-permute-done.8.refs_7_) | copy-start | bytes 393220
  33.6 37.0 %copy-start.4 = (bf16[2,128,256]{2,1,0:T(8,128)(2,1)}, bf16[2,128,256]{2,1,0:T(8,128)(2,1)S(1)}, u32[]{:S(2)}) copy-start(bf16[2,128,256]{2,1,0:T(8,128)(2,1)S(1)} %collective-permute-done.7.refs_1_) | copy-start | bytes 393220
  49.2 21.4 %collective-permute-start.10 = (bf16[2,256,128]{2,1,0:T(8,128)(2,1)S(1)}, bf16[2,256,128]{2,1,0:T(8,128)(2,1)S(1)}, u32[]{:S(2)}, u32[]{:S(2)}) collective-permute-start(bf16[2,256,128]{2,1,0:T(8,128)(2,1)S(1)} %gather_fusion.7), channel_id=1, source_target_pairs={{0,256},{128,384},{256,0},{384,128},{1,257},{129,385},{257,1},{385... | collective-permute-start | bytes 393224 | tf_op jit(solution)/shard_map/ppermute | solution.py:286
  57.3 13.3 %collective-permute-start.11 = (bf16[2,256,128]{2,1,0:T(8,128)(2,1)S(1)}, bf16[2,256,128]{2,1,0:T(8,128)(2,1)S(1)}, u32[]{:S(2)}, u32[]{:S(2)}) collective-permute-start(bf16[2,256,128]{2,1,0:T(8,128)(2,1)S(1)} %gather_fusion.8), channel_id=1, source_target_pairs={{0,384},{128,0},{256,128},{384,256},{1,385},{129,1},{257,129},{385... | collective-permute-start | bytes 393224 | tf_op jit(solution)/shard_map/ppermute | solution.py:286
  59.8 10.7 %collective-permute-start.9 = (bf16[2,256,128]{2,1,0:T(8,128)(2,1)S(1)}, bf16[2,256,128]{2,1,0:T(8,128)(2,1)S(1)}, u32[]{:S(2)}, u32[]{:S(2)}) collective-permute-start(bf16[2,256,128]{2,1,0:T(8,128)(2,1)S(1)} %gather_fusion.6), channel_id=1, source_target_pairs={{0,128},{128,256},{256,384},{384,0},{1,129},{129,257},{257,385},{3... | collective-permute-start | bytes 393224 | tf_op jit(solution)/shard_map/ppermute | solution.py:286
  64.7 12.9 %collective-permute-start.13 = (bf16[2,128,256]{2,1,0:T(8,128)(2,1)}, bf16[2,128,256]{2,1,0:T(8,128)(2,1)S(1)}, u32[]{:S(2)}, u32[]{:S(2)}) collective-permute-start(bf16[2,128,256]{2,1,0:T(8,128)(2,1)} %pad_maximum_fusion.10), channel_id=1, source_target_pairs={{0,12},{2,14},{4,0},{6,2},{8,4},{10,6},{12,8},{14,10},{1,13},{3,15... | collective-permute-start | bytes 393224 | tf_op jit(solution)/shard_map/ppermute | solution.py:359
  78.3 41.0 %all-to-all-start.1 = ((bf16[16,256,128]{2,1,0:T(8,128)(2,1)}), bf16[16,256,128]{2,1,0:T(8,128)(2,1)S(1)}, u32[]{:S(2)}, u32[]{:S(2)}) async-start(bf16[16,256,128]{2,1,0:T(8,128)(2,1)} %bitcast.70), calls=%async_computation.1 | async-start | bytes 2097152 | tf_op jit(solution)/shard_map/all_to_all | solution.py:394
  84.4 30.2 %collective-permute-start.17 = (bf16[2,128,256]{2,1,0:T(8,128)(2,1)S(1)}, bf16[2,128,256]{2,1,0:T(8,128)(2,1)S(1)}, u32[]{:S(2)}, u32[]{:S(2)}) collective-permute-start(bf16[2,128,256]{2,1,0:T(8,128)(2,1)S(1)} %pad_maximum_fusion.12), channel_id=1, source_target_pairs={{0,6},{2,8},{4,10},{6,12},{8,14},{10,0},{12,2},{14,4},{1,7},{3,9},... | collective-permute-start | bytes 393224 | tf_op jit(solution)/shard_map/ppermute | solution.py:359
  91.2 28.1 %collective-permute-start.18 = (bf16[2,128,256]{2,1,0:T(8,128)(2,1)}, bf16[2,128,256]{2,1,0:T(8,128)(2,1)}, u32[]{:S(2)}, u32[]{:S(2)}) collective-permute-start(bf16[2,128,256]{2,1,0:T(8,128)(2,1)} %pad_maximum_fusion.13), channel_id=1, source_target_pairs={{0,8},{2,10},{4,12},{6,14},{8,0},{10,2},{12,4},{14,6},{1,9},{3,11}... | collective-permute-start | bytes 393224 | tf_op jit(solution)/shard_map/ppermute | solution.py:359
  96.1 23.3 %collective-permute-start.19 = (bf16[2,128,256]{2,1,0:T(8,128)(2,1)}, bf16[2,128,256]{2,1,0:T(8,128)(2,1)}, u32[]{:S(2)}, u32[]{:S(2)}) collective-permute-start(bf16[2,128,256]{2,1,0:T(8,128)(2,1)} %pad_maximum_fusion.14), channel_id=1, source_target_pairs={{0,10},{2,12},{4,14},{6,0},{8,2},{10,4},{12,6},{14,8},{1,11},{3,13... | collective-permute-start | bytes 393224 | tf_op jit(solution)/shard_map/ppermute | solution.py:359
  101.7 24.7 %collective-permute-start.15 = (bf16[4,256,128]{2,1,0:T(8,128)(2,1)}, bf16[4,256,128]{2,1,0:T(8,128)(2,1)S(1)}, u32[]{:S(2)}, u32[]{:S(2)}) collective-permute-start(bf16[4,256,128]{2,1,0:T(8,128)(2,1)} %gather_fusion.10), channel_id=1, source_target_pairs={{0,256},{128,384},{256,0},{384,128},{1,257},{129,385},{257,1},{385... | collective-permute-start | bytes 786440 | tf_op jit(solution)/shard_map/ppermute | solution.py:286
  107.8 24.0 %collective-permute-start.16 = (bf16[4,256,128]{2,1,0:T(8,128)(2,1)}, bf16[4,256,128]{2,1,0:T(8,128)(2,1)S(1)}, u32[]{:S(2)}, u32[]{:S(2)}) collective-permute-start(bf16[4,256,128]{2,1,0:T(8,128)(2,1)} %gather_fusion.11), channel_id=1, source_target_pairs={{0,384},{128,0},{256,128},{384,256},{1,385},{129,1},{257,129},{385... | collective-permute-start | bytes 786440 | tf_op jit(solution)/shard_map/ppermute | solution.py:286
  114.6 17.2 %collective-permute-start.14 = (bf16[4,256,128]{2,1,0:T(8,128)(2,1)}, bf16[4,256,128]{2,1,0:T(8,128)(2,1)S(1)}, u32[]{:S(2)}, u32[]{:S(2)}) collective-permute-start(bf16[4,256,128]{2,1,0:T(8,128)(2,1)} %gather_fusion.9), channel_id=1, source_target_pairs={{0,128},{128,256},{256,384},{384,0},{1,129},{129,257},{257,385},{3... | collective-permute-start | bytes 786440 | tf_op jit(solution)/shard_map/ppermute | solution.py:286
  131.8 10.5 %all-to-all-start.2 = ((f32[8,2,1024]{2,1,0:T(2,128)}), f32[8,2,1024]{2,1,0:T(2,128)S(1)}, u32[]{:S(2)}, u32[]{:S(2)}) async-start(f32[8,2,1024]{2,1,0:T(2,128)} %get-tuple-element.135), calls=%async_computation.2 | async-start | bytes 131072 | tf_op jit(solution)/shard_map/all_to_all | solution.py:255
  142.3 23.5 %all-to-all-start.3 = ((bf16[8,2,256,128]{3,2,1,0:T(8,128)(2,1)}), bf16[8,2,256,128]{3,2,1,0:T(8,128)(2,1)S(1)}, u32[]{:S(2)}, u32[]{:S(2)}) async-start(bf16[8,2,256,128]{3,2,1,0:T(8,128)(2,1)} %get-tuple-element.191), calls=%async_computation.3 | async-start | bytes 2097152 | tf_op jit(solution)/shard_map/all_to_all | solution.py:259
  154.1 11.7 %collective-permute-start.21 = (bf16[1024,128]{1,0:T(8,128)(2,1)}, bf16[1024,128]{1,0:T(8,128)(2,1)S(1)}, u32[]{:S(2)}, u32[]{:S(2)}) collective-permute-start(bf16[1024,128]{1,0:T(8,128)(2,1)} %get-tuple-element.143), channel_id=1, source_target_pairs={{0,1},{1,0},{2,3},{3,2},{4,5},{5,4},{6,7},{7,6},{8,9},{9,8},{10,11... | collective-permute-start | bytes 786440 | tf_op jit(solution)/shard_map/ppermute | solution.py:251
  163.3 9.7 %collective-permute-start.20 = (bf16[1024,128]{1,0:T(8,128)(2,1)}, bf16[1024,128]{1,0:T(8,128)(2,1)S(1)}, u32[]{:S(2)}, u32[]{:S(2)}) collective-permute-start(bf16[1024,128]{1,0:T(8,128)(2,1)} %get-tuple-element.141), channel_id=1, source_target_pairs={{0,1},{1,0},{2,3},{3,2},{4,5},{5,4},{6,7},{7,6},{8,9},{9,8},{10,11... | collective-permute-start | bytes 786440 | tf_op jit(solution)/shard_map/ppermute | solution.py:251
  (20 other events, 171.5 us)
Sparse Core Ops, SparseCore 0:
  10.1 69.7 all-gather.2

commit v7 on v6

--- a/solution.py
+++ b/solution.py
@@ -21,7 +21,8 @@
 PLANES = 4
 FEW = 2
 LANES = 128
-VMEM_LIMIT = 56 * 1024 * 1024
+VMEM_LIMIT = 24 * 1024 * 1024
+FORWARD_LIMIT = 48 * 1024 * 1024
 KINDS = 3
 HALVES = 2
 
@@ -146,7 +147,7 @@
             jax.ShapeDtypeStruct((tokens, block), jnp.float32),
             jax.ShapeDtypeStruct((shifts, 2, tokens), jnp.float32),
         ],
-        compiler_params=pltpu.CompilerParams(vmem_limit_bytes=VMEM_LIMIT),
+        compiler_params=pltpu.CompilerParams(vmem_limit_bytes=FORWARD_LIMIT),
         cost_estimate=pl.CostEstimate(
             flops=2 * tokens * depth * block, bytes_accessed=7 * 1024 * 1024, transcendentals=0
         ),
@@ -270,55 +271,68 @@
     same = (here[None, :] == here[:, None]) & (there[None, :] == there[:, None])
     rank = jnp.sum((earlier & same).astype(jnp.int32), axis=1)
     most = jnp.max(jnp.where(offset > 0, rank, 0))
-    shifts = jnp.arange(1, planes, dtype=jnp.int32)[:, None, None]
+    targets = jnp.arange(planes, dtype=jnp.int32)[:, None, None]
     slots = jnp.arange(columns, dtype=jnp.int32)[None, :, None]
-    leaving = (there == me)[None, None, :] & (offset[None, None, :] == shifts) & (rank[None, None, :] == slots)
-    outgoing = jnp.sum(jnp.where(leaving, lax.rem(sources, columns)[None, None, :], 0), axis=2)
+    leaving = (there == me) & (rank == slots)
+    column = lax.rem(sources, columns)
+    by_plane = jnp.sum(jnp.where(leaving & (here == targets), column, 0), axis=2)
+    by_shift = jnp.sum(jnp.where(leaving & (offset == targets[1:]), column, 0), axis=2)
     mine = lambda values: lax.dynamic_slice_in_dim(values, me * columns, columns)
-    return mine(lax.rem(sources, columns)), mine(offset), mine(rank), outgoing, most
-
-
-def send_planes(pieces, outgoing, low, high):
+    return dict(
+        column=mine(column),
+        plane=mine(there),
+        offset=mine(offset),
+        rank=mine(rank),
+        by_plane=by_plane,
+        by_shift=by_shift,
+        most=most,
+    )
+
+
+def pick(pieces, slots, low, high):
+    kinds = jnp.arange(low, high, dtype=jnp.int32)
+    return pieces[(slots[..., None] * KINDS + kinds).reshape(-1)]
+
+
+def send_at_once(pieces, slots):
+    return [lax.all_to_all(pick(pieces, slots, 0, 1), "plane", split_axis=0, concat_axis=0, tiled=True)]
+
+
+def send_by_shift(pieces, slots):
     planes = lax.axis_size("plane")
-    kinds = jnp.arange(low, high, dtype=jnp.int32)
-    index = (outgoing[:, :, None] * KINDS + kinds).reshape(planes - 1, -1)
     return [
-        lax.ppermute(pieces[index[shift - 1]], "plane", [(i, (i + shift) % planes) for i in range(planes)])
+        lax.ppermute(
+            pick(pieces, slots[shift - 1], 1, KINDS), "plane", [(i, (i + shift) % planes) for i in range(planes)]
+        )
         for shift in range(1, planes)
     ]
 
 
-def choose_kernel(low, kinds, copies, column_ref, offset_ref, rank_ref, pieces_ref, *refs):
-    received, out_ref, sems = refs[:-2], refs[-2], refs[-1]
+def choose_kernel(kinds, copies, which_ref, start_ref, *refs):
+    refs, out_ref, sems = refs[:-2], refs[-2], refs[-1]
     columns = out_ref.shape[0]
     slot = lambda place, copy: out_ref.at[place, copy] if copies else out_ref.at[place]
     for place in range(columns):
-        column, offset, rank = column_ref[place], offset_ref[place], rank_ref[place]
-        sources = [pieces_ref.at[pl.ds(column * KINDS + low, kinds)]]
-        sources += [ref.at[pl.ds(rank * kinds, kinds)] for ref in received]
-        for number, source in enumerate(sources):
-            @pl.when(offset == number)
+        for number, ref in enumerate(refs):
+            @pl.when(which_ref[place] == number)
             def _():
                 for copy in range(max(copies, 1)):
+                    source = ref.at[pl.ds(start_ref[place], kinds)]
                     pltpu.make_async_copy(source, slot(place, copy), sems.at[place, copy]).start()
 
     for place in range(columns):
         for copy in range(max(copies, 1)):
-            pltpu.make_async_copy(pieces_ref.at[pl.ds(0, kinds)], slot(place, copy), sems.at[place, copy]).wait()
-
-
-def choose(pieces, received, plan, low, high, copies):
-    column, offset, rank = plan[:3]
-    columns = column.shape[0]
-    kinds = high - low
+            pltpu.make_async_copy(refs[0].at[pl.ds(0, kinds)], slot(place, copy), sems.at[place, copy]).wait()
+
+
+def choose(pieces, received, which, start, kinds, copies):
+    columns = which.shape[0]
     lead = (columns, copies) if copies else (columns,)
-    limit = received[0].shape[0] // kinds - 1
-    rank = jnp.where(offset == 0, 0, jnp.minimum(rank, limit))
     anywhere = pl.BlockSpec(memory_space=pl.ANY)
     return pl.pallas_call(
-        functools.partial(choose_kernel, low, kinds, copies),
+        functools.partial(choose_kernel, kinds, copies),
         grid_spec=pltpu.PrefetchScalarGridSpec(
-            num_scalar_prefetch=3,
+            num_scalar_prefetch=2,
             grid=(1,),
             in_specs=[anywhere] * (1 + len(received)),
             out_specs=anywhere,
@@ -327,19 +341,43 @@
         out_shape=jax.ShapeDtypeStruct(lead + (kinds,) + pieces.shape[1:], pieces.dtype),
         compiler_params=pltpu.CompilerParams(vmem_limit_bytes=VMEM_LIMIT),
         name="choose",
-    )(column, offset, rank, pieces, *received)
-
-
-def cross_planes(pieces, received, plan, low, high, copies):
+    )(which, start, pieces, *received)
+
+
+def choose_weights(pieces, received, plan):
+    stays = plan["offset"] == 0
+    count = received[0].shape[0] // lax.axis_size("plane")
+    away = plan["plane"] * count + jnp.minimum(plan["rank"], count - 1)
+    start = jnp.where(stays, plan["column"] * KINDS, away)
+    return choose(pieces, received, jnp.where(stays, 0, 1), start, 1, MINOR)
+
+
+def choose_moments(pieces, received, plan):
+    kinds = KINDS - 1
+    last = received[0].shape[0] // kinds - 1
+    away = jnp.minimum(plan["rank"], last) * kinds
+    start = jnp.where(plan["offset"] == 0, plan["column"] * KINDS + 1, away)
+    return choose(pieces, received, plan["offset"], start, kinds, 0)
+
+
+def weights_across(pieces, received, plan):
     def all_slots(pieces, received):
-        rest = send_planes(pieces, plan[3][:, FEW:], low, high)
-        whole = [jnp.concatenate(pair) for pair in zip(received, rest)]
-        return choose(pieces, whole, plan, low, high, copies)
+        return choose_weights(pieces, send_at_once(pieces, plan["by_plane"]), plan)
 
     def few_slots(pieces, received):
-        return choose(pieces, received, plan, low, high, copies)
-
-    return lax.cond(plan[4] >= FEW, all_slots, few_slots, pieces, received)
+        return choose_weights(pieces, received, plan)
+
+    return lax.cond(plan["most"] >= FEW, all_slots, few_slots, pieces, received)
+
+
+def moments_across(pieces, received, plan):
+    def all_slots(pieces, received):
+        return choose_moments(pieces, send_by_shift(pieces, plan["by_shift"]), plan)
+
+    def few_slots(pieces, received):
+        return choose_moments(pieces, received, plan)
+
+    return lax.cond(plan["most"] >= FEW, all_slots, few_slots, pieces, received)
 
 
 def spread_features(residual, upstream):
@@ -380,27 +418,28 @@
 
     gathered = lax.all_gather(attention_out[0], "major", axis=0, tiled=True)
     plan = plan_moves(sources)
-    few = plan[3][:, :FEW]
     state = jnp.stack(
         [array[0].reshape(columns, rows, width) for array in (weight, first_moment, second_moment)], axis=1
     )
+    state, residual, upstream = lax.optimization_barrier((state, residual, upstream))
     state = spread_columns(state).reshape(columns * KINDS, rows, width)
     parts = spread_features(residual[0], upstream[0])
     gain_other = swap_minor(norm_gain[0])
-    state, gain_other, parts[1], parts[7] = lax.optimization_barrier((state, gain_other, parts[1], parts[7]))
-    weights_in = send_planes(state, few, 0, 1)
-    weights = cross_planes(state, weights_in, plan, 0, 1, MINOR)
-    weights, state, parts[2], parts[6] = lax.optimization_barrier((weights, state, parts[2], parts[6]))
-    weights = lax.all_to_all(
-        weights.reshape(columns * MINOR, rows, width), ("column", "minor"), split_axis=0, concat_axis=0, tiled=True
-    ).reshape(columns, MINOR, rows, width)
-    moments_in = send_planes(state, few, 1, KINDS)
-
     gain = jnp.where(
         minor == 0,
         jnp.concatenate((norm_gain[0], gain_other)),
         jnp.concatenate((gain_other, norm_gain[0])),
     ).astype(jnp.float32)[None, :]
+    state, gain, parts[0], parts[1], parts[7] = lax.optimization_barrier(
+        (state, gain, parts[0], parts[1], parts[7])
+    )
+    weights_in = send_at_once(state, plan["by_plane"][:, :FEW])
+    weights = weights_across(state, weights_in, plan)
+    weights, state, parts[2], parts[6] = lax.optimization_barrier((weights, state, parts[2], parts[6]))
+    weights = lax.all_to_all(
+        weights.reshape(columns * MINOR, rows, width), ("column", "minor"), split_axis=0, concat_axis=0, tiled=True
+    ).reshape(columns, MINOR, rows, width)
+    moments_in = send_by_shift(state, plan["by_shift"][:, :FEW])
 
     inv_scale = 1.0 / math.sqrt(depth)
     side = minor.astype(jnp.int32)[None]
@@ -408,7 +447,7 @@
     hidden, sums = forward(major, gathered, weights, gain, parts, inv_scale)
     moments_in, sums = lax.optimization_barrier((moments_in, sums))
     sums = sums_of_all(sums)
-    moments = cross_planes(state, moments_in, plan, 1, KINDS, 0)
+    moments = moments_across(state, moments_in, plan)
     moments, sums = lax.optimization_barrier((moments, sums))
     moments = spread_columns(moments)
     halves = backward(side, major, gathered, hidden, gain, sums, parts, inv_scale, features)

time: 185 us -> 236 us (1.28)
  Pallas kernels: 27.6 us -> 65.4 us
  local copies, waits for them, and re-layouts: 12.1 us -> 25 us
  other arithmetic: 10.4 us -> 6.91 us
  waiting for transfers between devices: 31.2 us -> 34.2 us
    pallas_call x2, Pallas kernels: 4.11 us -> 51.2 us  [choose(): pl.pallas_call(functools.partial(choose_kernel, kinds, copies), grid_spec...]
    unnamed x46 -> x44, local copies, waits for them, and re-layouts: 3.5 us -> 12.7 us
    ppermute x6 -> x3, starting transfers between devices: 25.9 us -> 17.7 us  [send_by_shift(): lax.ppermute(pick(pieces, slots[shift - 1], 1, KINDS), 'plane', [(i, (i +...]
    all_to_all x0 -> x1, starting transfers between devices: none -> 7.67 us  [send_at_once(): lax.all_to_all(pick(pieces, slots, 0, 1), 'plane', split_axis=0, concat_a...]
    ppermute x6 -> x3, waiting for transfers between devices: 5.43 us -> 0.01 us  [send_by_shift(): lax.ppermute(pick(pieces, slots[shift - 1], 1, KINDS), 'plane', [(i, (i +...]
    gather x6 -> x4, local copies, waits for them, and re-layouts: 5.57 us -> 10.9 us  [pick(): return pieces[(slots[..., None] * KINDS + kinds).reshape(-1)]]
    all_to_all x2, waiting for transfers between devices: 15 us -> 20.3 us  [spread_columns(): lax.all_to_all(array, 'column', split_axis=0, concat_axis=0, tiled=True)]
    ppermute x7, waiting for transfers between devices: 3.44 us -> 8.45 us  [spread_features(): lax.ppermute(part, 'major', [(i, (i + shift) % size) for i in range(size)])]
  transfers between devices with their start and end apart: 21 -> 19, of which waited for: 5 -> 4; matrix products, arithmetic and copies ran while one was open for 10% -> 8% of each run, Pallas kernels for 13% -> 27%
where the time goes in v7:
time: 236 us; the launch traced here: 234 us
  starting transfers between devices  86.8 us (37%)
  Pallas kernels  65.4 us (28%)
  waiting for transfers between devices  34.2 us (14%)
  local copies, waits for them, and re-layouts  25 us (11%)
  between operations  15.8 us (7%)
  other arithmetic  6.91 us (3%)
    pallas_call x2, Pallas kernels, choose(): pl.pallas_call(functools.partial(choose_kernel, kinds, copies), grid_spec...  51.2 us
    ppermute x7, starting transfers between devices, spread_features(): lax.ppermute(part, 'major', [(i, (i + shift) % size) for i in range(size)])  28.3 us
    all_to_all x2, waiting for transfers between devices, spread_columns(): lax.all_to_all(array, 'column', split_axis=0, concat_axis=0, tiled=True)  20.3 us
    ppermute x3, starting transfers between devices, send_by_shift(): lax.ppermute(pick(pieces, slots[shift - 1], 1, KINDS), 'plane', [(i, (i +...  17.7 us
    all_to_all x2, starting transfers between devices, spread_columns(): lax.all_to_all(array, 'column', split_axis=0, concat_axis=0, tiled=True)  14.2 us
    unnamed x44, local copies, waits for them, and re-layouts  12.7 us
    gather x4, local copies, waits for them, and re-layouts, pick(): return pieces[(slots[..., None] * KINDS + kinds).reshape(-1)]  10.9 us
    ppermute x3, starting transfers between devices, swap_minor(): return lax.ppermute(array, 'minor', [(0, 1), (1, 0)])  9.28 us
  transfers between devices with their start and end apart: 19, of which 4 were waited for; matrix products, arithmetic and copies ran while one was open for 8% of the time, Pallas kernels for 27%

profile of v7, /device:TPU:1, one launch (start us, length us, event | category | flops | bytes accessed | tf_op | source)
XLA Modules:
  0.0 234.2 jit_solution(12751803444724136546)
XLA Ops:
  8.0 2.8 %pad_maximum_fusion = bf16[8,3,256,128]{3,2,1,0:T(8,128)(2,1)} fusion(bf16[8,1,256,128]{3,2,1,0:T(8,128)(2,1)} %bitcast.54, bf16[8,1,256,128]{3,2,1,0:T(8,128)(2,1)} %bitcast.55, bf16[8,1,256,128]{3,2,1,0:T(8,128)(2,1)} %bitcast.56), kind=kLoop, calls=%fused_computation.34 | loop fusion | flops 1572864 | bytes 3145728 | tf_op jit(solution)/shard_map/stack | solution.py:421
  11.0 5.9 %collective-permute-start.5 = (bf16[2,128,256]{2,1,0:T(8,128)(2,1)S(1)}, bf16[2,128,256]{2,1,0:T(8,128)(2,1)S(1)}, u32[]{:S(2)}, u32[]{:S(2)}) collective-permute-start(bf16[2,128,256]{2,1,0:T(8,128)(2,1)S(1)} %pad_maximum_fusion.3), channel_id=1, source_target_pairs={{0,14},{2,0},{4,2},{6,4},{8,6},{10,8},{12,10},{14,12},{1,15},{3,1}... | collective-permute-start | bytes 393224 | tf_op jit(solution)/shard_map/ppermute | solution.py:397
  18.9 4.0 %collective-permute-start.3 = (bf16[128]{0:T(256)(128)(2,1)S(1)}, bf16[128]{0:T(256)(128)(2,1)S(1)}, u32[]{:S(2)}, u32[]{:S(2)}) collective-permute-start(bf16[128]{0:T(256)(128)(2,1)S(1)} %bitcast.57), channel_id=1, source_target_pairs={{0,1},{1,0},{2,3},{3,2},{4,5},{5,4},{6,7},{7,6},{8,9},{9,8},{10,11... | collective-permute-start | bytes 776 | tf_op jit(solution)/shard_map/ppermute | solution.py:252
  22.9 7.0 %all-to-all-start.1 = ((bf16[8,3,256,128]{3,2,1,0:T(8,128)(2,1)}), bf16[8,3,256,128]{3,2,1,0:T(8,128)(2,1)}, u32[]{:S(2)}, u32[]{:S(2)}) async-start(bf16[8,3,256,128]{3,2,1,0:T(8,128)(2,1)} %pad_maximum_fusion), calls=%async_computation.1 | async-start | bytes 3145728 | tf_op jit(solution)/shard_map/all_to_all | solution.py:260
  30.5 20.3 %all-to-all-done.1 = bf16[8,3,256,128]{3,2,1,0:T(8,128)(2,1)} async-done(((bf16[8,3,256,128]{3,2,1,0:T(8,128)(2,1)}), bf16[8,3,256,128]{3,2,1,0:T(8,128)(2,1)}, u32[]{:S(2)}, u32[]{:S(2)}) %all-to-all-start.1) | async-done | bytes 1572896 | tf_op jit(solution)/shard_map/all_to_all | solution.py:260
  50.7 2.8 %gather_fusion.4 = bf16[8,256,128]{2,1,0:T(8,128)(2,1)} fusion(bf16[24,256,128]{2,1,0:T(8,128)(2,1)} %bitcast.14, s32[1024]{0:T(1024)S(1)} %pad_clamp_fusion.7), kind=kCustom, calls=%fused_computation.4 | custom fusion | bytes 1048608 | tf_op jit(solution)/shard_map/gather | solution.py:294
  53.6 7.7 %all-to-all-start.2 = ((bf16[8,256,128]{2,1,0:T(8,128)(2,1)}), bf16[8,256,128]{2,1,0:T(8,128)(2,1)S(1)}, u32[]{:S(2)}, u32[]{:S(2)}) async-start(bf16[8,256,128]{2,1,0:T(8,128)(2,1)} %gather_fusion.4), calls=%async_computation.2 | async-start | bytes 1048576 | tf_op jit(solution)/shard_map/all_to_all | solution.py:298
  61.2 5.0 %collective-permute-start.11 = (bf16[2,128,256]{2,1,0:T(8,128)(2,1)S(1)}, bf16[2,128,256]{2,1,0:T(8,128)(2,1)S(1)}, u32[]{:S(2)}, u32[]{:S(2)}) collective-permute-start(bf16[2,128,256]{2,1,0:T(8,128)(2,1)S(1)} %pad_maximum_fusion.6), channel_id=1, source_target_pairs={{0,6},{2,8},{4,10},{6,12},{8,14},{10,0},{12,2},{14,4},{1,7},{3,9},... | collective-permute-start | bytes 393224 | tf_op jit(solution)/shard_map/ppermute | solution.py:397
  66.3 4.8 %collective-permute-start.12 = (bf16[2,128,256]{2,1,0:T(8,128)(2,1)S(1)}, bf16[2,128,256]{2,1,0:T(8,128)(2,1)S(1)}, u32[]{:S(2)}, u32[]{:S(2)}) collective-permute-start(bf16[2,128,256]{2,1,0:T(8,128)(2,1)S(1)} %pad_maximum_fusion.7), channel_id=1, source_target_pairs={{0,8},{2,10},{4,12},{6,14},{8,0},{10,2},{12,4},{14,6},{1,9},{3,11}... | collective-permute-start | bytes 393224 | tf_op jit(solution)/shard_map/ppermute | solution.py:397
  71.7 3.8 %collective-permute-start.7 = (bf16[2,128,256]{2,1,0:T(8,128)(2,1)}, bf16[2,128,256]{2,1,0:T(8,128)(2,1)S(1)}, u32[]{:S(2)}, u32[]{:S(2)}) collective-permute-start(bf16[2,128,256]{2,1,0:T(8,128)(2,1)} %pad_maximum_fusion.5), channel_id=1, source_target_pairs={{0,12},{2,14},{4,0},{6,2},{8,4},{10,6},{12,8},{14,10},{1,13},{3,15... | collective-permute-start | bytes 393224 | tf_op jit(solution)/shard_map/ppermute | solution.py:397
  80.7 26.3 %conditional.2 = (bf16[8,2,1,256,128]{4,3,2,1,0:T(8,128)(2,1)}) conditional(s32[]{:T(128)} %convert_element_type.18, (s32[8]{0:T(128)S(1)}, s32[8]{0:T(128)}, s32[8]{0:T(128)S(1)}, s32[8]{0:T(128)S(1)}, bf16[24,256,128]{2,1,0:T(8,128)(2,1)}, /*index=5*/bf16[8,256,128]{2,1,0:T(8,128)(2,1)S(1)}) %tuple.26, (s32[8]{0:T(128)S(1)}, s32[8]{0:T(128)}, ...), branch_computations={%region_3.4_spmd, %region_4.5_spmd} | conditional | flops 1208 | bytes 10491112 | solution.py:370
  81.3 25.6 %choose.4 = bf16[8,2,1,256,128]{4,3,2,1,0:T(8,128)(2,1)} custom-call(s32[8]{0:T(128)S(1)} %get-tuple-element.143.which_ref, s32[8]{0:T(128)S(1)} %get-tuple-element.142.start_ref, bf16[24,256,128]{2,1,0:T(8,128)(2,1)} %get-tuple-element.58.refs_0_, bf16[8,256,128]{2,1,0:T(8,128)(2,1)S(1)} %get-tuple-element.59.refs_1_), custom_call_target="tpu_custom_call" | custom-call | tf_op jit(solution)/shard_map/cond/branch_0_fun/choose/pallas_call | solution.py:332
  107.0 5.7 %all-to-all-start.3 = ((bf16[16,256,128]{2,1,0:T(8,128)(2,1)}), bf16[16,256,128]{2,1,0:T(8,128)(2,1)S(1)}, u32[]{:S(2)}, u32[]{:S(2)}) async-start(bf16[16,256,128]{2,1,0:T(8,128)(2,1)} %bitcast.18), calls=%async_computation.3 | async-start | bytes 2097152 | tf_op jit(solution)/shard_map/all_to_all | solution.py:439
  116.2 11.5 %collective-permute-start.9 = (bf16[4,256,128]{2,1,0:T(8,128)(2,1)}, bf16[4,256,128]{2,1,0:T(8,128)(2,1)S(1)}, u32[]{:S(2)}, u32[]{:S(2)}) collective-permute-start(bf16[4,256,128]{2,1,0:T(8,128)(2,1)} %gather_fusion.6), channel_id=1, source_target_pairs={{0,256},{128,384},{256,0},{384,128},{1,257},{129,385},{257,1},{385... | collective-permute-start | bytes 786440 | tf_op jit(solution)/shard_map/ppermute | solution.py:304
  135.0 4.2 %collective-permute-start.8 = (bf16[4,256,128]{2,1,0:T(8,128)(2,1)}, bf16[4,256,128]{2,1,0:T(8,128)(2,1)S(1)}, u32[]{:S(2)}, u32[]{:S(2)}) collective-permute-start(bf16[4,256,128]{2,1,0:T(8,128)(2,1)} %gather_fusion.5), channel_id=1, source_target_pairs={{0,128},{128,256},{256,384},{384,0},{1,129},{129,257},{257,385},{3... | collective-permute-start | bytes 786440 | tf_op jit(solution)/shard_map/ppermute | solution.py:304
  139.9 4.5 %collective-permute-start.13 = (bf16[2,128,256]{2,1,0:T(8,128)(2,1)S(1)}, bf16[2,128,256]{2,1,0:T(8,128)(2,1)S(1)}, u32[]{:S(2)}, u32[]{:S(2)}) collective-permute-start(bf16[2,128,256]{2,1,0:T(8,128)(2,1)S(1)} %pad_maximum_fusion.8), channel_id=1, source_target_pairs={{0,10},{2,12},{4,14},{6,0},{8,2},{10,4},{12,6},{14,8},{1,11},{3,13... | collective-permute-start | bytes 393224 | tf_op jit(solution)/shard_map/ppermute | solution.py:397
  145.1 8.4 %collective-permute-done.13.refs_5_ = bf16[2,128,256]{2,1,0:T(8,128)(2,1)S(1)} collective-permute-done((bf16[2,128,256]{2,1,0:T(8,128)(2,1)S(1)}, bf16[2,128,256]{2,1,0:T(8,128)(2,1)S(1)}, u32[]{:S(2)}, u32[]{:S(2)}) %collective-permute-start.13) | collective-permute-done | bytes 131104 | tf_op jit(solution)/shard_map/ppermute | solution.py:397
  157.2 5.1 %forward.1 = (f32[1024,256]{1,0:T(8,128)S(1)}, f32[8,2,1024]{2,1,0:T(2,128)}) custom-call(s32[1]{0:T(128)} %bitcast.27.major_ref, bf16[1024,2048]{1,0:T(8,128)(2,1)} %bitcast.47, bf16[1024,2048]{1,0:T(8,128)(2,1)} %bitcast.48, bf16[8,2,256,128]{3,2,1,0:T(8,128)(2,1)S(1)} %bitcast.51, f32[1,256]{1,0:T(1,128)S(1)} %fusion.6.gain_ref, ...), custom_call_target="tpu_custom_call" | custom-call | flops 1073741824 | bytes 7340032 | tf_op jit(solution)/shard_map/forward/pallas_call | solution.py:124
  162.3 4.0 %all-to-all-start.4 = ((f32[8,2,1024]{2,1,0:T(2,128)}), f32[8,2,1024]{2,1,0:T(2,128)}, u32[]{:S(2)}, u32[]{:S(2)}) async-start(f32[8,2,1024]{2,1,0:T(2,128)} %get-tuple-element.125), calls=%async_computation.4 | async-start | bytes 131072 | tf_op jit(solution)/shard_map/all_to_all | solution.py:256
  166.3 26.2 %conditional.3 = (bf16[8,2,256,128]{3,2,1,0:T(8,128)(2,1)}) conditional(s32[]{:T(128)} %convert_element_type.18, (s32[8]{0:T(128)S(1)}, s32[8]{0:T(128)}, s32[8]{0:T(128)S(1)}, bf16[24,256,128]{2,1,0:T(8,128)(2,1)}, bf16[4,256,128]{2,1,0:T(8,128)(2,1)S(1)}, /*index=5*/bf16[4,256,128]{2,1,0:T(8,128)(2,1)S(1)}, ...), branch_computations={%region_6.7_spmd, %region_7.8_spmd} | conditional | flops 3338 | bytes 18888872 | solution.py:380
  167.0 25.6 %choose.6 = bf16[8,2,256,128]{3,2,1,0:T(8,128)(2,1)} custom-call(s32[8]{0:T(128)S(1)} %get-tuple-element.66.which_ref, s32[8]{0:T(128)S(1)} %compare_select_fusion.2.start_ref, bf16[24,256,128]{2,1,0:T(8,128)(2,1)} %get-tuple-element.69.refs_0_, bf16[4,256,128]{2,1,0:T(8,128)(2,1)S(1)} %get-tuple-element.70.refs_1_, ...), custom_call_target="tpu_custom_call" | custom-call | tf_op jit(solution)/shard_map/cond/branch_0_fun/choose/pallas_call | solution.py:332
  192.5 7.2 %all-to-all-start.5 = ((bf16[8,2,256,128]{3,2,1,0:T(8,128)(2,1)}), bf16[8,2,256,128]{3,2,1,0:T(8,128)(2,1)S(1)}, u32[]{:S(2)}, u32[]{:S(2)}) async-start(bf16[8,2,256,128]{3,2,1,0:T(8,128)(2,1)} %get-tuple-element.185), calls=%async_computation.5 | async-start | bytes 2097152 | tf_op jit(solution)/shard_map/all_to_all | solution.py:260
  206.5 3.7 %backward_first.1 = (f32[1024,128]{1,0:T(8,128)S(1)}, bf16[1024,128]{1,0:T(8,128)(2,1)S(1)}, bf16[256,1024]{1,0:T(8,128)(2,1)S(1)}) custom-call(s32[1]{0:T(128)} %bitcast.7.side_ref, s32[1]{0:T(128)} %bitcast.27.major_ref, bf16[1024,2048]{1,0:T(8,128)(2,1)S(1)} %bitcast.49, f32[1024,256]{1,0:T(8,128)S(1)} %get-tuple-element.127.hidden_ref, ...), custom_call_target="tpu_custom_call" | custom-call | flops 536870912 | bytes 5242880 | tf_op jit(solution)/shard_map/backward_first/pallas_call | solution.py:214
  210.2 3.1 %collective-permute-start.15 = (bf16[1024,128]{1,0:T(8,128)(2,1)S(1)}, bf16[1024,128]{1,0:T(8,128)(2,1)S(1)}, u32[]{:S(2)}, u32[]{:S(2)}) collective-permute-start(bf16[1024,128]{1,0:T(8,128)(2,1)S(1)} %get-tuple-element.133), channel_id=1, source_target_pairs={{0,1},{1,0},{2,3},{3,2},{4,5},{5,4},{6,7},{7,6},{8,9},{9,8},{10,11... | collective-permute-start | bytes 786440 | tf_op jit(solution)/shard_map/ppermute | solution.py:252
  (115 shorter events, 45.6 us)
Async XLA Ops:
  7.2 146.3 %all-gather.3.cloned.1.call-start = ((), (), s32[]{:S(2)}) async-start(), calls=%async_computation.6 | async-start | bytes 4718592 | tf_op jit(solution)/shard_map/all_gather | solution.py:419
  10.8 8.1 %copy-start.23 = (bf16[1,128]{1,0:T(2,128)(2,1)S(1)}, bf16[1,128]{1,0:T(2,128)(2,1)}, u32[]{:S(2)}) copy-start(bf16[1,128]{1,0:T(2,128)(2,1)} %param.16) | copy-start | bytes 772
  11.0 19.5 %collective-permute-start.5 = (bf16[2,128,256]{2,1,0:T(8,128)(2,1)S(1)}, bf16[2,128,256]{2,1,0:T(8,128)(2,1)S(1)}, u32[]{:S(2)}, u32[]{:S(2)}) collective-permute-start(bf16[2,128,256]{2,1,0:T(8,128)(2,1)S(1)} %pad_maximum_fusion.3), channel_id=1, source_target_pairs={{0,14},{2,0},{4,2},{6,4},{8,6},{10,8},{12,10},{14,12},{1,15},{3,1}... | collective-permute-start | bytes 393224 | tf_op jit(solution)/shard_map/ppermute | solution.py:397
  16.9 13.5 %collective-permute-start.4 = (bf16[2,128,256]{2,1,0:T(8,128)(2,1)S(1)}, bf16[2,128,256]{2,1,0:T(8,128)(2,1)S(1)}, u32[]{:S(2)}, u32[]{:S(2)}) collective-permute-start(bf16[2,128,256]{2,1,0:T(8,128)(2,1)S(1)} %pad_maximum_fusion.2), channel_id=1, source_target_pairs={{0,2},{2,4},{4,6},{6,8},{8,10},{10,12},{12,14},{14,0},{1,3},{3,5},... | collective-permute-start | bytes 393224 | tf_op jit(solution)/shard_map/ppermute | solution.py:397
  18.9 11.0 %copy-start.22 = (s32[32]{0:T(128)S(1)}, s32[32]{0:T(128)}, u32[]{:S(2)}) copy-start(s32[32]{0:T(128)} %param.20) | copy-start | bytes 388
  18.9 11.5 %collective-permute-start.3 = (bf16[128]{0:T(256)(128)(2,1)S(1)}, bf16[128]{0:T(256)(128)(2,1)S(1)}, u32[]{:S(2)}, u32[]{:S(2)}) collective-permute-start(bf16[128]{0:T(256)(128)(2,1)S(1)} %bitcast.57), channel_id=1, source_target_pairs={{0,1},{1,0},{2,3},{3,2},{4,5},{5,4},{6,7},{7,6},{8,9},{9,8},{10,11... | collective-permute-start | bytes 776 | tf_op jit(solution)/shard_map/ppermute | solution.py:252
  22.9 27.8 %all-to-all-start.1 = ((bf16[8,3,256,128]{3,2,1,0:T(8,128)(2,1)}), bf16[8,3,256,128]{3,2,1,0:T(8,128)(2,1)}, u32[]{:S(2)}, u32[]{:S(2)}) async-start(bf16[8,3,256,128]{3,2,1,0:T(8,128)(2,1)} %pad_maximum_fusion), calls=%async_computation.1 | async-start | bytes 3145728 | tf_op jit(solution)/shard_map/all_to_all | solution.py:260
  53.6 27.1 %all-to-all-start.2 = ((bf16[8,256,128]{2,1,0:T(8,128)(2,1)}), bf16[8,256,128]{2,1,0:T(8,128)(2,1)S(1)}, u32[]{:S(2)}, u32[]{:S(2)}) async-start(bf16[8,256,128]{2,1,0:T(8,128)(2,1)} %gather_fusion.4), calls=%async_computation.2 | async-start | bytes 1048576 | tf_op jit(solution)/shard_map/all_to_all | solution.py:298
  61.2 78.0 %collective-permute-start.11 = (bf16[2,128,256]{2,1,0:T(8,128)(2,1)S(1)}, bf16[2,128,256]{2,1,0:T(8,128)(2,1)S(1)}, u32[]{:S(2)}, u32[]{:S(2)}) collective-permute-start(bf16[2,128,256]{2,1,0:T(8,128)(2,1)S(1)} %pad_maximum_fusion.6), channel_id=1, source_target_pairs={{0,6},{2,8},{4,10},{6,12},{8,14},{10,0},{12,2},{14,4},{1,7},{3,9},... | collective-permute-start | bytes 393224 | tf_op jit(solution)/shard_map/ppermute | solution.py:397
  66.3 78.1 %collective-permute-start.12 = (bf16[2,128,256]{2,1,0:T(8,128)(2,1)S(1)}, bf16[2,128,256]{2,1,0:T(8,128)(2,1)S(1)}, u32[]{:S(2)}, u32[]{:S(2)}) collective-permute-start(bf16[2,128,256]{2,1,0:T(8,128)(2,1)S(1)} %pad_maximum_fusion.7), channel_id=1, source_target_pairs={{0,8},{2,10},{4,12},{6,14},{8,0},{10,2},{12,4},{14,6},{1,9},{3,11}... | collective-permute-start | bytes 393224 | tf_op jit(solution)/shard_map/ppermute | solution.py:397
  71.7 35.3 %collective-permute-start.7 = (bf16[2,128,256]{2,1,0:T(8,128)(2,1)}, bf16[2,128,256]{2,1,0:T(8,128)(2,1)S(1)}, u32[]{:S(2)}, u32[]{:S(2)}) collective-permute-start(bf16[2,128,256]{2,1,0:T(8,128)(2,1)} %pad_maximum_fusion.5), channel_id=1, source_target_pairs={{0,12},{2,14},{4,0},{6,2},{8,4},{10,6},{12,8},{14,10},{1,13},{3,15... | collective-permute-start | bytes 393224 | tf_op jit(solution)/shard_map/ppermute | solution.py:397
  76.1 30.9 %collective-permute-start.6 = (bf16[2,128,256]{2,1,0:T(8,128)(2,1)}, bf16[2,128,256]{2,1,0:T(8,128)(2,1)S(1)}, u32[]{:S(2)}, u32[]{:S(2)}) collective-permute-start(bf16[2,128,256]{2,1,0:T(8,128)(2,1)} %pad_maximum_fusion.4), channel_id=1, source_target_pairs={{0,4},{2,6},{4,8},{6,10},{8,12},{10,14},{12,0},{14,2},{1,5},{3,7},... | collective-permute-start | bytes 393224 | tf_op jit(solution)/shard_map/ppermute | solution.py:397
  107.0 23.3 %copy-start.8 = (bf16[2,128,256]{2,1,0:T(8,128)(2,1)}, bf16[2,128,256]{2,1,0:T(8,128)(2,1)S(1)}, u32[]{:S(2)}) copy-start(bf16[2,128,256]{2,1,0:T(8,128)(2,1)S(1)} %collective-permute-done.7.refs_6_) | copy-start | bytes 393220
  107.0 23.3 %copy-start.11 = (bf16[2,128,256]{2,1,0:T(8,128)(2,1)}, bf16[2,128,256]{2,1,0:T(8,128)(2,1)S(1)}, u32[]{:S(2)}) copy-start(bf16[2,128,256]{2,1,0:T(8,128)(2,1)S(1)} %collective-permute-done.6.refs_2_) | copy-start | bytes 393220
  107.0 46.5 %all-to-all-start.3 = ((bf16[16,256,128]{2,1,0:T(8,128)(2,1)}), bf16[16,256,128]{2,1,0:T(8,128)(2,1)S(1)}, u32[]{:S(2)}, u32[]{:S(2)}) async-start(bf16[16,256,128]{2,1,0:T(8,128)(2,1)} %bitcast.18), calls=%async_computation.3 | async-start | bytes 2097152 | tf_op jit(solution)/shard_map/all_to_all | solution.py:439
  116.2 46.2 %collective-permute-start.9 = (bf16[4,256,128]{2,1,0:T(8,128)(2,1)}, bf16[4,256,128]{2,1,0:T(8,128)(2,1)S(1)}, u32[]{:S(2)}, u32[]{:S(2)}) collective-permute-start(bf16[4,256,128]{2,1,0:T(8,128)(2,1)} %gather_fusion.6), channel_id=1, source_target_pairs={{0,256},{128,384},{256,0},{384,128},{1,257},{129,385},{257,1},{385... | collective-permute-start | bytes 786440 | tf_op jit(solution)/shard_map/ppermute | solution.py:304
  130.4 32.0 %collective-permute-start.10 = (bf16[4,256,128]{2,1,0:T(8,128)(2,1)}, bf16[4,256,128]{2,1,0:T(8,128)(2,1)S(1)}, u32[]{:S(2)}, u32[]{:S(2)}) collective-permute-start(bf16[4,256,128]{2,1,0:T(8,128)(2,1)} %gather_fusion.7), channel_id=1, source_target_pairs={{0,384},{128,0},{256,128},{384,256},{1,385},{129,1},{257,129},{385... | collective-permute-start | bytes 786440 | tf_op jit(solution)/shard_map/ppermute | solution.py:304
  135.0 27.4 %collective-permute-start.8 = (bf16[4,256,128]{2,1,0:T(8,128)(2,1)}, bf16[4,256,128]{2,1,0:T(8,128)(2,1)S(1)}, u32[]{:S(2)}, u32[]{:S(2)}) collective-permute-start(bf16[4,256,128]{2,1,0:T(8,128)(2,1)} %gather_fusion.5), channel_id=1, source_target_pairs={{0,128},{128,256},{256,384},{384,0},{1,129},{129,257},{257,385},{3... | collective-permute-start | bytes 786440 | tf_op jit(solution)/shard_map/ppermute | solution.py:304
  139.9 13.6 %collective-permute-start.13 = (bf16[2,128,256]{2,1,0:T(8,128)(2,1)S(1)}, bf16[2,128,256]{2,1,0:T(8,128)(2,1)S(1)}, u32[]{:S(2)}, u32[]{:S(2)}) collective-permute-start(bf16[2,128,256]{2,1,0:T(8,128)(2,1)S(1)} %pad_maximum_fusion.8), channel_id=1, source_target_pairs={{0,10},{2,12},{4,14},{6,0},{8,2},{10,4},{12,6},{14,8},{1,11},{3,13... | collective-permute-start | bytes 393224 | tf_op jit(solution)/shard_map/ppermute | solution.py:397
  153.5 8.8 %copy-start.14 = (bf16[2,128,256]{2,1,0:T(8,128)(2,1)}, bf16[2,128,256]{2,1,0:T(8,128)(2,1)S(1)}, u32[]{:S(2)}) copy-start(bf16[2,128,256]{2,1,0:T(8,128)(2,1)S(1)} %collective-permute-done.13.refs_5_) | copy-start | bytes 393220
  162.3 30.2 %all-to-all-start.4 = ((f32[8,2,1024]{2,1,0:T(2,128)}), f32[8,2,1024]{2,1,0:T(2,128)}, u32[]{:S(2)}, u32[]{:S(2)}) async-start(f32[8,2,1024]{2,1,0:T(2,128)} %get-tuple-element.125), calls=%async_computation.4 | async-start | bytes 131072 | tf_op jit(solution)/shard_map/all_to_all | solution.py:256
  192.5 27.5 %all-to-all-start.5 = ((bf16[8,2,256,128]{3,2,1,0:T(8,128)(2,1)}), bf16[8,2,256,128]{3,2,1,0:T(8,128)(2,1)S(1)}, u32[]{:S(2)}, u32[]{:S(2)}) async-start(bf16[8,2,256,128]{3,2,1,0:T(8,128)(2,1)} %get-tuple-element.185), calls=%async_computation.5 | async-start | bytes 2097152 | tf_op jit(solution)/shard_map/all_to_all | solution.py:260
  210.2 9.8 %collective-permute-start.15 = (bf16[1024,128]{1,0:T(8,128)(2,1)S(1)}, bf16[1024,128]{1,0:T(8,128)(2,1)S(1)}, u32[]{:S(2)}, u32[]{:S(2)}) collective-permute-start(bf16[1024,128]{1,0:T(8,128)(2,1)S(1)} %get-tuple-element.133), channel_id=1, source_target_pairs={{0,1},{1,0},{2,3},{3,2},{4,5},{5,4},{6,7},{7,6},{8,9},{9,8},{10,11... | collective-permute-start | bytes 786440 | tf_op jit(solution)/shard_map/ppermute | solution.py:252
  215.2 10.4 %collective-permute-start.14 = (bf16[1024,128]{1,0:T(8,128)(2,1)S(1)}, bf16[1024,128]{1,0:T(8,128)(2,1)S(1)}, u32[]{:S(2)}, u32[]{:S(2)}) collective-permute-start(bf16[1024,128]{1,0:T(8,128)(2,1)S(1)} %get-tuple-element.131), channel_id=1, source_target_pairs={{0,1},{1,0},{2,3},{3,2},{4,5},{5,4},{6,7},{7,6},{8,9},{9,8},{10,11... | collective-permute-start | bytes 786440 | tf_op jit(solution)/shard_map/ppermute | solution.py:252
  (17 other events, 30.2 us)
Sparse Core Ops, SparseCore 0:
  10.1 73.3 all-gather.2

commit v8 on v7

v8 whole, which is shorter than its diff:
```python
import functools
import math

import jax
import jax.numpy as jnp
from jax import lax
from jax.experimental import pallas as pl
from jax.experimental.pallas import tpu as pltpu
from jax.sharding import Mesh
from jax.sharding import PartitionSpec as P

EPS = 1e-06
ADAM_EPS = 1e-08
BETA_ONE = 0.9
BETA_TWO = 0.95
DECAY = 0.1
bias_one = 1.0 - 0.9**10
bias_two = 1.0 - 0.95**10
RATE_TABLE = (0.02, 0.032, 0.05, 0.08, 0.125)
MINOR = 2
PLANES = 4
FEW = 2
LANES = 128
VMEM_LIMIT = 24 * 1024 * 1024
FORWARD_LIMIT = 48 * 1024 * 1024
KINDS = 3
HALVES = 2


def adamw_kernel(side_ref, rate_ref, weight_ref, moments_ref, mine_ref, theirs_ref, *refs):
    weight_out, first_out, second_out = refs[-3:]
    rate = jnp.float32(0.0)
    for slot, value in enumerate(RATE_TABLE):
        rate = jnp.where(rate_ref[0] == slot, jnp.float32(value), rate)
    gradient = mine_ref[...] + theirs_ref[...].astype(jnp.float32)
    weight_now = weight_ref[0, 0].astype(jnp.float32)
    first_now = moments_ref[0, 0].astype(jnp.float32)
    second_now = moments_ref[0, 1].astype(jnp.float32)
    first_sum = BETA_ONE * first_now + (1.0 - BETA_ONE) * gradient
    second_sum = BETA_TWO * second_now + (1.0 - BETA_TWO) * gradient * gradient
    update = first_sum / bias_one / (jnp.sqrt(second_sum / bias_two) + ADAM_EPS)
    weight_new = weight_now * (1.0 - rate * DECAY) - rate * update
    weight_out[0] = weight_new.astype(jnp.bfloat16)
    first_out[0] = first_sum.astype(jnp.bfloat16)
    second_out[0] = second_sum.astype(jnp.bfloat16)


def adamw(half, side, rate_index, weight, moments, mine, theirs, earlier):
    pieces, _, rows, width = weight.shape
    steps = pieces // HALVES
    first = half * steps
    flat = pl.BlockSpec((rows, width), lambda i, m, r: (i, 0))
    out = pl.BlockSpec((1, rows, width), lambda i, m, r: (0, first + i, 0))
    count = len(earlier)
    return pl.pallas_call(
        adamw_kernel,
        grid_spec=pltpu.PrefetchScalarGridSpec(
            num_scalar_prefetch=2,
            grid=(steps,),
            in_specs=[
                pl.BlockSpec((1, 1, rows, width), lambda i, m, r: (first + i, m[0], 0, 0)),
                pl.BlockSpec((1, KINDS - 1, rows, width), lambda i, m, r: (first + i, 0, 0, 0)),
                flat,
                flat,
            ]
            + [pl.BlockSpec(memory_space=pl.ANY)] * count,
            out_specs=[out, out, out],
        ),
        out_shape=[jax.ShapeDtypeStruct((1, pieces * rows, width), jnp.bfloat16)] * KINDS,
        input_output_aliases={6 + i: i for i in range(count)},
        compiler_params=pltpu.CompilerParams(vmem_limit_bytes=VMEM_LIMIT),
        cost_estimate=pl.CostEstimate(
            flops=20 * steps * rows * width,
            bytes_accessed=18 * steps * rows * width,
            transcendentals=steps * rows * width,
        ),
        name="adamw",
    )(side, rate_index, weight, moments, mine, theirs, *earlier)


def pack_kernel(residual_ref, upstream_ref, out_ref):
    out_ref[0, 0] = residual_ref[...]
    out_ref[0, 1] = upstream_ref[...]


def pack(residual, upstream, blocks):
    tokens, features = residual.shape
    block = features // blocks
    columns = pl.BlockSpec((tokens, block), lambda i: (0, i))
    return pl.pallas_call(
        pack_kernel,
        grid=(blocks,),
        in_specs=[columns, columns],
        out_specs=pl.BlockSpec((1, 2, tokens, block), lambda i: (i, 0, 0, 0)),
        out_shape=jax.ShapeDtypeStruct((blocks, 2, tokens, block), residual.dtype),
        compiler_params=pltpu.CompilerParams(vmem_limit_bytes=VMEM_LIMIT),
        name="pack",
    )(residual, upstream)


def forward_kernel(inv_scale, rows_ref, weight_ref, stream_ref, gain_ref, hidden_ref, sums_ref, both_ref):
    pieces, halves, rows, width = weight_ref.shape

    @pl.when(pl.program_id(0) == 0)
    def _():
        for piece in range(pieces):
            for half in range(halves):
                both_ref[piece * rows : (piece + 1) * rows, half * width : (half + 1) * width] = weight_ref[piece, half]

    linear = jnp.dot(rows_ref[...], both_ref[...], preferred_element_type=jnp.float32)
    count, block = linear.shape
    stream = stream_ref[...]
    resid = stream[:, 0].reshape(count, block).astype(jnp.float32)
    upstream = stream[:, 1].reshape(count, block).astype(jnp.float32)
    hidden = resid + linear * inv_scale
    hidden_ref[...] = hidden
    scaled = upstream * gain_ref[...]
    squares = jnp.sum(hidden * hidden, axis=1, keepdims=True)
    inner = jnp.sum(scaled * hidden, axis=1, keepdims=True)
    lane = lax.broadcasted_iota(jnp.int32, (count, LANES), 1)
    packed = jnp.where(lane == 0, squares, jnp.where(lane == 1, inner, 0.0)).T[:2]
    for target in range(sums_ref.shape[0]):
        sums_ref[target] = packed


def forward(rows, weight, gain, stream, inv_scale):
    tokens, depth = rows.shape
    blocks, _, per, block = stream.shape
    step = 2 * per
    return pl.pallas_call(
        functools.partial(forward_kernel, inv_scale),
        grid=(tokens // step,),
        in_specs=[
            pl.BlockSpec((step, depth), lambda i: (i, 0)),
            pl.BlockSpec(weight.shape, lambda i: (0, 0, 0, 0)),
            pl.BlockSpec((2, 2, per, block), lambda i: (i, 0, 0, 0)),
            pl.BlockSpec(gain.shape, lambda i: (0, 0)),
        ],
        out_specs=[
            pl.BlockSpec((step, block), lambda i: (i, 0)),
            pl.BlockSpec((blocks, 2, step), lambda i: (0, 0, i)),
        ],
        scratch_shapes=[pltpu.VMEM((depth, block), jnp.bfloat16)],
        out_shape=[
            jax.ShapeDtypeStruct((tokens, block), jnp.float32),
            jax.ShapeDtypeStruct((blocks, 2, tokens), jnp.float32),
        ],
        compiler_params=pltpu.CompilerParams(vmem_limit_bytes=FORWARD_LIMIT),
        cost_estimate=pl.CostEstimate(
            flops=2 * tokens * depth * block, bytes_accessed=7 * 1024 * 1024, transcendentals=0
        ),
        name="forward",
    )(rows, weight, stream, gain)


def multiply(inv_scale, side_ref, delta, rows_ref, mine_ref, theirs_ref):
    width = mine_ref.shape[1]
    grad = jnp.dot(delta, rows_ref[...], preferred_element_type=jnp.float32) * inv_scale
    low = grad[:width].T
    high = grad[width:].T
    first = side_ref[0] == 0
    mine_ref[...] = jnp.where(first, low, high)
    theirs_ref[...] = jnp.where(first, high, low).astype(jnp.bfloat16)


def backward_first_kernel(inv_scale, features, side_ref, rows_ref, hidden_ref, gain_ref, sums_ref, stream_ref, mine_ref, theirs_ref, delta_ref):
    width = mine_ref.shape[1]
    blocks, _, per, _ = stream_ref.shape

    @pl.when(pl.program_id(0) == 0)
    def _():
        sums = jnp.sum(sums_ref[...], axis=0)
        inverse = lax.rsqrt(sums[0:1] / features + EPS)
        factor = sums[1:2] / features * (inverse * inverse * inverse)
        for block in range(blocks):
            place = slice(block * per, (block + 1) * per)
            inverse_here = jnp.broadcast_to(inverse[:, place], (LANES, per)).T
            factor_here = jnp.broadcast_to(factor[:, place], (LANES, per)).T
            for half in range(2):
                cols = slice(half * width, (half + 1) * width)
                scaled = stream_ref[block, 1, :, cols].astype(jnp.float32) * gain_ref[:, cols]
                delta = scaled * inverse_here - hidden_ref[place, cols] * factor_here
                delta_ref[cols, place] = delta.T.astype(jnp.bfloat16)

    multiply(inv_scale, side_ref, delta_ref[...], rows_ref, mine_ref, theirs_ref)


def backward_next_kernel(inv_scale, side_ref, rows_ref, delta_ref, mine_ref, theirs_ref):
    multiply(inv_scale, side_ref, delta_ref[...], rows_ref, mine_ref, theirs_ref)


def backward(side, rows, hidden, gain, sums, stream, inv_scale, features):
    tokens, depth = rows.shape
    block = hidden.shape[1]
    width = block // 2
    step = 256
    steps = depth // step // HALVES
    params = pltpu.CompilerParams(vmem_limit_bytes=VMEM_LIMIT)
    cost = pl.CostEstimate(
        flops=2 * tokens * depth * block // HALVES, bytes_accessed=5 * 1024 * 1024, transcendentals=0
    )
    outs = [
        jax.ShapeDtypeStruct((depth // HALVES, width), jnp.float32),
        jax.ShapeDtypeStruct((depth // HALVES, width), jnp.bfloat16),
    ]
    whole = lambda array: pl.BlockSpec(array.shape, lambda i, *_: (0,) * array.ndim)
    delta = jax.ShapeDtypeStruct((block, tokens), jnp.bfloat16)
    out = pl.BlockSpec((step, width), lambda i, *_: (i, 0))
    *first, delta = pl.pallas_call(
        functools.partial(backward_first_kernel, inv_scale, features),
        grid_spec=pltpu.PrefetchScalarGridSpec(
            num_scalar_prefetch=1,
            grid=(steps,),
            in_specs=[pl.BlockSpec((tokens, step), lambda i, *_: (0, i))]
            + [whole(array) for array in (hidden, gain, sums, stream)],
            out_specs=[out, out, whole(delta)],
        ),
        out_shape=outs + [delta],
        compiler_params=params,
        cost_estimate=cost,
        name="backward_first",
    )(side, rows, hidden, gain, sums, stream)
    result = [first]
    for half in range(1, HALVES):
        result.append(
            pl.pallas_call(
                functools.partial(backward_next_kernel, inv_scale),
                grid_spec=pltpu.PrefetchScalarGridSpec(
                    num_scalar_prefetch=1,
                    grid=(steps,),
                    in_specs=[
                        pl.BlockSpec((tokens, step), lambda i, *_, half=half: (0, half * steps + i)),
                        whole(delta),
                    ],
                    out_specs=[out, out],
                ),
                out_shape=outs,
                compiler_params=params,
                cost_estimate=cost,
                name="backward_next",
            )(side, rows, delta)
        )
    return result


def swap_minor(array):
    return lax.ppermute(array, "minor", [(0, 1), (1, 0)])


def sums_of_all(sums):
    return lax.all_to_all(sums, "major", split_axis=0, concat_axis=0, tiled=True)


def spread_columns(array):
    return lax.all_to_all(array, "column", split_axis=0, concat_axis=0, tiled=True)


def plan_moves(sources):
    planes = lax.axis_size("plane")
    columns = lax.axis_size("column")
    me = lax.axis_index("plane")
    member = jnp.arange(planes * columns, dtype=jnp.int32)
    here, there = member // columns, sources // columns
    offset = lax.rem(here - there + planes, planes)
    earlier = member[None, :] < member[:, None]
    same = (here[None, :] == here[:, None]) & (there[None, :] == there[:, None])
    rank = jnp.sum((earlier & same).astype(jnp.int32), axis=1)
    most = jnp.max(jnp.where(offset > 0, rank, 0))
    targets = jnp.arange(1, planes, dtype=jnp.int32)[:, None, None]
    slots = jnp.arange(columns, dtype=jnp.int32)[None, :, None]
    leaving = (there == me) & (rank == slots)
    column = lax.rem(sources, columns)
    by_shift = jnp.sum(jnp.where(leaving & (offset == targets), column, 0), axis=2)
    mine = lambda values: lax.dynamic_slice_in_dim(values, me * columns, columns)
    return dict(
        column=mine(column),
        offset=mine(offset),
        rank=mine(rank),
        by_shift=by_shift,
        most=most,
    )


def pick(pieces, slots):
    kinds = pieces.shape[0] // lax.axis_size("column")
    return pieces[(slots[:, None] * kinds + jnp.arange(kinds, dtype=jnp.int32)).reshape(-1)]


def send_planes(pieces, slots):
    planes = lax.axis_size("plane")
    return [
        lax.ppermute(pick(pieces, slots[shift - 1]), "plane", [(i, (i + shift) % planes) for i in range(planes)])
        for shift in range(1, planes)
    ]


def choose_kernel(kinds, copies, which_ref, start_ref, *refs):
    refs, out_ref, sems = refs[:-2], refs[-2], refs[-1]
    columns = out_ref.shape[0]
    slot = lambda place, copy: out_ref.at[place, copy] if copies else out_ref.at[place]
    for place in range(columns):
        for number, ref in enumerate(refs):
            @pl.when(which_ref[place] == number)
            def _():
                for copy in range(max(copies, 1)):
                    source = ref.at[pl.ds(start_ref[place], kinds)]
                    pltpu.make_async_copy(source, slot(place, copy), sems.at[place, copy]).start()

    for place in range(columns):
        for copy in range(max(copies, 1)):
            pltpu.make_async_copy(refs[0].at[pl.ds(0, kinds)], slot(place, copy), sems.at[place, copy]).wait()


def choose(pieces, received, which, start, kinds, copies):
    columns = which.shape[0]
    shape = ((columns, copies) if copies else (columns,)) + (kinds,) + pieces.shape[1:]
    anywhere = pl.BlockSpec(memory_space=pl.ANY)
    return pl.pallas_call(
        functools.partial(choose_kernel, kinds, copies),
        grid_spec=pltpu.PrefetchScalarGridSpec(
            num_scalar_prefetch=2,
            grid=(1,),
            in_specs=[anywhere] * (1 + len(received)),
            out_specs=pl.BlockSpec(shape, lambda i, *_: (0,) * len(shape)),
            scratch_shapes=[pltpu.SemaphoreType.DMA((columns, max(copies, 1)))],
        ),
        out_shape=jax.ShapeDtypeStruct(shape, pieces.dtype),
        compiler_params=pltpu.CompilerParams(vmem_limit_bytes=VMEM_LIMIT),
        name="choose",
    )(which, start, pieces, *received)


def across(pieces, received, plan, copies):
    kinds = pieces.shape[0] // lax.axis_size("column")

    def take(pieces, received):
        last = received[0].shape[0] // kinds - 1
        place = jnp.where(plan["offset"] == 0, plan["column"], jnp.minimum(plan["rank"], last))
        return choose(pieces, received, plan["offset"], place * kinds, kinds, copies)

    def all_slots(pieces, received):
        return take(pieces, send_planes(pieces, plan["by_shift"]))

    return lax.cond(plan["most"] >= FEW, all_slots, take, pieces, received)


def local(
    attention_out,
    residual,
    upstream,
    norm_gain,
    weight,
    first_moment,
    second_moment,
    sources,
    rate_index,
):
    columns = lax.axis_size("column")
    minor = lax.axis_index("minor")
    depth, width = weight.shape[1:]
    rows = depth // columns
    features = residual.shape[2]

    gathered = lax.all_gather(attention_out[0], "major", axis=0, tiled=True)
    plan = plan_moves(sources)
    few = plan["by_shift"][:, :FEW]
    gain_other = swap_minor(norm_gain[0])
    gain = jnp.where(
        minor == 0,
        jnp.concatenate((norm_gain[0], gain_other)),
        jnp.concatenate((gain_other, norm_gain[0])),
    ).astype(jnp.float32)[None, :]
    weights = spread_columns(weight[0].reshape(columns, rows, width))
    moments = jnp.stack(
        [array[0].reshape(columns, rows, width) for array in (first_moment, second_moment)], axis=1
    )
    weights, moments, gain = lax.optimization_barrier((weights, moments, gain))
    moments = spread_columns(moments).reshape(columns * (KINDS - 1), rows, width)
    weights_in = send_planes(weights, few)
    weights_in, moments = lax.optimization_barrier((weights_in, moments))
    weights = across(weights, weights_in, plan, MINOR)
    weights, moments = lax.optimization_barrier((weights, moments))
    weights = lax.all_to_all(
        weights.reshape(columns * MINOR, rows, width), ("column", "minor"), split_axis=0, concat_axis=0, tiled=True
    ).reshape(columns, MINOR, rows, width)
    moments_in = send_planes(moments, few)
    stream = pack(residual[0], upstream[0], lax.axis_size("major"))
    weights, stream = lax.optimization_barrier((weights, stream))
    stream = lax.all_to_all(stream, "major", split_axis=0, concat_axis=0, tiled=True)

    inv_scale = 1.0 / math.sqrt(depth)
    side = minor.astype(jnp.int32)[None]
    hidden, sums = forward(gathered, weights, gain, stream, inv_scale)
    moments_in, sums = lax.optimization_barrier((moments_in, sums))
    sums = sums_of_all(sums)
    moments = across(moments, moments_in, plan, 0)
    moments, sums = lax.optimization_barrier((moments, sums))
    moments = spread_columns(moments)
    halves = backward(side, gathered, hidden, gain, sums, stream, inv_scale, features)
    result = []
    for half, (mine, theirs) in enumerate(halves):
        result = adamw(half, side, rate_index, weights, moments, mine, swap_minor(theirs), result)
    return tuple(result)


def solution(mesh):
    members, shards = mesh.devices.shape
    split = Mesh(
        mesh.devices.reshape(PLANES, members // PLANES, shards // MINOR, MINOR),
        ("plane", "column", "major", "minor"),
    )
    member, fsdp = ("plane", "column"), ("major", "minor")
    in_specs = (
        P(member, fsdp, None),
        P(member, fsdp, None),
        P(member, fsdp, None),
        P(member, fsdp),
        P(member, None, fsdp),
        P(member, None, fsdp),
        P(member, None, fsdp),
        P(),
        P(member),
    )
    out_specs = (P(member, None, fsdp),) * 3
    return jax.shard_map(local, mesh=split, in_specs=in_specs, out_specs=out_specs, check_vma=False)
```

time: 236 us -> 172 us (0.73)
  Pallas kernels: 65.4 us -> 22.9 us
  starting transfers between devices: 86.8 us -> 71.9 us
  local copies, waits for them, and re-layouts: 25 us -> 11.4 us
  waiting for transfers between devices: 34.2 us -> 43.1 us
    pallas_call x2, Pallas kernels: 51.2 us -> 6.87 us  [choose(): pl.pallas_call(functools.partial(choose_kernel, kinds, copies), grid_spec...]
    ppermute x10 -> x6, starting transfers between devices: 45.9 us -> 27.2 us  [send_planes(): lax.ppermute(pick(pieces, slots[shift - 1]), 'plane', [(i, (i + shift) %...]
    all_to_all x2 -> x3, waiting for transfers between devices: 20.3 us -> 4.95 us  [spread_columns(): lax.all_to_all(array, 'column', split_axis=0, concat_axis=0, tiled=True)]
    all_to_all x1, waiting for transfers between devices: 0.01 us -> 12.4 us  [local(): lax.all_to_all(weights.reshape(columns * MINOR, rows, width), ('column',...]
    all_to_all x1, waiting for transfers between devices: 0.01 us -> 12.2 us  [local(): lax.all_to_all(stream, 'major', split_axis=0, concat_axis=0, tiled=True)]
    unnamed x44 -> x14, local copies, waits for them, and re-layouts: 12.7 us -> 5.46 us
    gather x4 -> x6, local copies, waits for them, and re-layouts: 10.9 us -> 4.88 us  [pick(): pieces[(slots[:, None] * kinds + jnp.arange(kinds, dtype=jnp.int32)).resh...]
    ppermute x10 -> x6, waiting for transfers between devices: 8.46 us -> 5.07 us  [send_planes(): lax.ppermute(pick(pieces, slots[shift - 1]), 'plane', [(i, (i + shift) %...]
  transfers between devices with their start and end apart: 19 -> 16, of which waited for: 4 -> 7; matrix products, arithmetic and copies ran while one was open for 8% -> 7% of each run, Pallas kernels for 27% -> 12%
where the time goes in v8:
time: 172 us; the launch traced here: 171 us
  starting transfers between devices  71.9 us (42%)
  waiting for transfers between devices  43.1 us (25%)
  Pallas kernels  22.9 us (13%)
  between operations  15.6 us (9%)
  local copies, waits for them, and re-layouts  11.4 us (7%)
  other arithmetic  6.33 us (4%)
    ppermute x6, starting transfers between devices, send_planes(): lax.ppermute(pick(pieces, slots[shift - 1]), 'plane', [(i, (i + shift) %...  27.2 us
    all_to_all x3, starting transfers between devices, spread_columns(): lax.all_to_all(array, 'column', split_axis=0, concat_axis=0, tiled=True)  17 us
    all_to_all x1, waiting for transfers between devices, local(): lax.all_to_all(weights.reshape(columns * MINOR, rows, width), ('column',...  12.4 us
    all_to_all x1, waiting for transfers between devices, local(): lax.all_to_all(stream, 'major', split_axis=0, concat_axis=0, tiled=True)  12.2 us
    ppermute x3, starting transfers between devices, swap_minor(): return lax.ppermute(array, 'minor', [(0, 1), (1, 0)])  10.1 us
    pallas_call x2, Pallas kernels, choose(): pl.pallas_call(functools.partial(choose_kernel, kinds, copies), grid_spec...  6.87 us
    all_to_all x1, starting transfers between devices, local(): lax.all_to_all(stream, 'major', split_axis=0, concat_axis=0, tiled=True)  6.82 us
    all_to_all x1, starting transfers between devices, local(): lax.all_to_all(weights.reshape(columns * MINOR, rows, width), ('column',...  6.42 us
  transfers between devices with their start and end apart: 16, of which 7 were waited for; matrix products, arithmetic and copies ran while one was open for 7% of the time, Pallas kernels for 12%

profile of v8, /device:TPU:1, one launch (start us, length us, event | category | flops | bytes accessed | tf_op | source)
XLA Modules:
  0.0 171.3 jit_solution(5881971272895445374)
XLA Ops:
  7.9 4.8 %collective-permute-start.6 = (bf16[128]{0:T(256)(128)(2,1)}, bf16[128]{0:T(256)(128)(2,1)S(1)}, u32[]{:S(2)}, u32[]{:S(2)}) collective-permute-start(bf16[128]{0:T(256)(128)(2,1)} %bitcast.81), channel_id=1, source_target_pairs={{0,1},{1,0},{2,3},{3,2},{4,5},{5,4},{6,7},{7,6},{8,9},{9,8},{10,11... | collective-permute-start | bytes 776 | tf_op jit(solution)/shard_map/ppermute | solution.py:247
  12.7 7.4 %all-to-all-start = ((bf16[8,256,128]{2,1,0:T(8,128)(2,1)}), bf16[8,256,128]{2,1,0:T(8,128)(2,1)S(1)}, u32[]{:S(2)}, u32[]{:S(2)}) async-start(bf16[8,256,128]{2,1,0:T(8,128)(2,1)} %bitcast.78), calls=%async_computation | async-start | bytes 1048576 | tf_op jit(solution)/shard_map/all_to_all | solution.py:255
  24.7 4.9 %all-to-all-done = bf16[8,256,128]{2,1,0:T(8,128)(2,1)S(1)} async-done(((bf16[8,256,128]{2,1,0:T(8,128)(2,1)}), bf16[8,256,128]{2,1,0:T(8,128)(2,1)S(1)}, u32[]{:S(2)}, u32[]{:S(2)}) %all-to-all-start) | async-done | bytes 524320 | tf_op jit(solution)/shard_map/all_to_all | solution.py:255
  29.6 4.3 %all-to-all-start.1 = ((bf16[8,2,256,128]{3,2,1,0:T(8,128)(2,1)}), bf16[8,2,256,128]{3,2,1,0:T(8,128)(2,1)S(1)}, u32[]{:S(2)}, u32[]{:S(2)}) async-start(bf16[8,2,256,128]{3,2,1,0:T(8,128)(2,1)} %pad_maximum_fusion), calls=%async_computation.1 | async-start | bytes 2097152 | tf_op jit(solution)/shard_map/all_to_all | solution.py:255
  34.8 7.6 %collective-permute-start.8 = (bf16[2,256,128]{2,1,0:T(8,128)(2,1)S(1)}, bf16[2,256,128]{2,1,0:T(8,128)(2,1)S(1)}, u32[]{:S(2)}, u32[]{:S(2)}) collective-permute-start(bf16[2,256,128]{2,1,0:T(8,128)(2,1)S(1)} %gather_fusion.7), channel_id=1, source_target_pairs={{0,256},{128,384},{256,0},{384,128},{1,257},{129,385},{257,1},{385... | collective-permute-start | bytes 393224 | tf_op jit(solution)/shard_map/ppermute | solution.py:292
  45.5 4.2 %collective-permute-start.7 = (bf16[2,256,128]{2,1,0:T(8,128)(2,1)S(1)}, bf16[2,256,128]{2,1,0:T(8,128)(2,1)S(1)}, u32[]{:S(2)}, u32[]{:S(2)}) collective-permute-start(bf16[2,256,128]{2,1,0:T(8,128)(2,1)S(1)} %gather_fusion.6), channel_id=1, source_target_pairs={{0,128},{128,256},{256,384},{384,0},{1,129},{129,257},{257,385},{3... | collective-permute-start | bytes 393224 | tf_op jit(solution)/shard_map/ppermute | solution.py:292
  51.2 5.1 %collective-permute-done.9 = bf16[2,256,128]{2,1,0:T(8,128)(2,1)S(1)} collective-permute-done((bf16[2,256,128]{2,1,0:T(8,128)(2,1)S(1)}, bf16[2,256,128]{2,1,0:T(8,128)(2,1)S(1)}, u32[]{:S(2)}, u32[]{:S(2)}) %collective-permute-start.9) | collective-permute-done | bytes 131104 | tf_op jit(solution)/shard_map/ppermute | solution.py:292
  56.3 4.1 %conditional.2 = (bf16[8,2,1,256,128]{4,3,2,1,0:T(8,128)(2,1)}) conditional(s32[]{:T(128)} %convert_element_type.18, (s32[8]{0:T(128)S(1)}, s32[8]{0:T(128)S(1)}, s32[8]{0:T(128)}, bf16[8,256,128]{2,1,0:T(8,128)(2,1)S(1)}, bf16[2,256,128]{2,1,0:T(8,128)(2,1)S(1)}, /*index=5*/bf16[2,256,128]{2,1,0:T(8,128)(2,1)S(1)}, ...), branch_computations={%region_3.4_spmd, %region_4.5_spmd} | conditional | flops 3168 | bytes 11547292 | solution.py:344
  57.1 3.3 %choose.4 = bf16[8,2,1,256,128]{4,3,2,1,0:T(8,128)(2,1)} custom-call(s32[8]{0:T(128)S(1)} %get-tuple-element.48.which_ref, s32[8]{0:T(128)S(1)} %compare_select_fusion.start_ref, bf16[8,256,128]{2,1,0:T(8,128)(2,1)S(1)} %get-tuple-element.57.refs_0_, bf16[2,256,128]{2,1,0:T(8,128)(2,1)S(1)} %get-tuple-element.58.refs_1_, ...), custom_call_target="tpu_custom_call" | custom-call | tf_op jit(solution)/shard_map/cond/branch_0_fun/choose/pallas_call | solution.py:318
  60.4 6.4 %all-to-all-start.2 = ((bf16[16,256,128]{2,1,0:T(8,128)(2,1)}), bf16[16,256,128]{2,1,0:T(8,128)(2,1)S(1)}, u32[]{:S(2)}, u32[]{:S(2)}) async-start(bf16[16,256,128]{2,1,0:T(8,128)(2,1)} %bitcast.77), calls=%async_computation.2 | async-start | bytes 2097152 | tf_op jit(solution)/shard_map/all_to_all | solution.py:383
  66.8 2.9 %pack.1 = bf16[8,2,128,256]{3,2,1,0:T(8,128)(2,1)} custom-call(bf16[128,2048]{1,0:T(8,128)(2,1)S(1)} %bitcast.70, bf16[128,2048]{1,0:T(8,128)(2,1)S(1)} %bitcast.71), custom_call_target="tpu_custom_call" | custom-call | tf_op jit(solution)/shard_map/pack/pallas_call | solution.py:90
  69.7 12.4 %all-to-all-done.2 = bf16[16,256,128]{2,1,0:T(8,128)(2,1)S(1)} async-done(((bf16[16,256,128]{2,1,0:T(8,128)(2,1)}), bf16[16,256,128]{2,1,0:T(8,128)(2,1)S(1)}, u32[]{:S(2)}, u32[]{:S(2)}) %all-to-all-start.2) | async-done | bytes 1048608 | tf_op jit(solution)/shard_map/all_to_all | solution.py:383
  82.1 6.8 %all-to-all-start.3 = ((bf16[8,2,128,256]{3,2,1,0:T(8,128)(2,1)}), bf16[8,2,128,256]{3,2,1,0:T(8,128)(2,1)S(1)}, u32[]{:S(2)}, u32[]{:S(2)}) async-start(bf16[8,2,128,256]{3,2,1,0:T(8,128)(2,1)} %pack.1), calls=%async_computation.3 | async-start | bytes 2097152 | tf_op jit(solution)/shard_map/all_to_all | solution.py:389
  90.0 7.3 %collective-permute-start.11 = (bf16[4,256,128]{2,1,0:T(8,128)(2,1)S(1)}, bf16[4,256,128]{2,1,0:T(8,128)(2,1)}, u32[]{:S(2)}, u32[]{:S(2)}) collective-permute-start(bf16[4,256,128]{2,1,0:T(8,128)(2,1)S(1)} %gather_fusion.10), channel_id=1, source_target_pairs={{0,256},{128,384},{256,0},{384,128},{1,257},{129,385},{257,1},{385... | collective-permute-start | bytes 786440 | tf_op jit(solution)/shard_map/ppermute | solution.py:292
  101.7 4.3 %collective-permute-start.10 = (bf16[4,256,128]{2,1,0:T(8,128)(2,1)}, bf16[4,256,128]{2,1,0:T(8,128)(2,1)}, u32[]{:S(2)}, u32[]{:S(2)}) collective-permute-start(bf16[4,256,128]{2,1,0:T(8,128)(2,1)} %gather_fusion.9), channel_id=1, source_target_pairs={{0,128},{128,256},{256,384},{384,0},{1,129},{129,257},{257,385},{3... | collective-permute-start | bytes 786440 | tf_op jit(solution)/shard_map/ppermute | solution.py:292
  106.0 12.2 %all-to-all-done.3.stream_ref = bf16[8,2,128,256]{3,2,1,0:T(8,128)(2,1)S(1)} async-done(((bf16[8,2,128,256]{3,2,1,0:T(8,128)(2,1)}), bf16[8,2,128,256]{3,2,1,0:T(8,128)(2,1)S(1)}, u32[]{:S(2)}, u32[]{:S(2)}) %all-to-all-start.3) | async-done | bytes 1048608 | tf_op jit(solution)/shard_map/all_to_all | solution.py:389
  118.2 5.1 %forward.1 = (f32[1024,256]{1,0:T(8,128)S(1)}, f32[8,2,1024]{2,1,0:T(2,128)}) custom-call(bf16[1024,2048]{1,0:T(8,128)(2,1)} %bitcast.64, bf16[8,2,256,128]{3,2,1,0:T(8,128)(2,1)S(1)} %bitcast.67, bf16[8,2,128,256]{3,2,1,0:T(8,128)(2,1)S(1)} %all-to-all-done.3.stream_ref, f32[1,256]{1,0:T(1,128)S(1)} %fusion.10.gain_ref), custom_call_target="tpu_custom_call" | custom-call | flops 1073741824 | bytes 7340032 | tf_op jit(solution)/shard_map/forward/pallas_call | solution.py:130
  124.3 4.2 %all-to-all-start.4 = ((f32[8,2,1024]{2,1,0:T(2,128)}), f32[8,2,1024]{2,1,0:T(2,128)S(1)}, u32[]{:S(2)}, u32[]{:S(2)}) async-start(f32[8,2,1024]{2,1,0:T(2,128)} %get-tuple-element.123), calls=%async_computation.4 | async-start | bytes 131072 | tf_op jit(solution)/shard_map/all_to_all | solution.py:251
  128.5 4.2 %conditional.3 = (bf16[8,2,256,128]{3,2,1,0:T(8,128)(2,1)}) conditional(s32[]{:T(128)} %convert_element_type.18, (s32[8]{0:T(128)S(1)}, s32[8]{0:T(128)S(1)}, s32[8]{0:T(128)}, bf16[16,256,128]{2,1,0:T(8,128)(2,1)S(1)}, bf16[4,256,128]{2,1,0:T(8,128)(2,1)}, /*index=5*/bf16[4,256,128]{2,1,0:T(8,128)(2,1)}, bf16[4,256,128]{2,1,0:T(8,128)(2,1)}) %tuple.54, ...), branch_computations={%region_5.6_spmd, %region_6.7_spmd} | conditional | flops 3320 | bytes 23082876 | solution.py:344
  129.1 3.5 %choose.6 = bf16[8,2,256,128]{3,2,1,0:T(8,128)(2,1)} custom-call(s32[8]{0:T(128)S(1)} %get-tuple-element.66.which_ref, s32[8]{0:T(128)S(1)} %fusion.start_ref, bf16[16,256,128]{2,1,0:T(8,128)(2,1)S(1)} %get-tuple-element.69.refs_0_, bf16[4,256,128]{2,1,0:T(8,128)(2,1)} %get-tuple-element.70.refs_1_, bf16[4,256,128]{2,1,0:T(8,128)(2,1)} %get-tuple-element.71.refs_2_, ...), custom_call_target="tpu_custom_call" | custom-call | tf_op jit(solution)/shard_map/cond/branch_0_fun/choose/pallas_call | solution.py:318
  132.7 3.1 %all-to-all-done.4.sums_ref = f32[8,2,1024]{2,1,0:T(2,128)S(1)} async-done(((f32[8,2,1024]{2,1,0:T(2,128)}), f32[8,2,1024]{2,1,0:T(2,128)S(1)}, u32[]{:S(2)}, u32[]{:S(2)}) %all-to-all-start.4) | async-done | bytes 65568 | tf_op jit(solution)/shard_map/all_to_all | solution.py:251
  135.8 5.3 %all-to-all-start.5 = ((bf16[8,2,256,128]{3,2,1,0:T(8,128)(2,1)}), bf16[8,2,256,128]{3,2,1,0:T(8,128)(2,1)S(1)}, u32[]{:S(2)}, u32[]{:S(2)}) async-start(bf16[8,2,256,128]{3,2,1,0:T(8,128)(2,1)} %get-tuple-element.157), calls=%async_computation.5 | async-start | bytes 2097152 | tf_op jit(solution)/shard_map/all_to_all | solution.py:255
  151.1 3.4 %collective-permute-start.13 = (bf16[1024,128]{1,0:T(8,128)(2,1)S(1)}, bf16[1024,128]{1,0:T(8,128)(2,1)S(1)}, u32[]{:S(2)}, u32[]{:S(2)}) collective-permute-start(bf16[1024,128]{1,0:T(8,128)(2,1)S(1)} %get-tuple-element.129), channel_id=1, source_target_pairs={{0,1},{1,0},{2,3},{3,2},{4,5},{5,4},{6,7},{7,6},{8,9},{9,8},{10,11... | collective-permute-start | bytes 786440 | tf_op jit(solution)/shard_map/ppermute | solution.py:247
  159.9 2.8 %collective-permute-done.13.theirs_ref = bf16[1024,128]{1,0:T(8,128)(2,1)S(1)} collective-permute-done((bf16[1024,128]{1,0:T(8,128)(2,1)S(1)}, bf16[1024,128]{1,0:T(8,128)(2,1)S(1)}, u32[]{:S(2)}, u32[]{:S(2)}) %collective-permute-start.13) | collective-permute-done | bytes 262176 | tf_op jit(solution)/shard_map/ppermute | solution.py:247
  (70 shorter events, 34.2 us)
Async XLA Ops:
  7.2 111.0 %all-gather.3.cloned.1.call-start = ((), (), s32[]{:S(2)}) async-start(), calls=%async_computation.6 | async-start | bytes 4718592 | tf_op jit(solution)/shard_map/all_gather | solution.py:364
  7.9 16.0 %collective-permute-start.6 = (bf16[128]{0:T(256)(128)(2,1)}, bf16[128]{0:T(256)(128)(2,1)S(1)}, u32[]{:S(2)}, u32[]{:S(2)}) collective-permute-start(bf16[128]{0:T(256)(128)(2,1)} %bitcast.81), channel_id=1, source_target_pairs={{0,1},{1,0},{2,3},{3,2},{4,5},{5,4},{6,7},{7,6},{8,9},{9,8},{10,11... | collective-permute-start | bytes 776 | tf_op jit(solution)/shard_map/ppermute | solution.py:247
  12.7 16.9 %all-to-all-start = ((bf16[8,256,128]{2,1,0:T(8,128)(2,1)}), bf16[8,256,128]{2,1,0:T(8,128)(2,1)S(1)}, u32[]{:S(2)}, u32[]{:S(2)}) async-start(bf16[8,256,128]{2,1,0:T(8,128)(2,1)} %bitcast.78), calls=%async_computation | async-start | bytes 1048576 | tf_op jit(solution)/shard_map/all_to_all | solution.py:255
  29.6 26.7 %all-to-all-start.1 = ((bf16[8,2,256,128]{3,2,1,0:T(8,128)(2,1)}), bf16[8,2,256,128]{3,2,1,0:T(8,128)(2,1)S(1)}, u32[]{:S(2)}, u32[]{:S(2)}) async-start(bf16[8,2,256,128]{3,2,1,0:T(8,128)(2,1)} %pad_maximum_fusion), calls=%async_computation.1 | async-start | bytes 2097152 | tf_op jit(solution)/shard_map/all_to_all | solution.py:255
  34.8 16.4 %collective-permute-start.8 = (bf16[2,256,128]{2,1,0:T(8,128)(2,1)S(1)}, bf16[2,256,128]{2,1,0:T(8,128)(2,1)S(1)}, u32[]{:S(2)}, u32[]{:S(2)}) collective-permute-start(bf16[2,256,128]{2,1,0:T(8,128)(2,1)S(1)} %gather_fusion.7), channel_id=1, source_target_pairs={{0,256},{128,384},{256,0},{384,128},{1,257},{129,385},{257,1},{385... | collective-permute-start | bytes 393224 | tf_op jit(solution)/shard_map/ppermute | solution.py:292
  43.0 13.3 %collective-permute-start.9 = (bf16[2,256,128]{2,1,0:T(8,128)(2,1)S(1)}, bf16[2,256,128]{2,1,0:T(8,128)(2,1)S(1)}, u32[]{:S(2)}, u32[]{:S(2)}) collective-permute-start(bf16[2,256,128]{2,1,0:T(8,128)(2,1)S(1)} %gather_fusion.8), channel_id=1, source_target_pairs={{0,384},{128,0},{256,128},{384,256},{1,385},{129,1},{257,129},{385... | collective-permute-start | bytes 393224 | tf_op jit(solution)/shard_map/ppermute | solution.py:292
  45.5 10.7 %collective-permute-start.7 = (bf16[2,256,128]{2,1,0:T(8,128)(2,1)S(1)}, bf16[2,256,128]{2,1,0:T(8,128)(2,1)S(1)}, u32[]{:S(2)}, u32[]{:S(2)}) collective-permute-start(bf16[2,256,128]{2,1,0:T(8,128)(2,1)S(1)} %gather_fusion.6), channel_id=1, source_target_pairs={{0,128},{128,256},{256,384},{384,0},{1,129},{129,257},{257,385},{3... | collective-permute-start | bytes 393224 | tf_op jit(solution)/shard_map/ppermute | solution.py:292
  56.3 10.5 %copy-start.3 = (bf16[1,128,2048]{2,1,0:T(8,128)(2,1)S(1)}, bf16[1,128,2048]{2,1,0:T(8,128)(2,1)}, u32[]{:S(2)}) copy-start(bf16[1,128,2048]{2,1,0:T(8,128)(2,1)} %param.14) | copy-start | bytes 1572868
  56.3 10.5 %copy-start.4 = (bf16[1,128,2048]{2,1,0:T(8,128)(2,1)S(1)}, bf16[1,128,2048]{2,1,0:T(8,128)(2,1)}, u32[]{:S(2)}) copy-start(bf16[1,128,2048]{2,1,0:T(8,128)(2,1)} %param.15) | copy-start | bytes 1572868
  60.4 21.7 %all-to-all-start.2 = ((bf16[16,256,128]{2,1,0:T(8,128)(2,1)}), bf16[16,256,128]{2,1,0:T(8,128)(2,1)S(1)}, u32[]{:S(2)}, u32[]{:S(2)}) async-start(bf16[16,256,128]{2,1,0:T(8,128)(2,1)} %bitcast.77), calls=%async_computation.2 | async-start | bytes 2097152 | tf_op jit(solution)/shard_map/all_to_all | solution.py:383
  82.1 36.1 %all-to-all-start.3 = ((bf16[8,2,128,256]{3,2,1,0:T(8,128)(2,1)}), bf16[8,2,128,256]{3,2,1,0:T(8,128)(2,1)S(1)}, u32[]{:S(2)}, u32[]{:S(2)}) async-start(bf16[8,2,128,256]{3,2,1,0:T(8,128)(2,1)} %pack.1), calls=%async_computation.3 | async-start | bytes 2097152 | tf_op jit(solution)/shard_map/all_to_all | solution.py:389
  90.0 34.3 %collective-permute-start.11 = (bf16[4,256,128]{2,1,0:T(8,128)(2,1)S(1)}, bf16[4,256,128]{2,1,0:T(8,128)(2,1)}, u32[]{:S(2)}, u32[]{:S(2)}) collective-permute-start(bf16[4,256,128]{2,1,0:T(8,128)(2,1)S(1)} %gather_fusion.10), channel_id=1, source_target_pairs={{0,256},{128,384},{256,0},{384,128},{1,257},{129,385},{257,1},{385... | collective-permute-start | bytes 786440 | tf_op jit(solution)/shard_map/ppermute | solution.py:292
  98.5 25.7 %collective-permute-start.12 = (bf16[4,256,128]{2,1,0:T(8,128)(2,1)}, bf16[4,256,128]{2,1,0:T(8,128)(2,1)}, u32[]{:S(2)}, u32[]{:S(2)}) collective-permute-start(bf16[4,256,128]{2,1,0:T(8,128)(2,1)} %gather_fusion.11), channel_id=1, source_target_pairs={{0,384},{128,0},{256,128},{384,256},{1,385},{129,1},{257,129},{385... | collective-permute-start | bytes 786440 | tf_op jit(solution)/shard_map/ppermute | solution.py:292
  101.7 22.5 %collective-permute-start.10 = (bf16[4,256,128]{2,1,0:T(8,128)(2,1)}, bf16[4,256,128]{2,1,0:T(8,128)(2,1)}, u32[]{:S(2)}, u32[]{:S(2)}) collective-permute-start(bf16[4,256,128]{2,1,0:T(8,128)(2,1)} %gather_fusion.9), channel_id=1, source_target_pairs={{0,128},{128,256},{256,384},{384,0},{1,129},{129,257},{257,385},{3... | collective-permute-start | bytes 786440 | tf_op jit(solution)/shard_map/ppermute | solution.py:292
  123.3 1.0 copy-start.1
  124.3 11.5 %all-to-all-start.4 = ((f32[8,2,1024]{2,1,0:T(2,128)}), f32[8,2,1024]{2,1,0:T(2,128)S(1)}, u32[]{:S(2)}, u32[]{:S(2)}) async-start(f32[8,2,1024]{2,1,0:T(2,128)} %get-tuple-element.123), calls=%async_computation.4 | async-start | bytes 131072 | tf_op jit(solution)/shard_map/all_to_all | solution.py:251
  135.8 21.3 %all-to-all-start.5 = ((bf16[8,2,256,128]{3,2,1,0:T(8,128)(2,1)}), bf16[8,2,256,128]{3,2,1,0:T(8,128)(2,1)S(1)}, u32[]{:S(2)}, u32[]{:S(2)}) async-start(bf16[8,2,256,128]{3,2,1,0:T(8,128)(2,1)} %get-tuple-element.157), calls=%async_computation.5 | async-start | bytes 2097152 | tf_op jit(solution)/shard_map/all_to_all | solution.py:255
  141.1 2.2 %copy-start = (bf16[1,1024,2048]{2,1,0:T(8,128)(2,1)S(1)}, bf16[1,1024,2048]{2,1,0:T(8,128)(2,1)}, u32[]{:S(2)}) copy-start(bf16[1,1024,2048]{2,1,0:T(8,128)(2,1)} %all-gather.3.cloned.1.call-done) | copy-start | bytes 12582916
  143.3 1.2 copy-start.2
  147.3 7.9 %copy-start.5 = (f32[1024,128]{1,0:T(8,128)}, f32[1024,128]{1,0:T(8,128)S(1)}, u32[]{:S(2)}) copy-start(f32[1024,128]{1,0:T(8,128)S(1)} %get-tuple-element.130.mine_ref) | copy-start | bytes 1572868
  147.3 9.8 %collective-permute-start.14 = (bf16[1024,128]{1,0:T(8,128)(2,1)S(1)}, bf16[1024,128]{1,0:T(8,128)(2,1)S(1)}, u32[]{:S(2)}, u32[]{:S(2)}) collective-permute-start(bf16[1024,128]{1,0:T(8,128)(2,1)S(1)} %get-tuple-element.131), channel_id=1, source_target_pairs={{0,1},{1,0},{2,3},{3,2},{4,5},{5,4},{6,7},{7,6},{8,9},{9,8},{10,11... | collective-permute-start | bytes 786440 | tf_op jit(solution)/shard_map/ppermute | solution.py:247
  151.1 11.6 %collective-permute-start.13 = (bf16[1024,128]{1,0:T(8,128)(2,1)S(1)}, bf16[1024,128]{1,0:T(8,128)(2,1)S(1)}, u32[]{:S(2)}, u32[]{:S(2)}) collective-permute-start(bf16[1024,128]{1,0:T(8,128)(2,1)S(1)} %get-tuple-element.129), channel_id=1, source_target_pairs={{0,1},{1,0},{2,3},{3,2},{4,5},{5,4},{6,7},{7,6},{8,9},{9,8},{10,11... | collective-permute-start | bytes 786440 | tf_op jit(solution)/shard_map/ppermute | solution.py:247
  157.1 1.0 copy-start.6
Sparse Core Ops, SparseCore 0:
  10.1 62.6 all-gather.2

commit v9 on v8

--- a/solution.py
+++ b/solution.py
@@ -22,18 +22,17 @@
 FEW = 2
 LANES = 128
 VMEM_LIMIT = 24 * 1024 * 1024
-FORWARD_LIMIT = 48 * 1024 * 1024
 KINDS = 3
 HALVES = 2
 
 
-def adamw_kernel(side_ref, rate_ref, weight_ref, moments_ref, mine_ref, theirs_ref, *refs):
+def adamw_kernel(rate_ref, weight_ref, moments_ref, mine_ref, theirs_ref, *refs):
     weight_out, first_out, second_out = refs[-3:]
     rate = jnp.float32(0.0)
     for slot, value in enumerate(RATE_TABLE):
         rate = jnp.where(rate_ref[0] == slot, jnp.float32(value), rate)
     gradient = mine_ref[...] + theirs_ref[...].astype(jnp.float32)
-    weight_now = weight_ref[0, 0].astype(jnp.float32)
+    weight_now = weight_ref[...].astype(jnp.float32)
     first_now = moments_ref[0, 0].astype(jnp.float32)
     second_now = moments_ref[0, 1].astype(jnp.float32)
     first_sum = BETA_ONE * first_now + (1.0 - BETA_ONE) * gradient
@@ -45,21 +44,21 @@
     second_out[0] = second_sum.astype(jnp.bfloat16)
 
 
-def adamw(half, side, rate_index, weight, moments, mine, theirs, earlier):
-    pieces, _, rows, width = weight.shape
+def adamw(half, rate_index, weight, moments, mine, theirs, earlier):
+    pieces, _, rows, width = moments.shape
     steps = pieces // HALVES
     first = half * steps
-    flat = pl.BlockSpec((rows, width), lambda i, m, r: (i, 0))
-    out = pl.BlockSpec((1, rows, width), lambda i, m, r: (0, first + i, 0))
+    flat = pl.BlockSpec((rows, width), lambda i, r: (i, 0))
+    out = pl.BlockSpec((1, rows, width), lambda i, r: (0, first + i, 0))
     count = len(earlier)
     return pl.pallas_call(
         adamw_kernel,
         grid_spec=pltpu.PrefetchScalarGridSpec(
-            num_scalar_prefetch=2,
+            num_scalar_prefetch=1,
             grid=(steps,),
             in_specs=[
-                pl.BlockSpec((1, 1, rows, width), lambda i, m, r: (first + i, m[0], 0, 0)),
-                pl.BlockSpec((1, KINDS - 1, rows, width), lambda i, m, r: (first + i, 0, 0, 0)),
+                pl.BlockSpec((rows, width), lambda i, r: (first + i, 0)),
+                pl.BlockSpec((1, KINDS - 1, rows, width), lambda i, r: (first + i, 0, 0, 0)),
                 flat,
                 flat,
             ]
@@ -67,7 +66,7 @@
             out_specs=[out, out, out],
         ),
         out_shape=[jax.ShapeDtypeStruct((1, pieces * rows, width), jnp.bfloat16)] * KINDS,
-        input_output_aliases={6 + i: i for i in range(count)},
+        input_output_aliases={5 + i: i for i in range(count)},
         compiler_params=pltpu.CompilerParams(vmem_limit_bytes=VMEM_LIMIT),
         cost_estimate=pl.CostEstimate(
             flops=20 * steps * rows * width,
@@ -75,7 +74,7 @@
             transcendentals=steps * rows * width,
         ),
         name="adamw",
-    )(side, rate_index, weight, moments, mine, theirs, *earlier)
+    )(rate_index, weight, moments, mine, theirs, *earlier)
 
 
 def pack_kernel(residual_ref, upstream_ref, out_ref):
@@ -98,14 +97,20 @@
     )(residual, upstream)
 
 
-def forward_kernel(inv_scale, rows_ref, weight_ref, stream_ref, gain_ref, hidden_ref, sums_ref, both_ref):
-    pieces, halves, rows, width = weight_ref.shape
+def forward_kernel(inv_scale, side_ref, rows_ref, own_ref, other_ref, stream_ref, gain_ref, hidden_ref, sums_ref, both_ref):
+    width = own_ref.shape[1]
 
     @pl.when(pl.program_id(0) == 0)
     def _():
-        for piece in range(pieces):
-            for half in range(halves):
-                both_ref[piece * rows : (piece + 1) * rows, half * width : (half + 1) * width] = weight_ref[piece, half]
+        @pl.when(side_ref[0] == 0)
+        def _():
+            both_ref[:, :width] = own_ref[...]
+            both_ref[:, width:] = other_ref[...]
+
+        @pl.when(side_ref[0] != 0)
+        def _():
+            both_ref[:, :width] = other_ref[...]
+            both_ref[:, width:] = own_ref[...]
 
     linear = jnp.dot(rows_ref[...], both_ref[...], preferred_element_type=jnp.float32)
     count, block = linear.shape
@@ -123,34 +128,38 @@
         sums_ref[target] = packed
 
 
-def forward(rows, weight, gain, stream, inv_scale):
+def forward(side, rows, own, other, gain, stream, inv_scale):
     tokens, depth = rows.shape
     blocks, _, per, block = stream.shape
     step = 2 * per
     return pl.pallas_call(
         functools.partial(forward_kernel, inv_scale),
-        grid=(tokens // step,),
-        in_specs=[
-            pl.BlockSpec((step, depth), lambda i: (i, 0)),
-            pl.BlockSpec(weight.shape, lambda i: (0, 0, 0, 0)),
-            pl.BlockSpec((2, 2, per, block), lambda i: (i, 0, 0, 0)),
-            pl.BlockSpec(gain.shape, lambda i: (0, 0)),
-        ],
-        out_specs=[
-            pl.BlockSpec((step, block), lambda i: (i, 0)),
-            pl.BlockSpec((blocks, 2, step), lambda i: (0, 0, i)),
-        ],
-        scratch_shapes=[pltpu.VMEM((depth, block), jnp.bfloat16)],
+        grid_spec=pltpu.PrefetchScalarGridSpec(
+            num_scalar_prefetch=1,
+            grid=(tokens // step,),
+            in_specs=[
+                pl.BlockSpec((step, depth), lambda i, m: (i, 0)),
+                pl.BlockSpec(own.shape, lambda i, m: (0, 0)),
+                pl.BlockSpec(other.shape, lambda i, m: (0, 0)),
+                pl.BlockSpec((2, 2, per, block), lambda i, m: (i, 0, 0, 0)),
+                pl.BlockSpec(gain.shape, lambda i, m: (0, 0)),
+            ],
+            out_specs=[
+                pl.BlockSpec((step, block), lambda i, m: (i, 0)),
+                pl.BlockSpec((blocks, 2, step), lambda i, m: (0, 0, i)),
+            ],
+            scratch_shapes=[pltpu.VMEM((depth, block), jnp.bfloat16)],
+        ),
         out_shape=[
             jax.ShapeDtypeStruct((tokens, block), jnp.float32),
             jax.ShapeDtypeStruct((blocks, 2, tokens), jnp.float32),
         ],
-        compiler_params=pltpu.CompilerParams(vmem_limit_bytes=FORWARD_LIMIT),
+        compiler_params=pltpu.CompilerParams(vmem_limit_bytes=VMEM_LIMIT),
         cost_estimate=pl.CostEstimate(
             flops=2 * tokens * depth * block, bytes_accessed=7 * 1024 * 1024, transcendentals=0
         ),
         name="forward",
-    )(rows, weight, stream, gain)
+    )(side, rows, own, other, stream, gain)
 
 
 def multiply(inv_scale, side_ref, delta, rows_ref, mine_ref, theirs_ref):
@@ -286,43 +295,40 @@
     return pieces[(slots[:, None] * kinds + jnp.arange(kinds, dtype=jnp.int32)).reshape(-1)]
 
 
+def send_plane(pieces, slots, shift):
+    planes = lax.axis_size("plane")
+    return lax.ppermute(pick(pieces, slots[shift - 1]), "plane", [(i, (i + shift) % planes) for i in range(planes)])
+
+
 def send_planes(pieces, slots):
-    planes = lax.axis_size("plane")
-    return [
-        lax.ppermute(pick(pieces, slots[shift - 1]), "plane", [(i, (i + shift) % planes) for i in range(planes)])
-        for shift in range(1, planes)
-    ]
-
-
-def choose_kernel(kinds, copies, which_ref, start_ref, *refs):
+    return [send_plane(pieces, slots, shift) for shift in range(1, lax.axis_size("plane"))]
+
+
+def choose_kernel(kinds, which_ref, start_ref, *refs):
     refs, out_ref, sems = refs[:-2], refs[-2], refs[-1]
     columns = out_ref.shape[0]
-    slot = lambda place, copy: out_ref.at[place, copy] if copies else out_ref.at[place]
     for place in range(columns):
         for number, ref in enumerate(refs):
             @pl.when(which_ref[place] == number)
             def _():
-                for copy in range(max(copies, 1)):
-                    source = ref.at[pl.ds(start_ref[place], kinds)]
-                    pltpu.make_async_copy(source, slot(place, copy), sems.at[place, copy]).start()
+                source = ref.at[pl.ds(start_ref[place], kinds)]
+                pltpu.make_async_copy(source, out_ref.at[place], sems.at[place]).start()
 
     for place in range(columns):
-        for copy in range(max(copies, 1)):
-            pltpu.make_async_copy(refs[0].at[pl.ds(0, kinds)], slot(place, copy), sems.at[place, copy]).wait()
-
-
-def choose(pieces, received, which, start, kinds, copies):
-    columns = which.shape[0]
-    shape = ((columns, copies) if copies else (columns,)) + (kinds,) + pieces.shape[1:]
+        pltpu.make_async_copy(refs[0].at[pl.ds(0, kinds)], out_ref.at[place], sems.at[place]).wait()
+
+
+def choose(pieces, received, which, start, kinds):
+    shape = which.shape + (kinds,) + pieces.shape[1:]
     anywhere = pl.BlockSpec(memory_space=pl.ANY)
     return pl.pallas_call(
-        functools.partial(choose_kernel, kinds, copies),
+        functools.partial(choose_kernel, kinds),
         grid_spec=pltpu.PrefetchScalarGridSpec(
             num_scalar_prefetch=2,
             grid=(1,),
             in_specs=[anywhere] * (1 + len(received)),
             out_specs=pl.BlockSpec(shape, lambda i, *_: (0,) * len(shape)),
-            scratch_shapes=[pltpu.SemaphoreType.DMA((columns, max(copies, 1)))],
+            scratch_shapes=[pltpu.SemaphoreType.DMA(which.shape)],
         ),
         out_shape=jax.ShapeDtypeStruct(shape, pieces.dtype),
         compiler_params=pltpu.CompilerParams(vmem_limit_bytes=VMEM_LIMIT),
@@ -330,13 +336,13 @@
     )(which, start, pieces, *received)
 
 
-def across(pieces, received, plan, copies):
+def across(pieces, received, plan):
     kinds = pieces.shape[0] // lax.axis_size("column")
 
     def take(pieces, received):
         last = received[0].shape[0] // kinds - 1
         place = jnp.where(plan["offset"] == 0, plan["column"], jnp.minimum(plan["rank"], last))
-        return choose(pieces, received, plan["offset"], place * kinds, kinds, copies)
+        return choose(pieces, received, plan["offset"], place * kinds, kinds)
 
     def all_slots(pieces, received):
         return take(pieces, send_planes(pieces, plan["by_shift"]))
@@ -364,42 +370,44 @@
     gathered = lax.all_gather(attention_out[0], "major", axis=0, tiled=True)
     plan = plan_moves(sources)
     few = plan["by_shift"][:, :FEW]
+    weights = spread_columns(weight[0].reshape(columns, rows, width))
+    moments = jnp.stack(
+        [array[0].reshape(columns, rows, width) for array in (first_moment, second_moment)], axis=1
+    )
+    weights, moments = lax.optimization_barrier((weights, moments))
+    moments = spread_columns(moments).reshape(columns * (KINDS - 1), rows, width)
+    weights_in = send_planes(weights, few)
+    weights_in, moments = lax.optimization_barrier((weights_in, moments))
+    weights = across(weights, weights_in, plan)
+    weights, moments = lax.optimization_barrier((weights, moments))
+    weights = spread_columns(weights.reshape(columns, rows, width))
     gain_other = swap_minor(norm_gain[0])
     gain = jnp.where(
         minor == 0,
         jnp.concatenate((norm_gain[0], gain_other)),
         jnp.concatenate((gain_other, norm_gain[0])),
     ).astype(jnp.float32)[None, :]
-    weights = spread_columns(weight[0].reshape(columns, rows, width))
-    moments = jnp.stack(
-        [array[0].reshape(columns, rows, width) for array in (first_moment, second_moment)], axis=1
-    )
-    weights, moments, gain = lax.optimization_barrier((weights, moments, gain))
-    moments = spread_columns(moments).reshape(columns * (KINDS - 1), rows, width)
-    weights_in = send_planes(weights, few)
-    weights_in, moments = lax.optimization_barrier((weights_in, moments))
-    weights = across(weights, weights_in, plan, MINOR)
-    weights, moments = lax.optimization_barrier((weights, moments))
-    weights = lax.all_to_all(
-        weights.reshape(columns * MINOR, rows, width), ("column", "minor"), split_axis=0, concat_axis=0, tiled=True
-    ).reshape(columns, MINOR, rows, width)
-    moments_in = send_planes(moments, few)
     stream = pack(residual[0], upstream[0], lax.axis_size("major"))
-    weights, stream = lax.optimization_barrier((weights, stream))
+    weights, stream, gain = lax.optimization_barrier((weights, stream, gain))
     stream = lax.all_to_all(stream, "major", split_axis=0, concat_axis=0, tiled=True)
+    weights = weights.reshape(depth, width)
+    weights_other = swap_minor(weights)
+    moments_near = send_plane(moments, few, 1)
+    weights_other, moments = lax.optimization_barrier((weights_other, moments))
+    moments_in = [moments_near] + [send_plane(moments, few, shift) for shift in range(2, PLANES)]
 
     inv_scale = 1.0 / math.sqrt(depth)
     side = minor.astype(jnp.int32)[None]
-    hidden, sums = forward(gathered, weights, gain, stream, inv_scale)
+    hidden, sums = forward(side, gathered, weights, weights_other, gain, stream, inv_scale)
     moments_in, sums = lax.optimization_barrier((moments_in, sums))
     sums = sums_of_all(sums)
-    moments = across(moments, moments_in, plan, 0)
+    moments = across(moments, moments_in, plan)
     moments, sums = lax.optimization_barrier((moments, sums))
     moments = spread_columns(moments)
     halves = backward(side, gathered, hidden, gain, sums, stream, inv_scale, features)
     result = []
     for half, (mine, theirs) in enumerate(halves):
-        result = adamw(half, side, rate_index, weights, moments, mine, swap_minor(theirs), result)
+        result = adamw(half, rate_index, weights, moments, mine, swap_minor(theirs), result)
     return tuple(result)
 
 

time: 172 us -> 180 us (1.047)
  starting transfers between devices: 71.9 us -> 83.8 us
  Pallas kernels: 22.9 us -> 19.4 us
    all_to_all x3 -> x4, starting transfers between devices: 17 us -> 33.7 us  [spread_columns(): lax.all_to_all(array, 'column', split_axis=0, concat_axis=0, tiled=True)]
    ppermute x3 -> x4, waiting for transfers between devices: 4.7 us -> 17.6 us  [swap_minor(): return lax.ppermute(array, 'minor', [(0, 1), (1, 0)])]
    all_to_all x1 -> x0, waiting for transfers between devices: 12.4 us -> none  [local(): lax.all_to_all(weights.reshape(columns * MINOR, rows, width), ('column',...]
    all_to_all x1, waiting for transfers between devices: 12.2 us -> 0.01 us  [local(): lax.all_to_all(stream, 'major', split_axis=0, concat_axis=0, tiled=True)]
    ppermute x6, waiting for transfers between devices: 5.07 us -> 14.5 us  [send_plane(): lax.ppermute(pick(pieces, slots[shift - 1]), 'plane', [(i, (i + shift) %...]
    all_to_all x1 -> x0, starting transfers between devices: 6.42 us -> none  [local(): lax.all_to_all(weights.reshape(columns * MINOR, rows, width), ('column',...]
    ppermute x3 -> x4, starting transfers between devices: 10.1 us -> 15.9 us  [swap_minor(): return lax.ppermute(array, 'minor', [(0, 1), (1, 0)])]
    pallas_call x3, Pallas kernels: 11.9 us -> 8.43 us  [the longest x2 5.3 us: choose(): pl.pallas_call(functools.partial(choose_kernel, kinds), grid_spec=pltpu.P...]
  transfers between devices with their start and end apart: 16 -> 17, of which waited for: 7 -> 9; matrix products, arithmetic and copies ran while one was open for 7% -> 6% of each run, Pallas kernels for 12% -> 10%
where the time goes in v9:
time: 180 us; the launch traced here: 179 us
  starting transfers between devices  83.8 us (47%)
  waiting for transfers between devices  43.5 us (24%)
  Pallas kernels  19.4 us (11%)
  between operations  15.6 us (9%)
  local copies, waits for them, and re-layouts  12 us (7%)
  other arithmetic  4.97 us (3%)
    all_to_all x4, starting transfers between devices, spread_columns(): lax.all_to_all(array, 'column', split_axis=0, concat_axis=0, tiled=True)  33.7 us
    ppermute x6, starting transfers between devices, send_plane(): lax.ppermute(pick(pieces, slots[shift - 1]), 'plane', [(i, (i + shift) %...  23.9 us
    ppermute x4, waiting for transfers between devices, swap_minor(): return lax.ppermute(array, 'minor', [(0, 1), (1, 0)])  17.6 us
    ppermute x4, starting transfers between devices, swap_minor(): return lax.ppermute(array, 'minor', [(0, 1), (1, 0)])  15.9 us
    ppermute x6, waiting for transfers between devices, send_plane(): lax.ppermute(pick(pieces, slots[shift - 1]), 'plane', [(i, (i + shift) %...  14.5 us
    all_to_all x1, starting transfers between devices, local(): lax.all_to_all(stream, 'major', split_axis=0, concat_axis=0, tiled=True)  6.83 us
    unnamed x12, local copies, waits for them, and re-layouts  6.6 us
    all_to_all x4, waiting for transfers between devices, spread_columns(): lax.all_to_all(array, 'column', split_axis=0, concat_axis=0, tiled=True)  6.58 us
  transfers between devices with their start and end apart: 17, of which 9 were waited for; matrix products, arithmetic and copies ran while one was open for 6% of the time, Pallas kernels for 10%

profile of v9, /device:TPU:1, one launch (start us, length us, event | category | flops | bytes accessed | tf_op | source)
XLA Modules:
  0.0 179.3 jit_solution(17948601439563385058)
XLA Ops:
  7.9 10.3 %all-to-all-start = ((bf16[8,256,128]{2,1,0:T(8,128)(2,1)}), bf16[8,256,128]{2,1,0:T(8,128)(2,1)S(1)}, u32[]{:S(2)}, u32[]{:S(2)}) async-start(bf16[8,256,128]{2,1,0:T(8,128)(2,1)} %bitcast.78), calls=%async_computation | async-start | bytes 1048576 | tf_op jit(solution)/shard_map/all_to_all | solution.py:264
  22.0 5.7 %all-to-all-done = bf16[8,256,128]{2,1,0:T(8,128)(2,1)S(1)} async-done(((bf16[8,256,128]{2,1,0:T(8,128)(2,1)}), bf16[8,256,128]{2,1,0:T(8,128)(2,1)S(1)}, u32[]{:S(2)}, u32[]{:S(2)}) %all-to-all-start) | async-done | bytes 524320 | tf_op jit(solution)/shard_map/all_to_all | solution.py:264
  27.7 4.3 %all-to-all-start.1 = ((bf16[8,2,256,128]{3,2,1,0:T(8,128)(2,1)}), bf16[8,2,256,128]{3,2,1,0:T(8,128)(2,1)S(1)}, u32[]{:S(2)}, u32[]{:S(2)}) async-start(bf16[8,2,256,128]{3,2,1,0:T(8,128)(2,1)} %pad_maximum_fusion), calls=%async_computation.1 | async-start | bytes 2097152 | tf_op jit(solution)/shard_map/all_to_all | solution.py:264
  32.9 6.2 %collective-permute-start.7 = (bf16[2,256,128]{2,1,0:T(8,128)(2,1)S(1)}, bf16[2,256,128]{2,1,0:T(8,128)(2,1)S(1)}, u32[]{:S(2)}, u32[]{:S(2)}) collective-permute-start(bf16[2,256,128]{2,1,0:T(8,128)(2,1)S(1)} %gather_fusion.7), channel_id=1, source_target_pairs={{0,256},{128,384},{256,0},{384,128},{1,257},{129,385},{257,1},{385... | collective-permute-start | bytes 393224 | tf_op jit(solution)/shard_map/ppermute | solution.py:300
  42.2 4.4 %collective-permute-start.6 = (bf16[2,256,128]{2,1,0:T(8,128)(2,1)S(1)}, bf16[2,256,128]{2,1,0:T(8,128)(2,1)S(1)}, u32[]{:S(2)}, u32[]{:S(2)}) collective-permute-start(bf16[2,256,128]{2,1,0:T(8,128)(2,1)S(1)} %gather_fusion.6), channel_id=1, source_target_pairs={{0,128},{128,256},{256,384},{384,0},{1,129},{129,257},{257,385},{3... | collective-permute-start | bytes 393224 | tf_op jit(solution)/shard_map/ppermute | solution.py:300
  47.5 5.3 %collective-permute-done.8 = bf16[2,256,128]{2,1,0:T(8,128)(2,1)S(1)} collective-permute-done((bf16[2,256,128]{2,1,0:T(8,128)(2,1)S(1)}, bf16[2,256,128]{2,1,0:T(8,128)(2,1)S(1)}, u32[]{:S(2)}, u32[]{:S(2)}) %collective-permute-start.8) | collective-permute-done | bytes 131104 | tf_op jit(solution)/shard_map/ppermute | solution.py:300
  55.1 4.9 %all-to-all-start.2 = ((bf16[8,256,128]{2,1,0:T(8,128)(2,1)}), bf16[8,256,128]{2,1,0:T(8,128)(2,1)S(1)}, u32[]{:S(2)}, u32[]{:S(2)}) async-start(bf16[8,256,128]{2,1,0:T(8,128)(2,1)} %bitcast.24), calls=%async_computation.2 | async-start | bytes 1048576 | tf_op jit(solution)/shard_map/all_to_all | solution.py:264
  60.0 5.0 %collective-permute-start.9 = (bf16[128]{0:T(256)(128)(2,1)}, bf16[128]{0:T(256)(128)(2,1)S(1)}, u32[]{:S(2)}, u32[]{:S(2)}) collective-permute-start(bf16[128]{0:T(256)(128)(2,1)} %bitcast.81), channel_id=1, source_target_pairs={{0,1},{1,0},{2,3},{3,2},{4,5},{5,4},{6,7},{7,6},{8,9},{9,8},{10,11... | collective-permute-start | bytes 776 | tf_op jit(solution)/shard_map/ppermute | solution.py:256
  65.0 2.9 %pack.1 = bf16[8,2,128,256]{3,2,1,0:T(8,128)(2,1)} custom-call(bf16[128,2048]{1,0:T(8,128)(2,1)S(1)} %bitcast.71, bf16[128,2048]{1,0:T(8,128)(2,1)S(1)} %bitcast.72), custom_call_target="tpu_custom_call" | custom-call | tf_op jit(solution)/shard_map/pack/pallas_call | solution.py:89
  69.5 6.8 %all-to-all-start.3 = ((bf16[8,2,128,256]{3,2,1,0:T(8,128)(2,1)}), bf16[8,2,128,256]{3,2,1,0:T(8,128)(2,1)S(1)}, u32[]{:S(2)}, u32[]{:S(2)}) async-start(bf16[8,2,128,256]{3,2,1,0:T(8,128)(2,1)} %pack.1), calls=%async_computation.3 | async-start | bytes 2097152 | tf_op jit(solution)/shard_map/all_to_all | solution.py:392
  76.7 5.0 %collective-permute-start.10 = (bf16[2048,128]{1,0:T(8,128)(2,1)S(1)}, bf16[2048,128]{1,0:T(8,128)(2,1)S(1)}, u32[]{:S(2)}, u32[]{:S(2)}) collective-permute-start(bf16[2048,128]{1,0:T(8,128)(2,1)S(1)} %bitcast.67), channel_id=1, source_target_pairs={{0,1},{1,0},{2,3},{3,2},{4,5},{5,4},{6,7},{7,6},{8,9},{9,8},{10,11... | collective-permute-start | bytes 1572872 | tf_op jit(solution)/shard_map/ppermute | solution.py:256
  82.3 3.1 %collective-permute-start.11 = (bf16[4,256,128]{2,1,0:T(8,128)(2,1)S(1)}, bf16[4,256,128]{2,1,0:T(8,128)(2,1)}, u32[]{:S(2)}, u32[]{:S(2)}) collective-permute-start(bf16[4,256,128]{2,1,0:T(8,128)(2,1)S(1)} %gather_fusion.9), channel_id=1, source_target_pairs={{0,128},{128,256},{256,384},{384,0},{1,129},{129,257},{257,385},{3... | collective-permute-start | bytes 786440 | tf_op jit(solution)/shard_map/ppermute | solution.py:300
  85.5 11.9 %collective-permute-done.10.other_ref = bf16[2048,128]{1,0:T(8,128)(2,1)S(1)} collective-permute-done((bf16[2048,128]{1,0:T(8,128)(2,1)S(1)}, bf16[2048,128]{1,0:T(8,128)(2,1)S(1)}, u32[]{:S(2)}, u32[]{:S(2)}) %collective-permute-start.10) | collective-permute-done | bytes 524320 | tf_op jit(solution)/shard_map/ppermute | solution.py:256
  98.6 6.2 %collective-permute-start.12 = (bf16[4,256,128]{2,1,0:T(8,128)(2,1)}, bf16[4,256,128]{2,1,0:T(8,128)(2,1)}, u32[]{:S(2)}, u32[]{:S(2)}) collective-permute-start(bf16[4,256,128]{2,1,0:T(8,128)(2,1)} %gather_fusion.10), channel_id=1, source_target_pairs={{0,256},{128,384},{256,0},{384,128},{1,257},{129,385},{257,1},{385... | collective-permute-start | bytes 786440 | tf_op jit(solution)/shard_map/ppermute | solution.py:300
  110.5 3.1 %forward.1 = (f32[1024,256]{1,0:T(8,128)S(1)}, f32[8,2,1024]{2,1,0:T(2,128)}) custom-call(s32[1]{0:T(128)} %bitcast.36.side_ref, bf16[1024,2048]{1,0:T(8,128)(2,1)S(1)} %bitcast.64, bf16[2048,128]{1,0:T(8,128)(2,1)S(1)} %bitcast.68, bf16[2048,128]{1,0:T(8,128)(2,1)S(1)} %collective-permute-done.10.other_ref, ...), custom_call_target="tpu_custom_call" | custom-call | flops 1073741824 | bytes 7340032 | tf_op jit(solution)/shard_map/forward/pallas_call | solution.py:135
  114.6 4.8 %collective-permute-done.12 = bf16[4,256,128]{2,1,0:T(8,128)(2,1)} collective-permute-done((bf16[4,256,128]{2,1,0:T(8,128)(2,1)}, bf16[4,256,128]{2,1,0:T(8,128)(2,1)}, u32[]{:S(2)}, u32[]{:S(2)}) %collective-permute-start.12) | collective-permute-done | bytes 262176 | tf_op jit(solution)/shard_map/ppermute | solution.py:300
  119.4 4.5 %collective-permute-done.13 = bf16[4,256,128]{2,1,0:T(8,128)(2,1)} collective-permute-done((bf16[4,256,128]{2,1,0:T(8,128)(2,1)}, bf16[4,256,128]{2,1,0:T(8,128)(2,1)}, u32[]{:S(2)}, u32[]{:S(2)}) %collective-permute-start.13) | collective-permute-done | bytes 262176 | tf_op jit(solution)/shard_map/ppermute | solution.py:300
  123.8 3.4 %all-to-all-start.4 = ((f32[8,2,1024]{2,1,0:T(2,128)}), f32[8,2,1024]{2,1,0:T(2,128)S(1)}, u32[]{:S(2)}, u32[]{:S(2)}) async-start(f32[8,2,1024]{2,1,0:T(2,128)} %get-tuple-element.127), calls=%async_computation.4 | async-start | bytes 131072 | tf_op jit(solution)/shard_map/all_to_all | solution.py:260
  127.2 3.0 %conditional.3 = (bf16[8,2,256,128]{3,2,1,0:T(8,128)(2,1)}) conditional(s32[]{:T(128)} %convert_element_type.18, (s32[8]{0:T(128)S(1)}, s32[8]{0:T(128)S(1)}, s32[8]{0:T(128)S(1)}, bf16[16,256,128]{2,1,0:T(8,128)(2,1)S(1)}, bf16[4,256,128]{2,1,0:T(8,128)(2,1)}, /*index=5*/bf16[4,256,128]{2,1,0:T(8,128)(2,1)}, ...), branch_computations={%region_5.6_spmd, %region_6.7_spmd} | conditional | flops 3320 | bytes 23082876 | solution.py:350
  127.2 2.9 %choose.6 = bf16[8,2,256,128]{3,2,1,0:T(8,128)(2,1)} custom-call(s32[8]{0:T(128)S(1)} %get-tuple-element.66.which_ref, s32[8]{0:T(128)S(1)} %fusion.start_ref, bf16[16,256,128]{2,1,0:T(8,128)(2,1)S(1)} %get-tuple-element.69.refs_0_, bf16[4,256,128]{2,1,0:T(8,128)(2,1)} %get-tuple-element.70.refs_1_, bf16[4,256,128]{2,1,0:T(8,128)(2,1)} %get-tuple-element.71.refs_2_, ...), custom_call_target="tpu_custom_call" | custom-call | tf_op jit(solution)/shard_map/cond/branch_0_fun/choose/pallas_call | solution.py:324
  130.2 4.2 %all-to-all-done.4.sums_ref = f32[8,2,1024]{2,1,0:T(2,128)S(1)} async-done(((f32[8,2,1024]{2,1,0:T(2,128)}), f32[8,2,1024]{2,1,0:T(2,128)S(1)}, u32[]{:S(2)}, u32[]{:S(2)}) %all-to-all-start.4) | async-done | bytes 65568 | tf_op jit(solution)/shard_map/all_to_all | solution.py:260
  134.3 14.2 %all-to-all-start.5 = ((bf16[8,2,256,128]{3,2,1,0:T(8,128)(2,1)}), bf16[8,2,256,128]{3,2,1,0:T(8,128)(2,1)S(1)}, u32[]{:S(2)}, u32[]{:S(2)}) async-start(bf16[8,2,256,128]{3,2,1,0:T(8,128)(2,1)} %get-tuple-element.161), calls=%async_computation.5 | async-start | bytes 2097152 | tf_op jit(solution)/shard_map/all_to_all | solution.py:264
  154.7 4.1 %collective-permute-start.15 = (bf16[1024,128]{1,0:T(8,128)(2,1)S(1)}, bf16[1024,128]{1,0:T(8,128)(2,1)S(1)}, u32[]{:S(2)}, u32[]{:S(2)}) collective-permute-start(bf16[1024,128]{1,0:T(8,128)(2,1)S(1)} %get-tuple-element.135), channel_id=1, source_target_pairs={{0,1},{1,0},{2,3},{3,2},{4,5},{5,4},{6,7},{7,6},{8,9},{9,8},{10,11... | collective-permute-start | bytes 786440 | tf_op jit(solution)/shard_map/ppermute | solution.py:256
  167.1 3.6 %collective-permute-done.14.theirs_ref = bf16[1024,128]{1,0:T(8,128)(2,1)S(1)} collective-permute-done((bf16[1024,128]{1,0:T(8,128)(2,1)S(1)}, bf16[1024,128]{1,0:T(8,128)(2,1)S(1)}, u32[]{:S(2)}, u32[]{:S(2)}) %collective-permute-start.14) | collective-permute-done | bytes 262176 | tf_op jit(solution)/shard_map/ppermute | solution.py:256
  (70 shorter events, 39.4 us)
Async XLA Ops:
  7.2 101.1 %all-gather.3.cloned.1.call-start = ((), (), s32[]{:S(2)}) async-start(), calls=%async_computation.6 | async-start | bytes 4718592 | tf_op jit(solution)/shard_map/all_gather | solution.py:370
  7.9 19.8 %all-to-all-start = ((bf16[8,256,128]{2,1,0:T(8,128)(2,1)}), bf16[8,256,128]{2,1,0:T(8,128)(2,1)S(1)}, u32[]{:S(2)}, u32[]{:S(2)}) async-start(bf16[8,256,128]{2,1,0:T(8,128)(2,1)} %bitcast.78), calls=%async_computation | async-start | bytes 1048576 | tf_op jit(solution)/shard_map/all_to_all | solution.py:264
  27.7 25.0 %all-to-all-start.1 = ((bf16[8,2,256,128]{3,2,1,0:T(8,128)(2,1)}), bf16[8,2,256,128]{3,2,1,0:T(8,128)(2,1)S(1)}, u32[]{:S(2)}, u32[]{:S(2)}) async-start(bf16[8,2,256,128]{3,2,1,0:T(8,128)(2,1)} %pad_maximum_fusion), calls=%async_computation.1 | async-start | bytes 2097152 | tf_op jit(solution)/shard_map/all_to_all | solution.py:264
  32.9 14.6 %collective-permute-start.7 = (bf16[2,256,128]{2,1,0:T(8,128)(2,1)S(1)}, bf16[2,256,128]{2,1,0:T(8,128)(2,1)S(1)}, u32[]{:S(2)}, u32[]{:S(2)}) collective-permute-start(bf16[2,256,128]{2,1,0:T(8,128)(2,1)S(1)} %gather_fusion.7), channel_id=1, source_target_pairs={{0,256},{128,384},{256,0},{384,128},{1,257},{129,385},{257,1},{385... | collective-permute-start | bytes 393224 | tf_op jit(solution)/shard_map/ppermute | solution.py:300
  39.6 13.1 %collective-permute-start.8 = (bf16[2,256,128]{2,1,0:T(8,128)(2,1)S(1)}, bf16[2,256,128]{2,1,0:T(8,128)(2,1)S(1)}, u32[]{:S(2)}, u32[]{:S(2)}) collective-permute-start(bf16[2,256,128]{2,1,0:T(8,128)(2,1)S(1)} %gather_fusion.8), channel_id=1, source_target_pairs={{0,384},{128,0},{256,128},{384,256},{1,385},{129,1},{257,129},{385... | collective-permute-start | bytes 393224 | tf_op jit(solution)/shard_map/ppermute | solution.py:300
  42.2 22.8 %copy-start.4 = (bf16[1,128,2048]{2,1,0:T(8,128)(2,1)S(1)}, bf16[1,128,2048]{2,1,0:T(8,128)(2,1)}, u32[]{:S(2)}) copy-start(bf16[1,128,2048]{2,1,0:T(8,128)(2,1)} %param.14) | copy-start | bytes 1572868
  42.2 22.8 %copy-start.5 = (bf16[1,128,2048]{2,1,0:T(8,128)(2,1)S(1)}, bf16[1,128,2048]{2,1,0:T(8,128)(2,1)}, u32[]{:S(2)}) copy-start(bf16[1,128,2048]{2,1,0:T(8,128)(2,1)} %param.15) | copy-start | bytes 1572868
  42.2 10.5 %collective-permute-start.6 = (bf16[2,256,128]{2,1,0:T(8,128)(2,1)S(1)}, bf16[2,256,128]{2,1,0:T(8,128)(2,1)S(1)}, u32[]{:S(2)}, u32[]{:S(2)}) collective-permute-start(bf16[2,256,128]{2,1,0:T(8,128)(2,1)S(1)} %gather_fusion.6), channel_id=1, source_target_pairs={{0,128},{128,256},{256,384},{384,0},{1,129},{129,257},{257,385},{3... | collective-permute-start | bytes 393224 | tf_op jit(solution)/shard_map/ppermute | solution.py:300
  55.1 14.4 %all-to-all-start.2 = ((bf16[8,256,128]{2,1,0:T(8,128)(2,1)}), bf16[8,256,128]{2,1,0:T(8,128)(2,1)S(1)}, u32[]{:S(2)}, u32[]{:S(2)}) async-start(bf16[8,256,128]{2,1,0:T(8,128)(2,1)} %bitcast.24), calls=%async_computation.2 | async-start | bytes 1048576 | tf_op jit(solution)/shard_map/all_to_all | solution.py:264
  60.0 7.9 %collective-permute-start.9 = (bf16[128]{0:T(256)(128)(2,1)}, bf16[128]{0:T(256)(128)(2,1)S(1)}, u32[]{:S(2)}, u32[]{:S(2)}) collective-permute-start(bf16[128]{0:T(256)(128)(2,1)} %bitcast.81), channel_id=1, source_target_pairs={{0,1},{1,0},{2,3},{3,2},{4,5},{5,4},{6,7},{7,6},{8,9},{9,8},{10,11... | collective-permute-start | bytes 776 | tf_op jit(solution)/shard_map/ppermute | solution.py:256
  69.5 38.8 %all-to-all-start.3 = ((bf16[8,2,128,256]{3,2,1,0:T(8,128)(2,1)}), bf16[8,2,128,256]{3,2,1,0:T(8,128)(2,1)S(1)}, u32[]{:S(2)}, u32[]{:S(2)}) async-start(bf16[8,2,128,256]{3,2,1,0:T(8,128)(2,1)} %pack.1), calls=%async_computation.3 | async-start | bytes 2097152 | tf_op jit(solution)/shard_map/all_to_all | solution.py:392
  76.7 20.6 %collective-permute-start.10 = (bf16[2048,128]{1,0:T(8,128)(2,1)S(1)}, bf16[2048,128]{1,0:T(8,128)(2,1)S(1)}, u32[]{:S(2)}, u32[]{:S(2)}) collective-permute-start(bf16[2048,128]{1,0:T(8,128)(2,1)S(1)} %bitcast.67), channel_id=1, source_target_pairs={{0,1},{1,0},{2,3},{3,2},{4,5},{5,4},{6,7},{7,6},{8,9},{9,8},{10,11... | collective-permute-start | bytes 1572872 | tf_op jit(solution)/shard_map/ppermute | solution.py:256
  82.3 32.2 %collective-permute-start.11 = (bf16[4,256,128]{2,1,0:T(8,128)(2,1)S(1)}, bf16[4,256,128]{2,1,0:T(8,128)(2,1)}, u32[]{:S(2)}, u32[]{:S(2)}) collective-permute-start(bf16[4,256,128]{2,1,0:T(8,128)(2,1)S(1)} %gather_fusion.9), channel_id=1, source_target_pairs={{0,128},{128,256},{256,384},{384,0},{1,129},{129,257},{257,385},{3... | collective-permute-start | bytes 786440 | tf_op jit(solution)/shard_map/ppermute | solution.py:300
  98.6 20.7 %collective-permute-start.12 = (bf16[4,256,128]{2,1,0:T(8,128)(2,1)}, bf16[4,256,128]{2,1,0:T(8,128)(2,1)}, u32[]{:S(2)}, u32[]{:S(2)}) collective-permute-start(bf16[4,256,128]{2,1,0:T(8,128)(2,1)} %gather_fusion.10), channel_id=1, source_target_pairs={{0,256},{128,384},{256,0},{384,128},{1,257},{129,385},{257,1},{385... | collective-permute-start | bytes 786440 | tf_op jit(solution)/shard_map/ppermute | solution.py:300
  106.1 17.7 %collective-permute-start.13 = (bf16[4,256,128]{2,1,0:T(8,128)(2,1)}, bf16[4,256,128]{2,1,0:T(8,128)(2,1)}, u32[]{:S(2)}, u32[]{:S(2)}) collective-permute-start(bf16[4,256,128]{2,1,0:T(8,128)(2,1)} %gather_fusion.11), channel_id=1, source_target_pairs={{0,384},{128,0},{256,128},{384,256},{1,385},{129,1},{257,129},{385... | collective-permute-start | bytes 786440 | tf_op jit(solution)/shard_map/ppermute | solution.py:300
  108.3 2.2 %copy-start = (bf16[1,1024,2048]{2,1,0:T(8,128)(2,1)S(1)}, bf16[1,1024,2048]{2,1,0:T(8,128)(2,1)}, u32[]{:S(2)}) copy-start(bf16[1,1024,2048]{2,1,0:T(8,128)(2,1)} %all-gather.3.cloned.1.call-done) | copy-start | bytes 12582916
  113.6 1.0 copy-start.2
  123.8 10.5 %all-to-all-start.4 = ((f32[8,2,1024]{2,1,0:T(2,128)}), f32[8,2,1024]{2,1,0:T(2,128)S(1)}, u32[]{:S(2)}, u32[]{:S(2)}) async-start(f32[8,2,1024]{2,1,0:T(2,128)} %get-tuple-element.127), calls=%async_computation.4 | async-start | bytes 131072 | tf_op jit(solution)/shard_map/all_to_all | solution.py:260
  134.3 31.0 %all-to-all-start.5 = ((bf16[8,2,256,128]{3,2,1,0:T(8,128)(2,1)}), bf16[8,2,256,128]{3,2,1,0:T(8,128)(2,1)S(1)}, u32[]{:S(2)}, u32[]{:S(2)}) async-start(bf16[8,2,256,128]{3,2,1,0:T(8,128)(2,1)} %get-tuple-element.161), calls=%async_computation.5 | async-start | bytes 2097152 | tf_op jit(solution)/shard_map/all_to_all | solution.py:264
  148.5 2.2 %copy-start.1 = (bf16[1,1024,2048]{2,1,0:T(8,128)(2,1)S(1)}, bf16[1,1024,2048]{2,1,0:T(8,128)(2,1)}, u32[]{:S(2)}) copy-start(bf16[1,1024,2048]{2,1,0:T(8,128)(2,1)} %all-gather.3.cloned.1.call-done) | copy-start | bytes 12582916
  150.7 1.2 copy-start.3
  154.7 10.6 %collective-permute-start.15 = (bf16[1024,128]{1,0:T(8,128)(2,1)S(1)}, bf16[1024,128]{1,0:T(8,128)(2,1)S(1)}, u32[]{:S(2)}, u32[]{:S(2)}) collective-permute-start(bf16[1024,128]{1,0:T(8,128)(2,1)S(1)} %get-tuple-element.135), channel_id=1, source_target_pairs={{0,1},{1,0},{2,3},{3,2},{4,5},{5,4},{6,7},{7,6},{8,9},{9,8},{10,11... | collective-permute-start | bytes 786440 | tf_op jit(solution)/shard_map/ppermute | solution.py:256
  160.6 10.0 %collective-permute-start.14 = (bf16[1024,128]{1,0:T(8,128)(2,1)S(1)}, bf16[1024,128]{1,0:T(8,128)(2,1)S(1)}, u32[]{:S(2)}, u32[]{:S(2)}) collective-permute-start(bf16[1024,128]{1,0:T(8,128)(2,1)S(1)} %get-tuple-element.133), channel_id=1, source_target_pairs={{0,1},{1,0},{2,3},{3,2},{4,5},{5,4},{6,7},{7,6},{8,9},{9,8},{10,11... | collective-permute-start | bytes 786440 | tf_op jit(solution)/shard_map/ppermute | solution.py:256
Sparse Core Ops, SparseCore 0:
  10.1 62.6 all-gather.2

commit v10 on v9

--- a/solution.py
+++ b/solution.py
@@ -392,14 +392,12 @@
     stream = lax.all_to_all(stream, "major", split_axis=0, concat_axis=0, tiled=True)
     weights = weights.reshape(depth, width)
     weights_other = swap_minor(weights)
-    moments_near = send_plane(moments, few, 1)
-    weights_other, moments = lax.optimization_barrier((weights_other, moments))
-    moments_in = [moments_near] + [send_plane(moments, few, shift) for shift in range(2, PLANES)]
+    moments_in = send_planes(moments, few)
 
     inv_scale = 1.0 / math.sqrt(depth)
     side = minor.astype(jnp.int32)[None]
     hidden, sums = forward(side, gathered, weights, weights_other, gain, stream, inv_scale)
-    moments_in, sums = lax.optimization_barrier((moments_in, sums))
+    moments, sums = lax.optimization_barrier((moments, sums))
     sums = sums_of_all(sums)
     moments = across(moments, moments_in, plan)
     moments, sums = lax.optimization_barrier((moments, sums))

time: 180 us -> 162 us (0.900)
  waiting for transfers between devices: 43.5 us -> 30.7 us
  starting transfers between devices: 83.8 us -> 78.3 us
    ppermute x4, waiting for transfers between devices: 17.6 us -> 5.78 us  [swap_minor(): return lax.ppermute(array, 'minor', [(0, 1), (1, 0)])]
    ppermute x6, waiting for transfers between devices: 14.5 us -> 5.28 us  [send_plane(): lax.ppermute(pick(pieces, slots[shift - 1]), 'plane', [(i, (i + shift) %...]
    all_to_all x1, waiting for transfers between devices: 0.01 us -> 8.29 us  [local(): lax.all_to_all(stream, 'major', split_axis=0, concat_axis=0, tiled=True)]
    all_to_all x4, starting transfers between devices: 33.7 us -> 28 us  [spread_columns(): lax.all_to_all(array, 'column', split_axis=0, concat_axis=0, tiled=True)]
  transfers between devices with their start and end apart: 17 -> 17, of which waited for: 9 -> 7; matrix products, arithmetic and copies ran while one was open for 6% -> 6% of each run, Pallas kernels for 10% -> 11%
where the time goes in v10:
time: 162 us; the launch traced here: 161 us
  starting transfers between devices  78.3 us (48%)
  waiting for transfers between devices  30.7 us (19%)
  Pallas kernels  19.4 us (12%)
  between operations  15.6 us (10%)
  local copies, waits for them, and re-layouts  12 us (7%)
  other arithmetic  4.97 us (3%)
    all_to_all x4, starting transfers between devices, spread_columns(): lax.all_to_all(array, 'column', split_axis=0, concat_axis=0, tiled=True)  28 us
    ppermute x6, starting transfers between devices, send_plane(): lax.ppermute(pick(pieces, slots[shift - 1]), 'plane', [(i, (i + shift) %...  24.9 us
    ppermute x4, starting transfers between devices, swap_minor(): return lax.ppermute(array, 'minor', [(0, 1), (1, 0)])  15.2 us
    all_to_all x1, waiting for transfers between devices, local(): lax.all_to_all(stream, 'major', split_axis=0, concat_axis=0, tiled=True)  8.29 us
    all_to_all x1, starting transfers between devices, local(): lax.all_to_all(stream, 'major', split_axis=0, concat_axis=0, tiled=True)  6.83 us
    unnamed x12, local copies, waits for them, and re-layouts  6.61 us
    all_to_all x4, waiting for transfers between devices, spread_columns(): lax.all_to_all(array, 'column', split_axis=0, concat_axis=0, tiled=True)  6.58 us
    ppermute x4, waiting for transfers between devices, swap_minor(): return lax.ppermute(array, 'minor', [(0, 1), (1, 0)])  5.78 us
  transfers between devices with their start and end apart: 17, of which 7 were waited for; matrix products, arithmetic and copies ran while one was open for 6% of the time, Pallas kernels for 11%

profile of v10, /device:TPU:1, one launch (start us, length us, event | category | flops | bytes accessed | tf_op | source)
XLA Modules:
  0.0 161.0 jit_solution(4304554850861963798)
XLA Ops:
  7.9 10.3 %all-to-all-start = ((bf16[8,256,128]{2,1,0:T(8,128)(2,1)}), bf16[8,256,128]{2,1,0:T(8,128)(2,1)S(1)}, u32[]{:S(2)}, u32[]{:S(2)}) async-start(bf16[8,256,128]{2,1,0:T(8,128)(2,1)} %bitcast.78), calls=%async_computation | async-start | bytes 1048576 | tf_op jit(solution)/shard_map/all_to_all | solution.py:264
  22.0 5.7 %all-to-all-done = bf16[8,256,128]{2,1,0:T(8,128)(2,1)S(1)} async-done(((bf16[8,256,128]{2,1,0:T(8,128)(2,1)}), bf16[8,256,128]{2,1,0:T(8,128)(2,1)S(1)}, u32[]{:S(2)}, u32[]{:S(2)}) %all-to-all-start) | async-done | bytes 524320 | tf_op jit(solution)/shard_map/all_to_all | solution.py:264
  27.7 4.3 %all-to-all-start.1 = ((bf16[8,2,256,128]{3,2,1,0:T(8,128)(2,1)}), bf16[8,2,256,128]{3,2,1,0:T(8,128)(2,1)S(1)}, u32[]{:S(2)}, u32[]{:S(2)}) async-start(bf16[8,2,256,128]{3,2,1,0:T(8,128)(2,1)} %pad_maximum_fusion), calls=%async_computation.1 | async-start | bytes 2097152 | tf_op jit(solution)/shard_map/all_to_all | solution.py:264
  32.9 6.2 %collective-permute-start.7 = (bf16[2,256,128]{2,1,0:T(8,128)(2,1)S(1)}, bf16[2,256,128]{2,1,0:T(8,128)(2,1)S(1)}, u32[]{:S(2)}, u32[]{:S(2)}) collective-permute-start(bf16[2,256,128]{2,1,0:T(8,128)(2,1)S(1)} %gather_fusion.7), channel_id=1, source_target_pairs={{0,256},{128,384},{256,0},{384,128},{1,257},{129,385},{257,1},{385... | collective-permute-start | bytes 393224 | tf_op jit(solution)/shard_map/ppermute | solution.py:300
  42.2 4.4 %collective-permute-start.6 = (bf16[2,256,128]{2,1,0:T(8,128)(2,1)S(1)}, bf16[2,256,128]{2,1,0:T(8,128)(2,1)S(1)}, u32[]{:S(2)}, u32[]{:S(2)}) collective-permute-start(bf16[2,256,128]{2,1,0:T(8,128)(2,1)S(1)} %gather_fusion.6), channel_id=1, source_target_pairs={{0,128},{128,256},{256,384},{384,0},{1,129},{129,257},{257,385},{3... | collective-permute-start | bytes 393224 | tf_op jit(solution)/shard_map/ppermute | solution.py:300
  47.5 5.3 %collective-permute-done.8 = bf16[2,256,128]{2,1,0:T(8,128)(2,1)S(1)} collective-permute-done((bf16[2,256,128]{2,1,0:T(8,128)(2,1)S(1)}, bf16[2,256,128]{2,1,0:T(8,128)(2,1)S(1)}, u32[]{:S(2)}, u32[]{:S(2)}) %collective-permute-start.8) | collective-permute-done | bytes 131104 | tf_op jit(solution)/shard_map/ppermute | solution.py:300
  52.7 2.4 %conditional.2 = (bf16[8,1,256,128]{3,2,1,0:T(8,128)(2,1)}) conditional(s32[]{:T(128)} %convert_element_type.18, (s32[8]{0:T(128)S(1)}, s32[8]{0:T(128)S(1)}, s32[8]{0:T(128)S(1)}, bf16[8,256,128]{2,1,0:T(8,128)(2,1)S(1)}, bf16[2,256,128]{2,1,0:T(8,128)(2,1)S(1)}, /*index=5*/bf16[2,256,128]{2,1,0:T(8,128)(2,1)S(1)}, ...), branch_computations={%region_3.4_spmd, %region_4.5_spmd} | conditional | flops 3168 | bytes 11547292 | solution.py:350
  55.1 4.9 %all-to-all-start.2 = ((bf16[8,256,128]{2,1,0:T(8,128)(2,1)}), bf16[8,256,128]{2,1,0:T(8,128)(2,1)S(1)}, u32[]{:S(2)}, u32[]{:S(2)}) async-start(bf16[8,256,128]{2,1,0:T(8,128)(2,1)} %bitcast.24), calls=%async_computation.2 | async-start | bytes 1048576 | tf_op jit(solution)/shard_map/all_to_all | solution.py:264
  60.0 5.0 %collective-permute-start.9 = (bf16[128]{0:T(256)(128)(2,1)}, bf16[128]{0:T(256)(128)(2,1)S(1)}, u32[]{:S(2)}, u32[]{:S(2)}) collective-permute-start(bf16[128]{0:T(256)(128)(2,1)} %bitcast.81), channel_id=1, source_target_pairs={{0,1},{1,0},{2,3},{3,2},{4,5},{5,4},{6,7},{7,6},{8,9},{9,8},{10,11... | collective-permute-start | bytes 776 | tf_op jit(solution)/shard_map/ppermute | solution.py:256
  65.0 2.9 %pack.1 = bf16[8,2,128,256]{3,2,1,0:T(8,128)(2,1)} custom-call(bf16[128,2048]{1,0:T(8,128)(2,1)S(1)} %bitcast.71, bf16[128,2048]{1,0:T(8,128)(2,1)S(1)} %bitcast.72), custom_call_target="tpu_custom_call" | custom-call | tf_op jit(solution)/shard_map/pack/pallas_call | solution.py:89
  69.5 6.8 %all-to-all-start.3 = ((bf16[8,2,128,256]{3,2,1,0:T(8,128)(2,1)}), bf16[8,2,128,256]{3,2,1,0:T(8,128)(2,1)S(1)}, u32[]{:S(2)}, u32[]{:S(2)}) async-start(bf16[8,2,128,256]{3,2,1,0:T(8,128)(2,1)} %pack.1), calls=%async_computation.3 | async-start | bytes 2097152 | tf_op jit(solution)/shard_map/all_to_all | solution.py:392
  76.6 5.0 %collective-permute-start.10 = (bf16[2048,128]{1,0:T(8,128)(2,1)S(1)}, bf16[2048,128]{1,0:T(8,128)(2,1)S(1)}, u32[]{:S(2)}, u32[]{:S(2)}) collective-permute-start(bf16[2048,128]{1,0:T(8,128)(2,1)S(1)} %bitcast.67), channel_id=1, source_target_pairs={{0,1},{1,0},{2,3},{3,2},{4,5},{5,4},{6,7},{7,6},{8,9},{9,8},{10,11... | collective-permute-start | bytes 1572872 | tf_op jit(solution)/shard_map/ppermute | solution.py:256
  82.3 6.2 %collective-permute-start.12 = (bf16[4,256,128]{2,1,0:T(8,128)(2,1)S(1)}, bf16[4,256,128]{2,1,0:T(8,128)(2,1)}, u32[]{:S(2)}, u32[]{:S(2)}) collective-permute-start(bf16[4,256,128]{2,1,0:T(8,128)(2,1)S(1)} %gather_fusion.10), channel_id=1, source_target_pairs={{0,256},{128,384},{256,0},{384,128},{1,257},{129,385},{257,1},{385... | collective-permute-start | bytes 786440 | tf_op jit(solution)/shard_map/ppermute | solution.py:300
  93.2 4.1 %collective-permute-start.11 = (bf16[4,256,128]{2,1,0:T(8,128)(2,1)}, bf16[4,256,128]{2,1,0:T(8,128)(2,1)}, u32[]{:S(2)}, u32[]{:S(2)}) collective-permute-start(bf16[4,256,128]{2,1,0:T(8,128)(2,1)} %gather_fusion.9), channel_id=1, source_target_pairs={{0,128},{128,256},{256,384},{384,0},{1,129},{129,257},{257,385},{3... | collective-permute-start | bytes 786440 | tf_op jit(solution)/shard_map/ppermute | solution.py:300
  97.3 8.3 %all-to-all-done.3.stream_ref = bf16[8,2,128,256]{3,2,1,0:T(8,128)(2,1)S(1)} async-done(((bf16[8,2,128,256]{3,2,1,0:T(8,128)(2,1)}), bf16[8,2,128,256]{3,2,1,0:T(8,128)(2,1)S(1)}, u32[]{:S(2)}, u32[]{:S(2)}) %all-to-all-start.3) | async-done | bytes 1048608 | tf_op jit(solution)/shard_map/all_to_all | solution.py:392
  107.8 3.1 %forward.1 = (f32[1024,256]{1,0:T(8,128)S(1)}, f32[8,2,1024]{2,1,0:T(2,128)}) custom-call(s32[1]{0:T(128)} %bitcast.30.side_ref, bf16[1024,2048]{1,0:T(8,128)(2,1)S(1)} %bitcast.64, bf16[2048,128]{1,0:T(8,128)(2,1)S(1)} %bitcast.68, bf16[2048,128]{1,0:T(8,128)(2,1)S(1)} %collective-permute-done.10.other_ref, ...), custom_call_target="tpu_custom_call" | custom-call | flops 1073741824 | bytes 7340032 | tf_op jit(solution)/shard_map/forward/pallas_call | solution.py:135
  111.9 3.4 %all-to-all-start.4 = ((f32[8,2,1024]{2,1,0:T(2,128)}), f32[8,2,1024]{2,1,0:T(2,128)S(1)}, u32[]{:S(2)}, u32[]{:S(2)}) async-start(f32[8,2,1024]{2,1,0:T(2,128)} %get-tuple-element.119), calls=%async_computation.4 | async-start | bytes 131072 | tf_op jit(solution)/shard_map/all_to_all | solution.py:260
  115.3 3.0 %conditional.3 = (bf16[8,2,256,128]{3,2,1,0:T(8,128)(2,1)}) conditional(s32[]{:T(128)} %convert_element_type.18, (s32[8]{0:T(128)S(1)}, s32[8]{0:T(128)S(1)}, s32[8]{0:T(128)S(1)}, bf16[16,256,128]{2,1,0:T(8,128)(2,1)S(1)}, bf16[4,256,128]{2,1,0:T(8,128)(2,1)}, /*index=5*/bf16[4,256,128]{2,1,0:T(8,128)(2,1)}, ...), branch_computations={%region_5.6_spmd, %region_6.7_spmd} | conditional | flops 3320 | bytes 23082876 | solution.py:350
  115.3 2.9 %choose.6 = bf16[8,2,256,128]{3,2,1,0:T(8,128)(2,1)} custom-call(s32[8]{0:T(128)S(1)} %get-tuple-element.66.which_ref, s32[8]{0:T(128)S(1)} %fusion.start_ref, bf16[16,256,128]{2,1,0:T(8,128)(2,1)S(1)} %get-tuple-element.69.refs_0_, bf16[4,256,128]{2,1,0:T(8,128)(2,1)} %get-tuple-element.70.refs_1_, bf16[4,256,128]{2,1,0:T(8,128)(2,1)} %get-tuple-element.71.refs_2_, ...), custom_call_target="tpu_custom_call" | custom-call | tf_op jit(solution)/shard_map/cond/branch_0_fun/choose/pallas_call | solution.py:324
  118.3 4.1 %all-to-all-done.4.sums_ref = f32[8,2,1024]{2,1,0:T(2,128)S(1)} async-done(((f32[8,2,1024]{2,1,0:T(2,128)}), f32[8,2,1024]{2,1,0:T(2,128)S(1)}, u32[]{:S(2)}, u32[]{:S(2)}) %all-to-all-start.4) | async-done | bytes 65568 | tf_op jit(solution)/shard_map/all_to_all | solution.py:260
  122.4 8.5 %all-to-all-start.5 = ((bf16[8,2,256,128]{3,2,1,0:T(8,128)(2,1)}), bf16[8,2,256,128]{3,2,1,0:T(8,128)(2,1)S(1)}, u32[]{:S(2)}, u32[]{:S(2)}) async-start(bf16[8,2,256,128]{3,2,1,0:T(8,128)(2,1)} %get-tuple-element.153), calls=%async_computation.5 | async-start | bytes 2097152 | tf_op jit(solution)/shard_map/all_to_all | solution.py:264
  134.3 2.7 %backward_first.1 = (f32[1024,128]{1,0:T(8,128)S(1)}, bf16[1024,128]{1,0:T(8,128)(2,1)S(1)}, bf16[256,1024]{1,0:T(8,128)(2,1)S(1)}) custom-call(s32[1]{0:T(128)} %bitcast.30.side_ref, bf16[1024,2048]{1,0:T(8,128)(2,1)S(1)} %bitcast.65, f32[1024,256]{1,0:T(8,128)S(1)} %copy-done.3, f32[1,256]{1,0:T(1,128)S(1)} %fusion.10.gain_ref, ...), custom_call_target="tpu_custom_call" | custom-call | flops 536870912 | bytes 5242880 | tf_op jit(solution)/shard_map/backward_first/pallas_call | solution.py:218
  140.8 3.4 %collective-permute-start.14 = (bf16[1024,128]{1,0:T(8,128)(2,1)S(1)}, bf16[1024,128]{1,0:T(8,128)(2,1)S(1)}, u32[]{:S(2)}, u32[]{:S(2)}) collective-permute-start(bf16[1024,128]{1,0:T(8,128)(2,1)S(1)} %get-tuple-element.125), channel_id=1, source_target_pairs={{0,1},{1,0},{2,3},{3,2},{4,5},{5,4},{6,7},{7,6},{8,9},{9,8},{10,11... | collective-permute-start | bytes 786440 | tf_op jit(solution)/shard_map/ppermute | solution.py:256
  148.6 3.8 %collective-permute-done.14.theirs_ref = bf16[1024,128]{1,0:T(8,128)(2,1)S(1)} collective-permute-done((bf16[1024,128]{1,0:T(8,128)(2,1)S(1)}, bf16[1024,128]{1,0:T(8,128)(2,1)S(1)}, u32[]{:S(2)}, u32[]{:S(2)}) %collective-permute-start.14) | collective-permute-done | bytes 262176 | tf_op jit(solution)/shard_map/ppermute | solution.py:256
  (70 shorter events, 34.2 us)
Async XLA Ops:
  7.2 98.4 %all-gather.3.cloned.1.call-start = ((), (), s32[]{:S(2)}) async-start(), calls=%async_computation.6 | async-start | bytes 4718592 | tf_op jit(solution)/shard_map/all_gather | solution.py:370
  7.9 19.8 %all-to-all-start = ((bf16[8,256,128]{2,1,0:T(8,128)(2,1)}), bf16[8,256,128]{2,1,0:T(8,128)(2,1)S(1)}, u32[]{:S(2)}, u32[]{:S(2)}) async-start(bf16[8,256,128]{2,1,0:T(8,128)(2,1)} %bitcast.78), calls=%async_computation | async-start | bytes 1048576 | tf_op jit(solution)/shard_map/all_to_all | solution.py:264
  27.7 25.0 %all-to-all-start.1 = ((bf16[8,2,256,128]{3,2,1,0:T(8,128)(2,1)}), bf16[8,2,256,128]{3,2,1,0:T(8,128)(2,1)S(1)}, u32[]{:S(2)}, u32[]{:S(2)}) async-start(bf16[8,2,256,128]{3,2,1,0:T(8,128)(2,1)} %pad_maximum_fusion), calls=%async_computation.1 | async-start | bytes 2097152 | tf_op jit(solution)/shard_map/all_to_all | solution.py:264
  32.9 14.6 %collective-permute-start.7 = (bf16[2,256,128]{2,1,0:T(8,128)(2,1)S(1)}, bf16[2,256,128]{2,1,0:T(8,128)(2,1)S(1)}, u32[]{:S(2)}, u32[]{:S(2)}) collective-permute-start(bf16[2,256,128]{2,1,0:T(8,128)(2,1)S(1)} %gather_fusion.7), channel_id=1, source_target_pairs={{0,256},{128,384},{256,0},{384,128},{1,257},{129,385},{257,1},{385... | collective-permute-start | bytes 393224 | tf_op jit(solution)/shard_map/ppermute | solution.py:300
  39.6 13.1 %collective-permute-start.8 = (bf16[2,256,128]{2,1,0:T(8,128)(2,1)S(1)}, bf16[2,256,128]{2,1,0:T(8,128)(2,1)S(1)}, u32[]{:S(2)}, u32[]{:S(2)}) collective-permute-start(bf16[2,256,128]{2,1,0:T(8,128)(2,1)S(1)} %gather_fusion.8), channel_id=1, source_target_pairs={{0,384},{128,0},{256,128},{384,256},{1,385},{129,1},{257,129},{385... | collective-permute-start | bytes 393224 | tf_op jit(solution)/shard_map/ppermute | solution.py:300
  42.2 22.8 %copy-start.4 = (bf16[1,128,2048]{2,1,0:T(8,128)(2,1)S(1)}, bf16[1,128,2048]{2,1,0:T(8,128)(2,1)}, u32[]{:S(2)}) copy-start(bf16[1,128,2048]{2,1,0:T(8,128)(2,1)} %param.14) | copy-start | bytes 1572868
  42.2 22.8 %copy-start.5 = (bf16[1,128,2048]{2,1,0:T(8,128)(2,1)S(1)}, bf16[1,128,2048]{2,1,0:T(8,128)(2,1)}, u32[]{:S(2)}) copy-start(bf16[1,128,2048]{2,1,0:T(8,128)(2,1)} %param.15) | copy-start | bytes 1572868
  42.2 10.5 %collective-permute-start.6 = (bf16[2,256,128]{2,1,0:T(8,128)(2,1)S(1)}, bf16[2,256,128]{2,1,0:T(8,128)(2,1)S(1)}, u32[]{:S(2)}, u32[]{:S(2)}) collective-permute-start(bf16[2,256,128]{2,1,0:T(8,128)(2,1)S(1)} %gather_fusion.6), channel_id=1, source_target_pairs={{0,128},{128,256},{256,384},{384,0},{1,129},{129,257},{257,385},{3... | collective-permute-start | bytes 393224 | tf_op jit(solution)/shard_map/ppermute | solution.py:300
  55.1 14.4 %all-to-all-start.2 = ((bf16[8,256,128]{2,1,0:T(8,128)(2,1)}), bf16[8,256,128]{2,1,0:T(8,128)(2,1)S(1)}, u32[]{:S(2)}, u32[]{:S(2)}) async-start(bf16[8,256,128]{2,1,0:T(8,128)(2,1)} %bitcast.24), calls=%async_computation.2 | async-start | bytes 1048576 | tf_op jit(solution)/shard_map/all_to_all | solution.py:264
  60.0 7.9 %collective-permute-start.9 = (bf16[128]{0:T(256)(128)(2,1)}, bf16[128]{0:T(256)(128)(2,1)S(1)}, u32[]{:S(2)}, u32[]{:S(2)}) collective-permute-start(bf16[128]{0:T(256)(128)(2,1)} %bitcast.81), channel_id=1, source_target_pairs={{0,1},{1,0},{2,3},{3,2},{4,5},{5,4},{6,7},{7,6},{8,9},{9,8},{10,11... | collective-permute-start | bytes 776 | tf_op jit(solution)/shard_map/ppermute | solution.py:256
  69.5 36.1 %all-to-all-start.3 = ((bf16[8,2,128,256]{3,2,1,0:T(8,128)(2,1)}), bf16[8,2,128,256]{3,2,1,0:T(8,128)(2,1)S(1)}, u32[]{:S(2)}, u32[]{:S(2)}) async-start(bf16[8,2,128,256]{3,2,1,0:T(8,128)(2,1)} %pack.1), calls=%async_computation.3 | async-start | bytes 2097152 | tf_op jit(solution)/shard_map/all_to_all | solution.py:392
  76.6 20.7 %collective-permute-start.10 = (bf16[2048,128]{1,0:T(8,128)(2,1)S(1)}, bf16[2048,128]{1,0:T(8,128)(2,1)S(1)}, u32[]{:S(2)}, u32[]{:S(2)}) collective-permute-start(bf16[2048,128]{1,0:T(8,128)(2,1)S(1)} %bitcast.67), channel_id=1, source_target_pairs={{0,1},{1,0},{2,3},{3,2},{4,5},{5,4},{6,7},{7,6},{8,9},{9,8},{10,11... | collective-permute-start | bytes 1572872 | tf_op jit(solution)/shard_map/ppermute | solution.py:256
  82.3 33.0 %collective-permute-start.12 = (bf16[4,256,128]{2,1,0:T(8,128)(2,1)S(1)}, bf16[4,256,128]{2,1,0:T(8,128)(2,1)}, u32[]{:S(2)}, u32[]{:S(2)}) collective-permute-start(bf16[4,256,128]{2,1,0:T(8,128)(2,1)S(1)} %gather_fusion.10), channel_id=1, source_target_pairs={{0,256},{128,384},{256,0},{384,128},{1,257},{129,385},{257,1},{385... | collective-permute-start | bytes 786440 | tf_op jit(solution)/shard_map/ppermute | solution.py:300
  89.8 25.4 %collective-permute-start.13 = (bf16[4,256,128]{2,1,0:T(8,128)(2,1)}, bf16[4,256,128]{2,1,0:T(8,128)(2,1)}, u32[]{:S(2)}, u32[]{:S(2)}) collective-permute-start(bf16[4,256,128]{2,1,0:T(8,128)(2,1)} %gather_fusion.11), channel_id=1, source_target_pairs={{0,384},{128,0},{256,128},{384,256},{1,385},{129,1},{257,129},{385... | collective-permute-start | bytes 786440 | tf_op jit(solution)/shard_map/ppermute | solution.py:300
  93.2 22.1 %collective-permute-start.11 = (bf16[4,256,128]{2,1,0:T(8,128)(2,1)}, bf16[4,256,128]{2,1,0:T(8,128)(2,1)}, u32[]{:S(2)}, u32[]{:S(2)}) collective-permute-start(bf16[4,256,128]{2,1,0:T(8,128)(2,1)} %gather_fusion.9), channel_id=1, source_target_pairs={{0,128},{128,256},{256,384},{384,0},{1,129},{129,257},{257,385},{3... | collective-permute-start | bytes 786440 | tf_op jit(solution)/shard_map/ppermute | solution.py:300
  105.6 2.2 %copy-start = (bf16[1,1024,2048]{2,1,0:T(8,128)(2,1)S(1)}, bf16[1,1024,2048]{2,1,0:T(8,128)(2,1)}, u32[]{:S(2)}) copy-start(bf16[1,1024,2048]{2,1,0:T(8,128)(2,1)} %all-gather.3.cloned.1.call-done) | copy-start | bytes 12582916
  110.9 1.0 copy-start.2
  111.9 10.5 %all-to-all-start.4 = ((f32[8,2,1024]{2,1,0:T(2,128)}), f32[8,2,1024]{2,1,0:T(2,128)S(1)}, u32[]{:S(2)}, u32[]{:S(2)}) async-start(f32[8,2,1024]{2,1,0:T(2,128)} %get-tuple-element.119), calls=%async_computation.4 | async-start | bytes 131072 | tf_op jit(solution)/shard_map/all_to_all | solution.py:260
  122.4 24.4 %all-to-all-start.5 = ((bf16[8,2,256,128]{3,2,1,0:T(8,128)(2,1)}), bf16[8,2,256,128]{3,2,1,0:T(8,128)(2,1)S(1)}, u32[]{:S(2)}, u32[]{:S(2)}) async-start(bf16[8,2,256,128]{3,2,1,0:T(8,128)(2,1)} %get-tuple-element.153), calls=%async_computation.5 | async-start | bytes 2097152 | tf_op jit(solution)/shard_map/all_to_all | solution.py:264
  130.9 2.2 %copy-start.1 = (bf16[1,1024,2048]{2,1,0:T(8,128)(2,1)S(1)}, bf16[1,1024,2048]{2,1,0:T(8,128)(2,1)}, u32[]{:S(2)}) copy-start(bf16[1,1024,2048]{2,1,0:T(8,128)(2,1)} %all-gather.3.cloned.1.call-done) | copy-start | bytes 12582916
  133.1 1.2 copy-start.3
  137.0 9.8 %collective-permute-start.15 = (bf16[1024,128]{1,0:T(8,128)(2,1)S(1)}, bf16[1024,128]{1,0:T(8,128)(2,1)S(1)}, u32[]{:S(2)}, u32[]{:S(2)}) collective-permute-start(bf16[1024,128]{1,0:T(8,128)(2,1)S(1)} %get-tuple-element.127), channel_id=1, source_target_pairs={{0,1},{1,0},{2,3},{3,2},{4,5},{5,4},{6,7},{7,6},{8,9},{9,8},{10,11... | collective-permute-start | bytes 786440 | tf_op jit(solution)/shard_map/ppermute | solution.py:256
  140.8 11.6 %collective-permute-start.14 = (bf16[1024,128]{1,0:T(8,128)(2,1)S(1)}, bf16[1024,128]{1,0:T(8,128)(2,1)S(1)}, u32[]{:S(2)}, u32[]{:S(2)}) collective-permute-start(bf16[1024,128]{1,0:T(8,128)(2,1)S(1)} %get-tuple-element.125), channel_id=1, source_target_pairs={{0,1},{1,0},{2,3},{3,2},{4,5},{5,4},{6,7},{7,6},{8,9},{9,8},{10,11... | collective-permute-start | bytes 786440 | tf_op jit(solution)/shard_map/ppermute | solution.py:256
Sparse Core Ops, SparseCore 0:
  10.1 62.6 all-gather.2

commit v11 on v10

--- a/solution.py
+++ b/solution.py
@@ -336,18 +336,27 @@
     )(which, start, pieces, *received)
 
 
-def across(pieces, received, plan):
+def take(pieces, received, rest, plan):
     kinds = pieces.shape[0] // lax.axis_size("column")
-
-    def take(pieces, received):
-        last = received[0].shape[0] // kinds - 1
-        place = jnp.where(plan["offset"] == 0, plan["column"], jnp.minimum(plan["rank"], last))
-        return choose(pieces, received, plan["offset"], place * kinds, kinds)
-
-    def all_slots(pieces, received):
-        return take(pieces, send_planes(pieces, plan["by_shift"]))
-
-    return lax.cond(plan["most"] >= FEW, all_slots, take, pieces, received)
+    stays, late = plan["offset"] == 0, plan["rank"] >= FEW
+    place = jnp.where(stays, plan["column"], jnp.where(late, plan["rank"] - FEW, plan["rank"]))
+    which = jnp.where(stays | ~late, plan["offset"], plan["offset"] + len(received))
+    return choose(pieces, [*received, *rest], which, place * kinds, kinds)
+
+
+def rest_across(pieces, moments, plan):
+    more = plan["by_shift"][:, FEW:]
+
+    def send(pieces, moments):
+        return send_planes(pieces, more), send_planes(moments, more)
+
+    def skip(pieces, moments):
+        empty = lambda array: [
+            jnp.zeros((more.shape[1] * (array.shape[0] // lax.axis_size("column")),) + array.shape[1:], array.dtype)
+        ] * more.shape[0]
+        return empty(pieces), empty(moments)
+
+    return lax.cond(plan["most"] >= FEW, send, skip, pieces, moments)
 
 
 def local(
@@ -374,11 +383,13 @@
     moments = jnp.stack(
         [array[0].reshape(columns, rows, width) for array in (first_moment, second_moment)], axis=1
     )
-    weights, moments = lax.optimization_barrier((weights, moments))
+    stream = pack(residual[0], upstream[0], lax.axis_size("major"))
+    weights, moments, stream = lax.optimization_barrier((weights, moments, stream))
     moments = spread_columns(moments).reshape(columns * (KINDS - 1), rows, width)
     weights_in = send_planes(weights, few)
     weights_in, moments = lax.optimization_barrier((weights_in, moments))
-    weights = across(weights, weights_in, plan)
+    weights_rest, moments_rest = rest_across(weights, moments, plan)
+    weights = take(weights, weights_in, weights_rest, plan)
     weights, moments = lax.optimization_barrier((weights, moments))
     weights = spread_columns(weights.reshape(columns, rows, width))
     gain_other = swap_minor(norm_gain[0])
@@ -387,7 +398,6 @@
         jnp.concatenate((norm_gain[0], gain_other)),
         jnp.concatenate((gain_other, norm_gain[0])),
     ).astype(jnp.float32)[None, :]
-    stream = pack(residual[0], upstream[0], lax.axis_size("major"))
     weights, stream, gain = lax.optimization_barrier((weights, stream, gain))
     stream = lax.all_to_all(stream, "major", split_axis=0, concat_axis=0, tiled=True)
     weights = weights.reshape(depth, width)
@@ -399,10 +409,11 @@
     hidden, sums = forward(side, gathered, weights, weights_other, gain, stream, inv_scale)
     moments, sums = lax.optimization_barrier((moments, sums))
     sums = sums_of_all(sums)
-    moments = across(moments, moments_in, plan)
+    moments = take(moments, moments_in, moments_rest, plan)
     moments, sums = lax.optimization_barrier((moments, sums))
+    halves = backward(side, gathered, hidden, gain, sums, stream, inv_scale, features)
+    moments, halves[0][0] = lax.optimization_barrier((moments, halves[0][0]))
     moments = spread_columns(moments)
-    halves = backward(side, gathered, hidden, gain, sums, stream, inv_scale, features)
     result = []
     for half, (mine, theirs) in enumerate(halves):
         result = adamw(half, rate_index, weights, moments, mine, swap_minor(theirs), result)

time: 162 us -> 169 us (1.043)
  local copies, waits for them, and re-layouts: 12 us -> 22.8 us
  waiting for transfers between devices: 30.7 us -> 27.1 us
    another operation x0 -> x6, local copies, waits for them, and re-layouts: none -> 5.82 us
    unnamed x12 -> x18, local copies, waits for them, and re-layouts: 6.61 us -> 11.2 us
    ppermute x4, waiting for transfers between devices: 5.78 us -> 1.45 us  [swap_minor(): return lax.ppermute(array, 'minor', [(0, 1), (1, 0)])]
  transfers between devices with their start and end apart: 17 -> 17, of which waited for: 7 -> 7; matrix products, arithmetic and copies ran while one was open for 6% -> 10% of each run, Pallas kernels for 11% -> 9%
where the time goes in v11:
time: 169 us; the launch traced here: 167 us
  starting transfers between devices  77.5 us (46%)
  waiting for transfers between devices  27.1 us (16%)
  local copies, waits for them, and re-layouts  22.8 us (13%)
  Pallas kernels  19.4 us (11%)
  between operations  15.6 us (9%)
  other arithmetic  5.06 us (3%)
    all_to_all x4, starting transfers between devices, spread_columns(): lax.all_to_all(array, 'column', split_axis=0, concat_axis=0, tiled=True)  27.8 us
    ppermute x6, starting transfers between devices, send_plane(): lax.ppermute(pick(pieces, slots[shift - 1]), 'plane', [(i, (i + shift) %...  24.7 us
    ppermute x4, starting transfers between devices, swap_minor(): return lax.ppermute(array, 'minor', [(0, 1), (1, 0)])  14.8 us
    unnamed x18, local copies, waits for them, and re-layouts  11.2 us
    all_to_all x1, waiting for transfers between devices, local(): lax.all_to_all(stream, 'major', split_axis=0, concat_axis=0, tiled=True)  7.72 us
    all_to_all x4, waiting for transfers between devices, spread_columns(): lax.all_to_all(array, 'column', split_axis=0, concat_axis=0, tiled=True)  7.38 us
    all_to_all x1, starting transfers between devices, local(): lax.all_to_all(stream, 'major', split_axis=0, concat_axis=0, tiled=True)  6.83 us
    another operation x6, local copies, waits for them, and re-layouts  5.82 us
  transfers between devices with their start and end apart: 17, of which 7 were waited for; matrix products, arithmetic and copies ran while one was open for 10% of the time, Pallas kernels for 9%

profile of v11, /device:TPU:1, one launch (start us, length us, event | category | flops | bytes accessed | tf_op | source)
XLA Modules:
  0.0 167.5 jit_solution(13586906455605234425)
XLA Ops:
  7.9 10.3 %all-to-all-start = ((bf16[8,256,128]{2,1,0:T(8,128)(2,1)}), bf16[8,256,128]{2,1,0:T(8,128)(2,1)S(1)}, u32[]{:S(2)}, u32[]{:S(2)}) async-start(bf16[8,256,128]{2,1,0:T(8,128)(2,1)} %bitcast.78), calls=%async_computation | async-start | bytes 1048576 | tf_op jit(solution)/shard_map/all_to_all | solution.py:264
  23.4 2.8 %pack.1 = bf16[8,2,128,256]{3,2,1,0:T(8,128)(2,1)} custom-call(bf16[128,2048]{1,0:T(8,128)(2,1)S(1)} %bitcast.71, bf16[128,2048]{1,0:T(8,128)(2,1)S(1)} %bitcast.72), custom_call_target="tpu_custom_call" | custom-call | tf_op jit(solution)/shard_map/pack/pallas_call | solution.py:89
  27.7 4.3 %all-to-all-start.1 = ((bf16[8,2,256,128]{3,2,1,0:T(8,128)(2,1)}), bf16[8,2,256,128]{3,2,1,0:T(8,128)(2,1)S(1)}, u32[]{:S(2)}, u32[]{:S(2)}) async-start(bf16[8,2,256,128]{3,2,1,0:T(8,128)(2,1)} %pad_maximum_fusion), calls=%async_computation.1 | async-start | bytes 2097152 | tf_op jit(solution)/shard_map/all_to_all | solution.py:264
  32.9 6.2 %collective-permute-start.7 = (bf16[2,256,128]{2,1,0:T(8,128)(2,1)S(1)}, bf16[2,256,128]{2,1,0:T(8,128)(2,1)S(1)}, u32[]{:S(2)}, u32[]{:S(2)}) collective-permute-start(bf16[2,256,128]{2,1,0:T(8,128)(2,1)S(1)} %gather_fusion.7), channel_id=1, source_target_pairs={{0,256},{128,384},{256,0},{384,128},{1,257},{129,385},{257,1},{385... | collective-permute-start | bytes 393224 | tf_op jit(solution)/shard_map/ppermute | solution.py:300
  42.2 4.2 %collective-permute-start.6 = (bf16[2,256,128]{2,1,0:T(8,128)(2,1)S(1)}, bf16[2,256,128]{2,1,0:T(8,128)(2,1)S(1)}, u32[]{:S(2)}, u32[]{:S(2)}) collective-permute-start(bf16[2,256,128]{2,1,0:T(8,128)(2,1)S(1)} %gather_fusion.6), channel_id=1, source_target_pairs={{0,128},{128,256},{256,384},{384,0},{1,129},{129,257},{257,385},{3... | collective-permute-start | bytes 393224 | tf_op jit(solution)/shard_map/ppermute | solution.py:300
  47.1 5.6 %collective-permute-done.8.refs_3_ = bf16[2,256,128]{2,1,0:T(8,128)(2,1)S(1)} collective-permute-done((bf16[2,256,128]{2,1,0:T(8,128)(2,1)S(1)}, bf16[2,256,128]{2,1,0:T(8,128)(2,1)S(1)}, u32[]{:S(2)}, u32[]{:S(2)}) %collective-permute-start.8) | collective-permute-done | bytes 131104 | tf_op jit(solution)/shard_map/ppermute | solution.py:300
  52.7 5.8 %conditional.1 = (bf16[6,256,128]{2,1,0:T(8,128)(2,1)}, bf16[6,256,128]{2,1,0:T(8,128)(2,1)}, bf16[6,256,128]{2,1,0:T(8,128)(2,1)}, bf16[12,256,128]{2,1,0:T(8,1...) conditional(s32[]{:T(128)} %convert_element_type.17, () %tuple.24, (s32[3,8]{1,0:T(4,128)S(1)}, ...), branch_computations={%region_3.4_spmd, %region_4.5_spmd} | conditional | flops 6360 | bytes 21260040 | solution.py:359
  58.6 2.4 %choose.2 = bf16[8,1,256,128]{3,2,1,0:T(8,128)(2,1)} custom-call(s32[8]{0:T(128)S(1)} %get-tuple-element.102.which_ref, s32[8]{0:T(128)S(1)} %get-tuple-element.82.start_ref, bf16[8,256,128]{2,1,0:T(8,128)(2,1)S(1)} %all-to-all-done.refs_0_, bf16[2,256,128]{2,1,0:T(8,128)(2,1)S(1)} %collective-permute-done.6.refs_1_, ...), custom_call_target="tpu_custom_call" | custom-call | tf_op jit(solution)/shard_map/choose/pallas_call | solution.py:324
  61.0 4.9 %all-to-all-start.2 = ((bf16[8,256,128]{2,1,0:T(8,128)(2,1)}), bf16[8,256,128]{2,1,0:T(8,128)(2,1)S(1)}, u32[]{:S(2)}, u32[]{:S(2)}) async-start(bf16[8,256,128]{2,1,0:T(8,128)(2,1)} %bitcast.26), calls=%async_computation.2 | async-start | bytes 1048576 | tf_op jit(solution)/shard_map/all_to_all | solution.py:264
  65.8 4.8 %collective-permute-start.9 = (bf16[128]{0:T(256)(128)(2,1)}, bf16[128]{0:T(256)(128)(2,1)S(1)}, u32[]{:S(2)}, u32[]{:S(2)}) collective-permute-start(bf16[128]{0:T(256)(128)(2,1)} %bitcast.81), channel_id=1, source_target_pairs={{0,1},{1,0},{2,3},{3,2},{4,5},{5,4},{6,7},{7,6},{8,9},{9,8},{10,11... | collective-permute-start | bytes 776 | tf_op jit(solution)/shard_map/ppermute | solution.py:256
  72.8 2.5 %all-to-all-done.2 = bf16[8,256,128]{2,1,0:T(8,128)(2,1)S(1)} async-done(((bf16[8,256,128]{2,1,0:T(8,128)(2,1)}), bf16[8,256,128]{2,1,0:T(8,128)(2,1)S(1)}, u32[]{:S(2)}, u32[]{:S(2)}) %all-to-all-start.2) | async-done | bytes 524320 | tf_op jit(solution)/shard_map/all_to_all | solution.py:264
  75.3 6.8 %all-to-all-start.3 = ((bf16[8,2,128,256]{3,2,1,0:T(8,128)(2,1)}), bf16[8,2,128,256]{3,2,1,0:T(8,128)(2,1)S(1)}, u32[]{:S(2)}, u32[]{:S(2)}) async-start(bf16[8,2,128,256]{3,2,1,0:T(8,128)(2,1)} %pack.1), calls=%async_computation.3 | async-start | bytes 2097152 | tf_op jit(solution)/shard_map/all_to_all | solution.py:402
  82.5 4.7 %collective-permute-start.10 = (bf16[2048,128]{1,0:T(8,128)(2,1)S(1)}, bf16[2048,128]{1,0:T(8,128)(2,1)S(1)}, u32[]{:S(2)}, u32[]{:S(2)}) collective-permute-start(bf16[2048,128]{1,0:T(8,128)(2,1)S(1)} %bitcast.67), channel_id=1, source_target_pairs={{0,1},{1,0},{2,3},{3,2},{4,5},{5,4},{6,7},{7,6},{8,9},{9,8},{10,11... | collective-permute-start | bytes 1572872 | tf_op jit(solution)/shard_map/ppermute | solution.py:256
  88.6 6.2 %collective-permute-start.12 = (bf16[4,256,128]{2,1,0:T(8,128)(2,1)}, bf16[4,256,128]{2,1,0:T(8,128)(2,1)S(1)}, u32[]{:S(2)}, u32[]{:S(2)}) collective-permute-start(bf16[4,256,128]{2,1,0:T(8,128)(2,1)} %gather_fusion.10), channel_id=1, source_target_pairs={{0,256},{128,384},{256,0},{384,128},{1,257},{129,385},{257,1},{385... | collective-permute-start | bytes 786440 | tf_op jit(solution)/shard_map/ppermute | solution.py:300
  99.5 4.1 %collective-permute-start.11 = (bf16[4,256,128]{2,1,0:T(8,128)(2,1)}, bf16[4,256,128]{2,1,0:T(8,128)(2,1)}, u32[]{:S(2)}, u32[]{:S(2)}) collective-permute-start(bf16[4,256,128]{2,1,0:T(8,128)(2,1)} %gather_fusion.9), channel_id=1, source_target_pairs={{0,128},{128,256},{256,384},{384,0},{1,129},{129,257},{257,385},{3... | collective-permute-start | bytes 786440 | tf_op jit(solution)/shard_map/ppermute | solution.py:300
  103.6 7.7 %all-to-all-done.3.stream_ref = bf16[8,2,128,256]{3,2,1,0:T(8,128)(2,1)S(1)} async-done(((bf16[8,2,128,256]{3,2,1,0:T(8,128)(2,1)}), bf16[8,2,128,256]{3,2,1,0:T(8,128)(2,1)S(1)}, u32[]{:S(2)}, u32[]{:S(2)}) %all-to-all-start.3) | async-done | bytes 1048608 | tf_op jit(solution)/shard_map/all_to_all | solution.py:402
  113.5 3.2 %forward.1 = (f32[1024,256]{1,0:T(8,128)S(1)}, f32[8,2,1024]{2,1,0:T(2,128)}) custom-call(s32[1]{0:T(128)} %bitcast.30.side_ref, bf16[1024,2048]{1,0:T(8,128)(2,1)S(1)} %bitcast.64, bf16[2048,128]{1,0:T(8,128)(2,1)S(1)} %bitcast.68, bf16[2048,128]{1,0:T(8,128)(2,1)S(1)} %collective-permute-done.10.other_ref, ...), custom_call_target="tpu_custom_call" | custom-call | flops 1073741824 | bytes 7340032 | tf_op jit(solution)/shard_map/forward/pallas_call | solution.py:135
  116.7 3.3 %all-to-all-start.4 = ((f32[8,2,1024]{2,1,0:T(2,128)}), f32[8,2,1024]{2,1,0:T(2,128)S(1)}, u32[]{:S(2)}, u32[]{:S(2)}) async-start(f32[8,2,1024]{2,1,0:T(2,128)} %get-tuple-element.67), calls=%async_computation.4 | async-start | bytes 131072 | tf_op jit(solution)/shard_map/all_to_all | solution.py:260
  120.1 2.9 %choose.3 = bf16[8,2,256,128]{3,2,1,0:T(8,128)(2,1)} custom-call(s32[8]{0:T(128)S(1)} %get-tuple-element.102.which_ref, s32[8]{0:T(128)S(1)} %get-tuple-element.81.start_ref, bf16[16,256,128]{2,1,0:T(8,128)(2,1)} %bitcast.77, bf16[4,256,128]{2,1,0:T(8,128)(2,1)} %collective-permute-done.11.refs_1_, bf16[4,256,128]{2,1,0:T(8,128)(2,1)S(1)} %collective-permute-done.12.refs_2_, ...), custom_call_target="tpu_custom_call" | custom-call | tf_op jit(solution)/shard_map/choose/pallas_call | solution.py:324
  123.0 4.2 %all-to-all-done.4.sums_ref = f32[8,2,1024]{2,1,0:T(2,128)S(1)} async-done(((f32[8,2,1024]{2,1,0:T(2,128)}), f32[8,2,1024]{2,1,0:T(2,128)S(1)}, u32[]{:S(2)}, u32[]{:S(2)}) %all-to-all-start.4) | async-done | bytes 65568 | tf_op jit(solution)/shard_map/all_to_all | solution.py:260
  129.4 2.7 %backward_first.1 = (f32[1024,128]{1,0:T(8,128)S(1)}, bf16[1024,128]{1,0:T(8,128)(2,1)S(1)}, bf16[256,1024]{1,0:T(8,128)(2,1)S(1)}) custom-call(s32[1]{0:T(128)} %bitcast.30.side_ref, bf16[1024,2048]{1,0:T(8,128)(2,1)S(1)} %bitcast.65, f32[1024,256]{1,0:T(8,128)S(1)} %get-tuple-element.69.hidden_ref, f32[1,256]{1,0:T(1,128)S(1)} %fusion.10.gain_ref, ...), custom_call_target="tpu_custom_call" | custom-call | flops 536870912 | bytes 5242880 | tf_op jit(solution)/shard_map/backward_first/pallas_call | solution.py:218
  133.7 8.3 %all-to-all-start.5 = ((bf16[8,2,256,128]{3,2,1,0:T(8,128)(2,1)}), bf16[8,2,256,128]{3,2,1,0:T(8,128)(2,1)S(1)}, u32[]{:S(2)}, u32[]{:S(2)}) async-start(bf16[8,2,256,128]{3,2,1,0:T(8,128)(2,1)} %choose.3), calls=%async_computation.5 | async-start | bytes 2097152 | tf_op jit(solution)/shard_map/all_to_all | solution.py:264
  149.0 3.4 %collective-permute-start.14 = (bf16[1024,128]{1,0:T(8,128)(2,1)S(1)}, bf16[1024,128]{1,0:T(8,128)(2,1)S(1)}, u32[]{:S(2)}, u32[]{:S(2)}) collective-permute-start(bf16[1024,128]{1,0:T(8,128)(2,1)S(1)} %get-tuple-element.75), channel_id=1, source_target_pairs={{0,1},{1,0},{2,3},{3,2},{4,5},{5,4},{6,7},{7,6},{8,9},{9,8},{10,11... | collective-permute-start | bytes 786440 | tf_op jit(solution)/shard_map/ppermute | solution.py:256
  153.0 4.1 %all-to-all-done.5.moments_ref = bf16[8,2,256,128]{3,2,1,0:T(8,128)(2,1)S(1)} async-done(((bf16[8,2,256,128]{3,2,1,0:T(8,128)(2,1)}), bf16[8,2,256,128]{3,2,1,0:T(8,128)(2,1)S(1)}, u32[]{:S(2)}, u32[]{:S(2)}) %all-to-all-start.5) | async-done | bytes 1048608 | tf_op jit(solution)/shard_map/all_to_all | solution.py:264
  (77 shorter events, 42.2 us)
Async XLA Ops:
  7.2 104.2 %all-gather.3.cloned.1.call-start = ((), (), s32[]{:S(2)}) async-start(), calls=%async_computation.6 | async-start | bytes 4718592 | tf_op jit(solution)/shard_map/all_gather | solution.py:379
  7.9 19.8 %all-to-all-start = ((bf16[8,256,128]{2,1,0:T(8,128)(2,1)}), bf16[8,256,128]{2,1,0:T(8,128)(2,1)S(1)}, u32[]{:S(2)}, u32[]{:S(2)}) async-start(bf16[8,256,128]{2,1,0:T(8,128)(2,1)} %bitcast.78), calls=%async_computation | async-start | bytes 1048576 | tf_op jit(solution)/shard_map/all_to_all | solution.py:264
  21.4 1.0 copy-start.5
  22.4 1.0 copy-start.6
  27.7 25.0 %all-to-all-start.1 = ((bf16[8,2,256,128]{3,2,1,0:T(8,128)(2,1)}), bf16[8,2,256,128]{3,2,1,0:T(8,128)(2,1)S(1)}, u32[]{:S(2)}, u32[]{:S(2)}) async-start(bf16[8,2,256,128]{3,2,1,0:T(8,128)(2,1)} %pad_maximum_fusion), calls=%async_computation.1 | async-start | bytes 2097152 | tf_op jit(solution)/shard_map/all_to_all | solution.py:264
  32.9 14.3 %collective-permute-start.7 = (bf16[2,256,128]{2,1,0:T(8,128)(2,1)S(1)}, bf16[2,256,128]{2,1,0:T(8,128)(2,1)S(1)}, u32[]{:S(2)}, u32[]{:S(2)}) collective-permute-start(bf16[2,256,128]{2,1,0:T(8,128)(2,1)S(1)} %gather_fusion.7), channel_id=1, source_target_pairs={{0,256},{128,384},{256,0},{384,128},{1,257},{129,385},{257,1},{385... | collective-permute-start | bytes 393224 | tf_op jit(solution)/shard_map/ppermute | solution.py:300
  39.6 13.1 %collective-permute-start.8 = (bf16[2,256,128]{2,1,0:T(8,128)(2,1)S(1)}, bf16[2,256,128]{2,1,0:T(8,128)(2,1)S(1)}, u32[]{:S(2)}, u32[]{:S(2)}) collective-permute-start(bf16[2,256,128]{2,1,0:T(8,128)(2,1)S(1)} %gather_fusion.8), channel_id=1, source_target_pairs={{0,384},{128,0},{256,128},{384,256},{1,385},{129,1},{257,129},{385... | collective-permute-start | bytes 393224 | tf_op jit(solution)/shard_map/ppermute | solution.py:300
  42.2 10.6 %collective-permute-start.6 = (bf16[2,256,128]{2,1,0:T(8,128)(2,1)S(1)}, bf16[2,256,128]{2,1,0:T(8,128)(2,1)S(1)}, u32[]{:S(2)}, u32[]{:S(2)}) collective-permute-start(bf16[2,256,128]{2,1,0:T(8,128)(2,1)S(1)} %gather_fusion.6), channel_id=1, source_target_pairs={{0,128},{128,256},{256,384},{384,0},{1,129},{129,257},{257,385},{3... | collective-permute-start | bytes 393224 | tf_op jit(solution)/shard_map/ppermute | solution.py:300
  52.7 45.5 %copy-start.8 = (bf16[8,2,256,128]{3,2,1,0:T(8,128)(2,1)}, bf16[8,2,256,128]{3,2,1,0:T(8,128)(2,1)S(1)}, u32[]{:S(2)}) copy-start(bf16[8,2,256,128]{3,2,1,0:T(8,128)(2,1)S(1)} %all-to-all-done.1) | copy-start | bytes 3145732
  61.0 14.4 %all-to-all-start.2 = ((bf16[8,256,128]{2,1,0:T(8,128)(2,1)}), bf16[8,256,128]{2,1,0:T(8,128)(2,1)S(1)}, u32[]{:S(2)}, u32[]{:S(2)}) async-start(bf16[8,256,128]{2,1,0:T(8,128)(2,1)} %bitcast.26), calls=%async_computation.2 | async-start | bytes 1048576 | tf_op jit(solution)/shard_map/all_to_all | solution.py:264
  65.8 6.2 %collective-permute-start.9 = (bf16[128]{0:T(256)(128)(2,1)}, bf16[128]{0:T(256)(128)(2,1)S(1)}, u32[]{:S(2)}, u32[]{:S(2)}) collective-permute-start(bf16[128]{0:T(256)(128)(2,1)} %bitcast.81), channel_id=1, source_target_pairs={{0,1},{1,0},{2,3},{3,2},{4,5},{5,4},{6,7},{7,6},{8,9},{9,8},{10,11... | collective-permute-start | bytes 776 | tf_op jit(solution)/shard_map/ppermute | solution.py:256
  75.3 36.0 %all-to-all-start.3 = ((bf16[8,2,128,256]{3,2,1,0:T(8,128)(2,1)}), bf16[8,2,128,256]{3,2,1,0:T(8,128)(2,1)S(1)}, u32[]{:S(2)}, u32[]{:S(2)}) async-start(bf16[8,2,128,256]{3,2,1,0:T(8,128)(2,1)} %pack.1), calls=%async_computation.3 | async-start | bytes 2097152 | tf_op jit(solution)/shard_map/all_to_all | solution.py:402
  82.5 21.1 %collective-permute-start.10 = (bf16[2048,128]{1,0:T(8,128)(2,1)S(1)}, bf16[2048,128]{1,0:T(8,128)(2,1)S(1)}, u32[]{:S(2)}, u32[]{:S(2)}) collective-permute-start(bf16[2048,128]{1,0:T(8,128)(2,1)S(1)} %bitcast.67), channel_id=1, source_target_pairs={{0,1},{1,0},{2,3},{3,2},{4,5},{5,4},{6,7},{7,6},{8,9},{9,8},{10,11... | collective-permute-start | bytes 1572872 | tf_op jit(solution)/shard_map/ppermute | solution.py:256
  88.6 31.5 %collective-permute-start.12 = (bf16[4,256,128]{2,1,0:T(8,128)(2,1)}, bf16[4,256,128]{2,1,0:T(8,128)(2,1)S(1)}, u32[]{:S(2)}, u32[]{:S(2)}) collective-permute-start(bf16[4,256,128]{2,1,0:T(8,128)(2,1)} %gather_fusion.10), channel_id=1, source_target_pairs={{0,256},{128,384},{256,0},{384,128},{1,257},{129,385},{257,1},{385... | collective-permute-start | bytes 786440 | tf_op jit(solution)/shard_map/ppermute | solution.py:300
  96.1 24.0 %collective-permute-start.13 = (bf16[4,256,128]{2,1,0:T(8,128)(2,1)}, bf16[4,256,128]{2,1,0:T(8,128)(2,1)}, u32[]{:S(2)}, u32[]{:S(2)}) collective-permute-start(bf16[4,256,128]{2,1,0:T(8,128)(2,1)} %gather_fusion.11), channel_id=1, source_target_pairs={{0,384},{128,0},{256,128},{384,256},{1,385},{129,1},{257,129},{385... | collective-permute-start | bytes 786440 | tf_op jit(solution)/shard_map/ppermute | solution.py:300
  99.5 20.6 %collective-permute-start.11 = (bf16[4,256,128]{2,1,0:T(8,128)(2,1)}, bf16[4,256,128]{2,1,0:T(8,128)(2,1)}, u32[]{:S(2)}, u32[]{:S(2)}) collective-permute-start(bf16[4,256,128]{2,1,0:T(8,128)(2,1)} %gather_fusion.9), channel_id=1, source_target_pairs={{0,128},{128,256},{256,384},{384,0},{1,129},{129,257},{257,385},{3... | collective-permute-start | bytes 786440 | tf_op jit(solution)/shard_map/ppermute | solution.py:300
  111.3 2.2 %copy-start = (bf16[1,1024,2048]{2,1,0:T(8,128)(2,1)S(1)}, bf16[1,1024,2048]{2,1,0:T(8,128)(2,1)}, u32[]{:S(2)}) copy-start(bf16[1,1024,2048]{2,1,0:T(8,128)(2,1)} %all-gather.3.cloned.1.call-done) | copy-start | bytes 12582916
  116.7 10.5 %all-to-all-start.4 = ((f32[8,2,1024]{2,1,0:T(2,128)}), f32[8,2,1024]{2,1,0:T(2,128)S(1)}, u32[]{:S(2)}, u32[]{:S(2)}) async-start(f32[8,2,1024]{2,1,0:T(2,128)} %get-tuple-element.67), calls=%async_computation.4 | async-start | bytes 131072 | tf_op jit(solution)/shard_map/all_to_all | solution.py:260
  127.2 2.2 %copy-start.1 = (bf16[1,1024,2048]{2,1,0:T(8,128)(2,1)S(1)}, bf16[1,1024,2048]{2,1,0:T(8,128)(2,1)}, u32[]{:S(2)}) copy-start(bf16[1,1024,2048]{2,1,0:T(8,128)(2,1)} %all-gather.3.cloned.1.call-done) | copy-start | bytes 12582916
  133.7 23.4 %all-to-all-start.5 = ((bf16[8,2,256,128]{3,2,1,0:T(8,128)(2,1)}), bf16[8,2,256,128]{3,2,1,0:T(8,128)(2,1)S(1)}, u32[]{:S(2)}, u32[]{:S(2)}) async-start(bf16[8,2,256,128]{3,2,1,0:T(8,128)(2,1)} %choose.3), calls=%async_computation.5 | async-start | bytes 2097152 | tf_op jit(solution)/shard_map/all_to_all | solution.py:264
  142.0 11.1 %collective-permute-start.15 = (bf16[1024,128]{1,0:T(8,128)(2,1)}, bf16[1024,128]{1,0:T(8,128)(2,1)S(1)}, u32[]{:S(2)}, u32[]{:S(2)}) collective-permute-start(bf16[1024,128]{1,0:T(8,128)(2,1)} %copy-done.7), channel_id=1, source_target_pairs={{0,1},{1,0},{2,3},{3,2},{4,5},{5,4},{6,7},{7,6},{8,9},{9,8},{10,11... | collective-permute-start | bytes 786440 | tf_op jit(solution)/shard_map/ppermute | solution.py:256
  143.9 2.2 %copy-start.2 = (bf16[1,1024,2048]{2,1,0:T(8,128)(2,1)S(1)}, bf16[1,1024,2048]{2,1,0:T(8,128)(2,1)}, u32[]{:S(2)}) copy-start(bf16[1,1024,2048]{2,1,0:T(8,128)(2,1)} %all-gather.3.cloned.1.call-done) | copy-start | bytes 12582916
  146.1 1.0 copy-start.4
  149.0 9.9 %collective-permute-start.14 = (bf16[1024,128]{1,0:T(8,128)(2,1)S(1)}, bf16[1024,128]{1,0:T(8,128)(2,1)S(1)}, u32[]{:S(2)}, u32[]{:S(2)}) collective-permute-start(bf16[1024,128]{1,0:T(8,128)(2,1)S(1)} %get-tuple-element.75), channel_id=1, source_target_pairs={{0,1},{1,0},{2,3},{3,2},{4,5},{5,4},{6,7},{7,6},{8,9},{9,8},{10,11... | collective-permute-start | bytes 786440 | tf_op jit(solution)/shard_map/ppermute | solution.py:256
  (2 other events, 1.5 us)
Sparse Core Ops, SparseCore 0:
  10.1 62.6 all-gather.2

commit v12 on v11

--- a/solution.py
+++ b/solution.py
@@ -351,10 +351,20 @@
         return send_planes(pieces, more), send_planes(moments, more)
 
     def skip(pieces, moments):
-        empty = lambda array: [
-            jnp.zeros((more.shape[1] * (array.shape[0] // lax.axis_size("column")),) + array.shape[1:], array.dtype)
-        ] * more.shape[0]
-        return empty(pieces), empty(moments)
+        shapes = [
+            jax.ShapeDtypeStruct(
+                (more.shape[1] * (array.shape[0] // lax.axis_size("column")),) + array.shape[1:], array.dtype
+            )
+            for array in (pieces, moments)
+            for _ in range(more.shape[0])
+        ]
+        unused = pl.pallas_call(
+            lambda *refs: None,
+            out_specs=[pl.BlockSpec(memory_space=pl.ANY)] * len(shapes),
+            out_shape=shapes,
+            name="unused",
+        )()
+        return list(unused[: more.shape[0]]), list(unused[more.shape[0] :])
 
     return lax.cond(plan["most"] >= FEW, send, skip, pieces, moments)
 
@@ -411,9 +421,8 @@
     sums = sums_of_all(sums)
     moments = take(moments, moments_in, moments_rest, plan)
     moments, sums = lax.optimization_barrier((moments, sums))
+    moments = spread_columns(moments)
     halves = backward(side, gathered, hidden, gain, sums, stream, inv_scale, features)
-    moments, halves[0][0] = lax.optimization_barrier((moments, halves[0][0]))
-    moments = spread_columns(moments)
     result = []
     for half, (mine, theirs) in enumerate(halves):
         result = adamw(half, rate_index, weights, moments, mine, swap_minor(theirs), result)

time: 169 us -> 161 us (0.953)
  local copies, waits for them, and re-layouts: 22.8 us -> 18.8 us
    another operation x6 -> x0, local copies, waits for them, and re-layouts: 5.82 us -> none
    ppermute x4, waiting for transfers between devices: 1.45 us -> 5.93 us  [swap_minor(): return lax.ppermute(array, 'minor', [(0, 1), (1, 0)])]
    all_to_all x4, waiting for transfers between devices: 7.38 us -> 4.18 us  [spread_columns(): lax.all_to_all(array, 'column', split_axis=0, concat_axis=0, tiled=True)]
    all_to_all x1, waiting for transfers between devices: 7.72 us -> 5.37 us  [local(): lax.all_to_all(stream, 'major', split_axis=0, concat_axis=0, tiled=True)]
    gather x6, local copies, waits for them, and re-layouts: 5.57 us -> 7.87 us  [pick(): pieces[(slots[:, None] * kinds + jnp.arange(kinds, dtype=jnp.int32)).resh...]
    all_to_all x4, starting transfers between devices: 27.8 us -> 25.6 us  [spread_columns(): lax.all_to_all(array, 'column', split_axis=0, concat_axis=0, tiled=True)]
    unnamed x18 -> x20, local copies, waits for them, and re-layouts: 11.2 us -> 10.7 us
  transfers between devices with their start and end apart: 17 -> 17, of which waited for: 7 -> 8; matrix products, arithmetic and copies ran while one was open for 10% -> 8% of each run, Pallas kernels for 9% -> 11%
where the time goes in v12:
time: 161 us; the launch traced here: 160 us
  starting transfers between devices  76.4 us (47%)
  waiting for transfers between devices  25.8 us (16%)
  local copies, waits for them, and re-layouts  18.8 us (12%)
  Pallas kernels  18.6 us (12%)
  between operations  15.6 us (10%)
  other arithmetic  4.29 us (3%)
    all_to_all x4, starting transfers between devices, spread_columns(): lax.all_to_all(array, 'column', split_axis=0, concat_axis=0, tiled=True)  25.6 us
    ppermute x6, starting transfers between devices, send_plane(): lax.ppermute(pick(pieces, slots[shift - 1]), 'plane', [(i, (i + shift) %...  24.7 us
    ppermute x4, starting transfers between devices, swap_minor(): return lax.ppermute(array, 'minor', [(0, 1), (1, 0)])  15.9 us
    unnamed x20, local copies, waits for them, and re-layouts  10.7 us
    gather x6, local copies, waits for them, and re-layouts, pick(): pieces[(slots[:, None] * kinds + jnp.arange(kinds, dtype=jnp.int32)).resh...  7.87 us
    all_to_all x1, starting transfers between devices, local(): lax.all_to_all(stream, 'major', split_axis=0, concat_axis=0, tiled=True)  6.83 us
    ppermute x4, waiting for transfers between devices, swap_minor(): return lax.ppermute(array, 'minor', [(0, 1), (1, 0)])  5.93 us
    ppermute x6, waiting for transfers between devices, send_plane(): lax.ppermute(pick(pieces, slots[shift - 1]), 'plane', [(i, (i + shift) %...  5.59 us
  transfers between devices with their start and end apart: 17, of which 8 were waited for; matrix products, arithmetic and copies ran while one was open for 8% of the time, Pallas kernels for 11%

profile of v12, /device:TPU:1, one launch (start us, length us, event | category | flops | bytes accessed | tf_op | source)
XLA Modules:
  0.0 159.6 jit_solution(10881168361177173445)
XLA Ops:
  7.9 10.3 %all-to-all-start = ((bf16[8,256,128]{2,1,0:T(8,128)(2,1)}), bf16[8,256,128]{2,1,0:T(8,128)(2,1)S(1)}, u32[]{:S(2)}, u32[]{:S(2)}) async-start(bf16[8,256,128]{2,1,0:T(8,128)(2,1)} %bitcast.73), calls=%async_computation | async-start | bytes 1048576 | tf_op jit(solution)/shard_map/all_to_all | solution.py:264
  19.0 2.3 %pad_maximum_fusion = bf16[8,2,256,128]{3,2,1,0:T(8,128)(2,1)} fusion(bf16[8,1,256,128]{3,2,1,0:T(8,128)(2,1)} %bitcast.74, bf16[8,1,256,128]{3,2,1,0:T(8,128)(2,1)} %bitcast.75), kind=kLoop, calls=%fused_computation.36 | loop fusion | flops 524288 | bytes 2097152 | tf_op jit(solution)/shard_map/stack | solution.py:393
  23.4 2.8 %pack.1 = bf16[8,2,128,256]{3,2,1,0:T(8,128)(2,1)} custom-call(bf16[128,2048]{1,0:T(8,128)(2,1)S(1)} %bitcast.71, bf16[128,2048]{1,0:T(8,128)(2,1)S(1)} %bitcast.72), custom_call_target="tpu_custom_call" | custom-call | tf_op jit(solution)/shard_map/pack/pallas_call | solution.py:89
  27.7 5.0 %all-to-all-start.1 = ((bf16[8,2,256,128]{3,2,1,0:T(8,128)(2,1)}), bf16[8,2,256,128]{3,2,1,0:T(8,128)(2,1)}, u32[]{:S(2)}, u32[]{:S(2)}) async-start(bf16[8,2,256,128]{3,2,1,0:T(8,128)(2,1)} %pad_maximum_fusion), calls=%async_computation.1 | async-start | bytes 2097152 | tf_op jit(solution)/shard_map/all_to_all | solution.py:264
  33.5 6.1 %collective-permute-start.7 = (bf16[2,256,128]{2,1,0:T(8,128)(2,1)S(1)}, bf16[2,256,128]{2,1,0:T(8,128)(2,1)S(1)}, u32[]{:S(2)}, u32[]{:S(2)}) collective-permute-start(bf16[2,256,128]{2,1,0:T(8,128)(2,1)S(1)} %gather_fusion.7), channel_id=1, source_target_pairs={{0,256},{128,384},{256,0},{384,128},{1,257},{129,385},{257,1},{385... | collective-permute-start | bytes 393224 | tf_op jit(solution)/shard_map/ppermute | solution.py:300
  42.8 4.2 %collective-permute-start.6 = (bf16[2,256,128]{2,1,0:T(8,128)(2,1)S(1)}, bf16[2,256,128]{2,1,0:T(8,128)(2,1)S(1)}, u32[]{:S(2)}, u32[]{:S(2)}) collective-permute-start(bf16[2,256,128]{2,1,0:T(8,128)(2,1)S(1)} %gather_fusion.6), channel_id=1, source_target_pairs={{0,128},{128,256},{256,384},{384,0},{1,129},{129,257},{257,385},{3... | collective-permute-start | bytes 393224 | tf_op jit(solution)/shard_map/ppermute | solution.py:300
  47.8 5.6 %collective-permute-done.8.refs_3_ = bf16[2,256,128]{2,1,0:T(8,128)(2,1)S(1)} collective-permute-done((bf16[2,256,128]{2,1,0:T(8,128)(2,1)S(1)}, bf16[2,256,128]{2,1,0:T(8,128)(2,1)S(1)}, u32[]{:S(2)}, u32[]{:S(2)}) %collective-permute-start.8) | collective-permute-done | bytes 131104 | tf_op jit(solution)/shard_map/ppermute | solution.py:300
  53.4 2.4 %choose.2 = bf16[8,1,256,128]{3,2,1,0:T(8,128)(2,1)} custom-call(s32[8]{0:T(128)S(1)} %get-tuple-element.98.which_ref, s32[8]{0:T(128)S(1)} %get-tuple-element.78.start_ref, bf16[8,256,128]{2,1,0:T(8,128)(2,1)S(1)} %all-to-all-done.refs_0_, bf16[2,256,128]{2,1,0:T(8,128)(2,1)S(1)} %collective-permute-done.6.refs_1_, ...), custom_call_target="tpu_custom_call" | custom-call | tf_op jit(solution)/shard_map/choose/pallas_call | solution.py:324
  55.8 4.9 %all-to-all-start.2 = ((bf16[8,256,128]{2,1,0:T(8,128)(2,1)}), bf16[8,256,128]{2,1,0:T(8,128)(2,1)S(1)}, u32[]{:S(2)}, u32[]{:S(2)}) async-start(bf16[8,256,128]{2,1,0:T(8,128)(2,1)} %bitcast.26), calls=%async_computation.2 | async-start | bytes 1048576 | tf_op jit(solution)/shard_map/all_to_all | solution.py:264
  60.7 4.8 %collective-permute-start.9 = (bf16[128]{0:T(256)(128)(2,1)S(1)}, bf16[128]{0:T(256)(128)(2,1)S(1)}, u32[]{:S(2)}, u32[]{:S(2)}) collective-permute-start(bf16[128]{0:T(256)(128)(2,1)S(1)} %bitcast.76), channel_id=1, source_target_pairs={{0,1},{1,0},{2,3},{3,2},{4,5},{5,4},{6,7},{7,6},{8,9},{9,8},{10,11... | collective-permute-start | bytes 776 | tf_op jit(solution)/shard_map/ppermute | solution.py:256
  66.8 3.4 %all-to-all-done.2 = bf16[8,256,128]{2,1,0:T(8,128)(2,1)S(1)} async-done(((bf16[8,256,128]{2,1,0:T(8,128)(2,1)}), bf16[8,256,128]{2,1,0:T(8,128)(2,1)S(1)}, u32[]{:S(2)}, u32[]{:S(2)}) %all-to-all-start.2) | async-done | bytes 524320 | tf_op jit(solution)/shard_map/all_to_all | solution.py:264
  70.2 6.8 %all-to-all-start.3 = ((bf16[8,2,128,256]{3,2,1,0:T(8,128)(2,1)}), bf16[8,2,128,256]{3,2,1,0:T(8,128)(2,1)S(1)}, u32[]{:S(2)}, u32[]{:S(2)}) async-start(bf16[8,2,128,256]{3,2,1,0:T(8,128)(2,1)} %pack.1), calls=%async_computation.3 | async-start | bytes 2097152 | tf_op jit(solution)/shard_map/all_to_all | solution.py:412
  77.3 4.8 %collective-permute-start.10 = (bf16[2048,128]{1,0:T(8,128)(2,1)S(1)}, bf16[2048,128]{1,0:T(8,128)(2,1)S(1)}, u32[]{:S(2)}, u32[]{:S(2)}) collective-permute-start(bf16[2048,128]{1,0:T(8,128)(2,1)S(1)} %bitcast.67), channel_id=1, source_target_pairs={{0,1},{1,0},{2,3},{3,2},{4,5},{5,4},{6,7},{7,6},{8,9},{9,8},{10,11... | collective-permute-start | bytes 1572872 | tf_op jit(solution)/shard_map/ppermute | solution.py:256
  84.1 6.2 %collective-permute-start.12 = (bf16[4,256,128]{2,1,0:T(8,128)(2,1)S(1)}, bf16[4,256,128]{2,1,0:T(8,128)(2,1)S(1)}, u32[]{:S(2)}, u32[]{:S(2)}) collective-permute-start(bf16[4,256,128]{2,1,0:T(8,128)(2,1)S(1)} %gather_fusion.10), channel_id=1, source_target_pairs={{0,256},{128,384},{256,0},{384,128},{1,257},{129,385},{257,1},{385... | collective-permute-start | bytes 786440 | tf_op jit(solution)/shard_map/ppermute | solution.py:300
  94.2 2.5 %gather_fusion.9 = bf16[4,256,128]{2,1,0:T(8,128)(2,1)} fusion(bf16[16,256,128]{2,1,0:T(8,128)(2,1)} %bitcast.25.refs_0_, s32[1024]{0:T(1024)S(1)} %pad_clamp_fusion.8), kind=kCustom, calls=%fused_computation.9 | custom fusion | bytes 524304 | tf_op jit(solution)/shard_map/gather | solution.py:295
  96.7 4.1 %collective-permute-start.11 = (bf16[4,256,128]{2,1,0:T(8,128)(2,1)}, bf16[4,256,128]{2,1,0:T(8,128)(2,1)S(1)}, u32[]{:S(2)}, u32[]{:S(2)}) collective-permute-start(bf16[4,256,128]{2,1,0:T(8,128)(2,1)} %gather_fusion.9), channel_id=1, source_target_pairs={{0,128},{128,256},{256,384},{384,0},{1,129},{129,257},{257,385},{3... | collective-permute-start | bytes 786440 | tf_op jit(solution)/shard_map/ppermute | solution.py:300
  100.8 5.4 %all-to-all-done.3.stream_ref = bf16[8,2,128,256]{3,2,1,0:T(8,128)(2,1)S(1)} async-done(((bf16[8,2,128,256]{3,2,1,0:T(8,128)(2,1)}), bf16[8,2,128,256]{3,2,1,0:T(8,128)(2,1)S(1)}, u32[]{:S(2)}, u32[]{:S(2)}) %all-to-all-start.3) | async-done | bytes 1048608 | tf_op jit(solution)/shard_map/all_to_all | solution.py:412
  108.4 3.1 %forward.1 = (f32[1024,256]{1,0:T(8,128)S(1)}, f32[8,2,1024]{2,1,0:T(2,128)}) custom-call(s32[1]{0:T(128)} %bitcast.30.side_ref, bf16[1024,2048]{1,0:T(8,128)(2,1)S(1)} %bitcast.64, bf16[2048,128]{1,0:T(8,128)(2,1)S(1)} %bitcast.68, bf16[2048,128]{1,0:T(8,128)(2,1)S(1)} %collective-permute-done.10.other_ref, ...), custom_call_target="tpu_custom_call" | custom-call | flops 1073741824 | bytes 7340032 | tf_op jit(solution)/shard_map/forward/pallas_call | solution.py:135
  112.5 3.4 %all-to-all-start.4 = ((f32[8,2,1024]{2,1,0:T(2,128)}), f32[8,2,1024]{2,1,0:T(2,128)S(1)}, u32[]{:S(2)}, u32[]{:S(2)}) async-start(f32[8,2,1024]{2,1,0:T(2,128)} %get-tuple-element.65), calls=%async_computation.4 | async-start | bytes 131072 | tf_op jit(solution)/shard_map/all_to_all | solution.py:260
  119.0 4.0 %all-to-all-done.4.sums_ref = f32[8,2,1024]{2,1,0:T(2,128)S(1)} async-done(((f32[8,2,1024]{2,1,0:T(2,128)}), f32[8,2,1024]{2,1,0:T(2,128)S(1)}, u32[]{:S(2)}, u32[]{:S(2)}) %all-to-all-start.4) | async-done | bytes 65568 | tf_op jit(solution)/shard_map/all_to_all | solution.py:260
  123.1 5.4 %all-to-all-start.5 = ((bf16[8,2,256,128]{3,2,1,0:T(8,128)(2,1)}), bf16[8,2,256,128]{3,2,1,0:T(8,128)(2,1)S(1)}, u32[]{:S(2)}, u32[]{:S(2)}) async-start(bf16[8,2,256,128]{3,2,1,0:T(8,128)(2,1)} %copy-done.2), calls=%async_computation.5 | async-start | bytes 2097152 | tf_op jit(solution)/shard_map/all_to_all | solution.py:264
  131.9 2.7 %backward_first.1 = (f32[1024,128]{1,0:T(8,128)S(1)}, bf16[1024,128]{1,0:T(8,128)(2,1)S(1)}, bf16[256,1024]{1,0:T(8,128)(2,1)S(1)}) custom-call(s32[1]{0:T(128)} %bitcast.30.side_ref, bf16[1024,2048]{1,0:T(8,128)(2,1)S(1)} %bitcast.65, f32[1024,256]{1,0:T(8,128)S(1)} %copy-done.4, f32[1,256]{1,0:T(1,128)S(1)} %fusion.10.gain_ref, ...), custom_call_target="tpu_custom_call" | custom-call | flops 536870912 | bytes 5242880 | tf_op jit(solution)/shard_map/backward_first/pallas_call | solution.py:218
  134.6 4.4 %collective-permute-start.15 = (bf16[1024,128]{1,0:T(8,128)(2,1)S(1)}, bf16[1024,128]{1,0:T(8,128)(2,1)S(1)}, u32[]{:S(2)}, u32[]{:S(2)}) collective-permute-start(bf16[1024,128]{1,0:T(8,128)(2,1)S(1)} %get-tuple-element.73), channel_id=1, source_target_pairs={{0,1},{1,0},{2,3},{3,2},{4,5},{5,4},{6,7},{7,6},{8,9},{9,8},{10,11... | collective-permute-start | bytes 786440 | tf_op jit(solution)/shard_map/ppermute | solution.py:256
  148.4 2.5 %collective-permute-done.14.theirs_ref = bf16[1024,128]{1,0:T(8,128)(2,1)S(1)} collective-permute-done((bf16[1024,128]{1,0:T(8,128)(2,1)S(1)}, bf16[1024,128]{1,0:T(8,128)(2,1)S(1)}, u32[]{:S(2)}, u32[]{:S(2)}) %collective-permute-start.14) | collective-permute-done | bytes 262176 | tf_op jit(solution)/shard_map/ppermute | solution.py:256
  (74 shorter events, 36.8 us)
Async XLA Ops:
  7.2 99.0 %all-gather.3.cloned.1.call-start = ((), (), s32[]{:S(2)}) async-start(), calls=%async_computation.6 | async-start | bytes 4718592 | tf_op jit(solution)/shard_map/all_gather | solution.py:389
  7.9 19.8 %all-to-all-start = ((bf16[8,256,128]{2,1,0:T(8,128)(2,1)}), bf16[8,256,128]{2,1,0:T(8,128)(2,1)S(1)}, u32[]{:S(2)}, u32[]{:S(2)}) async-start(bf16[8,256,128]{2,1,0:T(8,128)(2,1)} %bitcast.73), calls=%async_computation | async-start | bytes 1048576 | tf_op jit(solution)/shard_map/all_to_all | solution.py:264
  21.3 1.0 copy-start.7
  27.7 25.7 %all-to-all-start.1 = ((bf16[8,2,256,128]{3,2,1,0:T(8,128)(2,1)}), bf16[8,2,256,128]{3,2,1,0:T(8,128)(2,1)}, u32[]{:S(2)}, u32[]{:S(2)}) async-start(bf16[8,2,256,128]{3,2,1,0:T(8,128)(2,1)} %pad_maximum_fusion), calls=%async_computation.1 | async-start | bytes 2097152 | tf_op jit(solution)/shard_map/all_to_all | solution.py:264
  33.5 14.2 %collective-permute-start.7 = (bf16[2,256,128]{2,1,0:T(8,128)(2,1)S(1)}, bf16[2,256,128]{2,1,0:T(8,128)(2,1)S(1)}, u32[]{:S(2)}, u32[]{:S(2)}) collective-permute-start(bf16[2,256,128]{2,1,0:T(8,128)(2,1)S(1)} %gather_fusion.7), channel_id=1, source_target_pairs={{0,256},{128,384},{256,0},{384,128},{1,257},{129,385},{257,1},{385... | collective-permute-start | bytes 393224 | tf_op jit(solution)/shard_map/ppermute | solution.py:300
  40.3 13.1 %collective-permute-start.8 = (bf16[2,256,128]{2,1,0:T(8,128)(2,1)S(1)}, bf16[2,256,128]{2,1,0:T(8,128)(2,1)S(1)}, u32[]{:S(2)}, u32[]{:S(2)}) collective-permute-start(bf16[2,256,128]{2,1,0:T(8,128)(2,1)S(1)} %gather_fusion.8), channel_id=1, source_target_pairs={{0,384},{128,0},{256,128},{384,256},{1,385},{129,1},{257,129},{385... | collective-permute-start | bytes 393224 | tf_op jit(solution)/shard_map/ppermute | solution.py:300
  42.8 10.6 %collective-permute-start.6 = (bf16[2,256,128]{2,1,0:T(8,128)(2,1)S(1)}, bf16[2,256,128]{2,1,0:T(8,128)(2,1)S(1)}, u32[]{:S(2)}, u32[]{:S(2)}) collective-permute-start(bf16[2,256,128]{2,1,0:T(8,128)(2,1)S(1)} %gather_fusion.6), channel_id=1, source_target_pairs={{0,128},{128,256},{256,384},{384,0},{1,129},{129,257},{257,385},{3... | collective-permute-start | bytes 393224 | tf_op jit(solution)/shard_map/ppermute | solution.py:300
  53.4 7.3 %copy-start.9 = (bf16[1,128]{1,0:T(2,128)(2,1)S(1)}, bf16[1,128]{1,0:T(2,128)(2,1)}, u32[]{:S(2)}) copy-start(bf16[1,128]{1,0:T(2,128)(2,1)} %param.14) | copy-start | bytes 772
  55.8 14.4 %all-to-all-start.2 = ((bf16[8,256,128]{2,1,0:T(8,128)(2,1)}), bf16[8,256,128]{2,1,0:T(8,128)(2,1)S(1)}, u32[]{:S(2)}, u32[]{:S(2)}) async-start(bf16[8,256,128]{2,1,0:T(8,128)(2,1)} %bitcast.26), calls=%async_computation.2 | async-start | bytes 1048576 | tf_op jit(solution)/shard_map/all_to_all | solution.py:264
  60.7 6.1 %collective-permute-start.9 = (bf16[128]{0:T(256)(128)(2,1)S(1)}, bf16[128]{0:T(256)(128)(2,1)S(1)}, u32[]{:S(2)}, u32[]{:S(2)}) collective-permute-start(bf16[128]{0:T(256)(128)(2,1)S(1)} %bitcast.76), channel_id=1, source_target_pairs={{0,1},{1,0},{2,3},{3,2},{4,5},{5,4},{6,7},{7,6},{8,9},{9,8},{10,11... | collective-permute-start | bytes 776 | tf_op jit(solution)/shard_map/ppermute | solution.py:256
  70.2 36.0 %all-to-all-start.3 = ((bf16[8,2,128,256]{3,2,1,0:T(8,128)(2,1)}), bf16[8,2,128,256]{3,2,1,0:T(8,128)(2,1)S(1)}, u32[]{:S(2)}, u32[]{:S(2)}) async-start(bf16[8,2,128,256]{3,2,1,0:T(8,128)(2,1)} %pack.1), calls=%async_computation.3 | async-start | bytes 2097152 | tf_op jit(solution)/shard_map/all_to_all | solution.py:412
  77.3 23.5 %collective-permute-start.10 = (bf16[2048,128]{1,0:T(8,128)(2,1)S(1)}, bf16[2048,128]{1,0:T(8,128)(2,1)S(1)}, u32[]{:S(2)}, u32[]{:S(2)}) collective-permute-start(bf16[2048,128]{1,0:T(8,128)(2,1)S(1)} %bitcast.67), channel_id=1, source_target_pairs={{0,1},{1,0},{2,3},{3,2},{4,5},{5,4},{6,7},{7,6},{8,9},{9,8},{10,11... | collective-permute-start | bytes 1572872 | tf_op jit(solution)/shard_map/ppermute | solution.py:256
  84.1 31.8 %collective-permute-start.12 = (bf16[4,256,128]{2,1,0:T(8,128)(2,1)S(1)}, bf16[4,256,128]{2,1,0:T(8,128)(2,1)S(1)}, u32[]{:S(2)}, u32[]{:S(2)}) collective-permute-start(bf16[4,256,128]{2,1,0:T(8,128)(2,1)S(1)} %gather_fusion.10), channel_id=1, source_target_pairs={{0,256},{128,384},{256,0},{384,128},{1,257},{129,385},{257,1},{385... | collective-permute-start | bytes 786440 | tf_op jit(solution)/shard_map/ppermute | solution.py:300
  92.1 23.7 %collective-permute-start.13 = (bf16[4,256,128]{2,1,0:T(8,128)(2,1)S(1)}, bf16[4,256,128]{2,1,0:T(8,128)(2,1)S(1)}, u32[]{:S(2)}, u32[]{:S(2)}) collective-permute-start(bf16[4,256,128]{2,1,0:T(8,128)(2,1)S(1)} %gather_fusion.11), channel_id=1, source_target_pairs={{0,384},{128,0},{256,128},{384,256},{1,385},{129,1},{257,129},{385... | collective-permute-start | bytes 786440 | tf_op jit(solution)/shard_map/ppermute | solution.py:300
  96.7 19.1 %collective-permute-start.11 = (bf16[4,256,128]{2,1,0:T(8,128)(2,1)}, bf16[4,256,128]{2,1,0:T(8,128)(2,1)S(1)}, u32[]{:S(2)}, u32[]{:S(2)}) collective-permute-start(bf16[4,256,128]{2,1,0:T(8,128)(2,1)} %gather_fusion.9), channel_id=1, source_target_pairs={{0,128},{128,256},{256,384},{384,0},{1,129},{129,257},{257,385},{3... | collective-permute-start | bytes 786440 | tf_op jit(solution)/shard_map/ppermute | solution.py:300
  106.2 2.2 %copy-start = (bf16[1,1024,2048]{2,1,0:T(8,128)(2,1)S(1)}, bf16[1,1024,2048]{2,1,0:T(8,128)(2,1)}, u32[]{:S(2)}) copy-start(bf16[1,1024,2048]{2,1,0:T(8,128)(2,1)} %all-gather.3.cloned.1.call-done) | copy-start | bytes 12582916
  112.5 10.6 %all-to-all-start.4 = ((f32[8,2,1024]{2,1,0:T(2,128)}), f32[8,2,1024]{2,1,0:T(2,128)S(1)}, u32[]{:S(2)}, u32[]{:S(2)}) async-start(f32[8,2,1024]{2,1,0:T(2,128)} %get-tuple-element.65), calls=%async_computation.4 | async-start | bytes 131072 | tf_op jit(solution)/shard_map/all_to_all | solution.py:260
  123.1 22.5 %all-to-all-start.5 = ((bf16[8,2,256,128]{3,2,1,0:T(8,128)(2,1)}), bf16[8,2,256,128]{3,2,1,0:T(8,128)(2,1)S(1)}, u32[]{:S(2)}, u32[]{:S(2)}) async-start(bf16[8,2,256,128]{3,2,1,0:T(8,128)(2,1)} %copy-done.2), calls=%async_computation.5 | async-start | bytes 2097152 | tf_op jit(solution)/shard_map/all_to_all | solution.py:264
  128.5 2.2 %copy-start.1 = (bf16[1,1024,2048]{2,1,0:T(8,128)(2,1)S(1)}, bf16[1,1024,2048]{2,1,0:T(8,128)(2,1)}, u32[]{:S(2)}) copy-start(bf16[1,1024,2048]{2,1,0:T(8,128)(2,1)} %all-gather.3.cloned.1.call-done) | copy-start | bytes 12582916
  130.7 1.2 copy-start.4
  134.6 8.9 %copy-start.5 = (f32[1024,128]{1,0:T(8,128)}, f32[1024,128]{1,0:T(8,128)S(1)}, u32[]{:S(2)}) copy-start(f32[1024,128]{1,0:T(8,128)S(1)} %get-tuple-element.72.mine_ref) | copy-start | bytes 1572868
  134.6 11.0 %collective-permute-start.15 = (bf16[1024,128]{1,0:T(8,128)(2,1)S(1)}, bf16[1024,128]{1,0:T(8,128)(2,1)S(1)}, u32[]{:S(2)}, u32[]{:S(2)}) collective-permute-start(bf16[1024,128]{1,0:T(8,128)(2,1)S(1)} %get-tuple-element.73), channel_id=1, source_target_pairs={{0,1},{1,0},{2,3},{3,2},{4,5},{5,4},{6,7},{7,6},{8,9},{9,8},{10,11... | collective-permute-start | bytes 786440 | tf_op jit(solution)/shard_map/ppermute | solution.py:256
  140.9 10.0 %collective-permute-start.14 = (bf16[1024,128]{1,0:T(8,128)(2,1)S(1)}, bf16[1024,128]{1,0:T(8,128)(2,1)S(1)}, u32[]{:S(2)}, u32[]{:S(2)}) collective-permute-start(bf16[1024,128]{1,0:T(8,128)(2,1)S(1)} %get-tuple-element.71), channel_id=1, source_target_pairs={{0,1},{1,0},{2,3},{3,2},{4,5},{5,4},{6,7},{7,6},{8,9},{9,8},{10,11... | collective-permute-start | bytes 786440 | tf_op jit(solution)/shard_map/ppermute | solution.py:256
  145.6 1.0 copy-start.6
  (3 other events, 3.0 us)
Sparse Core Ops, SparseCore 0:
  10.1 62.6 all-gather.2
